TPU v7x, 32 devices: a whole 2x2x4 slice. The times are simulated.
32 devices in a mesh: seq: 32 (over z, y, x, core).
Axes of the slice: x: 2, y: 2, z: 4, core: 2. Of those that a mesh axis runs over, the one named last changes fastest.
Arguments:
- byte_acts: bfloat16 [16384, 1024], P('seq'), may hold values from -6 to 6
- resets: int32 [2048], P('seq'), may hold values from 0 to 1, as said below
- out_grad: bfloat16 [16384, 1024], P('seq'), may hold values from -6 to 6
- patch_weight: bfloat16 [8192, 1024], P('seq'), may hold values from -0.0625 to 0.0625
- patch_gain: bfloat16 [1024], P('seq'), may hold values from 0.5 to 1.5
- mixer_in: bfloat16 [1024, 4384], P('seq'), may hold values from -0.1875 to 0.1875
- conv_weight: bfloat16 [4, 2304], P(None, 'seq'), may hold values from -3 to 3
- conv_bias: bfloat16 [2304], P('seq'), may hold values from -3 to 3
- head_params: float32 [3, 32], replicated, may hold values from -10 to 2
- mixer_gain: bfloat16 [2048], P('seq'), may hold values from 0.5 to 1.5
- mixer_out: bfloat16 [2048, 1024], P('seq'), may hold values from -0.125 to 0.125
- unpatch_weight: bfloat16 [1024, 8192], P('seq'), may hold values from -0.1875 to 0.1875
- attn_gain: bfloat16 [1024], P('seq'), may hold values from 0.5 to 1.5
- qkv_weight: bfloat16 [1024, 3072], P('seq'), may hold values from -0.1875 to 0.1875
- attn_out: bfloat16 [1024, 1024], P('seq'), may hold values from -0.375 to 0.375
- ffn_gain: bfloat16 [1024], P('seq'), may hold values from 0.5 to 1.5
- gate_up: bfloat16 [1024, 8192], P('seq'), may hold values from -0.1875 to 0.1875
- down_weight: bfloat16 [4096, 1024], P('seq'), may hold values from -0.09375 to 0.09375
Outputs:
- layer_out: bfloat16 [16384, 1024], P('seq')
- input_grad: bfloat16 [16384, 1024], P('seq')
- grad_patch: float32 [8192, 1024], P('seq')
- grad_patch_gain: float32 [1024], P('seq')
- grad_mixer_in: float32 [1024, 4384], P('seq')
- grad_conv_weight: float32 [4, 2304], P(None, 'seq')
- grad_conv_bias: float32 [2304], P('seq')
- grad_head: float32 [3, 32], replicated
- grad_mixer_gain: float32 [2048], P('seq')
- grad_mixer_out: float32 [2048, 1024], P('seq')
- grad_unpatch: float32 [1024, 8192], P('seq')
- grad_attn_gain: float32 [1024], P('seq')
- grad_qkv: float32 [1024, 3072], P('seq')
- grad_attn_out: float32 [1024, 1024], P('seq')
- grad_ffn_gain: float32 [1024], P('seq')
- grad_gate_up: float32 [1024, 8192], P('seq')
- grad_down: float32 [4096, 1024], P('seq')
Inputs may be any that keep to these rules, and one draw needn't show every extreme that they name: resets[0] = 1; one document begins within the first 64 patches and ends within the last 64; shorter documents lie before and after it.
All inputs are finite; a program needn't handle non-finite values.
Results may differ from a plain program's by a relative error of at most 0.035.
Values may be sent and summed in bfloat16 or wider, within the bound.
A program may use at most 640 MiB of HBM per device.

v0:
```python
import functools

import jax
import jax.numpy as jnp
from jax import lax
from jax.sharding import PartitionSpec as P

D = 1024
PATCH = 8
MHEADS = 32
MHEAD_DIM = 64
DI = 2048
NSTATE = 128
CONV = 4
AHEADS = 16
AHEAD_DIM = 64
FF = 4096
CONV_CH = 2304


EPS = 1e-05
HIGH = lax.Precision.HIGHEST


def passed_along(block, axis, distance):
    devices = range(lax.axis_size(axis))
    route = [(i - distance, i) for i in devices if i - distance in devices]
    return lax.ppermute(block, axis, route)


def carried_in(value, axis, join, neutral):
    count, mine = (lax.axis_size(axis), lax.axis_index(axis))
    pieces = jax.tree.map(lambda part: lax.all_gather(part, axis), value)
    total = jax.tree.map(
        lambda part, zero: jnp.full_like(part, 0) + jnp.asarray(zero, part.dtype), value, neutral
    )

    def step(position, total):
        longer = join(total, jax.tree.map(lambda part: part[position], pieces))
        return jax.tree.map(lambda new, old: jnp.where(position < mine, new, old), longer, total)

    return lax.fori_loop(0, count - 1, step, total)


def entering(value, axis, join, neutral):
    count = lax.axis_size(axis)
    place = lax.axis_index(axis)
    ahead = count - 1 - place
    gathered = jax.tree.map(
        lambda a, kind: lax.all_gather(a.astype(kind), axis),
        value,
        jax.tree.map(lambda a: jnp.bfloat16 if a.dtype == jnp.float32 else a.dtype, value),
    )
    state = jax.tree.map(lambda a, e: jnp.zeros_like(a) + jnp.asarray(e, a.dtype), value, neutral)

    def one(step, state):
        source = count - 1 - step
        return join(
            state,
            jax.tree.map(
                lambda a, own: lax.dynamic_index_in_dim(a, source, 0, False).astype(own.dtype),
                gathered,
                value,
            ),
        )

    return lax.fori_loop(0, ahead, one, state)


def rounding_tools():

    def lower_value(v):
        return lax.optimization_barrier(v.astype(jnp.bfloat16)).astype(jnp.float32)

    lowered = jax.custom_vjp(lower_value)

    def lower_keep(v):
        return (lowered(v), None)

    def lower_pass(kept, grad):
        return (grad,)

    lowered.defvjp(lower_keep, lower_pass)

    def same_value(v):
        return v

    back_lowered = jax.custom_vjp(same_value)

    def same_keep(v):
        return (v, None)

    def grad_lower(kept, grad):
        return (lower_value(grad),)

    back_lowered.defvjp(same_keep, grad_lower)

    def matmul_value(matrix, second):
        return jnp.dot(
            matrix.astype(jnp.bfloat16),
            second.astype(jnp.bfloat16),
            preferred_element_type=jnp.float32,
        )

    bf_product = jax.custom_vjp(matmul_value)

    def matmul_keep(matrix, second):
        return (
            matmul_value(matrix, second),
            (matrix.astype(jnp.bfloat16), second.astype(jnp.bfloat16)),
        )

    def matmul_back(kept, grad):
        left_low, right_low = kept
        grad_low = grad.astype(jnp.bfloat16)
        left_grad = jnp.dot(grad_low, right_low.T, preferred_element_type=jnp.float32)
        right_grad = jnp.dot(left_low.T, grad_low, preferred_element_type=jnp.float32)
        return (left_grad, right_grad)

    bf_product.defvjp(matmul_keep, matmul_back)
    return (lowered, back_lowered, bf_product)


def rms_scale(values, gain_vec):
    return values * lax.rsqrt(jnp.mean(values * values, axis=-1, keepdims=True) + EPS) * gain_vec


def global_front(patches, patch_weight, patch_gain, mixer_in):
    lowered, back_lowered, bf_product = rounding_tools()
    embedded = back_lowered(bf_product(patches, patch_weight))
    normed = lowered(rms_scale(embedded, patch_gain))
    projected = back_lowered(bf_product(normed, mixer_in))
    gate_z = projected[:, :DI]
    conv_in = lowered(projected[:, DI : DI + CONV_CH])
    dt_raw = projected[:, DI + CONV_CH :]
    return (embedded, gate_z, conv_in, dt_raw)


def tap_masks(flags_ext, row_count):
    not_reset = 1.0 - flags_ext.astype(jnp.float32)
    validity = [jnp.ones((row_count,), jnp.float32)]
    for offset in range(1, CONV):
        validity.append(validity[-1] * not_reset[CONV - offset : CONV - offset + row_count])
    return validity


def conv_apply(conv_ext, conv_weight, conv_bias, validity, row_count):
    summed = conv_bias + conv_ext[CONV - 1 : CONV - 1 + row_count] * conv_weight[0]
    for offset in range(1, CONV):
        summed = (
            summed
            + validity[offset][:, None]
            * conv_ext[CONV - 1 - offset : CONV - 1 - offset + row_count]
            * conv_weight[offset]
        )
    return jax.nn.silu(summed)


def block_parts(conv_out, dt_raw, head_params, starts):
    row_count = conv_out.shape[0]
    values = conv_out[:, :DI].reshape(row_count, MHEADS, MHEAD_DIM)
    key_rows = conv_out[:, DI : DI + NSTATE]
    queries = conv_out[:, DI + NSTATE :]
    step_size = jax.nn.softplus(dt_raw + head_params[0])
    cumlog = jnp.cumsum(-step_size * jnp.exp(head_params[1]), axis=0)
    segment = jnp.cumsum(starts, axis=0, dtype=jnp.int32)
    return (values, key_rows, queries, step_size, cumlog, segment)


def block_state(conv_out, dt_raw, head_params, starts):
    values, key_rows, queries, step_size, cumlog, segment = block_parts(
        conv_out, dt_raw, head_params, starts
    )
    same_doc = (segment == segment[-1]).astype(jnp.float32)
    weighting = jnp.exp(cumlog[-1][None, :] - cumlog) * same_doc[:, None] * step_size
    state_out = jnp.einsum("rh,rhp,rn->hpn", weighting, values, key_rows, precision=HIGH)
    decay_total = jnp.exp(cumlog[-1]) * (segment[-1] == 0).astype(jnp.float32)
    return (state_out, decay_total)


def block_output(conv_out, dt_raw, head_params, state_in, starts):
    values, key_rows, queries, step_size, cumlog, segment = block_parts(
        conv_out, dt_raw, head_params, starts
    )
    position = jnp.arange(conv_out.shape[0])
    causal = (position[:, None] >= position[None, :]) & (segment[:, None] == segment[None, :])
    log_gaps = jnp.where(causal[:, :, None], cumlog[:, None, :] - cumlog[None, :, :], 0.0)
    decays = jnp.exp(log_gaps) * causal[:, :, None].astype(jnp.float32)
    scores = jnp.dot(queries, key_rows.T, precision=HIGH)
    mixing = scores[:, :, None] * decays * step_size[None, :, :]
    within = jnp.einsum("tsh,shp->thp", mixing, values, precision=HIGH)
    inflow = jnp.exp(cumlog) * (segment == 0).astype(jnp.float32)[:, None]
    carried = jnp.einsum("tn,hpn->thp", queries, state_in, precision=HIGH) * inflow[:, :, None]
    skipped = head_params[2][None, :, None] * values
    return (within + carried + skipped).reshape(conv_out.shape[0], DI)


def global_tail(mixer_y, gate_z, embedded, mixer_gain, mixer_out, unpatch_weight, byte_acts):
    lowered, back_lowered, bf_product = rounding_tools()
    gated_norm = lowered(rms_scale(mixer_y * jax.nn.silu(gate_z), mixer_gain))
    branch = back_lowered(bf_product(gated_norm, mixer_out))
    hidden = lowered(embedded + branch)
    byte_slots = back_lowered(bf_product(hidden, unpatch_weight))
    return byte_acts + byte_slots.reshape(-1, D)


def local_section(stream, attn_gain, qkv_weight, attn_out, ffn_gain, gate_up, down_weight):
    lowered, back_lowered, bf_product = rounding_tools()
    row_count = stream.shape[0]
    normed = lowered(rms_scale(stream, attn_gain))
    triple = lowered(back_lowered(bf_product(normed, qkv_weight)))
    triple = triple.reshape(row_count // PATCH, PATCH, 3, AHEADS, AHEAD_DIM)
    queries = triple[:, :, 0]
    key_rows = triple[:, :, 1]
    value_rows = triple[:, :, 2]
    scores = back_lowered(jnp.einsum("bqhd,bkhd->bhqk", queries, key_rows) * AHEAD_DIM ** (-0.5))
    position = jnp.arange(PATCH)
    causal = position[:, None] >= position[None, :]
    attn_probs = jax.nn.softmax(jnp.where(causal, scores, -1e30), axis=-1)
    mixed_heads = lowered(
        back_lowered(jnp.einsum("bhqk,bkhd->bqhd", lowered(attn_probs), value_rows))
    )
    stream = stream + back_lowered(bf_product(mixed_heads.reshape(row_count, D), attn_out))
    normed = lowered(rms_scale(stream, ffn_gain))
    gate_both = back_lowered(bf_product(normed, gate_up))
    hidden = lowered(jax.nn.silu(gate_both[:, :FF]) * gate_both[:, FF:])
    return stream + back_lowered(bf_product(hidden, down_weight))


def combine_decay(earlier, later):
    return (earlier[0] * later[0], later[0][:, None, None] * earlier[1] + later[1])


def local(
    byte_acts,
    resets,
    out_grad,
    patch_weight,
    patch_gain,
    mixer_in,
    conv_weight,
    conv_bias,
    head_params,
    mixer_gain,
    mixer_out,
    unpatch_weight,
    attn_gain,
    qkv_weight,
    attn_out,
    ffn_gain,
    gate_up,
    down_weight,
):
    global_set = (
        lax.all_gather(patch_weight, "seq", axis=0, tiled=True),
        lax.all_gather(patch_gain, "seq", axis=0, tiled=True),
        lax.all_gather(mixer_in, "seq", axis=0, tiled=True),
        lax.all_gather(conv_weight, "seq", axis=1, tiled=True),
        lax.all_gather(conv_bias, "seq", axis=0, tiled=True),
        lax.all_gather(mixer_gain, "seq", axis=0, tiled=True),
        lax.all_gather(mixer_out, "seq", axis=0, tiled=True),
        lax.all_gather(unpatch_weight, "seq", axis=0, tiled=True),
    )
    global_wide = [piece.astype(jnp.float32) for piece in global_set]
    byte_wide = byte_acts.astype(jnp.float32)
    patches = byte_wide.reshape(-1, PATCH * D)
    patch_rows = patches.shape[0]
    front_out, front_back = jax.vjp(
        global_front, patches, global_wide[0], global_wide[1], global_wide[2]
    )
    embedded, gate_z, conv_in, dt_raw = front_out
    not_reset = 1.0 - resets.astype(jnp.float32)
    keep_tail = jnp.concatenate(
        [jnp.cumprod(not_reset[patch_rows - CONV + 2 :][::-1])[::-1], jnp.ones((1,), jnp.float32)]
    )
    tail_sent = (conv_in[patch_rows - CONV + 1 :] * keep_tail[:, None]).astype(jnp.bfloat16)
    halo_rows = passed_along(tail_sent, "seq", 1)
    flags_ext = jnp.concatenate([jnp.zeros((CONV - 1,), jnp.int32), resets])
    validity = tap_masks(flags_ext, patch_rows)
    conv_ext = jnp.concatenate([halo_rows.astype(jnp.float32), conv_in])
    conv_out, conv_back = jax.vjp(
        functools.partial(conv_apply, validity=validity, row_count=patch_rows),
        conv_ext,
        global_wide[3],
        global_wide[4],
    )
    state_parts, state_back = jax.vjp(
        functools.partial(block_state, starts=resets), conv_out, dt_raw, head_params
    )
    local_state, decay_total = state_parts
    identity = (
        jnp.ones((MHEADS,), jnp.float32),
        jnp.zeros((MHEADS, MHEAD_DIM, NSTATE), jnp.float32),
    )
    state_in = carried_in((decay_total, local_state), "seq", combine_decay, identity)[1]
    mixer_y, output_back = jax.vjp(
        functools.partial(block_output, starts=resets), conv_out, dt_raw, head_params, state_in
    )
    stream, tail_back = jax.vjp(
        global_tail,
        mixer_y,
        gate_z,
        embedded,
        global_wide[5],
        global_wide[6],
        global_wide[7],
        byte_wide,
    )
    local_set = (
        lax.all_gather(attn_gain, "seq", axis=0, tiled=True),
        lax.all_gather(qkv_weight, "seq", axis=0, tiled=True),
        lax.all_gather(attn_out, "seq", axis=0, tiled=True),
        lax.all_gather(ffn_gain, "seq", axis=0, tiled=True),
        lax.all_gather(gate_up, "seq", axis=0, tiled=True),
        lax.all_gather(down_weight, "seq", axis=0, tiled=True),
    )
    local_wide = [piece.astype(jnp.float32) for piece in local_set]
    layer_out = local_section(
        stream,
        local_wide[0],
        local_wide[1],
        local_wide[2],
        local_wide[3],
        local_wide[4],
        local_wide[5],
    )
    local_set = (
        lax.all_gather(attn_gain, "seq", axis=0, tiled=True),
        lax.all_gather(qkv_weight, "seq", axis=0, tiled=True),
        lax.all_gather(attn_out, "seq", axis=0, tiled=True),
        lax.all_gather(ffn_gain, "seq", axis=0, tiled=True),
        lax.all_gather(gate_up, "seq", axis=0, tiled=True),
        lax.all_gather(down_weight, "seq", axis=0, tiled=True),
    )
    local_wide = [piece.astype(jnp.float32) for piece in local_set]
    _, local_back = jax.vjp(
        local_section,
        stream,
        local_wide[0],
        local_wide[1],
        local_wide[2],
        local_wide[3],
        local_wide[4],
        local_wide[5],
    )
    local_grads = local_back(out_grad.astype(jnp.float32))
    local_shares = (
        lax.psum_scatter(local_grads[1], "seq", scatter_dimension=0, tiled=True),
        lax.psum_scatter(local_grads[2], "seq", scatter_dimension=0, tiled=True),
        lax.psum_scatter(local_grads[3], "seq", scatter_dimension=0, tiled=True),
        lax.psum_scatter(local_grads[4], "seq", scatter_dimension=0, tiled=True),
        lax.psum_scatter(local_grads[5], "seq", scatter_dimension=0, tiled=True),
        lax.psum_scatter(local_grads[6], "seq", scatter_dimension=0, tiled=True),
    )
    tail_grads = tail_back(local_grads[0])
    output_grads = output_back(tail_grads[0])
    state_grad = entering((decay_total, output_grads[3]), "seq", combine_decay, identity)[1]
    decay_grad = jnp.sum(state_grad * state_in, axis=(1, 2))
    state_cot = state_back((state_grad, decay_grad))
    conv_cot = conv_back(output_grads[0] + state_cot[0])
    returned = passed_along(conv_cot[0][: CONV - 1], "seq", -1)
    conv_in_grad = conv_cot[0][CONV - 1 :] + jnp.concatenate(
        [jnp.zeros((patch_rows - CONV + 1, CONV_CH), jnp.float32), returned * keep_tail[:, None]]
    )
    front_grads = front_back(
        (tail_grads[2], tail_grads[1], conv_in_grad, output_grads[1] + state_cot[1])
    )
    input_grad = (tail_grads[6] + front_grads[0].reshape(-1, D)).astype(jnp.bfloat16)
    global_shares = (
        lax.psum_scatter(front_grads[1], "seq", scatter_dimension=0, tiled=True),
        lax.psum_scatter(front_grads[2], "seq", scatter_dimension=0, tiled=True),
        lax.psum_scatter(front_grads[3], "seq", scatter_dimension=0, tiled=True),
        lax.psum_scatter(conv_cot[1], "seq", scatter_dimension=1, tiled=True),
        lax.psum_scatter(conv_cot[2], "seq", scatter_dimension=0, tiled=True),
        lax.psum_scatter(tail_grads[3], "seq", scatter_dimension=0, tiled=True),
        lax.psum_scatter(tail_grads[4], "seq", scatter_dimension=0, tiled=True),
        lax.psum_scatter(tail_grads[5], "seq", scatter_dimension=0, tiled=True),
    )
    head_grad = lax.psum(output_grads[2] + state_cot[2], "seq")
    return (
        layer_out.astype(jnp.bfloat16),
        input_grad,
        global_shares[0],
        global_shares[1],
        global_shares[2],
        global_shares[3],
        global_shares[4],
        head_grad,
        global_shares[5],
        global_shares[6],
        global_shares[7],
        local_shares[0],
        local_shares[1],
        local_shares[2],
        local_shares[3],
        local_shares[4],
        local_shares[5],
    )


def solution(mesh):
    placed = (
        P("seq", None),
        P("seq"),
        P("seq", None),
        P("seq", None),
        P("seq"),
        P("seq", None),
        P(None, "seq"),
        P("seq"),
        P(),
        P("seq"),
        P("seq", None),
        P("seq", None),
        P("seq"),
        P("seq", None),
        P("seq", None),
        P("seq"),
        P("seq", None),
        P("seq", None),
    )
    return jax.shard_map(
        local,
        mesh=mesh,
        in_specs=placed,
        out_specs=(
            P("seq", None),
            P("seq", None),
            P("seq", None),
            P("seq"),
            P("seq", None),
            P(None, "seq"),
            P("seq"),
            P(),
            P("seq"),
            P("seq", None),
            P("seq", None),
            P("seq"),
            P("seq", None),
            P("seq", None),
            P("seq"),
            P("seq", None),
            P("seq", None),
        ),
        check_vma=False,
    )
```

profile of v0, /device:TPU:0, one launch (start us, length us, event | category | flops | bytes accessed | tf_op | source)
XLA Modules:
  0.0 3293.7 jit_solution(11389914492530686705)
XLA Ops:
  14.4 43.7 %all-reduce.42 = (bf16[1024]{0:T(1024)(128)(2,1)S(1)}, bf16[2304]{0:T(1024)(128)(2,1)S(1)}, bf16[2048]{0:T(1024)(128)(2,1)S(1)}, bf16[1024]{0:T(1024)(128)(2,1)}, bf16[1024]{0:T(1024)(128)(2,1)}) all-reduce(bf16[1024]{0:T(1024)(128)(2,1)S(1)} %dynamic-update-slice.1, ...), channel_id=1, replica_groups=mesh['seq'=32] {'seq'}, use_global_device_ids=true, to_apply=%add.31 | all-reduce | flops 7424 | bytes 29696
  61.5 41.3 %all-gather.2 = bf16[32,72,4]{1,2,0:T(4,128)(2,1)S(1)} all-gather(bf16[1,72,4]{1,2,0:T(4,128)(2,1)} %bitcast.204), channel_id=1, replica_groups=mesh['seq'=32] {'seq'}, dimensions={0}, use_global_device_ids=true | all-gather | bytes 19008 | tf_op jit(solution)/shard_map/all_gather | solution.py:258
  105.9 23.5 all-gather.16.cloned.1.call-done
  129.4 8.9 multiply_reduce_fusion.22
  138.5 72.8 %all-gather.18.cloned.1.call-done = bf16[1024,4384]{1,0:T(8,128)(2,1)} async-done(((bf16[32,4384]{1,0:T(8,128)(2,1)}), bf16[1024,4384]{1,0:T(8,128)(2,1)}) %all-gather.18.cloned.1.call-update) | async-done | bytes 8978448 | tf_op jit(solution)/shard_map/all_gather | solution.py:257
  211.3 5.3 fusion.115
  233.2 41.2 %all-gather.3 = f32[32,1,32]{2,1,0:T(1,128)S(1)} all-gather(f32[1,1,32]{2,1,0:T(1,128)} %get-tuple-element.401), channel_id=1, replica_groups=mesh['seq'=32] {'seq'}, dimensions={0}, use_global_device_ids=true | all-gather | bytes 4224 | tf_op jit(solution)/shard_map/all_gather | solution.py:33
  277.1 144.6 %all-gather.32.cloned.1.call-done = f32[1024,64,128]{2,1,0:T(8,128)} async-done(((f32[32,64,128]{2,1,0:T(8,128)}), f32[1024,64,128]{2,1,0:T(8,128)}) %all-gather.32.cloned.1.call-update) | async-done | bytes 33554448 | tf_op jit(solution)/shard_map/all_gather | solution.py:33
  421.7 46.9 %while.29 = (s32[]{:T(128)}, f32[32,64,128]{2,1,0:T(8,128)S(1)}, s32[]{:T(128)}, f32[32,32]{1,0:T(8,128)S(1)}, f32[32,32,64,128]{3,2,1,0:T(8,128)}, /*index=5*/s32[]{:T(128)}, s32[]{:T(128)}) while((s32[]{:T(128)}, f32[32,64,128]{2,1,0:T(8,128)S(1)}, s32[]{:T(128)}, f32[32,32]{1,0:T(8,128)S(1)}, f32[32,32,64,128]{3,2,1,0:T(8,128)}, ...), condition=%wide.region_5.7_spmd.clone, body=%wide.region_4.6_spmd.clone.sunk | while | flops 1048580 | bytes 3146217 | solution.py:42
  477.1 7.5 all-gather.20.cloned.1.call-done
  487.7 113.1 %all-gather.22.cloned.1.call-done = bf16[1024,8192]{1,0:T(8,128)(2,1)} async-done(((bf16[32,8192]{1,0:T(8,128)(2,1)}), bf16[1024,8192]{1,0:T(8,128)(2,1)}) %all-gather.22.cloned.1.call-update) | async-done | bytes 16777232 | tf_op jit(solution)/shard_map/all_gather | solution.py:262
  600.8 8.8 fusion.116
  613.4 57.8 %all-gather.24.cloned.1.call-done = bf16[1024,3072]{1,0:T(8,128)(2,1)} async-done(((bf16[32,3072]{1,0:T(8,128)(2,1)}), bf16[1024,3072]{1,0:T(8,128)(2,1)}) %all-gather.24.cloned.1.call-update) | async-done | bytes 6291472 | tf_op jit(solution)/shard_map/all_gather | solution.py:311
  671.2 7.5 convolution_convert_fusion
  678.8 9.0 reshape.409
  687.8 5.6 fusion.112
  695.5 15.9 fusion.113
  720.8 8.2 all-gather.26.cloned.1.call-done
  733.8 111.8 %all-gather.28.cloned.1.call-done = bf16[1024,8192]{1,0:T(8,128)(2,1)} async-done(((bf16[32,8192]{1,0:T(8,128)(2,1)}), bf16[1024,8192]{1,0:T(8,128)(2,1)}) %all-gather.28.cloned.1.call-update) | async-done | bytes 16777232 | tf_op jit(solution)/shard_map/all_gather | solution.py:314
  845.6 15.6 fusion.117
  861.2 62.9 %all-gather.30.cloned.1.call-done = bf16[4096,1024]{1,0:T(8,128)(2,1)} async-done(((bf16[128,1024]{1,0:T(8,128)(2,1)}), bf16[4096,1024]{1,0:T(8,128)(2,1)}) %all-gather.30.cloned.1.call-update) | async-done | bytes 8388624 | tf_op jit(solution)/shard_map/all_gather | solution.py:315
  924.1 21.6 fusion.35
  945.8 9.1 add_convert_fusion
  954.9 15.7 multiply_reduce_fusion.1
  994.5 5.7 add_convert_fusion.1
  1004.8 8.8 convert_element_type.305
  1013.6 7.5 multiply_reduce_fusion.2
  1025.1 12.1 fusion.114
  1047.6 39.6 %all-gather.4 = bf16[32,1,32]{2,1,0:T(2,128)(2,1)S(1)} all-gather(bf16[1,1,32]{2,1,0:T(2,128)(2,1)S(1)} %copy-done.130), channel_id=1, replica_groups=mesh['seq'=32] {'seq'}, dimensions={0}, use_global_device_ids=true | all-gather | bytes 2112 | tf_op jit(solution)/shard_map/all_gather | solution.py:50
  1105.6 55.6 %all-gather.34.cloned.1.call-done = bf16[1024,64,128]{2,1,0:T(8,128)(2,1)} async-done(((bf16[32,64,128]{2,1,0:T(8,128)(2,1)}), bf16[1024,64,128]{2,1,0:T(8,128)(2,1)}) %all-gather.34.cloned.1.call-update) | async-done | bytes 16777232 | tf_op jit(solution)/shard_map/all_gather | solution.py:50
  1161.3 42.0 %while.28 = (s32[]{:T(128)}, f32[32,64,128]{2,1,0:T(8,128)S(1)}, s32[]{:T(128)}, bf16[32,32]{1,0:T(8,128)(2,1)S(1)}, bf16[32,32,64,128]{3,2,1,0:T(8,128)(2,1)}, ...) while((s32[]{:T(128)}, f32[32,64,128]{2,1,0:T(8,128)S(1)}, s32[]{:T(128)}, ...), condition=%wide.region_21.23_spmd, body=%wide.region_20.22_spmd.sunk | while | flops 786470 | bytes 2621907 | solution.py:67
  1224.0 7.2 multiply_reduce_fusion.20
  1231.6 13.3 convolution_bitcast_fusion
  1250.9 8.3 fusion.122
  1266.0 10.4 fusion.125
  1277.7 13.2 fusion.121
  1292.1 18.8 fusion.124
  1311.8 7.7 fusion.119
  1321.1 10.1 add_convert_fusion.3
  1331.2 11.0 fusion.118
  1357.6 351.8 %reduce-scatter.10.cloned.1.call-done = f32[256,1024]{0,1:T(8,128)} async-done(((f32[8192,1024]{0,1:T(8,128)}), f32[256,1024]{0,1:T(8,128)}) %reduce-scatter.10.cloned.1.call-update) | async-done | bytes 1048592 | tf_op jit(solution)/shard_map/reduce_scatter | solution.py:370
  1711.9 149.3 %reduce-scatter.20.cloned.1.call-done = f32[32,1024]{1,0:T(8,128)} async-done(((f32[1024,1024]{1,0:T(8,128)}), f32[32,1024]{1,0:T(8,128)}) %reduce-scatter.20.cloned.1.call-update) | async-done | bytes 131088 | tf_op jit(solution)/shard_map/reduce_scatter | solution.py:350
  1861.1 158.8 %reduce-scatter.18.cloned.1.call-done = f32[32,3072]{1,0:T(8,128)} async-done(((f32[1024,3072]{1,0:T(8,128)}), f32[32,3072]{1,0:T(8,128)}) %reduce-scatter.18.cloned.1.call-update) | async-done | bytes 393232 | tf_op jit(solution)/shard_map/reduce_scatter | solution.py:349
  2019.9 150.8 %reduce-scatter.14.cloned.1.call-done = f32[64,1024]{1,0:T(8,128)} async-done(((f32[2048,1024]{1,0:T(8,128)}), f32[64,1024]{1,0:T(8,128)}) %reduce-scatter.14.cloned.1.call-update) | async-done | bytes 262160 | tf_op jit(solution)/shard_map/reduce_scatter | solution.py:376
  2170.7 181.5 %reduce-scatter.24.cloned.1.call-done = f32[128,1024]{1,0:T(8,128)} async-done(((f32[4096,1024]{1,0:T(8,128)}), f32[128,1024]{1,0:T(8,128)}) %reduce-scatter.24.cloned.1.call-update) | async-done | bytes 524304 | tf_op jit(solution)/shard_map/reduce_scatter | solution.py:353
  2352.2 358.6 %reduce-scatter.16.cloned.1.call-done = f32[32,8192]{1,0:T(8,128)} async-done(((f32[1024,8192]{1,0:T(8,128)}), f32[32,8192]{1,0:T(8,128)}) %reduce-scatter.16.cloned.1.call-update) | async-done | bytes 1048592 | tf_op jit(solution)/shard_map/reduce_scatter | solution.py:377
  2710.8 364.7 %reduce-scatter.22.cloned.1.call-done = f32[32,8192]{1,0:T(8,128)} async-done(((f32[1024,8192]{1,0:T(8,128)}), f32[32,8192]{1,0:T(8,128)}) %reduce-scatter.22.cloned.1.call-update) | async-done | bytes 1048592 | tf_op jit(solution)/shard_map/reduce_scatter | solution.py:352
  3075.5 209.9 %reduce-scatter.12.cloned.1.call-done = f32[32,4384]{1,0:T(8,128)} async-done(((f32[1024,4384]{1,0:T(8,128)}), f32[32,4384]{1,0:T(8,128)}) %reduce-scatter.12.cloned.1.call-update) | async-done | bytes 561168 | tf_op jit(solution)/shard_map/reduce_scatter | solution.py:372
  (599 shorter events, 268.1 us)
Async XLA Ops:
  7.2 122.2 %all-gather.16.cloned.1.call-start = ((), (), s32[]{:S(2)}) async-start(), calls=%async_computation.8 | async-start | bytes 17301504 | tf_op jit(solution)/shard_map/all_gather | solution.py:255
  7.9 203.4 %all-gather.18.cloned.1.call-start = ((), (), s32[]{:S(2)}) async-start(), calls=%async_computation.9 | async-start | bytes 9461760 | tf_op jit(solution)/shard_map/all_gather | solution.py:257
  8.7 413.0 %all-gather.32.cloned.1.call-start = ((), (), s32[]{:S(2)}) async-start(), calls=%async_computation.24 | async-start | bytes 34603008 | tf_op jit(solution)/shard_map/all_gather | solution.py:33
  58.1 80.2 %copy-start.97 = (f32[1024]{0:T(1024)}, f32[1024]{0:T(1024)S(1)}, u32[]{:S(2)}) copy-start(f32[1024]{0:T(1024)S(1)} %convert_element_type.271) | copy-start | bytes 12292
  103.7 113.0 %copy-start.127 = (f32[3]{0:T(128)}, f32[3]{0:T(128)S(1)}, u32[]{:S(2)}) copy-start(f32[3]{0:T(128)S(1)} %pad_maximum_fusion.1) | copy-start | bytes 40
  103.8 116.7 %copy-start.89 = (f32[2304]{0:T(1024)}, f32[2304]{0:T(1024)S(1)}, u32[]{:S(2)}) copy-start(f32[2304]{0:T(1024)S(1)} %get-tuple-element.324) | copy-start | bytes 27652
  103.8 116.7 %copy-start.91 = (f32[2304]{0:T(1024)}, f32[2304]{0:T(1024)S(1)}, u32[]{:S(2)}) copy-start(f32[2304]{0:T(1024)S(1)} %get-tuple-element.325) | copy-start | bytes 27652
  103.8 116.7 %copy-start.93 = (f32[2304]{0:T(1024)}, f32[2304]{0:T(1024)S(1)}, u32[]{:S(2)}) copy-start(f32[2304]{0:T(1024)S(1)} %get-tuple-element.326) | copy-start | bytes 27652
  103.8 116.7 %copy-start.95 = (f32[2304]{0:T(1024)}, f32[2304]{0:T(1024)S(1)}, u32[]{:S(2)}) copy-start(f32[2304]{0:T(1024)S(1)} %get-tuple-element.327) | copy-start | bytes 27652
  104.5 115.2 %copy-start.109 = (f32[64]{0:T(128)}, f32[64]{0:T(128)S(1)}, u32[]{:S(2)}) copy-start(f32[64]{0:T(128)S(1)} %get-tuple-element.412) | copy-start | bytes 772
  104.5 115.2 %copy-start.123 = (f32[64]{0:T(128)}, f32[64]{0:T(128)S(1)}, u32[]{:S(2)}) copy-start(f32[64]{0:T(128)S(1)} %get-tuple-element.411) | copy-start | bytes 772
  104.6 115.9 %copy-start.111 = (f32[64]{0:T(128)}, f32[64]{0:T(128)S(1)}, u32[]{:S(2)}) copy-start(f32[64]{0:T(128)S(1)} %get-tuple-element.381) | copy-start | bytes 772
  104.6 115.9 %copy-start.113 = (f32[64]{0:T(128)}, f32[64]{0:T(128)S(1)}, u32[]{:S(2)}) copy-start(f32[64]{0:T(128)S(1)} %get-tuple-element.382) | copy-start | bytes 772
  104.6 115.9 %copy-start.115 = (f32[64]{0:T(128)}, f32[64]{0:T(128)S(1)}, u32[]{:S(2)}) copy-start(f32[64]{0:T(128)S(1)} %get-tuple-element.413) | copy-start | bytes 772
  105.9 113.1 %copy-start.119 = (f32[32]{0:T(128)}, f32[32]{0:T(128)S(1)}, u32[]{:S(2)}) copy-start(f32[32]{0:T(128)S(1)} %get-tuple-element.407) | copy-start | bytes 388
  105.9 113.1 %copy-start.121 = (f32[32]{0:T(128)}, f32[32]{0:T(128)S(1)}, u32[]{:S(2)}) copy-start(f32[32]{0:T(128)S(1)} %get-tuple-element.408) | copy-start | bytes 388
  138.3 346.3 %copy-start.31 = (f32[64,1024]{1,0:T(8,128)}, f32[64,1024]{1,0:T(8,128)S(1)}, u32[]{:S(2)}) copy-start(f32[64,1024]{1,0:T(8,128)S(1)} %get-tuple-element.415) | copy-start | bytes 786436
  216.8 3.6 collective-permute-start
  221.9 246.8 %copy-start.33 = (f32[64,2304]{1,0:T(8,128)}, f32[64,2304]{1,0:T(8,128)S(1)}, u32[]{:S(2)}) copy-start(f32[64,2304]{1,0:T(8,128)S(1)} %get-tuple-element.379) | copy-start | bytes 1769476
  222.4 199.3 %copy-start.4 = (f32[64,32,64]{2,1,0:T(8,128)}, f32[64,32,64]{2,1,0:T(8,128)S(1)}, u32[]{:S(2)}) copy-start(f32[64,32,64]{2,1,0:T(8,128)S(1)} %reshape.405) | copy-start | bytes 1572868
  225.8 258.9 %all-gather.20.cloned.1.call-start = ((), (), s32[]{:S(2)}) async-start(), calls=%async_computation.10 | async-start | bytes 4325376 | tf_op jit(solution)/shard_map/all_gather | solution.py:261
  226.4 374.4 %all-gather.22.cloned.1.call-start = ((), (), s32[]{:S(2)}) async-start(), calls=%async_computation.11 | async-start | bytes 17301504 | tf_op jit(solution)/shard_map/all_gather | solution.py:262
  227.0 444.3 %all-gather.24.cloned.1.call-start = ((), (), s32[]{:S(2)}) async-start(), calls=%async_computation.12 | async-start | bytes 6488064 | tf_op jit(solution)/shard_map/all_gather | solution.py:311
  227.6 501.5 %all-gather.26.cloned.1.call-start = ((), (), s32[]{:S(2)}) async-start(), calls=%async_computation.13 | async-start | bytes 2162688 | tf_op jit(solution)/shard_map/all_gather | solution.py:312
  228.3 617.3 %all-gather.28.cloned.1.call-start = ((), (), s32[]{:S(2)}) async-start(), calls=%async_computation.14 | async-start | bytes 17301504 | tf_op jit(solution)/shard_map/all_gather | solution.py:314
  229.0 695.1 %all-gather.30.cloned.1.call-start = ((), (), s32[]{:S(2)}) async-start(), calls=%async_computation.15 | async-start | bytes 8650752 | tf_op jit(solution)/shard_map/all_gather | solution.py:315
  229.8 931.4 %all-gather.34.cloned.1.call-start = ((), (), s32[]{:S(2)}) async-start(), calls=%async_computation.25 | async-start | bytes 17301504 | tf_op jit(solution)/shard_map/all_gather | solution.py:50
  230.5 239.2 %copy-start.105 = (pred[64,64]{1,0:T(8,128)(4,1)}, pred[64,64]{1,0:T(8,128)(4,1)S(1)}, u32[]{:S(2)}) copy-start(pred[64,64]{1,0:T(8,128)(4,1)S(1)} %get-tuple-element.409) | copy-start | bytes 12292
  231.1 245.2 %copy-start.79 = (f32[2048]{0:T(1024)}, f32[2048]{0:T(1024)S(1)}, u32[]{:S(2)}) copy-start(f32[2048]{0:T(1024)S(1)} %convert_element_type.283) | copy-start | bytes 24580
  232.5 237.2 %copy-start.77 = (f32[64,32]{0,1:T(8,128)}, f32[64,32]{0,1:T(8,128)S(1)}, u32[]{:S(2)}) copy-start(f32[64,32]{0,1:T(8,128)S(1)} %copy.162) | copy-start | bytes 24580
  275.3 194.5 %copy-start.75 = (f32[64,32]{0,1:T(8,128)}, f32[64,32]{0,1:T(8,128)S(1)}, u32[]{:S(2)}) copy-start(f32[64,32]{0,1:T(8,128)S(1)} %copy.169) | copy-start | bytes 24580
  277.0 192.7 %copy-start.81 = (f32[64,64]{1,0:T(8,128)}, f32[64,64]{1,0:T(8,128)S(1)}, u32[]{:S(2)}) copy-start(f32[64,64]{1,0:T(8,128)S(1)} %fusion.84) | copy-start | bytes 49156
  476.2 133.4 %copy-start.137 = (f32[64]{0:T(128)}, f32[64]{0:T(128)S(1)}, u32[]{:S(2)}) copy-start(f32[64]{0:T(128)S(1)} %get-tuple-element.375) | copy-start | bytes 772
  476.3 133.3 %copy-start.125 = (f32[64]{0:T(128)}, f32[64]{0:T(128)S(1)}, u32[]{:S(2)}) copy-start(f32[64]{0:T(128)S(1)} %fusion.94) | copy-start | bytes 772
  487.7 113.1 %copy-start.60 = (bf16[64,1024]{1,0:T(8,128)(2,1)}, bf16[64,1024]{1,0:T(8,128)(2,1)S(1)}, u32[]{:S(2)}) copy-start(bf16[64,1024]{1,0:T(8,128)(2,1)S(1)} %fusion.24) | copy-start | bytes 393220
  613.1 115.9 %copy-start.6 = (f32[512,1024]{1,0:T(8,128)}, f32[512,1024]{1,0:T(8,128)S(1)}, u32[]{:S(2)}) copy-start(f32[512,1024]{1,0:T(8,128)S(1)} %get-tuple-element.374) | copy-start | bytes 6291460
  733.7 127.6 %copy-start.52 = (bf16[512,1024]{1,0:T(8,128)(2,1)}, bf16[512,1024]{1,0:T(8,128)(2,1)S(1)}, u32[]{:S(2)}) copy-start(bf16[512,1024]{1,0:T(8,128)(2,1)S(1)} %multiply_convert_fusion.1) | copy-start | bytes 3145732
  733.8 190.4 %copy-start.47 = (bf16[512,1024]{1,0:T(8,128)(2,1)S(1)}, bf16[512,1024]{1,0:T(8,128)(2,1)}, u32[]{:S(2)}) copy-start(bf16[512,1024]{1,0:T(8,128)(2,1)} %param.25) | copy-start | bytes 3145732
  1047.5 302.4 %all-reduce.45.cloned.1.call-start = ((), (), s32[]{:S(2)}) async-start(), calls=%async_computation.26 | async-start | bytes 143360
  1218.5 4.1 collective-permute-start.1
  1231.3 478.0 %reduce-scatter.10.cloned.1.call-start = ((), (), s32[]{:S(2)}) async-start(), calls=%async_computation.16 | async-start | bytes 34603008 | tf_op jit(solution)/shard_map/reduce_scatter | solution.py:370
  1244.9 616.3 %reduce-scatter.20.cloned.1.call-start = ((), (), s32[]{:S(2)}) async-start(), calls=%async_computation.21 | async-start | bytes 4325376 | tf_op jit(solution)/shard_map/reduce_scatter | solution.py:350
  1249.7 770.2 %reduce-scatter.18.cloned.1.call-start = ((), (), s32[]{:S(2)}) async-start(), calls=%async_computation.20 | async-start | bytes 12976128 | tf_op jit(solution)/shard_map/reduce_scatter | solution.py:349
  1259.3 911.4 %reduce-scatter.14.cloned.1.call-start = ((), (), s32[]{:S(2)}) async-start(), calls=%async_computation.18 | async-start | bytes 8650752 | tf_op jit(solution)/shard_map/reduce_scatter | solution.py:376
  1264.8 1087.4 %reduce-scatter.24.cloned.1.call-start = ((), (), s32[]{:S(2)}) async-start(), calls=%async_computation.23 | async-start | bytes 17301504 | tf_op jit(solution)/shard_map/reduce_scatter | solution.py:353
  1276.5 1434.3 %reduce-scatter.16.cloned.1.call-start = ((), (), s32[]{:S(2)}) async-start(), calls=%async_computation.19 | async-start | bytes 34603008 | tf_op jit(solution)/shard_map/reduce_scatter | solution.py:377
  1290.9 1784.7 %reduce-scatter.22.cloned.1.call-start = ((), (), s32[]{:S(2)}) async-start(), calls=%async_computation.22 | async-start | bytes 34603008 | tf_op jit(solution)/shard_map/reduce_scatter | solution.py:352
  1310.9 1974.5 %reduce-scatter.12.cloned.1.call-start = ((), (), s32[]{:S(2)}) async-start(), calls=%async_computation.17 | async-start | bytes 18923520 | tf_op jit(solution)/shard_map/reduce_scatter | solution.py:372
  (113 other events, 1416.4 us)
Sparse Core Ops, SparseCore 0:
  10.9 118.4 all-gather.15
  132.3 78.9 all-gather.17
  225.9 195.7 all-gather.31
  424.4 60.1 all-gather.19
  487.4 113.3 all-gather.21
  603.5 67.6 all-gather.23
  674.1 54.8 all-gather.25
  731.9 113.6 all-gather.27
  848.5 75.6 all-gather.29
  1047.6 113.4 all-gather.33
  1231.4 118.4 all-reduce.44
  1352.2 357.1 reduce-scatter.9
  1712.3 148.8 reduce-scatter.19
  1868.6 151.2 reduce-scatter.17
  2022.7 148.0 reduce-scatter.13
  2173.4 178.7 reduce-scatter.23
  2355.0 355.7 reduce-scatter.15
  2713.5 361.9 reduce-scatter.21
  3078.4 207.0 reduce-scatter.11
where the time goes:
time: 3310 us; the launch traced here: 3290 us
  waiting for transfers between devices  2590 us (78%)
  matrix products  267 us (8%)
  blocking collectives  166 us (5%)
  other arithmetic  151 us (5%)
  local copies, waits for them, and re-layouts  94.4 us (3%)
    reduce_scatter x1, waiting for transfers between devices, local(): lax.psum_scatter(local_grads[5], 'seq', scatter_dimension=0, tiled=True)  365 us
    reduce_scatter x1, waiting for transfers between devices, local(): lax.psum_scatter(tail_grads[5], 'seq', scatter_dimension=0, tiled=True)  359 us
    reduce_scatter x1, waiting for transfers between devices, local(): lax.psum_scatter(front_grads[1], 'seq', scatter_dimension=0, tiled=True)  352 us
    reduce_scatter x1, waiting for transfers between devices, local(): lax.psum_scatter(front_grads[3], 'seq', scatter_dimension=0, tiled=True)  210 us
    reduce_scatter x1, waiting for transfers between devices, local(): lax.psum_scatter(local_grads[6], 'seq', scatter_dimension=0, tiled=True)  182 us
    reduce_scatter x1, waiting for transfers between devices, local(): lax.psum_scatter(local_grads[2], 'seq', scatter_dimension=0, tiled=True)  159 us
    reduce_scatter x1, waiting for transfers between devices, local(): lax.psum_scatter(tail_grads[4], 'seq', scatter_dimension=0, tiled=True)  151 us
    reduce_scatter x1, waiting for transfers between devices, local(): lax.psum_scatter(local_grads[3], 'seq', scatter_dimension=0, tiled=True)  149 us
  transfers between devices with their start and end apart: 21, of which 19 were waited for; matrix products, arithmetic and copies ran while one was open for 9% of the time, Pallas kernels for 0%

commit v1 on v0

v1 whole, which is shorter than its diff:
```python
import functools

import jax
import jax.numpy as jnp
import numpy as np
from jax import lax
from jax.experimental import pallas as pl
from jax.experimental.pallas import tpu as pltpu
from jax.sharding import PartitionSpec as P

D = 1024
PATCH = 8
MHEADS = 32
MHEAD_DIM = 64
DI = 2048
NSTATE = 128
CONV = 4
AHEADS = 16
AHEAD_DIM = 64
FF = 4096
CONV_CH = 2304

EPS = 1e-05
HIGH = lax.Precision.HIGHEST
BF = jnp.bfloat16
F32 = jnp.float32


class Ring:
    def __init__(self, n):
        self.n = n
        self.depth = n // 8
        coords = [(i // 8, (i // 4) % 2, (i // 2) % 2, i % 2) for i in range(n)]

        def index(z, y, x, c):
            return ((z * 2 + y) * 2 + x) * 2 + c

        def flip(z, y, x, c, along_x):
            return index(z, y, 1 - x, c) if along_x else index(z, 1 - y, x, c)

        self.core = [(index(*p), index(*p) ^ 1) for p in coords]
        self.first = [(index(*p), flip(*p, p[3] == 0)) for p in coords]
        self.second = [(index(*p), flip(*p, p[3] == 1)) for p in coords]
        self.shift = [
            [(index(*p), index((p[0] + hop) % self.depth, *p[1:])) for p in coords]
            for hop in range(self.depth)
        ]
        table = np.zeros((n, n), np.int32)
        for me, (z, y, x, c) in enumerate(coords):
            place = 0
            for rc in range(2):
                owner = c ^ rc
                for r2 in range(2):
                    for r1 in range(2):
                        rx, ry = (r1, r2) if owner == 0 else (r2, r1)
                        for rz in range(self.depth):
                            table[me, place] = index((z + rz) % self.depth, y ^ ry, x ^ rx, owner)
                            place += 1
        self.table = table

    def order(self):
        return jnp.asarray(self.table)[lax.axis_index("seq")]


def swap(block, route):
    return lax.ppermute(block, "seq", route)


def after(value, earlier):
    return lax.optimization_barrier((value, earlier))[0]


def gather_weights(ring, shards):
    depth, count = ring.depth, len(shards)
    lines, firsts, pieces = [], [], []

    def along_z(place):
        shard = shards[place]
        if place >= 1:
            shard = after(shard, lines[place - 1])
        if place >= 2:
            shard = after(shard, firsts[place - 2])
        hops = [lax.ppermute(shard, "seq", ring.shift[hop]) for hop in range(1, depth)]
        lines.append([shard] + hops[::-1])

    along_z(0)
    for place in range(count):
        near = jnp.concatenate(lines[place], axis=0)
        if place >= 1:
            near = after(near, firsts[place - 1])
        across = swap(near, ring.first)
        firsts.append(across)
        if place + 1 < count:
            along_z(place + 1)
        mine = [near, across, swap(near, ring.second), swap(across, ring.second)]
        pieces.append(mine + [swap(piece, ring.core) for piece in mine])
    return pieces


def assemble_kernel(rows, per_piece, total, slots, table_ref, *refs):
    pieces, out_ref, held, in_sems, out_sems = refs[:-4], refs[-4], refs[-3], refs[-2], refs[-1]

    def load(place):
        source = pieces[place // per_piece].at[pl.ds((place % per_piece) * rows, rows)]
        slot = place % slots
        return pltpu.make_async_copy(source, held.at[slot], in_sems.at[slot])

    def store(place):
        start = pl.multiple_of(table_ref[place] * rows, rows)
        slot = place % slots
        return pltpu.make_async_copy(
            held.at[slot], out_ref.at[pl.ds(start, rows)], out_sems.at[slot]
        )

    lead = slots // 2
    for place in range(total + lead):
        if place < total:
            if place >= slots:
                store(place - slots).wait()
            load(place).start()
        if place >= lead:
            load(place - lead).wait()
            store(place - lead).start()
    for place in range(max(0, total - slots), total):
        store(place).wait()


def assemble(ring, pieces):
    n = ring.n
    per_piece = n // len(pieces)
    rows = pieces[0].shape[0] // per_piece
    columns = pieces[0].shape[1]
    if rows % 16:
        whole = jnp.concatenate(pieces, axis=0).reshape(n, rows, columns)
        back = jnp.argsort(ring.order())
        return jnp.take(whole, back, axis=0).reshape(n * rows, columns)
    slots = min(n, 16)
    return pl.pallas_call(
        functools.partial(assemble_kernel, rows, per_piece, n, slots),
        out_shape=jax.ShapeDtypeStruct((n * rows, columns), pieces[0].dtype),
        in_specs=[pl.BlockSpec(memory_space=pltpu.SMEM)]
        + [pl.BlockSpec(memory_space=pl.ANY)] * len(pieces),
        out_specs=pl.BlockSpec(memory_space=pl.ANY),
        scratch_shapes=[
            pltpu.VMEM((slots, rows, columns), pieces[0].dtype),
            pltpu.SemaphoreType.DMA((slots,)),
            pltpu.SemaphoreType.DMA((slots,)),
        ],
        compiler_params=pltpu.CompilerParams(vmem_limit_bytes=24 * 2**20),
        cost_estimate=pl.CostEstimate(
            flops=0, bytes_accessed=4 * n * rows * columns, transcendentals=0
        ),
    )(ring.order(), *pieces)


def gather_small(ring, vector):
    pieces = gather_weights(ring, [vector[None]])[0]
    return jnp.take(jnp.concatenate(pieces, axis=0), jnp.argsort(ring.order()), axis=0)


def scatter_sum(ring, part, wire):
    n, depth = ring.n, ring.depth
    quarter, eighth = n // 4, n // 8

    def send(block, route):
        return swap(block.astype(wire), route).astype(F32)

    one = send(part(n // 2, n), ring.core)
    two = send(part(quarter, n // 2) + one[quarter:], ring.second)
    three = send(part(eighth, quarter) + one[eighth:quarter] + two[eighth:], ring.first)
    total = (part(0, eighth) + one[:eighth] + two[:eighth] + three).astype(wire)
    held = total[0].astype(F32)
    for hop in range(1, depth):
        held = held + lax.ppermute(total[hop], "seq", ring.shift[hop]).astype(F32)
    return held


def blocks_kernel(count, table_ref, in_ref, out_ref):
    width = in_ref.shape[1] // count

    @pl.loop(0, count)
    def _(place):
        start = pl.multiple_of(table_ref[place] * width, width)
        out_ref[:, pl.ds(pl.multiple_of(place * width, width), width)] = in_ref[:, pl.ds(start, width)]


def column_blocks(ring, left):
    rows, width = left.shape
    n = ring.n
    block = width // n
    if block % 128 == 0:
        return pl.pallas_call(
            functools.partial(blocks_kernel, n),
            out_shape=jax.ShapeDtypeStruct(left.shape, left.dtype),
            in_specs=[
                pl.BlockSpec(memory_space=pltpu.SMEM),
                pl.BlockSpec(memory_space=pltpu.VMEM),
            ],
            out_specs=pl.BlockSpec(memory_space=pltpu.VMEM),
            compiler_params=pltpu.CompilerParams(vmem_limit_bytes=32 * 2**20),
        )(ring.order(), left)
    if rows * width >= 2**18:
        place = jnp.arange(width)
        source = jnp.repeat(ring.order() * block, block) + place % block
        picked = (place[:, None] == source[None, :]).astype(left.dtype)
        return dot(left, picked).astype(left.dtype)
    blocks = left.reshape(rows, n, block)
    return jnp.take(blocks, ring.order(), axis=1).reshape(rows, width)


def weight_grad(ring, left, right):
    width = left.shape[1]
    block = width // ring.n
    ordered = column_blocks(ring, left)

    def part(start, stop):
        product = lax.dot_general(
            ordered[:, start * block : stop * block],
            right,
            (((0,), (0,)), ((), ())),
            preferred_element_type=F32,
        )
        return product.reshape(stop - start, block, right.shape[1])

    return scatter_sum(ring, part, BF)


def dot(left, right):
    return jnp.dot(left, right, preferred_element_type=F32)


def dot_t(left, right):
    return lax.dot_general(left, right, (((1,), (1,)), ((), ())), preferred_element_type=F32)


def rms_scale(values, gain):
    return values * lax.rsqrt(jnp.mean(values * values, axis=-1, keepdims=True) + EPS) * gain


def rms_back(values, gain, grad):
    r = lax.rsqrt(jnp.mean(values * values, axis=-1, keepdims=True) + EPS)
    scaled = gain * grad
    inner = jnp.mean(values * scaled, axis=-1, keepdims=True)
    return r * scaled - values * (r * r * r) * inner, jnp.sum(values * r * grad, axis=0)


def silu(v):
    return v * jax.nn.sigmoid(v)


def silu_slope(v):
    s = jax.nn.sigmoid(v)
    return s * (1.0 + v * (1.0 - s))


def tap_masks(flags_ext, row_count):
    not_reset = 1.0 - flags_ext.astype(F32)
    validity = [jnp.ones((row_count,), F32)]
    for offset in range(1, CONV):
        validity.append(validity[-1] * not_reset[CONV - offset : CONV - offset + row_count])
    return validity


def conv_apply(conv_ext, conv_weight, conv_bias, validity, row_count):
    summed = conv_bias + conv_ext[CONV - 1 : CONV - 1 + row_count] * conv_weight[0]
    for offset in range(1, CONV):
        summed = (
            summed
            + validity[offset][:, None]
            * conv_ext[CONV - 1 - offset : CONV - 1 - offset + row_count]
            * conv_weight[offset]
        )
    return jax.nn.silu(summed)


def block_parts(conv_out, dt_raw, head_params, starts):
    row_count = conv_out.shape[0]
    values = conv_out[:, :DI].reshape(row_count, MHEADS, MHEAD_DIM)
    key_rows = conv_out[:, DI : DI + NSTATE]
    queries = conv_out[:, DI + NSTATE :]
    step_size = jax.nn.softplus(dt_raw + head_params[0])
    cumlog = jnp.cumsum(-step_size * jnp.exp(head_params[1]), axis=0)
    segment = jnp.cumsum(starts, axis=0, dtype=jnp.int32)
    return (values, key_rows, queries, step_size, cumlog, segment)


def block_state(conv_out, dt_raw, head_params, starts):
    values, key_rows, queries, step_size, cumlog, segment = block_parts(
        conv_out, dt_raw, head_params, starts
    )
    same_doc = (segment == segment[-1]).astype(F32)
    weighting = jnp.exp(cumlog[-1][None, :] - cumlog) * same_doc[:, None] * step_size
    state_out = jnp.einsum("rh,rhp,rn->hpn", weighting, values, key_rows, precision=HIGH)
    decay_total = jnp.exp(cumlog[-1]) * (segment[-1] == 0).astype(F32)
    return (state_out, decay_total)


def block_output(conv_out, dt_raw, head_params, state_in, starts):
    values, key_rows, queries, step_size, cumlog, segment = block_parts(
        conv_out, dt_raw, head_params, starts
    )
    position = jnp.arange(conv_out.shape[0])
    causal = (position[:, None] >= position[None, :]) & (segment[:, None] == segment[None, :])
    log_gaps = jnp.where(causal[:, :, None], cumlog[:, None, :] - cumlog[None, :, :], 0.0)
    decays = jnp.exp(log_gaps) * causal[:, :, None].astype(F32)
    scores = jnp.dot(queries, key_rows.T, precision=HIGH)
    mixing = scores[:, :, None] * decays * step_size[None, :, :]
    within = jnp.einsum("tsh,shp->thp", mixing, values, precision=HIGH)
    inflow = jnp.exp(cumlog) * (segment == 0).astype(F32)[:, None]
    carried = jnp.einsum("tn,hpn->thp", queries, state_in, precision=HIGH) * inflow[:, :, None]
    skipped = head_params[2][None, :, None] * values
    return (within + carried + skipped).reshape(conv_out.shape[0], DI)


def state_links(ring, logs, flags):
    n = ring.n
    place = jnp.arange(n)
    between = (place[None, None, :] > place[None, :, None]) & (
        place[None, None, :] < place[:, None, None]
    )
    gap = jnp.sum(jnp.where(between, logs[None, None, :], 0.0), axis=-1)
    cut = jnp.sum(jnp.where(between, flags[None, None, :], 0.0), axis=-1)
    later = place[:, None] > place[None, :]
    return jnp.exp(gap) * (later & (cut == 0)).astype(F32)


def pass_states(ring, states, links):
    n = ring.n
    rows = states.reshape(n, -1, NSTATE).astype(BF)
    spread = lax.all_to_all(rows, "seq", 0, 0, tiled=True)
    summed = jnp.einsum("de,erk->drk", links, spread.astype(F32), precision=HIGH)
    returned = lax.all_to_all(summed.astype(BF), "seq", 0, 0, tiled=True)
    return returned.astype(F32).reshape(MHEADS, MHEAD_DIM, NSTATE)


def attention(queries, key_rows, value_rows):
    scores = jnp.einsum(
        "bqhd,bkhd->bhqk", queries, key_rows, preferred_element_type=F32
    ) * AHEAD_DIM ** (-0.5)
    position = jnp.arange(PATCH)
    causal = position[:, None] >= position[None, :]
    probs = jax.nn.softmax(jnp.where(causal, scores, -1e30), axis=-1)
    mixed = jnp.einsum("bhqk,bkhd->bqhd", probs.astype(BF), value_rows, preferred_element_type=F32)
    return probs, mixed.astype(BF)


def attention_back(queries, key_rows, value_rows, probs, grad):
    d_probs = jnp.einsum("bqhd,bkhd->bhqk", grad, value_rows, preferred_element_type=F32)
    d_values = jnp.einsum("bhqk,bqhd->bkhd", probs.astype(BF), grad, preferred_element_type=F32)
    inner = jnp.sum(probs * d_probs, axis=-1, keepdims=True)
    d_scores = (probs * (d_probs - inner)).astype(BF)
    scale = AHEAD_DIM ** (-0.5)
    d_queries = scale * jnp.einsum("bhqk,bkhd->bqhd", d_scores, key_rows, preferred_element_type=F32)
    d_keys = scale * jnp.einsum("bhqk,bqhd->bkhd", d_scores, queries, preferred_element_type=F32)
    return d_queries, d_keys, d_values


def local(
    byte_acts,
    resets,
    out_grad,
    patch_weight,
    patch_gain,
    mixer_in,
    conv_weight,
    conv_bias,
    head_params,
    mixer_gain,
    mixer_out,
    unpatch_weight,
    attn_gain,
    qkv_weight,
    attn_out,
    ffn_gain,
    gate_up,
    down_weight,
):
    n = lax.axis_size("seq")
    me = lax.axis_index("seq")
    ring = Ring(n)

    def passed_along(block, distance):
        route = [(i - distance, i) for i in range(n) if 0 <= i - distance < n]
        return lax.ppermute(block, "seq", route)

    small = [patch_gain, conv_weight.reshape(-1), conv_bias, mixer_gain, attn_gain, ffn_gain]
    sizes = [piece.shape[0] for piece in small]
    cuts = list(np.cumsum(sizes))
    small_all = gather_small(ring, jnp.concatenate(small)).astype(F32)
    parts = jnp.split(small_all, cuts[:-1], axis=1)
    patch_gain_w = parts[0].reshape(-1)
    conv_weight_w = parts[1].reshape(n, CONV, -1).transpose(1, 0, 2).reshape(CONV, CONV_CH)
    conv_bias_w, mixer_gain_w, attn_gain_w, ffn_gain_w = [p.reshape(-1) for p in parts[2:]]

    shards = [patch_weight, mixer_in, mixer_out, unpatch_weight, qkv_weight, attn_out, gate_up, down_weight]
    wholes = [assemble(ring, pieces) for pieces in gather_weights(ring, shards)]
    patch_w, mixer_in_w, mixer_out_w, unpatch_w, qkv_w, attn_out_w, gate_up_w, down_w = wholes

    byte_wide = byte_acts.astype(F32)
    patches = byte_acts.reshape(-1, PATCH * D)
    patch_rows = patches.shape[0]
    embedded = dot(patches, patch_w)
    normed = rms_scale(embedded, patch_gain_w).astype(BF)
    projected = dot(normed, mixer_in_w)
    gate_z = projected[:, :DI]
    conv_in = projected[:, DI : DI + CONV_CH].astype(BF).astype(F32)
    dt_raw = projected[:, DI + CONV_CH :]

    logs = jnp.sum(-jax.nn.softplus(dt_raw + head_params[0]) * jnp.exp(head_params[1]), axis=0)
    flag = jnp.max(resets).astype(F32)
    links_all = gather_small(ring, jnp.concatenate([logs, flag[None]]))
    head = me * MHEADS // n
    links = state_links(
        ring, lax.dynamic_index_in_dim(links_all[:, :MHEADS], head, 1, False), links_all[:, MHEADS]
    )

    not_reset = 1.0 - resets.astype(F32)
    keep_tail = jnp.concatenate(
        [jnp.cumprod(not_reset[patch_rows - CONV + 2 :][::-1])[::-1], jnp.ones((1,), F32)]
    )
    tail_sent = (conv_in[patch_rows - CONV + 1 :] * keep_tail[:, None]).astype(BF)
    halo_rows = passed_along(tail_sent, 1)
    flags_ext = jnp.concatenate([jnp.zeros((CONV - 1,), jnp.int32), resets])
    validity = tap_masks(flags_ext, patch_rows)
    conv_ext = jnp.concatenate([halo_rows.astype(F32), conv_in])
    conv_out, conv_back = jax.vjp(
        functools.partial(conv_apply, validity=validity, row_count=patch_rows),
        conv_ext,
        conv_weight_w,
        conv_bias_w,
    )
    state_parts, state_back = jax.vjp(
        functools.partial(block_state, starts=resets), conv_out, dt_raw, head_params
    )
    local_state, decay_total = state_parts
    state_in = pass_states(ring, local_state, links)
    mixer_y, output_back = jax.vjp(
        functools.partial(block_output, starts=resets), conv_out, dt_raw, head_params, state_in
    )
    gate_act = silu(gate_z)
    gated = mixer_y * gate_act
    gated_norm = rms_scale(gated, mixer_gain_w).astype(BF)
    branch = dot(gated_norm, mixer_out_w)
    hidden = (embedded + branch).astype(BF)
    stream0 = byte_wide + dot(hidden, unpatch_w).reshape(-1, D)

    rows = stream0.shape[0]
    normed0 = rms_scale(stream0, attn_gain_w).astype(BF)
    triple = dot(normed0, qkv_w).astype(BF)
    triple_parts = triple.reshape(rows // PATCH, PATCH, 3, AHEADS, AHEAD_DIM)
    qkv = [triple_parts[:, :, i] for i in range(3)]
    probs, mixed = attention(*qkv)
    mixed = mixed.reshape(rows, D)
    stream1 = stream0 + dot(mixed, attn_out_w)
    normed1 = rms_scale(stream1, ffn_gain_w).astype(BF)
    gate_both = dot(normed1, gate_up_w)
    gate, up = gate_both[:, :FF], gate_both[:, FF:]
    act = silu(gate)
    hid = (act * up).astype(BF)
    layer_out = (stream1 + dot(hid, down_w)).astype(BF)

    d_out = out_grad.astype(F32)
    g_down = weight_grad(ring, hid, out_grad)
    d_hid = dot_t(out_grad, down_w)
    d_both = jnp.concatenate([d_hid * up * silu_slope(gate), d_hid * act], axis=1).astype(BF)
    g_gate_up = weight_grad(ring, normed1, d_both)
    d_stream1, g_ffn_gain = rms_back(stream1, ffn_gain_w, dot_t(d_both, gate_up_w))
    d_stream1 = d_out + d_stream1
    d_stream1_low = d_stream1.astype(BF)
    g_attn_out = weight_grad(ring, mixed, d_stream1_low)
    d_mixed = dot_t(d_stream1_low, attn_out_w).astype(BF)
    d_qkv = attention_back(*qkv, probs, d_mixed.reshape(rows // PATCH, PATCH, AHEADS, AHEAD_DIM))
    d_triple = jnp.stack(d_qkv, axis=2).astype(BF).reshape(rows, 3 * D)
    g_qkv = weight_grad(ring, normed0, d_triple)
    d_stream0, g_attn_gain = rms_back(stream0, attn_gain_w, dot_t(d_triple, qkv_w))
    d_stream0 = d_stream1 + d_stream0

    d_slots = d_stream0.astype(BF).reshape(patch_rows, PATCH * D)
    g_unpatch = weight_grad(ring, hidden, d_slots)
    d_hidden = dot_t(d_slots, unpatch_w)
    d_branch = d_hidden.astype(BF)
    g_mixer_out = weight_grad(ring, gated_norm, d_branch)
    d_gated, g_mixer_gain = rms_back(gated, mixer_gain_w, dot_t(d_branch, mixer_out_w))
    d_gate_z = d_gated * mixer_y * silu_slope(gate_z)
    output_grads = output_back(d_gated * gate_act)
    state_grad = pass_states(ring, output_grads[3], links.T)
    decay_grad = jnp.sum(state_grad * state_in, axis=(1, 2))
    state_cot = state_back((state_grad, decay_grad))
    conv_cot = conv_back(output_grads[0] + state_cot[0])
    returned = passed_along(conv_cot[0][: CONV - 1], -1)
    d_conv_in = conv_cot[0][CONV - 1 :] + jnp.concatenate(
        [jnp.zeros((patch_rows - CONV + 1, CONV_CH), F32), returned * keep_tail[:, None]]
    )
    d_dt = output_grads[1] + state_cot[1]
    d_projected = jnp.concatenate([d_gate_z, d_conv_in, d_dt], axis=1).astype(BF)
    g_mixer_in = weight_grad(ring, normed, d_projected)
    d_embedded, g_patch_gain = rms_back(embedded, patch_gain_w, dot_t(d_projected, mixer_in_w))
    d_embedded = (d_hidden + d_embedded).astype(BF)
    g_patch = weight_grad(ring, patches, d_embedded)
    input_grad = (d_stream0 + dot_t(d_embedded, patch_w).reshape(-1, D)).astype(BF)

    g_conv_weight = conv_cot[1].reshape(CONV, n, -1).transpose(1, 0, 2).reshape(n, -1)
    g_head = jnp.broadcast_to((output_grads[2] + state_cot[2]).reshape(1, -1), (n, 3 * MHEADS))
    g_small = [g_patch_gain, g_conv_weight, conv_cot[2], g_mixer_gain, g_attn_gain, g_ffn_gain, g_head]
    g_small = jnp.concatenate([piece.reshape(n, -1) for piece in g_small], axis=1)
    terms = jnp.take(g_small, ring.order(), axis=0)
    g_small = scatter_sum(ring, lambda start, stop: terms[start:stop], F32)
    s = jnp.split(g_small, cuts)
    return (
        layer_out,
        input_grad,
        g_patch,
        s[0],
        g_mixer_in,
        s[1].reshape(CONV, -1),
        s[2],
        s[6].reshape(3, MHEADS),
        s[3],
        g_mixer_out,
        g_unpatch,
        s[4],
        g_qkv,
        g_attn_out,
        s[5],
        g_gate_up,
        g_down,
    )


def solution(mesh):
    rows, vector = P("seq", None), P("seq")
    placed = (
        rows, vector, rows, rows, vector, rows, P(None, "seq"), vector, P(),
        vector, rows, rows, vector, rows, rows, vector, rows, rows,
    )
    returned = (
        rows, rows, rows, vector, rows, P(None, "seq"), vector, P(), vector,
        rows, rows, vector, rows, rows, vector, rows, rows,
    )
    return jax.shard_map(
        local, mesh=mesh, in_specs=placed, out_specs=returned, check_vma=False
    )
```

time: 3310 us -> 1490 us (0.45)
  waiting for transfers between devices: 2590 us -> 446 us
  starting transfers between devices: 4.67 us -> 244 us
  blocking collectives: 166 us -> 0 us
  local copies, waits for them, and re-layouts: 94.4 us -> 179 us
  Pallas kernels: 0 us -> 79.9 us
  other arithmetic: 151 us -> 229 us
  matrix products: 267 us -> 302 us
    reduce_scatter x8 -> x0, waiting for transfers between devices: 1930 us -> none  [the longest x1 365 us: local(): lax.psum_scatter(local_grads[5], 'seq', scatter_dimension=0, tiled=True)]
    all_gather x10 -> x0, waiting for transfers between devices: 658 us -> none  [the longest x1 145 us: carried_in(): pieces = jax.tree.map(lambda part: lax.all_gather(part, axis), value)]
    ppermute x2 -> x156, waiting for transfers between devices: 0.01 us -> 435 us  [the longest x97 208 us: swap(): return lax.ppermute(block, 'seq', route)]
    ppermute x2 -> x156, starting transfers between devices: 3.44 us -> 227 us  [the longest x30 82.2 us: along_z(): lax.ppermute(shard, 'seq', ring.shift[hop])]
    convert_element_type x54 -> x49, other arithmetic: 28 us -> 151 us  [the longest x28 110 us: send(): return swap(block.astype(wire), route).astype(F32)]
    all_gather x3 -> x0, blocking collectives: 122 us -> none  [the longest x1 41.3 us: local(): lax.all_gather(conv_weight, 'seq', axis=1, tiled=True)]
    pallas_call x0 -> x10, Pallas kernels: none -> 79.9 us  [the longest x8 77.2 us: assemble(): pl.pallas_call(functools.partial(assemble_kernel, rows, per_piece, n, slo...]
    unnamed x1 -> x0, blocking collectives: 43.7 us -> none
  transfers between devices with their start and end apart: 21 -> 160, of which waited for: 19 -> 46; matrix products, arithmetic and copies ran while one was open for 9% -> 34% of each run, Pallas kernels for 0% -> 4%
where the time goes in v1:
time: 1490 us; the launch traced here: 1480 us
  waiting for transfers between devices  446 us (30%)
  matrix products  302 us (20%)
  starting transfers between devices  244 us (16%)
  other arithmetic  229 us (15%)
  local copies, waits for them, and re-layouts  179 us (12%)
  Pallas kernels  79.9 us (5%)
    ppermute x97, waiting for transfers between devices, swap(): return lax.ppermute(block, 'seq', route)  208 us
    dot_general x32, matrix products, part(): lax.dot_general(ordered[:, start * block:stop * block], right, (((0,), (0...  119 us
    ppermute x27, waiting for transfers between devices, scatter_sum(): held = held + lax.ppermute(total[hop], 'seq', ring.shift[hop]).astype(F32)  117 us
    convert_element_type x28, other arithmetic, send(): return swap(block.astype(wire), route).astype(F32)  110 us
    ppermute x30, waiting for transfers between devices, along_z(): lax.ppermute(shard, 'seq', ring.shift[hop])  109 us
    ppermute x30, starting transfers between devices, along_z(): lax.ppermute(shard, 'seq', ring.shift[hop])  82.2 us
    pallas_call x8, Pallas kernels, assemble(): pl.pallas_call(functools.partial(assemble_kernel, rows, per_piece, n, slo...  77.2 us
    dot_general x8, matrix products, dot_t(): lax.dot_general(left, right, (((1,), (1,)), ((), ())), preferred_element_...  72.4 us
  transfers between devices with their start and end apart: 160, of which 46 were waited for; matrix products, arithmetic and copies ran while one was open for 34% of the time, Pallas kernels for 4%

profile of v1, /device:TPU:0, one launch (start us, length us, event | category | flops | bytes accessed | tf_op | source)
XLA Modules:
  0.0 1484.8 jit_solution(12692713822798621422)
XLA Ops:
  7.9 10.6 collective-permute-done
  18.5 32.3 %collective-permute-done.1 = bf16[256,1024]{1,0:T(8,128)(2,1)S(1)} collective-permute-done((bf16[256,1024]{1,0:T(8,128)(2,1)}, bf16[256,1024]{1,0:T(8,128)(2,1)S(1)}, u32[]{:S(2)}, u32[]{:S(2)}) %collective-permute-start.1) | collective-permute-done | bytes 524320 | tf_op jit(solution)/shard_map/ppermute | solution.py:83
  64.2 10.0 collective-permute-done.21
  104.8 26.1 %collective-permute-done.15 = bf16[4,520]{1,0:T(4,128)(2,1)S(1)} collective-permute-done((bf16[4,520]{1,0:T(4,128)(2,1)S(1)}, bf16[4,520]{1,0:T(4,128)(2,1)S(1)}, u32[]{:S(2)}, u32[]{:S(2)}) %collective-permute-start.15) | collective-permute-done | bytes 4192 | tf_op jit(solution)/shard_map/ppermute | solution.py:66
  136.3 11.9 collective-permute-done.53
  149.2 17.1 %collective-permute-done.52 = bf16[32,8192]{1,0:T(8,128)(2,1)S(1)} collective-permute-done((bf16[32,8192]{1,0:T(8,128)(2,1)S(1)}, bf16[32,8192]{1,0:T(8,128)(2,1)S(1)}, u32[]{:S(2)}, u32[]{:S(2)}) %collective-permute-start.52) | collective-permute-done | bytes 524320 | tf_op jit(solution)/shard_map/ppermute | solution.py:83
  169.8 11.6 collective-permute-start.63
  181.4 8.8 collective-permute-start.62
  212.7 14.6 collective-permute-done.25
  239.4 14.4 collective-permute-start.73
  299.2 12.2 shard_map.314
  311.4 8.9 multiply_reduce_fusion.22
  351.7 9.8 collective-permute-done.34
  394.8 9.2 shard_map.316
  416.1 12.2 collective-permute-done.76.refs_3_
  438.1 10.5 all-to-all-done
  469.4 14.2 shard_map.318
  517.5 12.4 shard_map.317
  529.9 10.1 fusion.218
  546.3 7.9 convolution_convert_fusion.5
  554.3 8.6 reshape.664
  571.9 15.9 %fusion.215 = (f32[64,16,8]{2,1,0:T(8,128)S(1)}, f32[64,16,8,8]{2,3,1,0:T(8,128)S(1)}) fusion(f32[64,16,8,8]{2,3,1,0:T(8,128)S(1)} %fusion.39, pred[8,8]{0,1:T(8,128)(4,1)S(1)} %copy-done.243), kind=kOutput, calls=%fused_computation.501 | output fusion | flops 393223 | bytes 557120 | tf_op jit(solution)/shard_map/sub | solution.py:342
  627.9 14.3 shard_map.320
  642.2 15.9 %fusion.198 = f32[512,8192]{1,0:T(8,128)} fusion(bf16[1024,8192]{1,0:T(8,128)(2,1)} %shard_map.320, f32[512,1024]{1,0:T(8,128)S(1)} %copy-done.105, f32[1024]{0:T(1024)S(1)} %mul.822, f32[512]{0:T(512)S(1)} %get-tuple-element.181), kind=kOutput, calls=%fused_computation.487 | convolution fusion | flops 8591507456 | bytes 35657728 | tf_op jit(solution)/shard_map/dot_general | solution.py:229
  658.1 13.8 fusion.5
  671.9 16.6 %multiply_reduce_fusion.1 = (f32[1024]{0:T(1024)S(1)}, f32[512]{0:T(512)S(1)}, f32[512,1024]{1,0:T(8,128)}) fusion(f32[512,1024]{1,0:T(8,128)} %get-tuple-element.201, f32[512]{0:T(512)S(1)} %get-tuple-element.181, f32[1024]{0:T(1024)S(1)} %mul.822, bf16[1024,8192]{1,0:T(8,128)(2,1)} %shard_map.320, bf16[512,4096]{1,0:T(8,128)(2,1)} %get-tuple-element.123, ...), kind=kOutput, calls=%fused_computation.94 | convolution fusion | flops 8609855488 | bytes 29372416 | tf_op jit(solution)/shard_map/dot_general | solution.py:233
  715.5 8.9 convert_element_type.504
  724.5 7.5 multiply_reduce_fusion.2
  736.6 12.1 fusion.216
  765.8 7.7 reshape.788
  781.4 8.1 fusion.122
  830.0 7.0 convolution_convert_fusion.1
  847.9 10.5 convolution_convert_fusion
  926.4 12.3 fusion.219
  1071.3 21.6 %collective-permute-done.152 = bf16[4,128,1024]{2,1,0:T(8,128)(2,1)S(1)} collective-permute-done((bf16[4,128,1024]{2,1,0:T(8,128)(2,1)S(1)}, bf16[4,128,1024]{2,1,0:T(8,128)(2,1)S(1)}, u32[]{:S(2)}, u32[]{:S(2)}) %collective-permute-start.152) | collective-permute-done | bytes 1048608 | tf_op jit(solution)/shard_map/ppermute | solution.py:66
  1095.9 11.4 convert_element_type.595
  1113.4 8.7 fusion.1
  1124.0 11.5 convert_element_type.554
  1149.5 11.4 convert_element_type.516
  1165.9 9.3 fusion.3
  1180.3 10.7 collective-permute-start.117
  1215.6 40.3 %collective-permute-done.145 = bf16[8,32,8192]{2,1,0:T(8,128)(2,1)} collective-permute-done((bf16[8,32,8192]{2,1,0:T(8,128)(2,1)}, bf16[8,32,8192]{2,1,0:T(8,128)(2,1)}, u32[]{:S(2)}, u32[]{:S(2)}) %collective-permute-start.145) | collective-permute-done | bytes 4194336 | tf_op jit(solution)/shard_map/ppermute | solution.py:66
  1267.9 58.0 %collective-permute-done.103 = bf16[8,256,1024]{2,1,0:T(8,128)(2,1)} collective-permute-done((bf16[8,256,1024]{2,1,0:T(8,128)(2,1)}, bf16[8,256,1024]{2,1,0:T(8,128)(2,1)}, u32[]{:S(2)}, u32[]{:S(2)}) %collective-permute-start.103) | collective-permute-done | bytes 4194336 | tf_op jit(solution)/shard_map/ppermute | solution.py:66
  1332.4 7.3 fusion.16
  1363.6 20.4 %collective-permute-start.148 = (bf16[32,8192]{1,0:T(8,128)(2,1)S(1)}, bf16[32,8192]{1,0:T(8,128)(2,1)S(1)}, u32[]{:S(2)}, u32[]{:S(2)}) collective-permute-start(bf16[32,8192]{1,0:T(8,128)(2,1)S(1)} %get-tuple-element.131), channel_id=1, source_target_pairs={{0,16},{1,17},{2,18},{3,19},{4,20},{5,21},{6,22},{7,23},{8,24},{9,... | collective-permute-start | bytes 1572872 | tf_op jit(solution)/shard_map/ppermute | solution.py:174
  1384.0 30.5 %collective-permute-done.130 = bf16[32,8192]{1,0:T(8,128)(2,1)} collective-permute-done((bf16[32,8192]{1,0:T(8,128)(2,1)}, bf16[32,8192]{1,0:T(8,128)(2,1)}, u32[]{:S(2)}, u32[]{:S(2)}) %collective-permute-start.130) | collective-permute-done | bytes 524320 | tf_op jit(solution)/shard_map/ppermute | solution.py:174
  1434.7 7.9 collective-permute-done.148
  1449.9 33.4 %collective-permute-done.106 = bf16[256,1024]{1,0:T(8,128)(2,1)S(1)} collective-permute-done((bf16[256,1024]{1,0:T(8,128)(2,1)S(1)}, bf16[256,1024]{1,0:T(8,128)(2,1)S(1)}, u32[]{:S(2)}, u32[]{:S(2)}) %collective-permute-start.106) | collective-permute-done | bytes 524320 | tf_op jit(solution)/shard_map/ppermute | solution.py:174
  (1146 shorter events, 772.8 us)
Async XLA Ops:
  5.8 45.0 %collective-permute-start.1 = (bf16[256,1024]{1,0:T(8,128)(2,1)}, bf16[256,1024]{1,0:T(8,128)(2,1)S(1)}, u32[]{:S(2)}, u32[]{:S(2)}) collective-permute-start(bf16[256,1024]{1,0:T(8,128)(2,1)} %param.25), channel_id=1, source_target_pairs={{0,16},{1,17},{2,18},{3,19},{4,20},{5,21},{6,22},{7,23},{8,24},{9,... | collective-permute-start | bytes 1572872 | tf_op jit(solution)/shard_map/ppermute | solution.py:83
  5.8 45.0 %collective-permute-start.2 = (bf16[256,1024]{1,0:T(8,128)(2,1)}, bf16[256,1024]{1,0:T(8,128)(2,1)S(1)}, u32[]{:S(2)}, u32[]{:S(2)}) collective-permute-start(bf16[256,1024]{1,0:T(8,128)(2,1)} %param.25), channel_id=1, source_target_pairs={{0,8},{1,9},{2,10},{3,11},{4,12},{5,13},{6,14},{7,15},{8,16},{9,17... | collective-permute-start | bytes 1572872 | tf_op jit(solution)/shard_map/ppermute | solution.py:83
  98.9 70.9 %collective-permute-start.4 = (bf16[1024,1024]{1,0:T(8,128)(2,1)}, bf16[1024,1024]{1,0:T(8,128)(2,1)}, u32[]{:S(2)}, u32[]{:S(2)}) collective-permute-start(bf16[1024,1024]{1,0:T(8,128)(2,1)} %copy-done.17), channel_id=1, source_target_pairs={{0,4},{1,3},{2,6},{3,1},{4,0},{5,7},{6,2},{7,5},{8,12},{9,11},{10,... | collective-permute-start | bytes 6291464 | tf_op jit(solution)/shard_map/ppermute | solution.py:66
  166.4 46.3 %collective-permute-start.5 = (bf16[1024,1024]{1,0:T(8,128)(2,1)}, bf16[1024,1024]{1,0:T(8,128)(2,1)}, u32[]{:S(2)}, u32[]{:S(2)}) collective-permute-start(bf16[1024,1024]{1,0:T(8,128)(2,1)} %collective-permute-done.3.refs_1_), channel_id=1, source_target_pairs={{0,4},{1,3},{2,6},{3,1},{4,0},{5,7},{6,2},{7,5},{8,12},{9,11},{10,... | collective-permute-start | bytes 6291464 | tf_op jit(solution)/shard_map/ppermute | solution.py:66
  168.1 64.1 %collective-permute-start.54 = (bf16[128,8192]{1,0:T(8,128)(2,1)}, bf16[128,8192]{1,0:T(8,128)(2,1)}, u32[]{:S(2)}, u32[]{:S(2)}) collective-permute-start(bf16[128,8192]{1,0:T(8,128)(2,1)} %pad_maximum_fusion.1.refs_0_), channel_id=1, source_target_pairs={{0,2},{1,5},{2,0},{3,7},{4,6},{5,1},{6,4},{7,3},{8,10},{9,13},{10,... | collective-permute-start | bytes 6291464 | tf_op jit(solution)/shard_map/ppermute | solution.py:66
  212.7 84.3 %collective-permute-start.6 = (bf16[1024,1024]{1,0:T(8,128)(2,1)}, bf16[1024,1024]{1,0:T(8,128)(2,1)}, u32[]{:S(2)}, u32[]{:S(2)}) collective-permute-start(bf16[1024,1024]{1,0:T(8,128)(2,1)} %copy-done.17), channel_id=1, source_target_pairs={{0,1},{1,0},{2,3},{3,2},{4,5},{5,4},{6,7},{7,6},{8,9},{9,8},{10,11... | collective-permute-start | bytes 6291464 | tf_op jit(solution)/shard_map/ppermute | solution.py:66
  227.3 69.8 %collective-permute-start.7 = (bf16[1024,1024]{1,0:T(8,128)(2,1)}, bf16[1024,1024]{1,0:T(8,128)(2,1)}, u32[]{:S(2)}, u32[]{:S(2)}) collective-permute-start(bf16[1024,1024]{1,0:T(8,128)(2,1)} %collective-permute-done.3.refs_1_), channel_id=1, source_target_pairs={{0,1},{1,0},{2,3},{3,2},{4,5},{5,4},{6,7},{7,6},{8,9},{9,8},{10,11... | collective-permute-start | bytes 6291464 | tf_op jit(solution)/shard_map/ppermute | solution.py:66
  227.3 70.9 %collective-permute-start.8 = (bf16[1024,1024]{1,0:T(8,128)(2,1)}, bf16[1024,1024]{1,0:T(8,128)(2,1)}, u32[]{:S(2)}, u32[]{:S(2)}) collective-permute-start(bf16[1024,1024]{1,0:T(8,128)(2,1)} %collective-permute-done.4.refs_2_), channel_id=1, source_target_pairs={{0,1},{1,0},{2,3},{3,2},{4,5},{5,4},{6,7},{7,6},{8,9},{9,8},{10,11... | collective-permute-start | bytes 6291464 | tf_op jit(solution)/shard_map/ppermute | solution.py:66
  227.8 71.4 %collective-permute-start.9 = (bf16[1024,1024]{1,0:T(8,128)(2,1)}, bf16[1024,1024]{1,0:T(8,128)(2,1)}, u32[]{:S(2)}, u32[]{:S(2)}) collective-permute-start(bf16[1024,1024]{1,0:T(8,128)(2,1)} %collective-permute-done.5.refs_3_), channel_id=1, source_target_pairs={{0,1},{1,0},{2,3},{3,2},{4,5},{5,4},{6,7},{7,6},{8,9},{9,8},{10,11... | collective-permute-start | bytes 6291464 | tf_op jit(solution)/shard_map/ppermute | solution.py:66
  297.1 70.6 %collective-permute-start.55 = (bf16[128,8192]{1,0:T(8,128)(2,1)}, bf16[128,8192]{1,0:T(8,128)(2,1)}, u32[]{:S(2)}, u32[]{:S(2)}) collective-permute-start(bf16[128,8192]{1,0:T(8,128)(2,1)} %pad_maximum_fusion.1.refs_0_), channel_id=1, source_target_pairs={{0,4},{1,3},{2,6},{3,1},{4,0},{5,7},{6,2},{7,5},{8,12},{9,11},{10,... | collective-permute-start | bytes 6291464 | tf_op jit(solution)/shard_map/ppermute | solution.py:66
  298.2 46.6 %collective-permute-start.46 = (bf16[256,1024]{1,0:T(8,128)(2,1)}, bf16[256,1024]{1,0:T(8,128)(2,1)}, u32[]{:S(2)}, u32[]{:S(2)}) collective-permute-start(bf16[256,1024]{1,0:T(8,128)(2,1)} %collective-permute-done.44.refs_1_), channel_id=1, source_target_pairs={{0,4},{1,3},{2,6},{3,1},{4,0},{5,7},{6,2},{7,5},{8,12},{9,11},{10,... | collective-permute-start | bytes 1572872 | tf_op jit(solution)/shard_map/ppermute | solution.py:66
  299.2 45.8 %collective-permute-start.48 = (bf16[256,1024]{1,0:T(8,128)(2,1)}, bf16[256,1024]{1,0:T(8,128)(2,1)}, u32[]{:S(2)}, u32[]{:S(2)}) collective-permute-start(bf16[256,1024]{1,0:T(8,128)(2,1)} %collective-permute-done.44.refs_1_), channel_id=1, source_target_pairs={{0,1},{1,0},{2,3},{3,2},{4,5},{5,4},{6,7},{7,6},{8,9},{9,8},{10,11... | collective-permute-start | bytes 1572872 | tf_op jit(solution)/shard_map/ppermute | solution.py:66
  383.6 65.1 %all-to-all-start = ((bf16[32,64,128]{2,1,0:T(8,128)(2,1)}), bf16[32,64,128]{2,1,0:T(8,128)(2,1)}, u32[]{:S(2)}, u32[]{:S(2)}) async-start(bf16[32,64,128]{2,1,0:T(8,128)(2,1)} %copy.258), calls=%async_computation | async-start | bytes 1048576 | tf_op jit(solution)/shard_map/all_to_all | solution.py:330
  387.3 48.3 %collective-permute-start.66 = (bf16[128,3072]{1,0:T(8,128)(2,1)}, bf16[128,3072]{1,0:T(8,128)(2,1)}, u32[]{:S(2)}, u32[]{:S(2)}) collective-permute-start(bf16[128,3072]{1,0:T(8,128)(2,1)} %collective-permute-done.64.refs_1_), channel_id=1, source_target_pairs={{0,4},{1,3},{2,6},{3,1},{4,0},{5,7},{6,2},{7,5},{8,12},{9,11},{10,... | collective-permute-start | bytes 2359304 | tf_op jit(solution)/shard_map/ppermute | solution.py:66
  389.1 78.7 %collective-permute-start.56 = (bf16[128,8192]{1,0:T(8,128)(2,1)}, bf16[128,8192]{1,0:T(8,128)(2,1)}, u32[]{:S(2)}, u32[]{:S(2)}) collective-permute-start(bf16[128,8192]{1,0:T(8,128)(2,1)} %collective-permute-done.54.refs_1_), channel_id=1, source_target_pairs={{0,4},{1,3},{2,6},{3,1},{4,0},{5,7},{6,2},{7,5},{8,12},{9,11},{10,... | collective-permute-start | bytes 6291464 | tf_op jit(solution)/shard_map/ppermute | solution.py:66
  467.0 47.7 %collective-permute-start.57 = (bf16[128,8192]{1,0:T(8,128)(2,1)}, bf16[128,8192]{1,0:T(8,128)(2,1)}, u32[]{:S(2)}, u32[]{:S(2)}) collective-permute-start(bf16[128,8192]{1,0:T(8,128)(2,1)} %pad_maximum_fusion.1.refs_0_), channel_id=1, source_target_pairs={{0,1},{1,0},{2,3},{3,2},{4,5},{5,4},{6,7},{7,6},{8,9},{9,8},{10,11... | collective-permute-start | bytes 6291464 | tf_op jit(solution)/shard_map/ppermute | solution.py:66
  467.1 48.2 %collective-permute-start.58 = (bf16[128,8192]{1,0:T(8,128)(2,1)}, bf16[128,8192]{1,0:T(8,128)(2,1)}, u32[]{:S(2)}, u32[]{:S(2)}) collective-permute-start(bf16[128,8192]{1,0:T(8,128)(2,1)} %collective-permute-done.54.refs_1_), channel_id=1, source_target_pairs={{0,1},{1,0},{2,3},{3,2},{4,5},{5,4},{6,7},{7,6},{8,9},{9,8},{10,11... | collective-permute-start | bytes 6291464 | tf_op jit(solution)/shard_map/ppermute | solution.py:66
  467.6 49.3 %collective-permute-start.59 = (bf16[128,8192]{1,0:T(8,128)(2,1)}, bf16[128,8192]{1,0:T(8,128)(2,1)}, u32[]{:S(2)}, u32[]{:S(2)}) collective-permute-start(bf16[128,8192]{1,0:T(8,128)(2,1)} %collective-permute-done.55.refs_2_), channel_id=1, source_target_pairs={{0,1},{1,0},{2,3},{3,2},{4,5},{5,4},{6,7},{7,6},{8,9},{9,8},{10,11... | collective-permute-start | bytes 6291464 | tf_op jit(solution)/shard_map/ppermute | solution.py:66
  467.7 45.7 %collective-permute-start.84 = (bf16[128,8192]{1,0:T(8,128)(2,1)S(1)}, bf16[128,8192]{1,0:T(8,128)(2,1)}, u32[]{:S(2)}, u32[]{:S(2)}) collective-permute-start(bf16[128,8192]{1,0:T(8,128)(2,1)S(1)} %pad_maximum_fusion.2.refs_0_), channel_id=1, source_target_pairs={{0,2},{1,5},{2,0},{3,7},{4,6},{5,1},{6,4},{7,3},{8,10},{9,13},{10,... | collective-permute-start | bytes 6291464 | tf_op jit(solution)/shard_map/ppermute | solution.py:66
  469.3 47.5 %collective-permute-start.60 = (bf16[128,8192]{1,0:T(8,128)(2,1)}, bf16[128,8192]{1,0:T(8,128)(2,1)}, u32[]{:S(2)}, u32[]{:S(2)}) collective-permute-start(bf16[128,8192]{1,0:T(8,128)(2,1)} %collective-permute-done.56.refs_3_), channel_id=1, source_target_pairs={{0,1},{1,0},{2,3},{3,2},{4,5},{5,4},{6,7},{7,6},{8,9},{9,8},{10,11... | collective-permute-start | bytes 6291464 | tf_op jit(solution)/shard_map/ppermute | solution.py:66
  513.4 58.6 %collective-permute-start.85 = (bf16[128,8192]{1,0:T(8,128)(2,1)S(1)}, bf16[128,8192]{1,0:T(8,128)(2,1)}, u32[]{:S(2)}, u32[]{:S(2)}) collective-permute-start(bf16[128,8192]{1,0:T(8,128)(2,1)S(1)} %pad_maximum_fusion.2.refs_0_), channel_id=1, source_target_pairs={{0,4},{1,3},{2,6},{3,1},{4,0},{5,7},{6,2},{7,5},{8,12},{9,11},{10,... | collective-permute-start | bytes 6291464 | tf_op jit(solution)/shard_map/ppermute | solution.py:66
  514.8 55.6 %collective-permute-start.94 = (bf16[512,1024]{1,0:T(8,128)(2,1)}, bf16[512,1024]{1,0:T(8,128)(2,1)}, u32[]{:S(2)}, u32[]{:S(2)}) collective-permute-start(bf16[512,1024]{1,0:T(8,128)(2,1)} %pad_maximum_fusion.4.refs_0_), channel_id=1, source_target_pairs={{0,2},{1,5},{2,0},{3,7},{4,6},{5,1},{6,4},{7,3},{8,10},{9,13},{10,... | collective-permute-start | bytes 3145736 | tf_op jit(solution)/shard_map/ppermute | solution.py:66
  515.4 74.8 %collective-permute-start.95 = (bf16[512,1024]{1,0:T(8,128)(2,1)}, bf16[512,1024]{1,0:T(8,128)(2,1)}, u32[]{:S(2)}, u32[]{:S(2)}) collective-permute-start(bf16[512,1024]{1,0:T(8,128)(2,1)} %pad_maximum_fusion.4.refs_0_), channel_id=1, source_target_pairs={{0,4},{1,3},{2,6},{3,1},{4,0},{5,7},{6,2},{7,5},{8,12},{9,11},{10,... | collective-permute-start | bytes 3145736 | tf_op jit(solution)/shard_map/ppermute | solution.py:66
  516.9 73.8 %collective-permute-start.97 = (bf16[512,1024]{1,0:T(8,128)(2,1)}, bf16[512,1024]{1,0:T(8,128)(2,1)}, u32[]{:S(2)}, u32[]{:S(2)}) collective-permute-start(bf16[512,1024]{1,0:T(8,128)(2,1)} %pad_maximum_fusion.4.refs_0_), channel_id=1, source_target_pairs={{0,1},{1,0},{2,3},{3,2},{4,5},{5,4},{6,7},{7,6},{8,9},{9,8},{10,11... | collective-permute-start | bytes 3145736 | tf_op jit(solution)/shard_map/ppermute | solution.py:66
  516.9 79.3 %collective-permute-start.86 = (bf16[128,8192]{1,0:T(8,128)(2,1)}, bf16[128,8192]{1,0:T(8,128)(2,1)}, u32[]{:S(2)}, u32[]{:S(2)}) collective-permute-start(bf16[128,8192]{1,0:T(8,128)(2,1)} %collective-permute-done.84.refs_1_), channel_id=1, source_target_pairs={{0,4},{1,3},{2,6},{3,1},{4,0},{5,7},{6,2},{7,5},{8,12},{9,11},{10,... | collective-permute-start | bytes 6291464 | tf_op jit(solution)/shard_map/ppermute | solution.py:66
  818.4 53.7 %all-to-all-start.2 = ((bf16[32,64,128]{2,1,0:T(8,128)(2,1)}), bf16[32,64,128]{2,1,0:T(8,128)(2,1)}, u32[]{:S(2)}, u32[]{:S(2)}) async-start(bf16[32,64,128]{2,1,0:T(8,128)(2,1)} %copy.282), calls=%async_computation.2 | async-start | bytes 1048576 | tf_op jit(solution)/shard_map/all_to_all | solution.py:330
  829.8 140.8 %collective-permute-start.120 = (bf16[16,64,1024]{2,1,0:T(8,128)(2,1)}, bf16[16,64,1024]{2,1,0:T(8,128)(2,1)}, u32[]{:S(2)}, u32[]{:S(2)}) collective-permute-start(bf16[16,64,1024]{2,1,0:T(8,128)(2,1)} %bitcast.373), channel_id=1, source_target_pairs={{0,1},{1,0},{2,3},{3,2},{4,5},{5,4},{6,7},{7,6},{8,9},{9,8},{10,11... | collective-permute-start | bytes 6291464 | tf_op jit(solution)/shard_map/ppermute | solution.py:66
  843.3 151.1 %collective-permute-start.132 = (bf16[16,32,3072]{2,1,0:T(8,128)(2,1)}, bf16[16,32,3072]{2,1,0:T(8,128)(2,1)}, u32[]{:S(2)}, u32[]{:S(2)}) collective-permute-start(bf16[16,32,3072]{2,1,0:T(8,128)(2,1)} %convolution_convert_fusion.4), channel_id=1, source_target_pairs={{0,1},{1,0},{2,3},{3,2},{4,5},{5,4},{6,7},{7,6},{8,9},{9,8},{10,11... | collective-permute-start | bytes 9437192 | tf_op jit(solution)/shard_map/ppermute | solution.py:66
  895.1 199.8 %collective-permute-start.144 = (bf16[16,32,8192]{2,1,0:T(8,128)(2,1)}, bf16[16,32,8192]{2,1,0:T(8,128)(2,1)}, u32[]{:S(2)}, u32[]{:S(2)}) collective-permute-start(bf16[16,32,8192]{2,1,0:T(8,128)(2,1)} %bitcast.400), channel_id=1, source_target_pairs={{0,1},{1,0},{2,3},{3,2},{4,5},{5,4},{6,7},{7,6},{8,9},{9,8},{10,11... | collective-permute-start | bytes 25165832 | tf_op jit(solution)/shard_map/ppermute | solution.py:66
  900.1 102.3 %collective-permute-start.150 = (bf16[16,128,1024]{2,1,0:T(8,128)(2,1)}, bf16[16,128,1024]{2,1,0:T(8,128)(2,1)}, u32[]{:S(2)}, u32[]{:S(2)}) collective-permute-start(bf16[16,128,1024]{2,1,0:T(8,128)(2,1)} %bitcast.401), channel_id=1, source_target_pairs={{0,1},{1,0},{2,3},{3,2},{4,5},{5,4},{6,7},{7,6},{8,9},{9,8},{10,11... | collective-permute-start | bytes 12582920 | tf_op jit(solution)/shard_map/ppermute | solution.py:66
  970.7 86.1 %collective-permute-start.114 = (bf16[16,32,4384]{2,1,0:T(8,128)(2,1)}, bf16[16,32,4384]{2,1,0:T(8,128)(2,1)}, u32[]{:S(2)}, u32[]{:S(2)}) collective-permute-start(bf16[16,32,4384]{2,1,0:T(8,128)(2,1)} %bitcast.362), channel_id=1, source_target_pairs={{0,1},{1,0},{2,3},{3,2},{4,5},{5,4},{6,7},{7,6},{8,9},{9,8},{10,11... | collective-permute-start | bytes 13467656 | tf_op jit(solution)/shard_map/ppermute | solution.py:66
  1002.3 45.7 %collective-permute-start.133 = (bf16[8,32,3072]{2,1,0:T(8,128)(2,1)}, bf16[8,32,3072]{2,1,0:T(8,128)(2,1)}, u32[]{:S(2)}, u32[]{:S(2)}) collective-permute-start(bf16[8,32,3072]{2,1,0:T(8,128)(2,1)} %fusion.23), channel_id=1, source_target_pairs={{0,4},{1,3},{2,6},{3,1},{4,0},{5,7},{6,2},{7,5},{8,12},{9,11},{10,... | collective-permute-start | bytes 4718600 | tf_op jit(solution)/shard_map/ppermute | solution.py:66
  1046.3 75.9 %collective-permute-start.126 = (bf16[16,32,8192]{2,1,0:T(8,128)(2,1)}, bf16[16,32,8192]{2,1,0:T(8,128)(2,1)}, u32[]{:S(2)}, u32[]{:S(2)}) collective-permute-start(bf16[16,32,8192]{2,1,0:T(8,128)(2,1)} %convolution_convert_fusion.1), channel_id=1, source_target_pairs={{0,1},{1,0},{2,3},{3,2},{4,5},{5,4},{6,7},{7,6},{8,9},{9,8},{10,11... | collective-permute-start | bytes 25165832 | tf_op jit(solution)/shard_map/ppermute | solution.py:66
  1048.0 101.2 %collective-permute-start.102 = (bf16[16,256,1024]{2,1,0:T(8,128)(2,1)}, bf16[16,256,1024]{2,1,0:T(8,128)(2,1)}, u32[]{:S(2)}, u32[]{:S(2)}) collective-permute-start(bf16[16,256,1024]{2,1,0:T(8,128)(2,1)} %bitcast.350), channel_id=1, source_target_pairs={{0,1},{1,0},{2,3},{3,2},{4,5},{5,4},{6,7},{7,6},{8,9},{9,8},{10,11... | collective-permute-start | bytes 25165832 | tf_op jit(solution)/shard_map/ppermute | solution.py:66
  1092.9 53.9 %collective-permute-start.137 = (bf16[32,3072]{1,0:T(8,128)(2,1)}, bf16[32,3072]{1,0:T(8,128)(2,1)}, u32[]{:S(2)}, u32[]{:S(2)}) collective-permute-start(bf16[32,3072]{1,0:T(8,128)(2,1)} %get-tuple-element.151), channel_id=1, source_target_pairs={{0,24},{1,25},{2,26},{3,27},{4,28},{5,29},{6,30},{7,31},{8,0},{9,1... | collective-permute-start | bytes 589832 | tf_op jit(solution)/shard_map/ppermute | solution.py:174
  1094.9 66.0 %collective-permute-start.136 = (bf16[32,3072]{1,0:T(8,128)(2,1)}, bf16[32,3072]{1,0:T(8,128)(2,1)}, u32[]{:S(2)}, u32[]{:S(2)}) collective-permute-start(bf16[32,3072]{1,0:T(8,128)(2,1)} %get-tuple-element.152), channel_id=1, source_target_pairs={{0,16},{1,17},{2,18},{3,19},{4,20},{5,21},{6,22},{7,23},{8,24},{9,... | collective-permute-start | bytes 589832 | tf_op jit(solution)/shard_map/ppermute | solution.py:174
  1142.3 62.3 %collective-permute-start.127 = (bf16[8,32,8192]{2,1,0:T(8,128)(2,1)}, bf16[8,32,8192]{2,1,0:T(8,128)(2,1)}, u32[]{:S(2)}, u32[]{:S(2)}) collective-permute-start(bf16[8,32,8192]{2,1,0:T(8,128)(2,1)} %fusion.2), channel_id=1, source_target_pairs={{0,4},{1,3},{2,6},{3,1},{4,0},{5,7},{6,2},{7,5},{8,12},{9,11},{10,... | collective-permute-start | bytes 12582920 | tf_op jit(solution)/shard_map/ppermute | solution.py:66
  1149.3 106.6 %collective-permute-start.145 = (bf16[8,32,8192]{2,1,0:T(8,128)(2,1)}, bf16[8,32,8192]{2,1,0:T(8,128)(2,1)}, u32[]{:S(2)}, u32[]{:S(2)}) collective-permute-start(bf16[8,32,8192]{2,1,0:T(8,128)(2,1)} %fusion.1), channel_id=1, source_target_pairs={{0,4},{1,3},{2,6},{3,1},{4,0},{5,7},{6,2},{7,5},{8,12},{9,11},{10,... | collective-permute-start | bytes 12582920 | tf_op jit(solution)/shard_map/ppermute | solution.py:66
  1191.0 134.9 %collective-permute-start.103 = (bf16[8,256,1024]{2,1,0:T(8,128)(2,1)}, bf16[8,256,1024]{2,1,0:T(8,128)(2,1)}, u32[]{:S(2)}, u32[]{:S(2)}) collective-permute-start(bf16[8,256,1024]{2,1,0:T(8,128)(2,1)} %fusion.3), channel_id=1, source_target_pairs={{0,4},{1,3},{2,6},{3,1},{4,0},{5,7},{6,2},{7,5},{8,12},{9,11},{10,... | collective-permute-start | bytes 12582920 | tf_op jit(solution)/shard_map/ppermute | solution.py:66
  1214.4 125.8 %collective-permute-start.128 = (bf16[4,32,8192]{2,1,0:T(8,128)(2,1)S(1)}, bf16[4,32,8192]{2,1,0:T(8,128)(2,1)}, u32[]{:S(2)}, u32[]{:S(2)}) collective-permute-start(bf16[4,32,8192]{2,1,0:T(8,128)(2,1)S(1)} %fusion.13), channel_id=1, source_target_pairs={{0,2},{1,5},{2,0},{3,7},{4,6},{5,1},{6,4},{7,3},{8,10},{9,13},{10,... | collective-permute-start | bytes 6291464 | tf_op jit(solution)/shard_map/ppermute | solution.py:66
  1267.9 84.9 %collective-permute-start.146 = (bf16[4,32,8192]{2,1,0:T(8,128)(2,1)}, bf16[4,32,8192]{2,1,0:T(8,128)(2,1)}, u32[]{:S(2)}, u32[]{:S(2)}) collective-permute-start(bf16[4,32,8192]{2,1,0:T(8,128)(2,1)} %fusion.10), channel_id=1, source_target_pairs={{0,2},{1,5},{2,0},{3,7},{4,6},{5,1},{6,4},{7,3},{8,10},{9,13},{10,... | collective-permute-start | bytes 6291464 | tf_op jit(solution)/shard_map/ppermute | solution.py:66
  1339.7 77.4 %collective-permute-start.104 = (bf16[4,256,1024]{2,1,0:T(8,128)(2,1)}, bf16[4,256,1024]{2,1,0:T(8,128)(2,1)}, u32[]{:S(2)}, u32[]{:S(2)}) collective-permute-start(bf16[4,256,1024]{2,1,0:T(8,128)(2,1)} %fusion.16), channel_id=1, source_target_pairs={{0,2},{1,5},{2,0},{3,7},{4,6},{5,1},{6,4},{7,3},{8,10},{9,13},{10,... | collective-permute-start | bytes 6291464 | tf_op jit(solution)/shard_map/ppermute | solution.py:66
  1350.7 63.9 %collective-permute-start.130 = (bf16[32,8192]{1,0:T(8,128)(2,1)}, bf16[32,8192]{1,0:T(8,128)(2,1)}, u32[]{:S(2)}, u32[]{:S(2)}) collective-permute-start(bf16[32,8192]{1,0:T(8,128)(2,1)} %get-tuple-element.134), channel_id=1, source_target_pairs={{0,16},{1,17},{2,18},{3,19},{4,20},{5,21},{6,22},{7,23},{8,24},{9,... | collective-permute-start | bytes 1572872 | tf_op jit(solution)/shard_map/ppermute | solution.py:174
  1350.8 63.8 %collective-permute-start.129 = (bf16[32,8192]{1,0:T(8,128)(2,1)}, bf16[32,8192]{1,0:T(8,128)(2,1)}, u32[]{:S(2)}, u32[]{:S(2)}) collective-permute-start(bf16[32,8192]{1,0:T(8,128)(2,1)} %get-tuple-element.132), channel_id=1, source_target_pairs={{0,8},{1,9},{2,10},{3,11},{4,12},{5,13},{6,14},{7,15},{8,16},{9,17... | collective-permute-start | bytes 1572872 | tf_op jit(solution)/shard_map/ppermute | solution.py:174
  1358.1 74.7 %collective-permute-start.149 = (bf16[32,8192]{1,0:T(8,128)(2,1)S(1)}, bf16[32,8192]{1,0:T(8,128)(2,1)S(1)}, u32[]{:S(2)}, u32[]{:S(2)}) collective-permute-start(bf16[32,8192]{1,0:T(8,128)(2,1)S(1)} %get-tuple-element.130), channel_id=1, source_target_pairs={{0,24},{1,25},{2,26},{3,27},{4,28},{5,29},{6,30},{7,31},{8,0},{9,1... | collective-permute-start | bytes 1572872 | tf_op jit(solution)/shard_map/ppermute | solution.py:174
  1363.6 78.9 %collective-permute-start.148 = (bf16[32,8192]{1,0:T(8,128)(2,1)S(1)}, bf16[32,8192]{1,0:T(8,128)(2,1)S(1)}, u32[]{:S(2)}, u32[]{:S(2)}) collective-permute-start(bf16[32,8192]{1,0:T(8,128)(2,1)S(1)} %get-tuple-element.131), channel_id=1, source_target_pairs={{0,16},{1,17},{2,18},{3,19},{4,20},{5,21},{6,22},{7,23},{8,24},{9,... | collective-permute-start | bytes 1572872 | tf_op jit(solution)/shard_map/ppermute | solution.py:174
  1427.0 56.3 %collective-permute-start.106 = (bf16[256,1024]{1,0:T(8,128)(2,1)S(1)}, bf16[256,1024]{1,0:T(8,128)(2,1)S(1)}, u32[]{:S(2)}, u32[]{:S(2)}) collective-permute-start(bf16[256,1024]{1,0:T(8,128)(2,1)S(1)} %get-tuple-element.137), channel_id=1, source_target_pairs={{0,16},{1,17},{2,18},{3,19},{4,20},{5,21},{6,22},{7,23},{8,24},{9,... | collective-permute-start | bytes 1572872 | tf_op jit(solution)/shard_map/ppermute | solution.py:174
  1432.8 50.5 %collective-permute-start.105 = (bf16[256,1024]{1,0:T(8,128)(2,1)S(1)}, bf16[256,1024]{1,0:T(8,128)(2,1)S(1)}, u32[]{:S(2)}, u32[]{:S(2)}) collective-permute-start(bf16[256,1024]{1,0:T(8,128)(2,1)S(1)} %get-tuple-element.135), channel_id=1, source_target_pairs={{0,8},{1,9},{2,10},{3,11},{4,12},{5,13},{6,14},{7,15},{8,16},{9,17... | collective-permute-start | bytes 1572872 | tf_op jit(solution)/shard_map/ppermute | solution.py:174
  (371 other events, 5895.8 us)

commit v2 on v1

v2 whole, which is shorter than its diff:
```python
import functools

import jax
import jax.numpy as jnp
import numpy as np
from jax import lax
from jax.experimental import pallas as pl
from jax.experimental.pallas import tpu as pltpu
from jax.sharding import PartitionSpec as P

D = 1024
PATCH = 8
MHEADS = 32
MHEAD_DIM = 64
DI = 2048
NSTATE = 128
CONV = 4
AHEADS = 16
AHEAD_DIM = 64
FF = 4096
CONV_CH = 2304

EPS = 1e-05
HIGH = lax.Precision.HIGHEST
BF = jnp.bfloat16
F32 = jnp.float32


class Ring:
    def __init__(self, n):
        self.n = n
        self.depth = n // 8
        coords = [(i // 8, (i // 4) % 2, (i // 2) % 2, i % 2) for i in range(n)]

        def index(z, y, x, c):
            return ((z * 2 + y) * 2 + x) * 2 + c

        def flip(z, y, x, c, along_x):
            return index(z, y, 1 - x, c) if along_x else index(z, 1 - y, x, c)

        self.core = [(index(*p), index(*p) ^ 1) for p in coords]
        self.first = [(index(*p), flip(*p, p[3] == 0)) for p in coords]
        self.second = [(index(*p), flip(*p, p[3] == 1)) for p in coords]
        self.bits = [1 << b for b in range(self.depth.bit_length() - 1)]
        self.along = {
            bit: [(index(*p), index(p[0] ^ bit, *p[1:])) for p in coords] for bit in self.bits
        }
        table = np.zeros((n, n), np.int32)
        for me, (z, y, x, c) in enumerate(coords):
            place = 0
            for rc in range(2):
                owner = c ^ rc
                for r2 in range(2):
                    for r1 in range(2):
                        rx, ry = (r1, r2) if owner == 0 else (r2, r1)
                        for rz in range(self.depth):
                            table[me, place] = index(z ^ rz, y ^ ry, x ^ rx, owner)
                            place += 1
        self.table = table

    def order(self):
        return jnp.asarray(self.table)[lax.axis_index("seq")]


def swap(block, route):
    return lax.ppermute(block, "seq", route)


def joined(pieces):
    return jnp.concatenate(pieces, axis=0) if len(pieces) > 1 else pieces[0]


def gather_near(ring, pieces, bits):
    for bit in bits:
        block = joined(pieces)
        pieces = [block, swap(block, ring.along[bit])]
    return pieces


def gather_near_low(ring, pieces):
    return gather_near(ring, pieces, ring.bits[: len(ring.bits) // 2])


def gather_near_high(ring, pieces):
    return gather_near(ring, pieces, ring.bits[len(ring.bits) // 2 :])


def gather_first(ring, pieces):
    block = joined(pieces)
    return [block, swap(block, ring.first)]


def gather_second(ring, pieces):
    block = joined(pieces)
    return [block, swap(block, ring.second)]


def gather_core(ring, pieces):
    return pieces + [swap(piece, ring.core) for piece in pieces]


GATHER = [gather_near_low, gather_near_high, gather_first, gather_second, gather_core]


def flat_kernel(*refs):
    out, first = refs[-1], 0
    for ref in refs[:-1]:
        rows = ref.shape[0]
        for column in range(0, ref.shape[1], D):
            out[pl.ds(first, rows)] = ref[:, pl.ds(column, D)]
            first += rows


def flat_rows(shards):
    total = sum(shard.shape[0] * shard.shape[1] // D for shard in shards)
    return pl.pallas_call(
        flat_kernel,
        out_shape=jax.ShapeDtypeStruct((total, D), BF),
        in_specs=[pl.BlockSpec(memory_space=pltpu.VMEM)] * len(shards),
        out_specs=pl.BlockSpec(memory_space=pltpu.VMEM),
    )(*shards)


def unpack_kernel(n, slots, shapes, flat_ref, *refs):
    outs, (held, in_sems, out_sems) = refs[:-3], refs[-3:]
    total = held.shape[1]

    def load(place):
        source = flat_ref.at[pl.ds(pl.multiple_of(place * total, 16), total)]
        return pltpu.make_async_copy(source, held.at[place % slots], in_sems.at[place % slots])

    def stores(place):
        offset, copies = 0, []
        for out, (rows, columns) in zip(outs, shapes):
            start = pl.multiple_of(place * rows, 16)
            for first in range(0, columns, D):
                source = held.at[place % slots, pl.ds(offset, rows)]
                target = out.at[pl.ds(start, rows), pl.ds(first, D)]
                sem = out_sems.at[place % slots, len(copies)]
                copies.append(pltpu.make_async_copy(source, target, sem))
                offset += rows
        return copies

    lead = slots // 2

    @pl.loop(0, n + lead)
    def _(time):
        @pl.when(time < n)
        def _():
            @pl.when(time >= slots)
            def _():
                for copy in stores(time - slots):
                    copy.wait()

            load(time).start()

        @pl.when(time >= lead)
        def _():
            load(time - lead).wait()
            for copy in stores(time - lead):
                copy.start()

    @pl.loop(n - slots, n)
    def _(place):
        for copy in stores(place):
            copy.wait()


def gather_flat(n, shards):
    if any(shard.shape[0] % 16 for shard in shards):
        return lambda: [lax.all_gather(shard, "seq", axis=0, tiled=True) for shard in shards]
    shapes = [shard.shape for shard in shards]
    flat = flat_rows(shards)
    total, slots = flat.shape[0], 8
    blocks = sum(columns // D for _, columns in shapes)
    flat = lax.all_gather(flat, "seq", axis=0, tiled=True)

    def unpack():
        return pl.pallas_call(
            functools.partial(unpack_kernel, n, slots, shapes),
            out_shape=[jax.ShapeDtypeStruct((n * rows, columns), BF) for rows, columns in shapes],
            in_specs=[pl.BlockSpec(memory_space=pltpu.HBM)],
            out_specs=[pl.BlockSpec(memory_space=pltpu.HBM)] * len(shapes),
            scratch_shapes=[
                pltpu.VMEM((slots, total, D), BF),
                pltpu.SemaphoreType.DMA((slots,)),
                pltpu.SemaphoreType.DMA((slots, blocks)),
            ],
            compiler_params=pltpu.CompilerParams(vmem_limit_bytes=24 * 2**20),
            cost_estimate=pl.CostEstimate(
                flops=0, bytes_accessed=4 * n * total * D, transcendentals=0
            ),
        )(flat)

    return unpack


def gather_rows(ring, shard):
    pieces = [shard]
    for phase in GATHER:
        pieces = phase(ring, pieces)
    return pieces


def gather_small(ring, vector):
    pieces = gather_rows(ring, vector[None])
    return jnp.take(jnp.concatenate(pieces, axis=0), jnp.argsort(ring.order()), axis=0)


class Live:
    def fence(self):
        vars(self).update(lax.optimization_barrier(dict(vars(self))))


def summed_grad(left, right):
    product = lax.dot_general(left, right, (((0,), (0,)), ((), ())), preferred_element_type=F32)
    summed = lax.psum_scatter(product.astype(BF), "seq", scatter_dimension=0, tiled=True)
    return summed.astype(F32)


def flat_grad_kernel(hid_ref, grad_ref, normed_ref, both_ref, out_ref):
    devices, block = out_ref.shape[:2]
    parts = block // SUM_ROWS

    def product(left, right):
        return lax.dot_general(
            left, right, (((0,), (0,)), ((), ())), preferred_element_type=F32
        ).astype(BF)

    @pl.when(pl.program_id(0) < 4)
    def _():
        few = devices // parts
        for part in range(parts):
            cut = pl.ds(part * few * block, few * block)
            found = product(hid_ref[:, cut], grad_ref[...])
            out_ref[pl.ds(part * few, few)] = found.reshape(few, block, D)

    @pl.when(pl.program_id(0) >= 4)
    def _():
        for part in range(parts):
            found = product(normed_ref[...], both_ref[:, pl.ds(part * D, D)])
            cut = pl.ds(part * SUM_ROWS, SUM_ROWS)
            out_ref[:, cut] = found.reshape(devices, SUM_ROWS, D)


def flat_grads(n, hid, out_grad, normed, both):
    rows, block, devices = hid.shape[0], hid.shape[1] // n, n // 4

    def late(step):
        return jnp.maximum(step - 4, 0)

    return pl.pallas_call(
        flat_grad_kernel,
        grid=(12,),
        out_shape=jax.ShapeDtypeStruct((n, 3 * block, D), BF),
        in_specs=[
            pl.BlockSpec((rows, devices * block), lambda i: (0, jnp.minimum(i, 3))),
            pl.BlockSpec((rows, D), lambda i: (0, 0)),
            pl.BlockSpec((rows, devices * SUM_ROWS), lambda i: (0, late(i) % 4)),
            pl.BlockSpec((rows, FF), lambda i: (0, late(i) // 4)),
        ],
        out_specs=pl.BlockSpec(
            (devices, block, D), lambda i: (i % 4, jnp.minimum(i // 4, 1) + late(i) // 4, 0)
        ),
        compiler_params=pltpu.CompilerParams(vmem_limit_bytes=32 * 2**20),
        cost_estimate=pl.CostEstimate(
            flops=6 * rows * FF * D, bytes_accessed=2**25, transcendentals=0
        ),
    )(hid, out_grad, normed, both)


def dot(left, right):
    return jnp.dot(left, right, preferred_element_type=F32)


def dot_t(left, right):
    return lax.dot_general(left, right, (((1,), (1,)), ((), ())), preferred_element_type=F32)


def rms_scale(values, gain):
    return values * lax.rsqrt(jnp.mean(values * values, axis=-1, keepdims=True) + EPS) * gain


def rms_back(values, gain, grad):
    r = lax.rsqrt(jnp.mean(values * values, axis=-1, keepdims=True) + EPS)
    scaled = gain * grad
    inner = jnp.mean(values * scaled, axis=-1, keepdims=True)
    return r * scaled - values * (r * r * r) * inner, jnp.sum(values * r * grad, axis=0)


def silu(v):
    return v * jax.nn.sigmoid(v)


def silu_slope(v):
    s = jax.nn.sigmoid(v)
    return s * (1.0 + v * (1.0 - s))


def tap_masks(flags_ext, row_count):
    not_reset = 1.0 - flags_ext.astype(F32)
    validity = [jnp.ones((row_count,), F32)]
    for offset in range(1, CONV):
        validity.append(validity[-1] * not_reset[CONV - offset : CONV - offset + row_count])
    return validity


def conv_apply(conv_ext, conv_weight, conv_bias, validity, row_count):
    summed = conv_bias + conv_ext[CONV - 1 : CONV - 1 + row_count] * conv_weight[0]
    for offset in range(1, CONV):
        summed = (
            summed
            + validity[offset][:, None]
            * conv_ext[CONV - 1 - offset : CONV - 1 - offset + row_count]
            * conv_weight[offset]
        )
    return jax.nn.silu(summed)


def block_parts(conv_out, dt_raw, head_params, starts):
    row_count = conv_out.shape[0]
    values = conv_out[:, :DI].reshape(row_count, MHEADS, MHEAD_DIM)
    key_rows = conv_out[:, DI : DI + NSTATE]
    queries = conv_out[:, DI + NSTATE :]
    step_size = jax.nn.softplus(dt_raw + head_params[0])
    cumlog = jnp.cumsum(-step_size * jnp.exp(head_params[1]), axis=0)
    segment = jnp.cumsum(starts, axis=0, dtype=jnp.int32)
    return (values, key_rows, queries, step_size, cumlog, segment)


def block_state(conv_out, dt_raw, head_params, starts):
    values, key_rows, queries, step_size, cumlog, segment = block_parts(
        conv_out, dt_raw, head_params, starts
    )
    same_doc = (segment == segment[-1]).astype(F32)
    weighting = jnp.exp(cumlog[-1][None, :] - cumlog) * same_doc[:, None] * step_size
    state_out = jnp.einsum("rh,rhp,rn->hpn", weighting, values, key_rows, precision=HIGH)
    decay_total = jnp.exp(cumlog[-1]) * (segment[-1] == 0).astype(F32)
    return (state_out, decay_total)


def block_output(conv_out, dt_raw, head_params, state_in, starts):
    values, key_rows, queries, step_size, cumlog, segment = block_parts(
        conv_out, dt_raw, head_params, starts
    )
    position = jnp.arange(conv_out.shape[0])
    causal = (position[:, None] >= position[None, :]) & (segment[:, None] == segment[None, :])
    log_gaps = jnp.where(causal[:, :, None], cumlog[:, None, :] - cumlog[None, :, :], 0.0)
    decays = jnp.exp(log_gaps) * causal[:, :, None].astype(F32)
    scores = jnp.dot(queries, key_rows.T, precision=HIGH)
    mixing = scores[:, :, None] * decays * step_size[None, :, :]
    within = jnp.einsum("tsh,shp->thp", mixing, values, precision=HIGH)
    inflow = jnp.exp(cumlog) * (segment == 0).astype(F32)[:, None]
    carried = jnp.einsum("tn,hpn->thp", queries, state_in, precision=HIGH) * inflow[:, :, None]
    skipped = head_params[2][None, :, None] * values
    return (within + carried + skipped).reshape(conv_out.shape[0], DI)


MESH = pl.DeviceIdType.MESH


class Place:
    def __init__(self, n):
        self.n, self.depth = n, n // 8
        self.me = me = lax.axis_index("seq")
        self.z, self.y, self.x, self.c = me // 8, (me // 4) % 2, (me // 2) % 2, me % 2

    def flipped(self, rz, ry, rx, rc):
        z, bit = 0, 1
        while bit < self.depth:
            z = z + ((self.z // bit + rz // bit) % 2) * bit
            bit *= 2
        y, x, c = (self.y + ry) % 2, (self.x + rx) % 2, (self.c + rc) % 2
        return ((z * 2 + y) * 2 + x) * 2 + c

    def split(self, place):
        depth = self.depth
        rz, r1, r2 = place % depth, (place // depth) % 2, (place // (2 * depth)) % 2
        return rz, r1, r2, place // (4 * depth)

    def device(self, place):
        rz, r1, r2, rc = self.split(place)
        owner = (self.c + rc) % 2
        return self.flipped(rz, r2 + owner * (r1 - r2), r1 + owner * (r2 - r1), rc)

    def place_there(self, place):
        rz, r1, r2, rc = self.split(place)
        s1, s2 = r1 + rc * (r2 - r1), r2 + rc * (r1 - r2)
        return ((rc * 2 + s2) * 2 + s1) * self.depth + rz

    def halves(self):
        steps, bit = [], 1
        while bit < self.depth:
            steps.append((bit, self.flipped(bit, 0, 0, 0)))
            bit *= 2
        steps.append((self.depth, self.flipped(0, self.c, 1 - self.c, 0)))
        steps.append((2 * self.depth, self.flipped(0, 1 - self.c, self.c, 0)))
        steps.append((4 * self.depth, self.flipped(0, 0, 0, 1)))
        return steps


def greet(n):
    barrier = pltpu.get_barrier_semaphore()
    me = lax.axis_index("seq")

    @pl.loop(1, n)
    def _(hop):
        other = lax.rem(me + hop, n)
        pl.semaphore_signal(barrier, inc=1, device_id=(other,), device_id_type=MESH)

    pl.semaphore_wait(barrier, n - 1)


def remote(source, target, send_sem, recv_sem, device):
    return pltpu.make_async_remote_copy(
        src_ref=source,
        dst_ref=target,
        send_sem=send_sem,
        recv_sem=recv_sem,
        device_id=(device,),
        device_id_type=MESH,
    )


def landed(ref, sem):
    pltpu.make_async_copy(ref, ref, sem).wait()


def rows_of(place, count, rows):
    return pl.ds(pl.multiple_of(place * rows, rows), count * rows)


GATHER_TIMES = [0, 1, 2, 3, 5, 6]


def gather_kernel(n, chunks, *refs):
    count = len(refs) // 2 - 1
    shards, wholes, (own_sem, send_sem, recv_sem) = refs[:count], refs[count : 2 * count], refs[2 * count :]
    here = Place(n)
    greet(n)
    owns = []
    for index in range(count):
        rows = shards[index].shape[0]
        target = wholes[index].at[rows_of(here.me, 1, rows)]
        owns.append(pltpu.make_async_copy(shards[index], target, own_sem.at[index]))
        owns[-1].start()
    for own in owns:
        own.wait()
    steps = here.halves()

    def block(chunk, place):
        index, first, rows, column, columns = chunks[chunk]
        start = here.device(place) * shards[index].shape[0] + first
        return wholes[index].at[pl.ds(pl.multiple_of(start, 16), rows), pl.ds(column, columns)]

    def sending(chunk, step, place):
        blocks, partner = steps[step]
        there = blocks + place
        ref = block(chunk, place)
        return remote(ref, ref, send_sem.at[chunk, there], recv_sem.at[chunk, there], partner)

    def arrive(chunk, step):
        blocks = steps[step][0]

        @pl.loop(blocks, 2 * blocks)
        def _(place):
            landed(block(chunk, place), recv_sem.at[chunk, place])

    def send(chunk, step):
        @pl.loop(0, steps[step][0])
        def _(place):
            sending(chunk, step, place).start()

    for time in range(len(chunks) + GATHER_TIMES[-1]):
        for step in range(len(steps), -1, -1):
            chunk = time - GATHER_TIMES[step]
            if 0 <= chunk < len(chunks):
                if step > 0:
                    arrive(chunk, step - 1)
                if step < len(steps):
                    send(chunk, step)
    for chunk in range(len(chunks)):
        for step in range(len(steps)):

            @pl.loop(0, steps[step][0])
            def _(place):
                sending(chunk, step, place).wait_send()


def gather_weights(n, shards, cuts):
    if n != 32 or any(shard.shape[0] % 16 for shard in shards):
        return [lax.all_gather(shard, "seq", axis=0, tiled=True) for shard in shards]
    chunks = [
        (index, first, rows, column, min(columns, shard.shape[1] - column))
        for index, (shard, (rows, columns)) in enumerate(zip(shards, cuts))
        for first in range(0, shard.shape[0], rows)
        for column in range(0, shard.shape[1], columns)
    ]
    sems = [pltpu.SemaphoreType.DMA((len(chunks), n))] * 2
    return pl.pallas_call(
        functools.partial(gather_kernel, n, chunks),
        out_shape=[
            jax.ShapeDtypeStruct((n * shard.shape[0], shard.shape[1]), shard.dtype) for shard in shards
        ],
        in_specs=[pl.BlockSpec(memory_space=pltpu.VMEM)] * len(shards),
        out_specs=[pl.BlockSpec(memory_space=pltpu.HBM)] * len(shards),
        scratch_shapes=[pltpu.SemaphoreType.DMA((len(shards),))] + sems,
        compiler_params=pltpu.CompilerParams(
            collective_id=0, has_side_effects=True, vmem_limit_bytes=16 * 2**20
        ),
        cost_estimate=pl.CostEstimate(flops=0, bytes_accessed=2**25, transcendentals=0),
    )(*shards)


SUM_ROWS, SUM_COLUMNS, SUM_SLOTS = 32, 512, 8
SUM_TIMES = [0, 1, 3, 4, 6, 7]


class Sums:
    def __init__(self, here, find, left, right, out, kept, sent, got, send_sem, recv_sem):
        self.here, self.find, self.left, self.right, self.out = here, find, left, right, out
        self.kept, self.sent, self.got = kept, sent, got
        self.send_sem, self.recv_sem = send_sem, recv_sem
        self.steps = here.halves()[::-1]
        self.chunks = got.shape[0]
        self.times = self.chunks + SUM_TIMES[-1]

    def copy(self, chunk, step):
        blocks, partner = self.steps[step]
        cut = pl.ds(blocks * SUM_ROWS, blocks * SUM_ROWS)
        return remote(
            self.sent.at[chunk % SUM_SLOTS, cut],
            self.got.at[chunk, cut],
            self.send_sem.at[chunk, step],
            self.recv_sem.at[chunk, step],
            partner,
        )

    def sent_all(self, chunk):
        for step in range(len(self.steps)):
            self.copy(chunk, step).wait_send()

    def product(self, chunk, first, rows):
        which, column = self.find(chunk)
        left = self.left[which, pl.ds(first, rows)]
        start = pl.multiple_of(column * SUM_COLUMNS, SUM_COLUMNS)
        return dot(left, self.right[:, pl.ds(start, SUM_COLUMNS)])

    def begin(self, chunk):
        half = self.here.n // 2 * SUM_ROWS
        slot = chunk % SUM_SLOTS

        @pl.when(chunk >= SUM_SLOTS)
        def _():
            self.sent_all(chunk - SUM_SLOTS)

        self.sent[slot, pl.ds(half, half)] = self.product(chunk, half, half).astype(BF)
        self.copy(chunk, 0).start()
        self.kept[slot] = self.product(chunk, 0, half)

    def go_on(self, chunk, step):
        slot, rows = chunk % SUM_SLOTS, self.steps[step - 1][0] * SUM_ROWS
        self.copy(chunk, step - 1).wait_recv()
        total = self.kept[slot, pl.ds(0, rows)] + self.got[chunk, pl.ds(rows, rows)].astype(F32)
        if step == len(self.steps):
            start = pl.multiple_of(chunk * SUM_COLUMNS, SUM_COLUMNS)
            self.out[:, pl.ds(start, SUM_COLUMNS)] = total
            return
        half = rows // 2
        self.sent[slot, pl.ds(half, half)] = total[half:].astype(BF)
        self.copy(chunk, step).start()
        self.kept[slot, pl.ds(0, half)] = total[:half]

    def run(self, first, stop):
        @pl.loop(first, stop)
        def _(time):
            for step in range(len(self.steps), -1, -1):
                chunk = time - SUM_TIMES[step]

                @pl.when((chunk >= 0) & (chunk < self.chunks))
                def _():
                    if step == 0:
                        self.begin(chunk)
                    else:
                        self.go_on(chunk, step)

    def end(self):
        @pl.loop(max(0, self.chunks - SUM_SLOTS), self.chunks)
        def _(chunk):
            self.sent_all(chunk)


def sums_scratch(n, chunks):
    rows, phases = n * SUM_ROWS, n.bit_length() - 1
    return [
        pltpu.VMEM((SUM_SLOTS, rows // 2, SUM_COLUMNS), F32),
        pltpu.VMEM((SUM_SLOTS, rows, SUM_COLUMNS), BF),
        pltpu.VMEM((chunks, rows, SUM_COLUMNS), BF),
        pltpu.SemaphoreType.DMA((chunks, phases)),
        pltpu.SemaphoreType.DMA((chunks, phases)),
    ]


def local_find(chunk):
    return (chunk + 6) // 8, chunk


def last_find(chunk):
    late, rest = chunk // 16, chunk - 16
    return late * (1 + (rest + 7) // 16 + (rest + 5) // 16), chunk


def last_kernel(
    n, grad_ref, parted_ref, small_ref, left_ref, right_ref,
    d_weight_ref, d_small_ref, out_ref,
    known, small_kept, small_got, g_send, g_recv, t_send, t_recv, *scratch
):
    here = Place(n)
    rows = grad_ref.shape[0]
    greet(n)
    known[pl.ds(0, rows)] = grad_ref[...]
    small_kept[...] = small_ref[...]
    sums = Sums(here, last_find, left_ref, right_ref, out_ref, *scratch)
    steps = here.halves()
    copies = []
    for step in range(len(steps)):
        blocks, partner = steps[step]
        source, target = pl.ds(0, blocks * rows), pl.ds(blocks * rows, blocks * rows)
        gather = remote(known.at[source], known.at[target], g_send.at[step], g_recv.at[step], partner)
        gather.start()
        blocks, partner = steps[::-1][step]
        cut, mine = pl.ds(blocks * LOG_ROWS, blocks * LOG_ROWS), pl.ds(0, blocks * LOG_ROWS)
        told = remote(small_kept.at[cut], small_got.at[cut], t_send.at[step], t_recv.at[step], partner)
        told.start()
        copies += [gather, told]
        sums.run(3 * step, 3 * step + 3)
        gather.wait_recv()
        told.wait_recv()
        small_kept[mine] = small_kept[mine] + small_got[cut]
    sums.run(3 * len(steps), sums.times)
    d_small_ref[...] = small_kept[pl.ds(0, LOG_ROWS)]
    d_weight_ref[...] = lax.dot_general(
        parted_ref[...], known[...], (((0,), (0,)), ((), ())), preferred_element_type=F32
    )
    for copy in copies:
        copy.wait_send()
    sums.end()


def last_sums(n, grad, parted, small, lefts, right):
    rows, width = grad.shape[0], parted.shape[1]
    phases, chunks = n.bit_length() - 1, right.shape[1] // SUM_COLUMNS
    return pl.pallas_call(
        functools.partial(last_kernel, n),
        out_shape=[
            jax.ShapeDtypeStruct((width, D), F32),
            jax.ShapeDtypeStruct((LOG_ROWS, 128), F32),
            jax.ShapeDtypeStruct((SUM_ROWS, right.shape[1]), F32),
        ],
        in_specs=[pl.BlockSpec(memory_space=pltpu.VMEM)] * 5,
        out_specs=[pl.BlockSpec(memory_space=pltpu.VMEM)] * 3,
        scratch_shapes=[
            pltpu.VMEM((n * rows, D), BF),
            pltpu.VMEM(small.shape, F32),
            pltpu.VMEM(small.shape, F32),
        ]
        + [pltpu.SemaphoreType.DMA((phases,))] * 4
        + sums_scratch(n, chunks),
        compiler_params=pltpu.CompilerParams(
            collective_id=1, has_side_effects=True, vmem_limit_bytes=60 * 2**20
        ),
        cost_estimate=pl.CostEstimate(flops=2**32, bytes_accessed=2**24, transcendentals=0),
    )(grad, parted, small, lefts, right)


LOG_ROWS = 8


def states_kernel(
    n, reverse, states_ref, logs_ref, left_ref, right_ref, out_ref, sum_ref, spread, logs, summed,
    s_send, s_recv, l_send, l_recv, b_send, b_recv, *scratch
):
    me = lax.axis_index("seq")
    rows = states_ref.shape[0] // n
    greet(n)
    sums = None
    if scratch:
        sums = Sums(Place(n), local_find, left_ref, right_ref, sum_ref, *scratch)

    def spreading(other):
        return remote(
            states_ref.at[rows_of(other, 1, rows)],
            spread.at[rows_of(me, 1, rows)],
            s_send.at[other],
            s_recv.at[me],
            other,
        )

    def telling(other):
        target = logs.at[rows_of(me, 1, LOG_ROWS)]
        return remote(logs_ref, target, l_send.at[other], l_recv.at[me], other)

    def returning(other):
        return remote(
            summed.at[rows_of(other, 1, rows)],
            out_ref.at[rows_of(me, 1, rows)],
            b_send.at[other],
            b_recv.at[me],
            other,
        )

    @pl.loop(1, n)
    def _(hop):
        other = lax.rem(me + hop, n)
        spreading(other).start()
        telling(other).start()

    own = pltpu.make_async_copy(
        states_ref.at[rows_of(me, 1, rows)], spread.at[rows_of(me, 1, rows)], s_recv.at[me]
    )
    own_logs = pltpu.make_async_copy(logs_ref, logs.at[rows_of(me, 1, LOG_ROWS)], l_recv.at[me])
    own.start()
    own_logs.start()
    if sums:
        sums.run(0, 4)

    @pl.loop(0, n)
    def _(other):
        landed(spread.at[rows_of(other, 1, rows)], s_recv.at[other])
        landed(logs.at[rows_of(other, 1, LOG_ROWS)], l_recv.at[other])

    head = me * MHEADS // n
    lane = lax.broadcasted_iota(jnp.int32, (LOG_ROWS, 128), 1)
    row = lax.broadcasted_iota(jnp.int32, (LOG_ROWS, 128), 0)

    def join(step, total):
        place = n - 1 - step if reverse else step
        cut = rows_of(place, 1, rows)
        summed[cut] = total.astype(BF)
        told = logs[rows_of(place, 1, LOG_ROWS)]
        log = jnp.sum(jnp.where((lane == head) & (row == 0), told, 0.0), keepdims=True)
        flag = jnp.sum(jnp.where((lane == MHEADS) & (row == 0), told, 0.0), keepdims=True)
        decay = jnp.where(flag > 0.0, 0.0, jnp.exp(log))
        return decay * total + spread[cut].astype(F32)

    lax.fori_loop(0, n, join, jnp.zeros((rows, NSTATE), F32))

    @pl.loop(1, n)
    def _(hop):
        returning(lax.rem(me + hop, n)).start()

    own_back = pltpu.make_async_copy(
        summed.at[rows_of(me, 1, rows)], out_ref.at[rows_of(me, 1, rows)], b_recv.at[me]
    )
    own_back.start()
    if sums:
        sums.run(4, sums.times)
        sums.end()

    @pl.loop(0, n)
    def _(other):
        landed(out_ref.at[rows_of(other, 1, rows)], b_recv.at[other])

    @pl.loop(1, n)
    def _(hop):
        other = lax.rem(me + hop, n)
        spreading(other).wait_send()
        telling(other).wait_send()
        returning(other).wait_send()


def pass_states(n, states, logs, lefts=None, right=None):
    total, reverse = MHEADS * MHEAD_DIM, lefts is not None
    told = jnp.zeros((LOG_ROWS, 128), F32).at[0, : logs.shape[0]].set(logs)
    summing = reverse and n == 32
    chunks = right.shape[1] // SUM_COLUMNS if summing else 0
    small = jnp.zeros((LOG_ROWS, 128), F32)
    operands = [states.reshape(total, NSTATE).astype(BF), told]
    operands += [lefts, right] if summing else [small, small]
    out, found = pl.pallas_call(
        functools.partial(states_kernel, n, reverse),
        out_shape=[
            jax.ShapeDtypeStruct((total, NSTATE), BF),
            jax.ShapeDtypeStruct((SUM_ROWS, chunks * SUM_COLUMNS) if summing else (LOG_ROWS, 128), F32),
        ],
        in_specs=[pl.BlockSpec(memory_space=pltpu.VMEM)] * 4,
        out_specs=[pl.BlockSpec(memory_space=pltpu.VMEM)] * 2,
        scratch_shapes=[
            pltpu.VMEM((total, NSTATE), BF),
            pltpu.VMEM((n * LOG_ROWS, 128), F32),
            pltpu.VMEM((total, NSTATE), BF),
        ]
        + [pltpu.SemaphoreType.DMA((n,))] * 6
        + (sums_scratch(n, chunks) if summing else []),
        compiler_params=pltpu.CompilerParams(
            collective_id=3 if reverse else 2,
            has_side_effects=True,
            vmem_limit_bytes=(48 if summing else 16) * 2**20,
        ),
        cost_estimate=pl.CostEstimate(flops=2**22, bytes_accessed=2**21, transcendentals=0),
    )(*operands)
    return out.astype(F32).reshape(MHEADS, MHEAD_DIM, NSTATE), found


ATTN_ROWS = 128


def tile_mask():
    row = lax.broadcasted_iota(jnp.int32, (ATTN_ROWS, ATTN_ROWS), 0)
    column = lax.broadcasted_iota(jnp.int32, (ATTN_ROWS, ATTN_ROWS), 1)
    return (row // PATCH == column // PATCH) & (row >= column)


def head_mask(which):
    lane = lax.broadcasted_iota(jnp.int32, (1, 2 * AHEAD_DIM), 1)
    return lane // AHEAD_DIM == which


def only(values, mask):
    return jnp.where(mask, values, jnp.zeros_like(values))


def tile_probs(queries, key_rows, mask):
    scores = dot_t(queries, key_rows) * AHEAD_DIM ** (-0.5)
    scores = jnp.where(mask, scores, -1e30)
    raised = jnp.exp(scores - jnp.max(scores, axis=-1, keepdims=True))
    return raised / jnp.sum(raised, axis=-1, keepdims=True)


def attention_kernel(triple_ref, out_ref):
    mask = tile_mask()
    width = 2 * AHEAD_DIM
    for pair in range(AHEADS // 2):
        queries, key_rows, value_rows = [
            triple_ref[:, part * D + pair * width : part * D + (pair + 1) * width] for part in range(3)
        ]
        total = None
        for which in range(2):
            lanes = head_mask(which)
            probs = tile_probs(only(queries, lanes), key_rows, mask)
            mixed = dot(probs.astype(BF), only(value_rows, lanes))
            total = mixed if total is None else total + mixed
        out_ref[:, pair * width : (pair + 1) * width] = total.astype(BF)


def attention(triple):
    rows = triple.shape[0]
    return pl.pallas_call(
        attention_kernel,
        grid=(rows // ATTN_ROWS,),
        out_shape=jax.ShapeDtypeStruct((rows, D), BF),
        in_specs=[pl.BlockSpec((ATTN_ROWS, 3 * D), lambda i: (i, 0))],
        out_specs=pl.BlockSpec((ATTN_ROWS, D), lambda i: (i, 0)),
    )(triple)


def attention_back_kernel(triple_ref, grad_ref, out_ref):
    mask = tile_mask()
    width = 2 * AHEAD_DIM
    scale = AHEAD_DIM ** (-0.5)
    rows_first = (((0,), (0,)), ((), ()))
    for pair in range(AHEADS // 2):
        lo, hi = pair * width, (pair + 1) * width
        queries, key_rows, value_rows = [
            triple_ref[:, part * D + lo : part * D + hi] for part in range(3)
        ]
        grad = grad_ref[:, lo:hi]
        totals = [None, None, None]
        for which in range(2):
            lanes = head_mask(which)
            probs = tile_probs(only(queries, lanes), key_rows, mask)
            grad_one = only(grad, lanes)
            d_probs = dot_t(grad_one, value_rows)
            d_scores = probs * (d_probs - jnp.sum(probs * d_probs, axis=-1, keepdims=True))
            d_scores = d_scores.astype(BF)
            found = [
                scale * dot(d_scores, only(key_rows, lanes)),
                scale
                * lax.dot_general(
                    d_scores, only(queries, lanes), rows_first, preferred_element_type=F32
                ),
                lax.dot_general(
                    probs.astype(BF), grad_one, rows_first, preferred_element_type=F32
                ),
            ]
            totals = found if which == 0 else [a + b for a, b in zip(totals, found)]
        for part in range(3):
            out_ref[:, part * D + lo : part * D + hi] = totals[part].astype(BF)


def attention_back(triple, grad):
    rows = triple.shape[0]
    return pl.pallas_call(
        attention_back_kernel,
        grid=(rows // ATTN_ROWS,),
        out_shape=jax.ShapeDtypeStruct((rows, 3 * D), BF),
        in_specs=[
            pl.BlockSpec((ATTN_ROWS, 3 * D), lambda i: (i, 0)),
            pl.BlockSpec((ATTN_ROWS, D), lambda i: (i, 0)),
        ],
        out_specs=pl.BlockSpec((ATTN_ROWS, 3 * D), lambda i: (i, 0)),
    )(triple, grad)


def local(
    byte_acts,
    resets,
    out_grad,
    patch_weight,
    patch_gain,
    mixer_in,
    conv_weight,
    conv_bias,
    head_params,
    mixer_gain,
    mixer_out,
    unpatch_weight,
    attn_gain,
    qkv_weight,
    attn_out,
    ffn_gain,
    gate_up,
    down_weight,
):
    n = lax.axis_size("seq")
    me = lax.axis_index("seq")
    ring = Ring(n)

    def passed_along(block, distance):
        route = [(i - distance, i) for i in range(n) if 0 <= i - distance < n]
        return lax.ppermute(block, "seq", route)

    live = Live()
    order = ring.order()

    byte_wide = byte_acts.astype(F32)
    patches = byte_acts.reshape(-1, PATCH * D)
    patch_rows = patches.shape[0]
    unpack_early = gather_flat(n, [unpatch_weight, qkv_weight, attn_out])
    unpack_late = gather_flat(n, [gate_up, down_weight])
    small = [patch_gain, conv_weight.reshape(-1), conv_bias, mixer_gain, attn_gain, ffn_gain]
    cuts = list(np.cumsum([piece.shape[0] for piece in small]))
    small_all = gather_small(ring, jnp.concatenate(small)).astype(F32)
    parts = jnp.split(small_all, cuts[:-1], axis=1)
    live.patch_gain = parts[0].reshape(-1)
    live.conv_weight = parts[1].reshape(n, CONV, -1).transpose(1, 0, 2).reshape(CONV, CONV_CH)
    live.conv_bias, live.mixer_gain, live.attn_gain, live.ffn_gain = [
        piece.reshape(-1) for piece in parts[2:]
    ]
    live.fence()

    live.patch_w, live.mixer_in, live.mixer_out = gather_weights(
        n,
        [patch_weight, jnp.pad(mixer_in, ((0, 0), (0, -mixer_in.shape[1] % 128))), mixer_out],
        [(32, D), (16, 2304), (32, D)],
    )
    live.embedded = dot(patches, live.patch_w)
    live.normed = rms_scale(live.embedded, live.patch_gain).astype(BF)
    projected = dot(live.normed, live.mixer_in)
    live.gate_z = projected[:, :DI]
    conv_in = projected[:, DI : DI + CONV_CH].astype(BF).astype(F32)
    dt_raw = projected[:, DI + CONV_CH : DI + CONV_CH + MHEADS]
    logs = jnp.sum(-jax.nn.softplus(dt_raw + head_params[0]) * jnp.exp(head_params[1]), axis=0)
    flag = jnp.max(resets).astype(F32)
    live.logs = jnp.concatenate([logs, flag[None]])
    not_reset = 1.0 - resets.astype(F32)
    keep_tail = jnp.concatenate(
        [jnp.cumprod(not_reset[patch_rows - CONV + 2 :][::-1])[::-1], jnp.ones((1,), F32)]
    )
    tail_sent = (conv_in[patch_rows - CONV + 1 :] * keep_tail[:, None]).astype(BF)
    halo_rows = passed_along(tail_sent, 1)
    flags_ext = jnp.concatenate([jnp.zeros((CONV - 1,), jnp.int32), resets])
    validity = tap_masks(flags_ext, patch_rows)
    conv_ext = jnp.concatenate([halo_rows.astype(F32), conv_in])
    conv_out, conv_back = jax.vjp(
        functools.partial(conv_apply, validity=validity, row_count=patch_rows),
        conv_ext,
        live.conv_weight,
        live.conv_bias,
    )
    state_parts, state_back = jax.vjp(
        functools.partial(block_state, starts=resets), conv_out, dt_raw, head_params
    )
    local_state, decay_total = state_parts
    live.state_in, _ = pass_states(n, local_state, live.logs)
    live.fence()

    mixer_y, output_back = jax.vjp(
        functools.partial(block_output, starts=resets),
        conv_out,
        dt_raw,
        head_params,
        live.state_in,
    )
    gate_act = silu(live.gate_z)
    gated = mixer_y * gate_act
    live.gated_norm = rms_scale(gated, live.mixer_gain).astype(BF)
    branch = dot(live.gated_norm, live.mixer_out)
    live.hidden = (live.embedded + branch).astype(BF)
    live.unpatch, live.qkv_w, live.attn_out = unpack_early()
    slots = dot(live.hidden, live.unpatch)
    live.stream0 = byte_wide + slots.reshape(-1, D)
    live.normed0 = rms_scale(live.stream0, live.attn_gain).astype(BF)
    live.fence()

    rows = byte_wide.shape[0]
    live.triple = dot(live.normed0, live.qkv_w).astype(BF)
    live.mixed = attention(live.triple)
    live.stream1 = live.stream0 + dot(live.mixed, live.attn_out)
    live.normed1 = rms_scale(live.stream1, live.ffn_gain).astype(BF)
    live.gate_up, live.down_w = unpack_late()
    both = dot(live.normed1, live.gate_up)
    live.both = both.astype(BF)
    live.hid = (silu(both[:, :FF]) * both[:, FF:]).astype(BF)
    parted = patches.reshape(patch_rows, n, -1).transpose(1, 0, 2)
    live.parted = lax.all_to_all(parted, "seq", 0, 0, tiled=True)
    live.fence()

    small_slice = n == 32

    def in_order(values):
        blocks = values.reshape(n, -1, values.shape[-1])
        return jnp.take(blocks, order, axis=0).reshape(-1, values.shape[-1])

    def lefts_of(values):
        if not small_slice:
            return values
        turned = in_order(values.T).reshape(n, -1, SUM_ROWS, values.shape[0])
        return turned.transpose(1, 0, 2, 3).reshape(-1, n * SUM_ROWS, values.shape[0])

    layer_out = (live.stream1 + dot(live.hid, live.down_w)).astype(BF)
    d_hid = dot_t(out_grad, live.down_w)
    gate, up = live.both[:, :FF].astype(F32), live.both[:, FF:].astype(F32)
    d_both = jnp.concatenate([d_hid * up * silu_slope(gate), d_hid * silu(gate)], axis=1).astype(BF)
    if small_slice:
        block = down_weight.shape[0]
        flat = flat_grads(n, live.hid, out_grad, live.normed1, d_both)
        found = lax.psum_scatter(flat, "seq", scatter_dimension=0, tiled=True)[0].astype(F32)
        g_down = found[:block]
        g_gate_up = found[block:].reshape(-1, SUM_ROWS, D).transpose(1, 0, 2)
        g_gate_up = g_gate_up.reshape(SUM_ROWS, -1)
    else:
        g_down = summed_grad(live.hid, out_grad)
        g_gate_up = summed_grad(live.normed1, d_both)
    d_normed1 = dot_t(d_both, live.gate_up)
    d_stream1, g_ffn_gain = rms_back(live.stream1, live.ffn_gain, d_normed1)
    d_stream1 = out_grad.astype(F32) + d_stream1
    d_stream1_low = d_stream1.astype(BF)
    d_mixed = dot_t(d_stream1_low, live.attn_out).astype(BF)
    d_triple = attention_back(live.triple, d_mixed)
    d_stream0, g_attn_gain = rms_back(live.stream0, live.attn_gain, dot_t(d_triple, live.qkv_w))
    live.d_stream0 = d_stream1 + d_stream0
    d_slots = live.d_stream0.astype(BF).reshape(patch_rows, PATCH * D)
    d_hidden = dot_t(d_slots, live.unpatch)
    d_branch = d_hidden.astype(BF)
    d_gated, g_mixer_gain = rms_back(gated, live.mixer_gain, dot_t(d_branch, live.mixer_out))
    d_gate_z = d_gated * mixer_y * silu_slope(live.gate_z)
    output_grads = output_back(d_gated * gate_act)
    state_grad, found = pass_states(
        n,
        output_grads[3],
        live.logs,
        jnp.concatenate([lefts_of(live.mixed), lefts_of(live.normed0)], axis=0),
        jnp.concatenate([d_stream1_low, d_triple], axis=1),
    )
    g_attn_out, g_qkv = found[:, :D], found[:, D:]
    decay_grad = jnp.sum(state_grad * live.state_in, axis=(1, 2))
    state_cot = state_back((state_grad, decay_grad))
    conv_cot = conv_back(output_grads[0] + state_cot[0])
    returned = passed_along(conv_cot[0][: CONV - 1], -1)
    d_conv_in = conv_cot[0][CONV - 1 :] + jnp.concatenate(
        [jnp.zeros((patch_rows - CONV + 1, CONV_CH), F32), returned * keep_tail[:, None]]
    )
    d_dt = output_grads[1] + state_cot[1]
    d_projected = jnp.concatenate([d_gate_z, d_conv_in, d_dt], axis=1).astype(BF)
    d_projected = jnp.pad(d_projected, ((0, 0), (0, -d_projected.shape[1] % 128)))
    d_embedded, g_patch_gain = rms_back(
        live.embedded, live.patch_gain, dot_t(d_projected, live.mixer_in)
    )
    d_embedded = (d_hidden + d_embedded).astype(BF)
    d_patches = dot_t(d_embedded, live.patch_w).reshape(-1, D)
    input_grad = (live.d_stream0 + d_patches).astype(BF)

    g_conv_weight = conv_cot[1].reshape(CONV, n, -1).transpose(1, 0, 2).reshape(n, -1)
    g_head = jnp.broadcast_to((output_grads[2] + state_cot[2]).reshape(1, -1), (n, 3 * MHEADS))
    g_small = [g_patch_gain, g_conv_weight, conv_cot[2], g_mixer_gain, g_attn_gain, g_ffn_gain, g_head]
    g_small = jnp.concatenate([piece.reshape(n, -1) for piece in g_small], axis=1)
    small_width = g_small.shape[1]
    g_small = jnp.pad(g_small, ((0, 0), (0, LOG_ROWS * 128 - small_width)))
    g_small = g_small.reshape(n * LOG_ROWS, 128)
    if small_slice:
        lefts = [lefts_of(live.hidden), lefts_of(live.normed), lefts_of(live.gated_norm)]
        d_projected = jnp.pad(d_projected, ((0, 0), (0, -d_projected.shape[1] % SUM_COLUMNS)))
        g_patch, g_small, found = last_sums(
            n,
            d_embedded,
            in_order(live.parted),
            in_order(g_small),
            jnp.concatenate(lefts, axis=0),
            jnp.concatenate([d_slots, d_projected, d_branch, d_branch], axis=1),
        )
        g_unpatch = found[:, : PATCH * D]
        g_mixer_in = found[:, PATCH * D : PATCH * D + mixer_in.shape[1]]
        g_mixer_out = found[:, found.shape[1] - 2 * D :].reshape(SUM_ROWS, 2, D)
        g_mixer_out = g_mixer_out.transpose(1, 0, 2).reshape(-1, D)
    else:
        g_attn_out = summed_grad(live.mixed, d_stream1_low)
        g_qkv = summed_grad(live.normed0, d_triple)
        known = lax.all_gather(d_embedded, "seq", axis=0, tiled=True)
        g_patch = dot(live.parted.reshape(n * patch_rows, -1).T, known)
        g_small = lax.psum_scatter(g_small, "seq", scatter_dimension=0, tiled=True)
        g_unpatch = summed_grad(live.hidden, d_slots)
        g_mixer_in = summed_grad(live.normed, d_projected)[:, : mixer_in.shape[1]]
        g_mixer_out = summed_grad(live.gated_norm, d_branch)
    g_small = g_small.reshape(-1)[:small_width]
    s = jnp.split(g_small, cuts)
    return (
        layer_out,
        input_grad,
        g_patch,
        s[0],
        g_mixer_in,
        s[1].reshape(CONV, -1),
        s[2],
        s[6].reshape(3, MHEADS),
        s[3],
        g_mixer_out,
        g_unpatch,
        s[4],
        g_qkv,
        g_attn_out,
        s[5],
        g_gate_up,
        g_down,
    )


def solution(mesh):
    rows, vector = P("seq", None), P("seq")
    placed = (
        rows, vector, rows, rows, vector, rows, P(None, "seq"), vector, P(),
        vector, rows, rows, vector, rows, rows, vector, rows, rows,
    )
    returned = (
        rows, rows, rows, vector, rows, P(None, "seq"), vector, P(), vector,
        rows, rows, vector, rows, rows, vector, rows, rows,
    )
    return jax.shard_map(
        local, mesh=mesh, in_specs=placed, out_specs=returned, check_vma=False
    )
```

time: 1490 us -> 1080 us (0.72)
  Pallas kernels: 79.9 us -> 682 us
  waiting for transfers between devices: 446 us -> 8.45 us
  starting transfers between devices: 244 us -> 15.7 us
  other arithmetic: 229 us -> 71.2 us
  matrix products: 302 us -> 160 us
  local copies, waits for them, and re-layouts: 179 us -> 111 us
    pallas_call x10 -> x11, Pallas kernels: 79.9 us -> 682 us  [the longest x1 250 us: gather_weights(): pl.pallas_call(functools.partial(gather_kernel, n, chunks), out_shape=[ja...]
    ppermute x57 -> x0, waiting for transfers between devices: 226 us -> none  [the longest x27 117 us: scatter_sum(): held = held + lax.ppermute(total[hop], 'seq', ring.shift[hop]).astype(F32)]
    ppermute x97 -> x6, waiting for transfers between devices: 208 us -> 8.35 us  [swap(): return lax.ppermute(block, 'seq', route)]
    ppermute x57 -> x0, starting transfers between devices: 153 us -> none  [the longest x30 82.2 us: along_z(): lax.ppermute(shard, 'seq', ring.shift[hop])]
    dot_general x40 -> x0, matrix products: 135 us -> none  [the longest x32 119 us: part(): lax.dot_general(ordered[:, start * block:stop * block], right, (((0,), (0...]
    convert_element_type x42 -> x8, other arithmetic: 143 us -> 15.1 us  [the longest x1 8.83 us: local(): live.hid = (silu(both[:, :FF]) * both[:, FF:]).astype(BF)]
    ppermute x97 -> x6, starting transfers between devices: 71.3 us -> 6.49 us  [swap(): return lax.ppermute(block, 'seq', route)]
    convert_element_type x11 -> x0, local copies, waits for them, and re-layouts: 33.9 us -> none  [the longest x3 21.2 us: local(): d_triple = jnp.stack(d_qkv, axis=2).astype(BF).reshape(rows, 3 * D)]
  transfers between devices with their start and end apart: 160 -> 12, of which waited for: 46 -> 3; matrix products, arithmetic and copies ran while one was open for 34% -> 26% of each run, Pallas kernels for 4% -> 62%
where the time goes in v2:
time: 1080 us; the launch traced here: 1060 us
  Pallas kernels  682 us (63%)
  matrix products  160 us (15%)
  local copies, waits for them, and re-layouts  111 us (10%)
  other arithmetic  71.2 us (7%)
  between operations  17.4 us (2%)
  starting transfers between devices  15.7 us (1%)
    pallas_call x1, Pallas kernels, gather_weights(): pl.pallas_call(functools.partial(gather_kernel, n, chunks), out_shape=[ja...  250 us
    pallas_call x1, Pallas kernels, last_sums(): pl.pallas_call(functools.partial(last_kernel, n), out_shape=[jax.ShapeDty...  176 us
    pallas_call x2, Pallas kernels, pass_states(): pl.pallas_call(functools.partial(states_kernel, n, reverse), out_shape=[j...  166 us
    dot_general x8, matrix products, dot_t(): lax.dot_general(left, right, (((1,), (1,)), ((), ())), preferred_element_...  73.5 us
    dot_general x8, matrix products, dot(): return jnp.dot(left, right, preferred_element_type=F32)  58.9 us
    unnamed x301, local copies, waits for them, and re-layouts  38.1 us
    pallas_call x1, Pallas kernels, attention_back(): pl.pallas_call(attention_back_kernel, grid=(rows // ATTN_ROWS,), out_shap...  26.8 us
    pallas_call x2, Pallas kernels, unpack(): pl.pallas_call(functools.partial(unpack_kernel, n, slots, shapes), out_sh...  25.3 us
  transfers between devices with their start and end apart: 12, of which 3 were waited for; matrix products, arithmetic and copies ran while one was open for 26% of the time, Pallas kernels for 62%

profile of v2, /device:TPU:0, one launch (start us, length us, event | category | flops | bytes accessed | tf_op | source)
XLA Modules:
  0.0 1064.9 jit_solution(15076965996381974222)
XLA Ops:
  11.9 3.1 collective-permute-start
  17.2 5.0 all-to-all-start
  26.7 249.7 %shard_map.314 = (bf16[8192,1024]{1,0:T(8,128)(2,1)S(1)}, bf16[1024,4480]{1,0:T(8,128)(2,1)S(1)}, bf16[2048,1024]{1,0:T(8,128)(2,1)S(1)}) custom-call(bf16[256,1024]{1,0:T(8,128)(2,1)S(1)} %copy-done.10, bf16[32,4480]{1,0:T(8,128)(2,1)S(1)} %pad.87.refs_1_, bf16[64,1024]{1,0:T(8,128)(2,1)S(1)} %copy-done.11), custom_call_target="tpu_custom_call" | custom-call | bytes 33554432 | tf_op jit(solution)/shard_map/pallas_call | solution.py:500
  276.4 3.6 copy-done.2
  283.1 5.2 multiply_reduce_fusion.24
  288.5 4.7 collective-permute-done.1
  303.8 5.4 fusion.103
  309.4 2.8 collective-permute-start.6
  323.6 50.1 %shard_map.315 = (bf16[2048,128]{1,0:T(8,128)(2,1)S(1)}, f32[8,128]{1,0:T(8,128)}) custom-call(bf16[2048,128]{1,0:T(8,128)(2,1)S(1)} %bitcast.165, f32[8,128]{1,0:T(8,128)S(1)} %scatter.6.logs_ref, f32[8,128]{1,0:T(8,128)S(1)} %broadcast_22_left_ref_right_ref.2.left_ref.right_ref, f32[8,128]{1,0:T(8,128)S(1)} %broadcast_22_left_ref_right_ref.2.left_ref.right_ref), custom_call_target="tpu_custom_call" | custom-call | flops 4194304 | bytes 2097152 | tf_op jit(solution)/shard_map/pallas_call | solution.py:780
  376.0 3.2 fusion.17
  383.0 3.2 fusion.18
  386.3 13.8 %shard_map.317 = (bf16[1024,8192]{1,0:T(8,128)(2,1)S(1)}, bf16[1024,3072]{1,0:T(8,128)(2,1)S(1)}, bf16[1024,1024]{1,0:T(8,128)(2,1)S(1)}) custom-call(bf16[12288,1024]{1,0:T(8,128)(2,1)} %all-gather.3.cloned.1.call-done.flat_ref), custom_call_target="tpu_custom_call" | custom-call | bytes 50331648 | tf_op jit(solution)/shard_map/pallas_call | solution.py:179
  400.1 5.8 copy-done.1
  405.8 2.7 copy-done.13
  409.9 10.2 fusion.104
  420.1 2.9 reshape.629
  427.6 4.8 convolution_convert_fusion.triple_ref
  432.4 14.7 %shard_map.318 = bf16[512,1024]{1,0:T(8,128)(2,1)} custom-call(bf16[512,3072]{1,0:T(8,128)(2,1)} %convolution_convert_fusion.triple_ref), custom_call_target="tpu_custom_call" | custom-call | tf_op jit(solution)/shard_map/pallas_call | solution.py:848
  447.1 3.3 multiply_reduce_fusion.6
  452.0 11.5 %shard_map.320 = (bf16[1024,8192]{1,0:T(8,128)(2,1)S(1)}, bf16[4096,1024]{1,0:T(8,128)(2,1)S(1)}) custom-call(bf16[12288,1024]{1,0:T(8,128)(2,1)} %all-gather.5.cloned.1.call-done.flat_ref), custom_call_target="tpu_custom_call" | custom-call | bytes 50331648 | tf_op jit(solution)/shard_map/pallas_call | solution.py:179
  463.5 5.8 copy-done.5
  469.4 3.3 copy-done.12
  472.7 18.5 %fusion.101 = (bf16[512,8192]{1,0:T(8,128)(2,1)}, f32[512,8192]{1,0:T(8,128)}) fusion(bf16[512,1024]{1,0:T(8,128)(2,1)S(1)} %multiply_convert_fusion.normed_ref, bf16[1024,8192]{1,0:T(8,128)(2,1)} %copy-done.5), kind=kOutput, calls=%fused_computation.266 | convolution fusion | flops 8594128896 | bytes 42991616 | tf_op jit(solution)/shard_map/dot_general | solution.py:273
  491.2 8.8 fusion.9.hid_ref
  500.0 14.0 %fusion.6 = (bf16[512,4096]{1,0:T(8,128)(2,1)}, bf16[512,4096]{1,0:T(8,128)(2,1)}) fusion(bf16[512,8192]{1,0:T(8,128)(2,1)} %get-tuple-element.177, bf16[4096,1024]{1,0:T(8,128)(2,1)} %copy-done.12, bf16[512,1024]{1,0:T(8,128)(2,1)S(1)} %copy-done.9), kind=kOutput, calls=%fused_computation.17 | convolution fusion | flops 4326424576 | bytes 26214400 | tf_op jit(solution)/shard_map/dot_general | solution.py:277
  514.0 7.8 pad_maximum_fusion.both_ref
  521.8 3.4 copy-done.6
  527.4 19.1 %shard_map.324 = bf16[32,384,1024]{2,1,0:T(8,128)(2,1)} custom-call(bf16[512,4096]{1,0:T(8,128)(2,1)S(1)} %copy-done.7, bf16[512,1024]{1,0:T(8,128)(2,1)S(1)} %copy-done.9, bf16[512,1024]{1,0:T(8,128)(2,1)S(1)} %multiply_convert_fusion.normed_ref, bf16[512,8192]{1,0:T(8,128)(2,1)S(1)} %copy-done.6), custom_call_target="tpu_custom_call" | custom-call | flops 12884901888 | bytes 33554432 | tf_op jit(solution)/shard_map/pallas_call | solution.py:252
  550.7 2.6 multiply_reduce_fusion.3
  553.3 17.0 %multiply_reduce_fusion = (f32[1024]{0:T(1024)}, f32[512]{0:T(512)S(1)}, f32[512,1024]{1,0:T(8,128)}) fusion(f32[512,1024]{1,0:T(8,128)} %copy-done.21, f32[512]{0:T(512)S(1)} %get-tuple-element.286, f32[1024]{0:T(1024)S(1)} %reshape.617, bf16[1024,8192]{1,0:T(8,128)(2,1)} %copy-done.5, bf16[512,4096]{1,0:T(8,128)(2,1)} %get-tuple-element.260, ...), kind=kOutput, calls=%fused_computation.32 | convolution fusion | flops 8609855488 | bytes 29372416 | tf_op jit(solution)/shard_map/dot_general | solution.py:277
  570.2 4.8 fusion.96
  578.3 26.8 %shard_map.321 = bf16[512,3072]{1,0:T(8,128)(2,1)} custom-call(bf16[512,3072]{1,0:T(8,128)(2,1)} %convolution_convert_fusion.triple_ref, bf16[512,1024]{1,0:T(8,128)(2,1)} %convolution_convert_fusion.2.grad_ref), custom_call_target="tpu_custom_call" | custom-call | tf_op jit(solution)/shard_map/pallas_call | solution.py:893
  605.1 8.5 multiply_reduce_fusion.1
  616.8 12.1 %fusion.102 = (bf16[64,1024]{1,0:T(8,128)(2,1)S(1)}, f32[64,1024]{1,0:T(8,128)}) fusion(bf16[64,8192]{1,0:T(8,128)(2,1)} %reshape.630, bf16[1024,8192]{1,0:T(8,128)(2,1)} %copy-done.1), kind=kOutput, calls=%fused_computation.267 | convolution fusion | flops 1073807360 | bytes 18219008 | tf_op jit(solution)/shard_map/dot_general | solution.py:277
  641.1 4.8 fusion.42
  652.2 2.5 pad_maximum_fusion.1.right_ref
  654.7 116.0 %shard_map.322 = (bf16[2048,128]{1,0:T(8,128)(2,1)S(1)}, f32[32,4096]{1,0:T(8,128)S(1)}) custom-call(bf16[2048,128]{1,0:T(8,128)(2,1)S(1)} %convolution_convert_fusion.1.states_ref, f32[8,128]{1,0:T(8,128)S(1)} %scatter.9.logs_ref, bf16[2,1024,512]{2,1,0:T(8,128)(2,1)S(1)} %pad_maximum_fusion.2.left_ref, bf16[512,4096]{1,0:T(8,128)(2,1)} %pad_maximum_fusion.1.right_ref), custom_call_target="tpu_custom_call" | custom-call | flops 4194304 | bytes 2097152 | tf_op jit(solution)/shard_map/pallas_call | solution.py:780
  771.1 3.3 broadcast_multiply_fusion.1
  778.4 2.8 copy.182
  783.6 4.0 fusion.15
  791.4 3.1 convolution_bitcast_fusion.5
  804.9 3.0 gather_fusion.1
  807.9 2.6 gather_fusion.3
  826.7 8.3 add_convert_fusion.1
  838.2 6.7 multiply_reduce_fusion.21
  848.9 175.9 %shard_map.323 = (f32[256,1024]{1,0:T(8,128)}, f32[8,128]{1,0:T(8,128)}, f32[32,14848]{1,0:T(8,128)}) custom-call(bf16[64,1024]{1,0:T(8,128)(2,1)} %add_convert_fusion.2.grad_ref, bf16[2048,256]{1,0:T(8,128)(2,1)} %bitcast_select_fusion.parted_ref, f32[256,128]{1,0:T(8,128)} %bitcast_select_fusion.1.small_ref, ...), custom_call_target="tpu_custom_call" | custom-call | flops 4294967296 | bytes 16777216 | tf_op jit(solution)/shard_map/pallas_call | solution.py:653
  1034.0 11.0 %fusion.105 = f32[64,8192]{1,0:T(8,128)S(1)} fusion(bf16[64,1024]{1,0:T(8,128)(2,1)S(1)} %copy-done.72, bf16[8192,1024]{1,0:T(8,128)(2,1)} %copy-done), kind=kOutput, calls=%fused_computation.270 | convolution fusion | flops 1073741824 | bytes 19005440 | tf_op jit(solution)/shard_map/dot_general | solution.py:277
  1050.2 3.5 add_convert_fusion
  (514 shorter events, 142.0 us)
Async XLA Ops:
  7.3 379.0 %all-gather.3.cloned.1.call-start = ((), (), s32[]{:S(2)}) async-start(), calls=%async_computation.2 | async-start | bytes 25952256 | tf_op jit(solution)/shard_map/all_gather | solution.py:176
  9.5 442.5 %all-gather.5.cloned.1.call-start = ((), (), s32[]{:S(2)}) async-start(), calls=%async_computation.3 | async-start | bytes 25952256 | tf_op jit(solution)/shard_map/all_gather | solution.py:176
  11.9 14.8 %copy-start.77 = (bf16[32,4384]{1,0:T(8,128)(2,1)S(1)}, bf16[32,4384]{1,0:T(8,128)(2,1)}, u32[]{:S(2)}) copy-start(bf16[32,4384]{1,0:T(8,128)(2,1)} %param.33) | copy-start | bytes 841732
  11.9 276.5 %collective-permute-start = (bf16[1,520]{1,0:T(2,128)(2,1)S(1)}, bf16[1,520]{1,0:T(2,128)(2,1)S(1)}, u32[]{:S(2)}, u32[]{:S(2)}) collective-permute-start(bf16[1,520]{1,0:T(2,128)(2,1)S(1)} %broadcast_in_dim.93), channel_id=1, source_target_pairs={{0,8},{1,9},{2,10},{3,11},{4,12},{5,13},{6,14},{7,15},{8,0},{9,1},... | collective-permute-start | bytes 3128 | tf_op jit(solution)/shard_map/ppermute | solution.py:66
  15.7 267.2 %copy-start.134 = (f32[3,32]{1,0:T(4,128)S(1)}, f32[3,32]{1,0:T(4,128)}, u32[]{:S(2)}) copy-start(f32[3,32]{1,0:T(4,128)} %param.36) | copy-start | bytes 1156
  17.2 482.8 %all-to-all-start = ((bf16[32,64,256]{2,1,0:T(8,128)(2,1)}), bf16[32,64,256]{2,1,0:T(8,128)(2,1)}, u32[]{:S(2)}, u32[]{:S(2)}) async-start(bf16[32,64,256]{2,1,0:T(8,128)(2,1)} %bitcast.160), calls=%async_computation | async-start | bytes 2097152 | tf_op jit(solution)/shard_map/all_to_all | solution.py:1016
  22.2 1031.5 %reduce-scatter.2.cloned.1.call-start = ((), (), s32[]{:S(2)}) async-start(), calls=%async_computation.4 | async-start | bytes 25952256 | tf_op jit(solution)/shard_map/reduce_scatter | solution.py:1038
  282.8 30.3 %copy-start.112 = (f32[64]{0:T(128)}, f32[64]{0:T(128)S(1)}, u32[]{:S(2)}) copy-start(f32[64]{0:T(128)S(1)} %get-tuple-element.301) | copy-start | bytes 772
  282.8 30.3 %copy-start.124 = (f32[64]{0:T(128)}, f32[64]{0:T(128)S(1)}, u32[]{:S(2)}) copy-start(f32[64]{0:T(128)S(1)} %get-tuple-element.300) | copy-start | bytes 772
  282.9 32.9 %copy-start.114 = (f32[64]{0:T(128)}, f32[64]{0:T(128)S(1)}, u32[]{:S(2)}) copy-start(f32[64]{0:T(128)S(1)} %get-tuple-element.254) | copy-start | bytes 772
  282.9 32.9 %copy-start.116 = (f32[64]{0:T(128)}, f32[64]{0:T(128)S(1)}, u32[]{:S(2)}) copy-start(f32[64]{0:T(128)S(1)} %get-tuple-element.255) | copy-start | bytes 772
  282.9 32.9 %copy-start.118 = (f32[64]{0:T(128)}, f32[64]{0:T(128)S(1)}, u32[]{:S(2)}) copy-start(f32[64]{0:T(128)S(1)} %get-tuple-element.302) | copy-start | bytes 772
  282.9 29.3 %copy-start.122 = (f32[32]{0:T(128)}, f32[32]{0:T(128)S(1)}, u32[]{:S(2)}) copy-start(f32[32]{0:T(128)S(1)} %get-tuple-element.288) | copy-start | bytes 388
  282.9 29.2 %copy-start.123 = (f32[32]{0:T(128)}, f32[32]{0:T(128)S(1)}, u32[]{:S(2)}) copy-start(f32[32]{0:T(128)S(1)} %get-tuple-element.289) | copy-start | bytes 388
  282.9 92.1 %copy-start.135 = (f32[32]{0:T(128)}, f32[32]{0:T(128)S(1)}, u32[]{:S(2)}) copy-start(f32[32]{0:T(128)S(1)} %get-tuple-element.287) | copy-start | bytes 388
  283.0 92.0 %copy-start.88 = (f32[64,64]{1,0:T(8,128)}, f32[64,64]{1,0:T(8,128)S(1)}, u32[]{:S(2)}) copy-start(f32[64,64]{1,0:T(8,128)S(1)} %get-tuple-element.299) | copy-start | bytes 49156
  283.1 92.0 %copy-start.109 = (pred[64,64]{1,0:T(8,128)(4,1)}, pred[64,64]{1,0:T(8,128)(4,1)S(1)}, u32[]{:S(2)}) copy-start(pred[64,64]{1,0:T(8,128)(4,1)S(1)} %get-tuple-element.298) | copy-start | bytes 12292
  288.3 94.6 %copy-start.26 = (f32[64,1024]{1,0:T(8,128)}, f32[64,1024]{1,0:T(8,128)S(1)}, u32[]{:S(2)}) copy-start(f32[64,1024]{1,0:T(8,128)S(1)} %get-tuple-element.185) | copy-start | bytes 786436
  288.4 4.8 collective-permute-start.1
  293.2 3.7 collective-permute-start.2
  296.9 3.7 collective-permute-start.3
  298.2 3.8 collective-permute-start.4
  300.6 1.4 collective-permute-start.5
  303.7 79.2 %copy-start.84 = (f32[2048]{0:T(1024)}, f32[2048]{0:T(1024)S(1)}, u32[]{:S(2)}) copy-start(f32[2048]{0:T(1024)S(1)} %reshape.618) | copy-start | bytes 24580
  309.4 6.4 collective-permute-start.6
  315.6 59.6 %copy-start.101 = (f32[64,32]{0,1:T(8,128)}, f32[64,32]{0,1:T(8,128)S(1)}, u32[]{:S(2)}) copy-start(f32[64,32]{0,1:T(8,128)S(1)} %copy.166) | copy-start | bytes 24580
  315.6 59.5 %copy-start.80 = (f32[64,32]{0,1:T(8,128)}, f32[64,32]{0,1:T(8,128)S(1)}, u32[]{:S(2)}) copy-start(f32[64,32]{0,1:T(8,128)S(1)} %copy.164) | copy-start | bytes 24580
  315.8 59.3 %copy-start.82 = (f32[64,32]{0,1:T(8,128)}, f32[64,32]{0,1:T(8,128)S(1)}, u32[]{:S(2)}) copy-start(f32[64,32]{0,1:T(8,128)S(1)} %copy.168) | copy-start | bytes 24580
  317.2 56.9 %copy-start.36 = (f32[64,2304]{1,0:T(8,128)}, f32[64,2304]{1,0:T(8,128)S(1)}, u32[]{:S(2)}) copy-start(f32[64,2304]{1,0:T(8,128)S(1)} %get-tuple-element.252) | copy-start | bytes 1769476
  319.6 55.4 %copy-start.19 = (f32[64,32,64]{2,1,0:T(8,128)}, f32[64,32,64]{2,1,0:T(8,128)S(1)}, u32[]{:S(2)}) copy-start(f32[64,32,64]{2,1,0:T(8,128)S(1)} %reshape.624) | copy-start | bytes 1572868
  321.2 54.8 %copy-start.47 = (f32[64,32,64]{0,2,1:T(8,128)S(1)}, f32[64,32,64]{0,2,1:T(8,128)}, u32[]{:S(2)}) copy-start(f32[64,32,64]{0,2,1:T(8,128)} %copy.167) | copy-start | bytes 1572868
  380.7 19.3 %copy-start.41 = (f32[64,2048]{1,0:T(8,128)}, f32[64,2048]{1,0:T(8,128)S(1)}, u32[]{:S(2)}) copy-start(f32[64,2048]{1,0:T(8,128)S(1)} %copy.203) | copy-start | bytes 1572868
  382.3 17.8 %copy-start.33 = (f32[64,2048]{1,0:T(8,128)}, f32[64,2048]{1,0:T(8,128)S(1)}, u32[]{:S(2)}) copy-start(f32[64,2048]{1,0:T(8,128)S(1)} %get-tuple-element.251) | copy-start | bytes 1572868
  382.8 17.2 %copy-start.126 = (f32[64]{0:T(128)}, f32[64]{0:T(128)S(1)}, u32[]{:S(2)}) copy-start(f32[64]{0:T(128)S(1)} %get-tuple-element.297) | copy-start | bytes 772
  383.0 17.1 %copy-start.52 = (bf16[64,2048]{1,0:T(8,128)(2,1)}, bf16[64,2048]{1,0:T(8,128)(2,1)S(1)}, u32[]{:S(2)}) copy-start(bf16[64,2048]{1,0:T(8,128)(2,1)S(1)} %multiply_convert_fusion.3) | copy-start | bytes 786436
  386.2 23.6 %copy-start.60 = (bf16[64,1024]{1,0:T(8,128)(2,1)}, bf16[64,1024]{1,0:T(8,128)(2,1)S(1)}, u32[]{:S(2)}) copy-start(bf16[64,1024]{1,0:T(8,128)(2,1)S(1)} %fusion.18) | copy-start | bytes 393220
  432.4 14.7 %copy-start.15 = (bf16[1024,1024]{1,0:T(8,128)(2,1)S(1)}, bf16[1024,1024]{1,0:T(8,128)(2,1)}, u32[]{:S(2)}) copy-start(bf16[1024,1024]{1,0:T(8,128)(2,1)} %copy-done.14) | copy-start | bytes 6291460
  550.1 89.4 %copy-start.111 = (s32[1024]{0:T(1024)}, s32[1024]{0:T(1024)S(1)}, u32[]{:S(2)}) copy-start(s32[1024]{0:T(1024)S(1)} %pad_clamp_fusion.1) | copy-start | bytes 12292
  578.3 26.8 %copy-start.18 = (f32[512,1024]{1,0:T(8,128)S(1)}, f32[512,1024]{1,0:T(8,128)}, u32[]{:S(2)}) copy-start(f32[512,1024]{1,0:T(8,128)} %copy-done.17) | copy-start | bytes 6291460
  654.7 116.1 %copy-start.24 = (f32[32,64,128]{2,1,0:T(8,128)S(1)}, f32[32,64,128]{2,1,0:T(8,128)}, u32[]{:S(2)}) copy-start(f32[32,64,128]{2,1,0:T(8,128)} %copy-done.23) | copy-start | bytes 3145732
  654.7 116.5 %copy-start.79 = (f32[64,32]{0,1:T(8,128)S(1)}, f32[64,32]{0,1:T(8,128)}, u32[]{:S(2)}) copy-start(f32[64,32]{0,1:T(8,128)} %copy-done.78) | copy-start | bytes 24580
  783.6 12.9 %copy-start.74 = (f32[3,2304]{1,0:T(4,128)S(1)}, f32[3,2304]{1,0:T(4,128)}, u32[]{:S(2)}) copy-start(f32[3,2304]{1,0:T(4,128)} %copy-done.73) | copy-start | bytes 82948
  783.6 12.9 %copy-start.115 = (f32[64]{0:T(128)S(1)}, f32[64]{0:T(128)}, u32[]{:S(2)}) copy-start(f32[64]{0:T(128)} %copy-done.114) | copy-start | bytes 772
  783.6 12.9 %copy-start.117 = (f32[64]{0:T(128)S(1)}, f32[64]{0:T(128)}, u32[]{:S(2)}) copy-start(f32[64]{0:T(128)} %copy-done.116) | copy-start | bytes 772
  783.6 12.9 %copy-start.119 = (f32[64]{0:T(128)S(1)}, f32[64]{0:T(128)}, u32[]{:S(2)}) copy-start(f32[64]{0:T(128)} %copy-done.118) | copy-start | bytes 772
  799.3 16.3 %copy-start.59 = (bf16[64,1024]{1,0:T(8,128)(2,1)S(1)}, bf16[64,1024]{1,0:T(8,128)(2,1)}, u32[]{:S(2)}) copy-start(bf16[64,1024]{1,0:T(8,128)(2,1)} %copy-done.58) | copy-start | bytes 393220
  799.3 37.8 %collective-permute-start.7 = (f32[3,2304]{1,0:T(4,128)}, f32[3,2304]{1,0:T(4,128)}, u32[]{:S(2)}, u32[]{:S(2)}) collective-permute-start(f32[3,2304]{1,0:T(4,128)} %pad_add_fusion.1), channel_id=1, source_target_pairs={{1,0},{2,1},{3,2},{4,3},{5,4},{6,5},{7,6},{8,7},{9,8},{10,9},{11,1... | collective-permute-start | bytes 82952 | tf_op jit(solution)/shard_map/ppermute | solution.py:931
  803.9 13.6 %copy-start.27 = (f32[64,1024]{1,0:T(8,128)S(1)}, f32[64,1024]{1,0:T(8,128)}, u32[]{:S(2)}) copy-start(f32[64,1024]{1,0:T(8,128)} %copy-done.26) | copy-start | bytes 786436
  (113 other events, 673.2 us)
Sparse Core Ops, SparseCore 0:
  11.5 250.0 all-gather.2
  264.5 171.2 all-gather.4
  546.6 295.7 reduce-scatter.1

commit v3 on v2

--- a/solution.py
+++ b/solution.py
@@ -66,42 +66,6 @@
     return lax.ppermute(block, "seq", route)
 
 
-def joined(pieces):
-    return jnp.concatenate(pieces, axis=0) if len(pieces) > 1 else pieces[0]
-
-
-def gather_near(ring, pieces, bits):
-    for bit in bits:
-        block = joined(pieces)
-        pieces = [block, swap(block, ring.along[bit])]
-    return pieces
-
-
-def gather_near_low(ring, pieces):
-    return gather_near(ring, pieces, ring.bits[: len(ring.bits) // 2])
-
-
-def gather_near_high(ring, pieces):
-    return gather_near(ring, pieces, ring.bits[len(ring.bits) // 2 :])
-
-
-def gather_first(ring, pieces):
-    block = joined(pieces)
-    return [block, swap(block, ring.first)]
-
-
-def gather_second(ring, pieces):
-    block = joined(pieces)
-    return [block, swap(block, ring.second)]
-
-
-def gather_core(ring, pieces):
-    return pieces + [swap(piece, ring.core) for piece in pieces]
-
-
-GATHER = [gather_near_low, gather_near_high, gather_first, gather_second, gather_core]
-
-
 def flat_kernel(*refs):
     out, first = refs[-1], 0
     for ref in refs[:-1]:
@@ -121,90 +85,91 @@
     )(*shards)
 
 
-def unpack_kernel(n, slots, shapes, flat_ref, *refs):
-    outs, (held, in_sems, out_sems) = refs[:-3], refs[-3:]
-    total = held.shape[1]
-
-    def load(place):
-        source = flat_ref.at[pl.ds(pl.multiple_of(place * total, 16), total)]
-        return pltpu.make_async_copy(source, held.at[place % slots], in_sems.at[place % slots])
-
-    def stores(place):
-        offset, copies = 0, []
-        for out, (rows, columns) in zip(outs, shapes):
-            start = pl.multiple_of(place * rows, 16)
-            for first in range(0, columns, D):
-                source = held.at[place % slots, pl.ds(offset, rows)]
-                target = out.at[pl.ds(start, rows), pl.ds(first, D)]
-                sem = out_sems.at[place % slots, len(copies)]
-                copies.append(pltpu.make_async_copy(source, target, sem))
-                offset += rows
-        return copies
-
-    lead = slots // 2
-
-    @pl.loop(0, n + lead)
-    def _(time):
-        @pl.when(time < n)
-        def _():
-            @pl.when(time >= slots)
-            def _():
-                for copy in stores(time - slots):
-                    copy.wait()
-
-            load(time).start()
-
-        @pl.when(time >= lead)
-        def _():
-            load(time - lead).wait()
-            for copy in stores(time - lead):
-                copy.start()
-
-    @pl.loop(n - slots, n)
-    def _(place):
-        for copy in stores(place):
-            copy.wait()
-
-
 def gather_flat(n, shards):
-    if any(shard.shape[0] % 16 for shard in shards):
-        return lambda: [lax.all_gather(shard, "seq", axis=0, tiled=True) for shard in shards]
-    shapes = [shard.shape for shard in shards]
-    flat = flat_rows(shards)
-    total, slots = flat.shape[0], 8
-    blocks = sum(columns // D for _, columns in shapes)
-    flat = lax.all_gather(flat, "seq", axis=0, tiled=True)
-
-    def unpack():
-        return pl.pallas_call(
-            functools.partial(unpack_kernel, n, slots, shapes),
-            out_shape=[jax.ShapeDtypeStruct((n * rows, columns), BF) for rows, columns in shapes],
-            in_specs=[pl.BlockSpec(memory_space=pltpu.HBM)],
-            out_specs=[pl.BlockSpec(memory_space=pltpu.HBM)] * len(shapes),
-            scratch_shapes=[
-                pltpu.VMEM((slots, total, D), BF),
-                pltpu.SemaphoreType.DMA((slots,)),
-                pltpu.SemaphoreType.DMA((slots, blocks)),
-            ],
-            compiler_params=pltpu.CompilerParams(vmem_limit_bytes=24 * 2**20),
-            cost_estimate=pl.CostEstimate(
-                flops=0, bytes_accessed=4 * n * total * D, transcendentals=0
-            ),
-        )(flat)
-
-    return unpack
-
-
-def gather_rows(ring, shard):
-    pieces = [shard]
-    for phase in GATHER:
-        pieces = phase(ring, pieces)
-    return pieces
-
-
-def gather_small(ring, vector):
-    pieces = gather_rows(ring, vector[None])
-    return jnp.take(jnp.concatenate(pieces, axis=0), jnp.argsort(ring.order()), axis=0)
+    return lax.all_gather(flat_rows(shards), "seq", axis=0)
+
+
+def flat_block(n, rows, place):
+    return pl.BlockSpec((n, rows, D), lambda i: (0, place(i), 0))
+
+
+def whole_of(ref):
+    return ref[...].reshape(-1, ref.shape[-1])
+
+
+def flat_dot_kernel(values_ref, flat_ref, out_ref):
+    out_ref[...] = dot(values_ref[...], whole_of(flat_ref)).astype(out_ref.dtype)
+
+
+def flat_dot(values, flat, first, count, kind):
+    n, rows = flat.shape[0], values.shape[0]
+    return pl.pallas_call(
+        flat_dot_kernel,
+        grid=(count,),
+        out_shape=jax.ShapeDtypeStruct((rows, count * D), kind),
+        in_specs=[
+            pl.BlockSpec((rows, D), lambda i: (0, 0)),
+            flat_block(n, D // n, lambda i: first + i),
+        ],
+        out_specs=pl.BlockSpec((rows, D), lambda i: (0, i)),
+        compiler_params=pltpu.CompilerParams(vmem_limit_bytes=56 * 2**20),
+        cost_estimate=pl.CostEstimate(
+            flops=2 * rows * D * D * count, bytes_accessed=2 * D * D * count, transcendentals=0
+        ),
+    )(values, flat)
+
+
+def flat_dot_t_kernel(values_ref, flat_ref, out_ref):
+    found = dot_t(values_ref[...], whole_of(flat_ref))
+
+    @pl.when(pl.program_id(0) == 0)
+    def _():
+        out_ref[...] = found
+
+    @pl.when(pl.program_id(0) > 0)
+    def _():
+        out_ref[...] += found
+
+
+def flat_dot_t(values, flat, first, count):
+    n, rows = flat.shape[0], values.shape[0]
+    return pl.pallas_call(
+        flat_dot_t_kernel,
+        grid=(count,),
+        out_shape=jax.ShapeDtypeStruct((rows, D), F32),
+        in_specs=[
+            pl.BlockSpec((rows, D), lambda i: (0, i)),
+            flat_block(n, D // n, lambda i: first + i),
+        ],
+        out_specs=pl.BlockSpec((rows, D), lambda i: (0, 0)),
+        compiler_params=pltpu.CompilerParams(vmem_limit_bytes=56 * 2**20),
+        cost_estimate=pl.CostEstimate(
+            flops=2 * rows * D * D * count, bytes_accessed=2 * D * D * count, transcendentals=0
+        ),
+    )(values, flat)
+
+
+def input_grad_kernel(direct_ref, grad_ref, weight_ref, out_ref):
+    out_ref[...] = (direct_ref[...] + dot_t(grad_ref[...], weight_ref[...])).astype(BF)
+
+
+def input_gradient(direct, grad, weight):
+    rows, columns = direct.shape
+    return pl.pallas_call(
+        input_grad_kernel,
+        grid=(columns // D,),
+        out_shape=jax.ShapeDtypeStruct((rows, columns), BF),
+        in_specs=[
+            pl.BlockSpec((rows, D), lambda i: (0, i)),
+            pl.BlockSpec((rows, D), lambda i: (0, 0)),
+            pl.BlockSpec((D, D), lambda i: (i, 0)),
+        ],
+        out_specs=pl.BlockSpec((rows, D), lambda i: (0, i)),
+        compiler_params=pltpu.CompilerParams(vmem_limit_bytes=56 * 2**20),
+        cost_estimate=pl.CostEstimate(
+            flops=2 * rows * columns * D, bytes_accessed=2 * columns * D, transcendentals=0
+        ),
+    )(direct, grad, weight)
 
 
 class Live:
@@ -238,7 +203,7 @@
     @pl.when(pl.program_id(0) >= 4)
     def _():
         for part in range(parts):
-            found = product(normed_ref[...], both_ref[:, pl.ds(part * D, D)])
+            found = product(normed_ref[...], both_ref[0, :, pl.ds(part * D, D)])
             cut = pl.ds(part * SUM_ROWS, SUM_ROWS)
             out_ref[:, cut] = found.reshape(devices, SUM_ROWS, D)
 
@@ -257,7 +222,7 @@
             pl.BlockSpec((rows, devices * block), lambda i: (0, jnp.minimum(i, 3))),
             pl.BlockSpec((rows, D), lambda i: (0, 0)),
             pl.BlockSpec((rows, devices * SUM_ROWS), lambda i: (0, late(i) % 4)),
-            pl.BlockSpec((rows, FF), lambda i: (0, late(i) // 4)),
+            pl.BlockSpec((1, rows, FF), lambda i: (late(i) // 4, 0, 0)),
         ],
         out_specs=pl.BlockSpec(
             (devices, block, D), lambda i: (i % 4, jnp.minimum(i // 4, 1) + late(i) // 4, 0)
@@ -433,9 +398,14 @@
 GATHER_TIMES = [0, 1, 2, 3, 5, 6]
 
 
-def gather_kernel(n, chunks, *refs):
-    count = len(refs) // 2 - 1
-    shards, wholes, (own_sem, send_sem, recv_sem) = refs[:count], refs[count : 2 * count], refs[2 * count :]
+EMBED_ROWS = 1024
+
+
+def gather_kernel(n, chunks, embed_time, *refs):
+    count = (len(refs) - 11) // 2
+    shards, patches_ref, wholes = refs[:count], refs[count], refs[count + 1 : -10]
+    embedded_ref, parted_ref, total, held, held_sem, own_sem = refs[-10:-4]
+    send_sem, recv_sem, part_send, part_recv = refs[-4:]
     here = Place(n)
     greet(n)
     owns = []
@@ -471,7 +441,44 @@
         def _(place):
             sending(chunk, step, place).start()
 
+    rows, width = patches_ref.shape[0], patches_ref.shape[1] // n
+
+    def part_of(place):
+        start = pl.multiple_of(here.device(place) * width, 128)
+        return patches_ref.at[:, pl.ds(start, width)]
+
+    def parting(place):
+        there = here.place_there(place)
+        target = parted_ref.at[rows_of(there, 1, rows)]
+        return remote(
+            part_of(place), target, part_send.at[place], part_recv.at[there], here.device(place)
+        )
+
+    pieces = wholes[0].shape[0] // EMBED_ROWS
+
+    def fetch(piece):
+        source = wholes[0].at[pl.ds(piece * EMBED_ROWS, EMBED_ROWS)]
+        return pltpu.make_async_copy(source, held.at[piece % 2], held_sem.at[piece % 2])
+
+    def embed(piece):
+        if piece == 0:
+            fetch(0).start()
+        if piece + 1 < pieces:
+            fetch(piece + 1).start()
+        fetch(piece).wait()
+        found = dot(patches_ref[:, pl.ds(piece * EMBED_ROWS, EMBED_ROWS)], held[piece % 2])
+        total[...] = found if piece == 0 else total[...] + found
+
+    done = 0
+    own_part = pltpu.make_async_copy(part_of(0), parted_ref.at[rows_of(0, 1, rows)], part_recv.at[0])
     for time in range(len(chunks) + GATHER_TIMES[-1]):
+        if time == embed_time:
+            own_part.start()
+
+            @pl.loop(1, n)
+            def _(place):
+                parting(place).start()
+
         for step in range(len(steps), -1, -1):
             chunk = time - GATHER_TIMES[step]
             if 0 <= chunk < len(chunks):
@@ -479,6 +486,22 @@
                     arrive(chunk, step - 1)
                 if step < len(steps):
                     send(chunk, step)
+        for _ in range(2):
+            if time >= embed_time and done < pieces:
+                embed(done)
+                done += 1
+    for piece in range(done, pieces):
+        embed(piece)
+    embedded_ref[...] = total[...]
+
+    @pl.loop(0, n)
+    def _(place):
+        landed(parted_ref.at[rows_of(place, 1, rows)], part_recv.at[place])
+
+    @pl.loop(1, n)
+    def _(place):
+        parting(place).wait_send()
+
     for chunk in range(len(chunks)):
         for step in range(len(steps)):
 
@@ -487,9 +510,14 @@
                 sending(chunk, step, place).wait_send()
 
 
-def gather_weights(n, shards, cuts):
+def gather_weights(n, shards, cuts, patches):
     if n != 32 or any(shard.shape[0] % 16 for shard in shards):
-        return [lax.all_gather(shard, "seq", axis=0, tiled=True) for shard in shards]
+        wholes = [lax.all_gather(shard, "seq", axis=0, tiled=True) for shard in shards]
+        parted = patches.reshape(patches.shape[0], n, -1).transpose(1, 0, 2)
+        parted = lax.all_to_all(parted, "seq", 0, 0, tiled=True)
+        return wholes + [dot(patches, wholes[0]), parted.reshape(-1, parted.shape[-1])]
+    rows = patches.shape[0]
+    embed_time = shards[0].shape[0] // cuts[0][0] + GATHER_TIMES[-1]
     chunks = [
         (index, first, rows, column, min(columns, shard.shape[1] - column))
         for index, (shard, (rows, columns)) in enumerate(zip(shards, cuts))
@@ -498,18 +526,30 @@
     ]
     sems = [pltpu.SemaphoreType.DMA((len(chunks), n))] * 2
     return pl.pallas_call(
-        functools.partial(gather_kernel, n, chunks),
+        functools.partial(gather_kernel, n, chunks, embed_time),
         out_shape=[
             jax.ShapeDtypeStruct((n * shard.shape[0], shard.shape[1]), shard.dtype) for shard in shards
+        ]
+        + [
+            jax.ShapeDtypeStruct((rows, D), F32),
+            jax.ShapeDtypeStruct((n * rows, patches.shape[1] // n), BF),
         ],
-        in_specs=[pl.BlockSpec(memory_space=pltpu.VMEM)] * len(shards),
-        out_specs=[pl.BlockSpec(memory_space=pltpu.HBM)] * len(shards),
-        scratch_shapes=[pltpu.SemaphoreType.DMA((len(shards),))] + sems,
+        in_specs=[pl.BlockSpec(memory_space=pltpu.VMEM)] * (len(shards) + 1),
+        out_specs=[pl.BlockSpec(memory_space=pltpu.HBM)] * len(shards)
+        + [pl.BlockSpec(memory_space=pltpu.VMEM)] * 2,
+        scratch_shapes=[
+            pltpu.VMEM((rows, D), F32),
+            pltpu.VMEM((2, EMBED_ROWS, D), BF),
+            pltpu.SemaphoreType.DMA((2,)),
+            pltpu.SemaphoreType.DMA((len(shards),)),
+        ]
+        + sems
+        + [pltpu.SemaphoreType.DMA((n,))] * 2,
         compiler_params=pltpu.CompilerParams(
-            collective_id=0, has_side_effects=True, vmem_limit_bytes=16 * 2**20
+            collective_id=0, has_side_effects=True, vmem_limit_bytes=24 * 2**20
         ),
         cost_estimate=pl.CostEstimate(flops=0, bytes_accessed=2**25, transcendentals=0),
-    )(*shards)
+    )(*shards, patches)
 
 
 SUM_ROWS, SUM_COLUMNS, SUM_SLOTS = 32, 512, 8
@@ -563,8 +603,7 @@
         self.copy(chunk, step - 1).wait_recv()
         total = self.kept[slot, pl.ds(0, rows)] + self.got[chunk, pl.ds(rows, rows)].astype(F32)
         if step == len(self.steps):
-            start = pl.multiple_of(chunk * SUM_COLUMNS, SUM_COLUMNS)
-            self.out[:, pl.ds(start, SUM_COLUMNS)] = total
+            self.out(chunk, total)
             return
         half = rows // 2
         self.sent[slot, pl.ds(half, half)] = total[half:].astype(BF)
@@ -588,6 +627,15 @@
         @pl.loop(max(0, self.chunks - SUM_SLOTS), self.chunks)
         def _(chunk):
             self.sent_all(chunk)
+
+
+def turn(order_ref, left_ref, values_ref):
+    for index in range(values_ref.shape[0]):
+        left_ref[index] = dot_t(order_ref[...], values_ref[index]).astype(BF)
+
+
+def lefts_scratch(n, lefts):
+    return [pltpu.VMEM((lefts.shape[0], n * SUM_ROWS, lefts.shape[1]), BF)]
 
 
 def sums_scratch(n, chunks):
@@ -601,6 +649,10 @@
     ]
 
 
+def columns_of(chunk):
+    return pl.ds(pl.multiple_of(chunk * SUM_COLUMNS, SUM_COLUMNS), SUM_COLUMNS)
+
+
 def local_find(chunk):
     return (chunk + 6) // 8, chunk
 
@@ -611,16 +663,42 @@
 
 
 def last_kernel(
-    n, grad_ref, parted_ref, small_ref, left_ref, right_ref,
-    d_weight_ref, d_small_ref, out_ref,
-    known, small_kept, small_got, g_send, g_recv, t_send, t_recv, *scratch
+    n, grad_ref, parted_ref, small_ref, order_ref, values_ref, right_ref,
+    d_weight_ref, d_small_ref, d_unpatch_ref, d_in_ref, d_out_ref,
+    known, small_kept, small_got, g_send, g_recv, t_send, t_recv, left_ref, *scratch
 ):
     here = Place(n)
     rows = grad_ref.shape[0]
     greet(n)
     known[pl.ds(0, rows)] = grad_ref[...]
-    small_kept[...] = small_ref[...]
-    sums = Sums(here, last_find, left_ref, right_ref, out_ref, *scratch)
+
+    @pl.loop(0, n)
+    def _(place):
+        device = here.device(place)
+        small_kept[rows_of(place, 1, LOG_ROWS)] = small_ref[rows_of(device, 1, LOG_ROWS)]
+
+    turn(order_ref, left_ref, values_ref)
+    spare = d_in_ref.shape[1] % SUM_COLUMNS
+
+    def store(chunk, total):
+        @pl.when(chunk < 16)
+        def _():
+            d_unpatch_ref[:, columns_of(chunk)] = total
+
+        @pl.when((chunk >= 16) & (chunk < 24))
+        def _():
+            d_in_ref[:, columns_of(chunk - 16)] = total
+
+        @pl.when(chunk == 24)
+        def _():
+            d_in_ref[:, pl.ds(8 * SUM_COLUMNS, spare)] = total[:, :spare]
+
+        @pl.when(chunk >= 25)
+        def _():
+            part = (chunk - 25) // 2
+            d_out_ref[rows_of(part, 1, SUM_ROWS), columns_of((chunk - 25) % 2)] = total
+
+    sums = Sums(here, last_find, left_ref, right_ref, store, *scratch)
     steps = here.halves()
     copies = []
     for step in range(len(steps)):
@@ -647,7 +725,7 @@
     sums.end()
 
 
-def last_sums(n, grad, parted, small, lefts, right):
+def last_sums(n, grad, parted, small, order, lefts, right, projections):
     rows, width = grad.shape[0], parted.shape[1]
     phases, chunks = n.bit_length() - 1, right.shape[1] // SUM_COLUMNS
     return pl.pallas_call(
@@ -655,37 +733,45 @@
         out_shape=[
             jax.ShapeDtypeStruct((width, D), F32),
             jax.ShapeDtypeStruct((LOG_ROWS, 128), F32),
-            jax.ShapeDtypeStruct((SUM_ROWS, right.shape[1]), F32),
+            jax.ShapeDtypeStruct((SUM_ROWS, PATCH * D), F32),
+            jax.ShapeDtypeStruct((SUM_ROWS, projections), F32),
+            jax.ShapeDtypeStruct((2 * SUM_ROWS, D), F32),
         ],
-        in_specs=[pl.BlockSpec(memory_space=pltpu.VMEM)] * 5,
-        out_specs=[pl.BlockSpec(memory_space=pltpu.VMEM)] * 3,
+        in_specs=[pl.BlockSpec(memory_space=pltpu.VMEM)] * 6,
+        out_specs=[pl.BlockSpec(memory_space=pltpu.VMEM)] * 5,
         scratch_shapes=[
             pltpu.VMEM((n * rows, D), BF),
             pltpu.VMEM(small.shape, F32),
             pltpu.VMEM(small.shape, F32),
         ]
         + [pltpu.SemaphoreType.DMA((phases,))] * 4
+        + lefts_scratch(n, lefts)
         + sums_scratch(n, chunks),
         compiler_params=pltpu.CompilerParams(
-            collective_id=1, has_side_effects=True, vmem_limit_bytes=60 * 2**20
+            collective_id=1, has_side_effects=True, vmem_limit_bytes=62 * 2**20
         ),
         cost_estimate=pl.CostEstimate(flops=2**32, bytes_accessed=2**24, transcendentals=0),
-    )(grad, parted, small, lefts, right)
+    )(grad, parted, small, order, lefts, right)
 
 
 LOG_ROWS = 8
 
 
 def states_kernel(
-    n, reverse, states_ref, logs_ref, left_ref, right_ref, out_ref, sum_ref, spread, logs, summed,
-    s_send, s_recv, l_send, l_recv, b_send, b_recv, *scratch
+    n, reverse, states_ref, logs_ref, order_ref, values_ref, right_ref, out_ref, sum_ref,
+    spread, logs, summed, s_send, s_recv, l_send, l_recv, b_send, b_recv, *scratch
 ):
     me = lax.axis_index("seq")
     rows = states_ref.shape[0] // n
     greet(n)
     sums = None
+
+    def store(chunk, total):
+        sum_ref[:, columns_of(chunk)] = total
+
     if scratch:
-        sums = Sums(Place(n), local_find, left_ref, right_ref, sum_ref, *scratch)
+        left_ref = scratch[0]
+        sums = Sums(Place(n), local_find, left_ref, right_ref, store, *scratch[1:])
 
     def spreading(other):
         return remote(
@@ -722,6 +808,7 @@
     own.start()
     own_logs.start()
     if sums:
+        turn(order_ref, left_ref, values_ref)
         sums.run(0, 4)
 
     @pl.loop(0, n)
@@ -769,21 +856,21 @@
         returning(other).wait_send()
 
 
-def pass_states(n, states, logs, lefts=None, right=None):
-    total, reverse = MHEADS * MHEAD_DIM, lefts is not None
+def pass_states(n, states, logs, reverse, order=None, lefts=None, right=None):
+    total = MHEADS * MHEAD_DIM
     told = jnp.zeros((LOG_ROWS, 128), F32).at[0, : logs.shape[0]].set(logs)
-    summing = reverse and n == 32
+    summing = lefts is not None
     chunks = right.shape[1] // SUM_COLUMNS if summing else 0
     small = jnp.zeros((LOG_ROWS, 128), F32)
     operands = [states.reshape(total, NSTATE).astype(BF), told]
-    operands += [lefts, right] if summing else [small, small]
+    operands += [order, lefts, right] if summing else [small] * 3
     out, found = pl.pallas_call(
         functools.partial(states_kernel, n, reverse),
         out_shape=[
             jax.ShapeDtypeStruct((total, NSTATE), BF),
             jax.ShapeDtypeStruct((SUM_ROWS, chunks * SUM_COLUMNS) if summing else (LOG_ROWS, 128), F32),
         ],
-        in_specs=[pl.BlockSpec(memory_space=pltpu.VMEM)] * 4,
+        in_specs=[pl.BlockSpec(memory_space=pltpu.VMEM)] * 5,
         out_specs=[pl.BlockSpec(memory_space=pltpu.VMEM)] * 2,
         scratch_shapes=[
             pltpu.VMEM((total, NSTATE), BF),
@@ -791,7 +878,7 @@
             pltpu.VMEM((total, NSTATE), BF),
         ]
         + [pltpu.SemaphoreType.DMA((n,))] * 6
-        + (sums_scratch(n, chunks) if summing else []),
+        + (lefts_scratch(n, lefts) + sums_scratch(n, chunks) if summing else []),
         compiler_params=pltpu.CompilerParams(
             collective_id=3 if reverse else 2,
             has_side_effects=True,
@@ -800,6 +887,128 @@
         cost_estimate=pl.CostEstimate(flops=2**22, bytes_accessed=2**21, transcendentals=0),
     )(*operands)
     return out.astype(F32).reshape(MHEADS, MHEAD_DIM, NSTATE), found
+
+
+FF_TILE = D
+
+
+def feed_forward_kernel(
+    stream_ref, normed_ref, gate_w_ref, up_w_ref, down_ref, out_ref, gate_ref, up_ref, hid_ref, total
+):
+    step = pl.program_id(0)
+    gate, up = dot(normed_ref[...], whole_of(gate_w_ref)), dot(normed_ref[...], whole_of(up_w_ref))
+    hid = (silu(gate) * up).astype(BF)
+    gate_ref[...], up_ref[...], hid_ref[...] = gate.astype(BF), up.astype(BF), hid
+    found = dot(hid, whole_of(down_ref))
+
+    @pl.when(step == 0)
+    def _():
+        total[...] = stream_ref[...] + found
+
+    @pl.when(step > 0)
+    def _():
+        total[...] += found
+
+    @pl.when(step == pl.num_programs(0) - 1)
+    def _():
+        out_ref[...] = total[...].astype(BF)
+
+
+def late_blocks(n):
+    tiles, block = FF // FF_TILE, FF // n
+    return [
+        flat_block(n, D // n, lambda i: i),
+        flat_block(n, D // n, lambda i: i + tiles),
+        pl.BlockSpec((n // tiles, block, D), lambda i: (i, 2 * FF // n // block, 0)),
+    ]
+
+
+def feed_forward(stream, normed, flat):
+    rows, tiles = stream.shape[0], FF // FF_TILE
+    wide = pl.BlockSpec((rows, D), lambda i: (0, 0))
+    tile = pl.BlockSpec((rows, FF_TILE), lambda i: (0, i))
+    return pl.pallas_call(
+        feed_forward_kernel,
+        grid=(tiles,),
+        out_shape=[jax.ShapeDtypeStruct((rows, D), BF)]
+        + [jax.ShapeDtypeStruct((rows, FF), BF)] * 3,
+        in_specs=[
+            wide,
+            wide,
+            *late_blocks(flat.shape[0]),
+        ],
+        out_specs=[wide, tile, tile, tile],
+        scratch_shapes=[pltpu.VMEM((rows, D), F32)],
+        compiler_params=pltpu.CompilerParams(vmem_limit_bytes=52 * 2**20),
+        cost_estimate=pl.CostEstimate(
+            flops=6 * rows * D * FF, bytes_accessed=2**25, transcendentals=rows * FF
+        ),
+    )(stream, normed, flat, flat, flat)
+
+
+def feed_forward_back_kernel(
+    grad_ref, stream_ref, gain_ref, gate_ref, up_ref, gate_w_ref, up_w_ref, down_ref,
+    both_ref, d_stream_ref, d_low_ref, d_gain_ref, total,
+):
+    step = pl.program_id(0)
+    d_hid = dot_t(grad_ref[...], whole_of(down_ref))
+    gate, up = gate_ref[...].astype(F32), up_ref[...].astype(F32)
+    s = jax.nn.sigmoid(gate)
+    d_gate = (d_hid * up * (s * (1.0 + gate * (1.0 - s)))).astype(BF)
+    d_up = (d_hid * (gate * s)).astype(BF)
+    both_ref[0], both_ref[1] = d_gate, d_up
+    found = dot_t(d_gate, whole_of(gate_w_ref)) + dot_t(d_up, whole_of(up_w_ref))
+
+    @pl.when(step == 0)
+    def _():
+        total[...] = found
+
+    @pl.when(step > 0)
+    def _():
+        total[...] += found
+
+    @pl.when(step == pl.num_programs(0) - 1)
+    def _():
+        stream, d_normed = stream_ref[...], total[...]
+        r = lax.rsqrt(jnp.mean(stream * stream, axis=-1, keepdims=True) + EPS)
+        scaled = gain_ref[...] * d_normed
+        inner = jnp.mean(stream * scaled, axis=-1, keepdims=True)
+        d_stream = grad_ref[...].astype(F32) + r * scaled - stream * (r * r * r) * inner
+        d_stream_ref[...] = d_stream
+        d_low_ref[...] = d_stream.astype(BF)
+        d_gain_ref[...] = jnp.sum(stream * r * d_normed, axis=0, keepdims=True)
+
+
+def feed_forward_back(grad, stream, gain, gate, up, flat):
+    rows, tiles = stream.shape[0], FF // FF_TILE
+    wide = pl.BlockSpec((rows, D), lambda i: (0, 0))
+    tile = pl.BlockSpec((rows, FF_TILE), lambda i: (0, i))
+    narrow = pl.BlockSpec((1, D), lambda i: (0, 0))
+    both, d_stream, d_low, d_gain = pl.pallas_call(
+        feed_forward_back_kernel,
+        grid=(tiles,),
+        out_shape=[
+            jax.ShapeDtypeStruct((2, rows, FF), BF),
+            jax.ShapeDtypeStruct((rows, D), F32),
+            jax.ShapeDtypeStruct((rows, D), BF),
+            jax.ShapeDtypeStruct((1, D), F32),
+        ],
+        in_specs=[
+            wide,
+            wide,
+            narrow,
+            tile,
+            tile,
+            *late_blocks(flat.shape[0]),
+        ],
+        out_specs=[pl.BlockSpec((2, rows, FF_TILE), lambda i: (0, 0, i)), wide, wide, narrow],
+        scratch_shapes=[pltpu.VMEM((rows, D), F32)],
+        compiler_params=pltpu.CompilerParams(vmem_limit_bytes=56 * 2**20),
+        cost_estimate=pl.CostEstimate(
+            flops=6 * rows * D * FF, bytes_accessed=2**25, transcendentals=rows * FF
+        ),
+    )(grad, stream, gain[None], gate, up, flat, flat, flat)
+    return both, d_stream, d_low, d_gain[0]
 
 
 ATTN_ROWS = 128
@@ -936,25 +1145,31 @@
     byte_wide = byte_acts.astype(F32)
     patches = byte_acts.reshape(-1, PATCH * D)
     patch_rows = patches.shape[0]
-    unpack_early = gather_flat(n, [unpatch_weight, qkv_weight, attn_out])
-    unpack_late = gather_flat(n, [gate_up, down_weight])
+    early = gather_flat(n, [unpatch_weight, qkv_weight, attn_out])
+    late = gather_flat(n, [gate_up, down_weight])
     small = [patch_gain, conv_weight.reshape(-1), conv_bias, mixer_gain, attn_gain, ffn_gain]
     cuts = list(np.cumsum([piece.shape[0] for piece in small]))
-    small_all = gather_small(ring, jnp.concatenate(small)).astype(F32)
+    small_shard = jnp.concatenate(small)
+    small_shard = jnp.pad(small_shard, (0, -small_shard.shape[0] % 2048)).reshape(-1, 128)
+    live.patch_w, live.mixer_in, live.mixer_out, small_all, embedded, live.parted = gather_weights(
+        n,
+        [
+            patch_weight,
+            jnp.pad(mixer_in, ((0, 0), (0, -mixer_in.shape[1] % 128))),
+            mixer_out,
+            small_shard,
+        ],
+        [(32, D), (16, 2304), (32, D), (16, 128)],
+        patches,
+    )
+    small_all = small_all.reshape(n, -1)[:, : cuts[-1]].astype(F32)
     parts = jnp.split(small_all, cuts[:-1], axis=1)
     live.patch_gain = parts[0].reshape(-1)
     live.conv_weight = parts[1].reshape(n, CONV, -1).transpose(1, 0, 2).reshape(CONV, CONV_CH)
     live.conv_bias, live.mixer_gain, live.attn_gain, live.ffn_gain = [
         piece.reshape(-1) for piece in parts[2:]
     ]
-    live.fence()
-
-    live.patch_w, live.mixer_in, live.mixer_out = gather_weights(
-        n,
-        [patch_weight, jnp.pad(mixer_in, ((0, 0), (0, -mixer_in.shape[1] % 128))), mixer_out],
-        [(32, D), (16, 2304), (32, D)],
-    )
-    live.embedded = dot(patches, live.patch_w)
+    live.embedded = embedded
     live.normed = rms_scale(live.embedded, live.patch_gain).astype(BF)
     projected = dot(live.normed, live.mixer_in)
     live.gate_z = projected[:, :DI]
@@ -982,7 +1197,7 @@
         functools.partial(block_state, starts=resets), conv_out, dt_raw, head_params
     )
     local_state, decay_total = state_parts
-    live.state_in, _ = pass_states(n, local_state, live.logs)
+    live.state_in, _ = pass_states(n, local_state, live.logs, False)
     live.fence()
 
     mixer_y, output_back = jax.vjp(
@@ -997,41 +1212,39 @@
     live.gated_norm = rms_scale(gated, live.mixer_gain).astype(BF)
     branch = dot(live.gated_norm, live.mixer_out)
     live.hidden = (live.embedded + branch).astype(BF)
-    live.unpatch, live.qkv_w, live.attn_out = unpack_early()
-    slots = dot(live.hidden, live.unpatch)
+    live.early = early
+    slots = flat_dot(live.hidden, live.early, 0, PATCH, F32)
     live.stream0 = byte_wide + slots.reshape(-1, D)
     live.normed0 = rms_scale(live.stream0, live.attn_gain).astype(BF)
     live.fence()
 
     rows = byte_wide.shape[0]
-    live.triple = dot(live.normed0, live.qkv_w).astype(BF)
+    live.triple = flat_dot(live.normed0, live.early, PATCH, 3, BF)
     live.mixed = attention(live.triple)
-    live.stream1 = live.stream0 + dot(live.mixed, live.attn_out)
+    live.stream1 = live.stream0 + flat_dot(live.mixed, live.early, PATCH + 3, 1, F32)
     live.normed1 = rms_scale(live.stream1, live.ffn_gain).astype(BF)
-    live.gate_up, live.down_w = unpack_late()
-    both = dot(live.normed1, live.gate_up)
-    live.both = both.astype(BF)
-    live.hid = (silu(both[:, :FF]) * both[:, FF:]).astype(BF)
-    parted = patches.reshape(patch_rows, n, -1).transpose(1, 0, 2)
-    live.parted = lax.all_to_all(parted, "seq", 0, 0, tiled=True)
+    live.late = late
+    layer_out, gate, up, hid = feed_forward(live.stream1, live.normed1, live.late)
+    live.gate, live.up, live.hid = gate, up, hid
     live.fence()
 
     small_slice = n == 32
 
-    def in_order(values):
-        blocks = values.reshape(n, -1, values.shape[-1])
-        return jnp.take(blocks, order, axis=0).reshape(-1, values.shape[-1])
-
-    def lefts_of(values):
-        if not small_slice:
-            return values
-        turned = in_order(values.T).reshape(n, -1, SUM_ROWS, values.shape[0])
-        return turned.transpose(1, 0, 2, 3).reshape(-1, n * SUM_ROWS, values.shape[0])
-
-    layer_out = (live.stream1 + dot(live.hid, live.down_w)).astype(BF)
-    d_hid = dot_t(out_grad, live.down_w)
-    gate, up = live.both[:, :FF].astype(F32), live.both[:, FF:].astype(F32)
-    d_both = jnp.concatenate([d_hid * up * silu_slope(gate), d_hid * silu(gate)], axis=1).astype(BF)
+    def lefts_of(*values):
+        parts = []
+        for value in values:
+            cut = value.reshape(value.shape[0], n, -1, SUM_ROWS).transpose(2, 0, 1, 3)
+            parts.append(cut.reshape(-1, value.shape[0], n * SUM_ROWS))
+        return jnp.concatenate(parts, axis=0)
+
+    if small_slice:
+        place = jnp.arange(n * SUM_ROWS)
+        source = jnp.repeat(order * SUM_ROWS, SUM_ROWS) + place % SUM_ROWS
+        live.order = (place[None, :] == source[:, None]).astype(BF)
+
+    d_both, d_stream1, d_stream1_low, g_ffn_gain = feed_forward_back(
+        out_grad, live.stream1, live.ffn_gain, live.gate, live.up, live.late
+    )
     if small_slice:
         block = down_weight.shape[0]
         flat = flat_grads(n, live.hid, out_grad, live.normed1, d_both)
@@ -1041,28 +1254,25 @@
         g_gate_up = g_gate_up.reshape(SUM_ROWS, -1)
     else:
         g_down = summed_grad(live.hid, out_grad)
-        g_gate_up = summed_grad(live.normed1, d_both)
-    d_normed1 = dot_t(d_both, live.gate_up)
-    d_stream1, g_ffn_gain = rms_back(live.stream1, live.ffn_gain, d_normed1)
-    d_stream1 = out_grad.astype(F32) + d_stream1
-    d_stream1_low = d_stream1.astype(BF)
-    d_mixed = dot_t(d_stream1_low, live.attn_out).astype(BF)
+        g_gate_up = summed_grad(live.normed1, jnp.concatenate([d_both[0], d_both[1]], axis=1))
+    d_mixed = flat_dot_t(d_stream1_low, live.early, PATCH + 3, 1).astype(BF)
     d_triple = attention_back(live.triple, d_mixed)
-    d_stream0, g_attn_gain = rms_back(live.stream0, live.attn_gain, dot_t(d_triple, live.qkv_w))
-    live.d_stream0 = d_stream1 + d_stream0
-    d_slots = live.d_stream0.astype(BF).reshape(patch_rows, PATCH * D)
-    d_hidden = dot_t(d_slots, live.unpatch)
+    d_stream0, g_attn_gain = rms_back(live.stream0, live.attn_gain, flat_dot_t(d_triple, live.early, PATCH, 3))
+    live.d_stream0 = (d_stream1 + d_stream0).reshape(patch_rows, PATCH * D)
+    d_slots = live.d_stream0.astype(BF)
+    d_hidden = flat_dot_t(d_slots, live.early, 0, PATCH)
     d_branch = d_hidden.astype(BF)
     d_gated, g_mixer_gain = rms_back(gated, live.mixer_gain, dot_t(d_branch, live.mixer_out))
     d_gate_z = d_gated * mixer_y * silu_slope(live.gate_z)
     output_grads = output_back(d_gated * gate_act)
-    state_grad, found = pass_states(
-        n,
-        output_grads[3],
-        live.logs,
-        jnp.concatenate([lefts_of(live.mixed), lefts_of(live.normed0)], axis=0),
-        jnp.concatenate([d_stream1_low, d_triple], axis=1),
-    )
+    summed = []
+    if small_slice:
+        summed = [
+            live.order,
+            jnp.stack([live.mixed, live.normed0]),
+            jnp.concatenate([d_stream1_low, d_triple], axis=1),
+        ]
+    state_grad, found = pass_states(n, output_grads[3], live.logs, True, *summed)
     g_attn_out, g_qkv = found[:, :D], found[:, D:]
     decay_grad = jnp.sum(state_grad * live.state_in, axis=(1, 2))
     state_cot = state_back((state_grad, decay_grad))
@@ -1078,8 +1288,7 @@
         live.embedded, live.patch_gain, dot_t(d_projected, live.mixer_in)
     )
     d_embedded = (d_hidden + d_embedded).astype(BF)
-    d_patches = dot_t(d_embedded, live.patch_w).reshape(-1, D)
-    input_grad = (live.d_stream0 + d_patches).astype(BF)
+    input_grad = input_gradient(live.d_stream0, d_embedded, live.patch_w).reshape(-1, D)
 
     g_conv_weight = conv_cot[1].reshape(CONV, n, -1).transpose(1, 0, 2).reshape(n, -1)
     g_head = jnp.broadcast_to((output_grads[2] + state_cot[2]).reshape(1, -1), (n, 3 * MHEADS))
@@ -1089,25 +1298,22 @@
     g_small = jnp.pad(g_small, ((0, 0), (0, LOG_ROWS * 128 - small_width)))
     g_small = g_small.reshape(n * LOG_ROWS, 128)
     if small_slice:
-        lefts = [lefts_of(live.hidden), lefts_of(live.normed), lefts_of(live.gated_norm)]
         d_projected = jnp.pad(d_projected, ((0, 0), (0, -d_projected.shape[1] % SUM_COLUMNS)))
-        g_patch, g_small, found = last_sums(
+        g_patch, g_small, g_unpatch, g_mixer_in, g_mixer_out = last_sums(
             n,
             d_embedded,
-            in_order(live.parted),
-            in_order(g_small),
-            jnp.concatenate(lefts, axis=0),
+            live.parted,
+            g_small,
+            live.order,
+            lefts_of(live.hidden, live.normed, live.gated_norm),
             jnp.concatenate([d_slots, d_projected, d_branch, d_branch], axis=1),
+            mixer_in.shape[1],
         )
-        g_unpatch = found[:, : PATCH * D]
-        g_mixer_in = found[:, PATCH * D : PATCH * D + mixer_in.shape[1]]
-        g_mixer_out = found[:, found.shape[1] - 2 * D :].reshape(SUM_ROWS, 2, D)
-        g_mixer_out = g_mixer_out.transpose(1, 0, 2).reshape(-1, D)
     else:
         g_attn_out = summed_grad(live.mixed, d_stream1_low)
         g_qkv = summed_grad(live.normed0, d_triple)
         known = lax.all_gather(d_embedded, "seq", axis=0, tiled=True)
-        g_patch = dot(live.parted.reshape(n * patch_rows, -1).T, known)
+        g_patch = dot(live.parted.T, known)
         g_small = lax.psum_scatter(g_small, "seq", scatter_dimension=0, tiled=True)
         g_unpatch = summed_grad(live.hidden, d_slots)
         g_mixer_in = summed_grad(live.normed, d_projected)[:, : mixer_in.shape[1]]

time: 1080 us -> 1010 us (0.935)
  matrix products: 160 us -> 41.7 us
  Pallas kernels: 682 us -> 781 us
  local copies, waits for them, and re-layouts: 111 us -> 70 us
  waiting for transfers between devices: 8.45 us -> 34.6 us
  other arithmetic: 71.2 us -> 51.7 us
  starting transfers between devices: 15.7 us -> 3.97 us
    pallas_call x3 -> x10, Pallas kernels: 275 us -> 371 us  [the longest x1 255 us: gather_weights(): pl.pallas_call(functools.partial(gather_kernel, n, chunks, embed_time), o...]
    dot_general x8 -> x2, matrix products: 73.5 us -> 8.71 us  [dot_t(): lax.dot_general(left, right, (((1,), (1,)), ((), ())), preferred_element_...]
    dot_general x8 -> x2, matrix products: 58.9 us -> 9.09 us  [dot(): return jnp.dot(left, right, preferred_element_type=F32)]
    all_gather x2, waiting for transfers between devices: 0.04 us -> 34.5 us  [gather_flat(): return lax.all_gather(flat_rows(shards), 'seq', axis=0)]
    unnamed x301 -> x226, local copies, waits for them, and re-layouts: 38.1 us -> 21 us
    gather x8 -> x0, local copies, waits for them, and re-layouts: 14.1 us -> none  [the longest x7 13.5 us: in_order(): return jnp.take(blocks, order, axis=0).reshape(-1, values.shape[-1])]
    convert_element_type x5, other arithmetic: 19.1 us -> 6.99 us  [the longest x1 2.94 us: local(): d_mixed = flat_dot_t(d_stream1_low, live.early, PATCH + 3, 1).astype(BF)]
  transfers between devices with their start and end apart: 12 -> 5, of which waited for: 3 -> 1; matrix products, arithmetic and copies ran while one was open for 26% -> 14% of each run, Pallas kernels for 62% -> 71%
where the time goes in v3:
time: 1010 us; the launch traced here: 1000 us
  Pallas kernels  781 us (77%)
  local copies, waits for them, and re-layouts  70 us (7%)
  other arithmetic  51.7 us (5%)
  matrix products  41.7 us (4%)
  waiting for transfers between devices  34.6 us (3%)
  between operations  16.9 us (2%)
    pallas_call x1, Pallas kernels, gather_weights(): pl.pallas_call(functools.partial(gather_kernel, n, chunks, embed_time), o...  255 us
    pallas_call x1, Pallas kernels, last_sums(): pl.pallas_call(functools.partial(last_kernel, n), out_shape=[jax.ShapeDty...  186 us
    pallas_call x2, Pallas kernels, pass_states(): pl.pallas_call(functools.partial(states_kernel, n, reverse), out_shape=[j...  161 us
    all_gather x2, waiting for transfers between devices, gather_flat(): return lax.all_gather(flat_rows(shards), 'seq', axis=0)  34.5 us
    pallas_call x1, Pallas kernels, feed_forward(): pl.pallas_call(feed_forward_kernel, grid=(tiles,), out_shape=[jax.ShapeDt...  28.9 us
    pallas_call x3, Pallas kernels, flat_dot_t(): pl.pallas_call(flat_dot_t_kernel, grid=(count,), out_shape=jax.ShapeDtype...  27.8 us
    pallas_call x1, Pallas kernels, attention_back(): pl.pallas_call(attention_back_kernel, grid=(rows // ATTN_ROWS,), out_shap...  27 us
    pallas_call x1, Pallas kernels, feed_forward_back(): pl.pallas_call(feed_forward_back_kernel, grid=(tiles,), out_shape=[jax.Sh...  24.2 us
  transfers between devices with their start and end apart: 5, of which 1 were waited for; matrix products, arithmetic and copies ran while one was open for 14% of the time, Pallas kernels for 71%

profile of v3, /device:TPU:0, one launch (start us, length us, event | category | flops | bytes accessed | tf_op | source)
XLA Modules:
  0.0 1000.1 jit_solution(13944134790073434516)
XLA Ops:
  7.3 2.1 shard_map.316
  9.5 2.1 shard_map.321
  12.7 254.7 %shard_map.314 = (bf16[8192,1024]{1,0:T(8,128)(2,1)}, bf16[1024,4480]{1,0:T(8,128)(2,1)S(1)}, bf16[2048,1024]{1,0:T(8,128)(2,1)S(1)}, bf16[512,128]{1,0:T(8,128)...) custom-call(bf16[256,1024]{1,0:T(8,128)(2,1)S(1)} %copy-done.7, bf16[32,4480]{1,0:T(8,128)(2,1)S(1)} %pad.91.refs_1_, ...), custom_call_target="tpu_custom_call" | custom-call | bytes 33554432 | tf_op jit(solution)/shard_map/pallas_call | solution.py:528
  267.4 3.5 copy-done
  275.7 5.3 fusion.92
  281.1 2.2 collective-permute-start
  292.2 2.4 convolution_convert_fusion.1
  294.6 54.0 %shard_map.315 = (bf16[2048,128]{1,0:T(8,128)(2,1)S(1)}, f32[8,128]{1,0:T(8,128)}) custom-call(bf16[2048,128]{1,0:T(8,128)(2,1)S(1)} %bitcast.109, f32[8,128]{1,0:T(8,128)S(1)} %scatter.6.logs_ref, f32[8,128]{1,0:T(8,128)S(1)} %broadcast_22_order_ref_values_ref_right_ref.2.order_ref.values_ref.right_ref, ...), custom_call_target="tpu_custom_call" | custom-call | flops 4194304 | bytes 2097152 | tf_op jit(solution)/shard_map/pallas_call | solution.py:867
  351.7 2.2 fusion.8
  354.6 3.8 fusion.9.values_ref
  358.4 11.7 %shard_map.317 = f32[64,8192]{1,0:T(8,128)} custom-call(bf16[64,1024]{1,0:T(8,128)(2,1)} %fusion.9.values_ref, bf16[32,384,1024]{2,1,0:T(8,128)(2,1)} %bitcast.111), custom_call_target="tpu_custom_call" | custom-call | flops 1073741824 | bytes 16777216 | tf_op jit(solution)/shard_map/pallas_call | solution.py:106
  370.1 2.9 reshape.565
  373.0 2.3 multiply_reduce_fusion.4
  376.7 7.4 shard_map.318.triple_ref
  384.1 14.4 %shard_map.319.values_ref = bf16[512,1024]{1,0:T(8,128)(2,1)} custom-call(bf16[512,3072]{1,0:T(8,128)(2,1)} %shard_map.318.triple_ref), custom_call_target="tpu_custom_call" | custom-call | tf_op jit(solution)/shard_map/pallas_call | solution.py:1057
  398.4 4.5 shard_map.320
  406.4 34.5 %all-gather.7.cloned.1.call-done = bf16[12288,1024]{1,0:T(8,128)(2,1)} async-done(((bf16[384,1024]{1,0:T(8,128)(2,1)}), bf16[12288,1024]{1,0:T(8,128)(2,1)}) %all-gather.7.cloned.1.call-update) | async-done | bytes 25165840 | tf_op jit(solution)/shard_map/all_gather | solution.py:89
  440.9 28.9 %shard_map.322 = (bf16[512,1024]{1,0:T(8,128)(2,1)}, bf16[512,4096]{1,0:T(8,128)(2,1)}, bf16[512,4096]{1,0:T(8,128)(2,1)}, bf16[512,4096]{1,0:T(8,128)(2,1)}) custom-call(f32[512,1024]{1,0:T(8,128)} %copy-done.14, bf16[512,1024]{1,0:T(8,128)(2,1)S(1)} %multiply_convert_fusion.normed_ref, bf16[32,384,1024]{2,1,0:T(8,128)(2,1)} %bitcast.117, ...), custom_call_target="tpu_custom_call" | custom-call | flops 12884901888 | bytes 33554432 | tf_op jit(solution)/shard_map/pallas_call | solution.py:930
  469.8 24.2 %shard_map.323 = (bf16[2,512,4096]{2,1,0:T(8,128)(2,1)}, f32[512,1024]{1,0:T(8,128)}, bf16[512,1024]{1,0:T(8,128)(2,1)}, f32[1,1024]{1,0:T(1,128)}) custom-call(bf16[512,1024]{1,0:T(8,128)(2,1)} %grad_ref.3, f32[512,1024]{1,0:T(8,128)} %copy-done.14, f32[1,1024]{1,0:T(1,128)} %bitcast.137, bf16[512,4096]{1,0:T(8,128)(2,1)} %get-tuple-element.167.gate_ref, ...), custom_call_target="tpu_custom_call" | custom-call | flops 12884901888 | bytes 33554432 | tf_op jit(solution)/shard_map/pallas_call | solution.py:987
  494.0 3.4 copy-done.9
  497.4 2.2 copy-done.10
  499.6 18.0 %shard_map.331 = bf16[32,384,1024]{2,1,0:T(8,128)(2,1)} custom-call(bf16[512,4096]{1,0:T(8,128)(2,1)S(1)} %copy-done.10, bf16[512,1024]{1,0:T(8,128)(2,1)S(1)} %copy-done.6, bf16[512,1024]{1,0:T(8,128)(2,1)S(1)} %multiply_convert_fusion.normed_ref, bf16[2,512,4096]{2,1,0:T(8,128)(2,1)S(1)} %copy-done.9), custom_call_target="tpu_custom_call" | custom-call | flops 12884901888 | bytes 33554432 | tf_op jit(solution)/shard_map/pallas_call | solution.py:217
  519.6 5.7 shard_map.324
  525.3 2.9 convert_element_type.123.grad_ref
  528.3 27.0 %shard_map.325.values_ref = bf16[512,3072]{1,0:T(8,128)(2,1)} custom-call(bf16[512,3072]{1,0:T(8,128)(2,1)} %shard_map.318.triple_ref, bf16[512,1024]{1,0:T(8,128)(2,1)} %convert_element_type.123.grad_ref), custom_call_target="tpu_custom_call" | custom-call | tf_op jit(solution)/shard_map/pallas_call | solution.py:1102
  557.3 8.8 shard_map.326
  566.1 3.1 multiply_reduce_fusion
  571.3 2.7 reshape.566.direct_ref
  574.0 2.7 convert_element_type.124.values_ref
  576.7 13.2 %shard_map.327 = f32[64,1024]{1,0:T(8,128)} custom-call(bf16[64,8192]{1,0:T(8,128)(2,1)} %convert_element_type.124.values_ref, bf16[32,384,1024]{2,1,0:T(8,128)(2,1)} %bitcast.116), custom_call_target="tpu_custom_call" | custom-call | flops 1073741824 | bytes 16777216 | tf_op jit(solution)/shard_map/pallas_call | solution.py:136
  594.8 2.5 reshape.567
  597.4 2.8 copy.147
  600.2 5.1 fusion.33
  605.5 2.9 broadcast_multiply_fusion
  608.5 2.1 pad_maximum_fusion.1.values_ref
  610.7 2.0 convolution_convert_fusion.states_ref
  612.7 2.3 pad_maximum_fusion.right_ref
  615.1 106.8 %shard_map.328 = (bf16[2048,128]{1,0:T(8,128)(2,1)S(1)}, f32[32,4096]{1,0:T(8,128)S(1)}) custom-call(bf16[2048,128]{1,0:T(8,128)(2,1)S(1)} %convolution_convert_fusion.states_ref, f32[8,128]{1,0:T(8,128)S(1)} %scatter.9.logs_ref, bf16[1024,1024]{1,0:T(8,128)(2,1)S(1)} %fusion.order_ref, bf16[2,512,1024]{2,1,0:T(8,128)(2,1)S(1)} %pad_maximum_fusion.1.values_ref, ...), custom_call_target="tpu_custom_call" | custom-call | flops 4194304 | bytes 2097152 | tf_op jit(solution)/shard_map/pallas_call | solution.py:867
  722.3 3.4 broadcast_multiply_fusion.1
  729.5 2.8 copy.154
  732.3 2.4 reshape.572
  734.7 2.4 fusion.6
  737.1 2.4 copy.175
  745.0 2.4 fusion.82
  769.6 6.7 multiply_reduce_fusion.18
  779.4 185.9 %shard_map.330 = (f32[256,1024]{1,0:T(8,128)}, f32[8,128]{1,0:T(8,128)}, f32[32,8192]{1,0:T(8,128)}, f32[32,4384]{1,0:T(8,128)}, f32[64,1024]{1,0:T(8,128)}) custom-call(bf16[64,1024]{1,0:T(8,128)(2,1)} %add_convert_fusion.grad_ref, bf16[2048,256]{1,0:T(8,128)(2,1)} %copy-done.11, f32[256,128]{1,0:T(8,128)} %reshape.590.small_ref, ...), custom_call_target="tpu_custom_call" | custom-call | flops 4294967296 | bytes 16777216 | tf_op jit(solution)/shard_map/pallas_call | solution.py:731
  969.3 11.9 %shard_map.329 = bf16[64,8192]{1,0:T(8,128)(2,1)} custom-call(f32[64,8192]{1,0:T(8,128)} %reshape.566.direct_ref, bf16[64,1024]{1,0:T(8,128)(2,1)} %add_convert_fusion.grad_ref, bf16[8192,1024]{1,0:T(8,128)(2,1)} %get-tuple-element.188.weight_ref), custom_call_target="tpu_custom_call" | custom-call | flops 1073741824 | bytes 16777216 | tf_op jit(solution)/shard_map/pallas_call | solution.py:158
  981.1 2.3 reshape.575
  (390 shorter events, 80.9 us)
Async XLA Ops:
  7.2 4.5 copy-start.104
  7.2 4.6 copy-start.37
  7.2 351.2 %all-gather.5.cloned.1.call-start = ((), (), s32[]{:S(2)}) async-start(), calls=%async_computation.2 | async-start | bytes 25952256 | tf_op jit(solution)/shard_map/all_gather | solution.py:89
  9.4 431.5 %all-gather.7.cloned.1.call-start = ((), (), s32[]{:S(2)}) async-start(), calls=%async_computation.3 | async-start | bytes 25952256 | tf_op jit(solution)/shard_map/all_gather | solution.py:89
  11.6 974.5 %reduce-scatter.2.cloned.1.call-start = ((), (), s32[]{:S(2)}) async-start(), calls=%async_computation.1 | async-start | bytes 25952256 | tf_op jit(solution)/shard_map/reduce_scatter | solution.py:1251
  11.8 262.5 %copy-start.105 = (s32[64]{0:T(128)S(1)}, s32[64]{0:T(128)}, u32[]{:S(2)}) copy-start(s32[64]{0:T(128)} %param.25) | copy-start | bytes 772
  274.0 80.6 %copy-start.3 = (f32[64,1024]{1,0:T(8,128)}, f32[64,1024]{1,0:T(8,128)S(1)}, u32[]{:S(2)}) copy-start(f32[64,1024]{1,0:T(8,128)S(1)} %get-tuple-element.176) | copy-start | bytes 786436
  274.8 6.3 copy-start.100
  275.7 10.0 %copy-start.103 = (f32[3,32]{1,0:T(4,128)S(1)}, f32[3,32]{1,0:T(4,128)}, u32[]{:S(2)}) copy-start(f32[3,32]{1,0:T(4,128)} %param.32) | copy-start | bytes 1156
  281.0 7.7 copy-start.30
  281.1 8.9 copy-start.28
  281.1 7.5 collective-permute-start
  287.6 66.6 %copy-start.33 = (f32[64,2048]{1,0:T(8,128)}, f32[64,2048]{1,0:T(8,128)S(1)}, u32[]{:S(2)}) copy-start(f32[64,2048]{1,0:T(8,128)S(1)} %slice.180) | copy-start | bytes 1572868
  288.0 116.8 %copy-start.80 = (f32[1024]{0:T(1024)}, f32[1024]{0:T(1024)S(1)}, u32[]{:S(2)}) copy-start(f32[1024]{0:T(1024)S(1)} %reshape.554) | copy-start | bytes 12292
  290.0 58.9 %copy-start.26 = (f32[64,2304]{1,0:T(8,128)}, f32[64,2304]{1,0:T(8,128)S(1)}, u32[]{:S(2)}) copy-start(f32[64,2304]{1,0:T(8,128)S(1)} %get-tuple-element.242) | copy-start | bytes 1769476
  290.6 58.0 %copy-start.16 = (f32[64,32,64]{2,1,0:T(8,128)}, f32[64,32,64]{2,1,0:T(8,128)S(1)}, u32[]{:S(2)}) copy-start(f32[64,32,64]{2,1,0:T(8,128)S(1)} %reshape.560) | copy-start | bytes 1572868
  294.6 57.1 %copy-start.39 = (f32[64,32,64]{0,2,1:T(8,128)S(1)}, f32[64,32,64]{0,2,1:T(8,128)}, u32[]{:S(2)}) copy-start(f32[64,32,64]{0,2,1:T(8,128)} %copy.143) | copy-start | bytes 1572868
  375.3 27.7 %copy-start.12 = (f32[512,1024]{1,0:T(8,128)}, f32[512,1024]{1,0:T(8,128)S(1)}, u32[]{:S(2)}) copy-start(f32[512,1024]{1,0:T(8,128)S(1)} %get-tuple-element.171) | copy-start | bytes 6291460
  469.8 24.2 %copy-start.6 = (bf16[512,1024]{1,0:T(8,128)(2,1)S(1)}, bf16[512,1024]{1,0:T(8,128)(2,1)}, u32[]{:S(2)}) copy-start(bf16[512,1024]{1,0:T(8,128)(2,1)} %grad_ref.3) | copy-start | bytes 3145732
  519.6 95.5 %copy-start.5 = (bf16[1024,1024]{1,0:T(8,128)(2,1)}, bf16[1024,1024]{1,0:T(8,128)(2,1)S(1)}, u32[]{:S(2)}) copy-start(bf16[1024,1024]{1,0:T(8,128)(2,1)S(1)} %fusion.order_ref) | copy-start | bytes 6291460
  557.3 8.8 copy-start.13
  576.7 14.2 %copy-start.2 = (bf16[2048,1024]{1,0:T(8,128)(2,1)S(1)}, bf16[2048,1024]{1,0:T(8,128)(2,1)}, u32[]{:S(2)}) copy-start(bf16[2048,1024]{1,0:T(8,128)(2,1)} %copy-done.1) | copy-start | bytes 12582916
  615.1 106.8 %copy-start.20 = (f32[32,64,128]{2,1,0:T(8,128)S(1)}, f32[32,64,128]{2,1,0:T(8,128)}, u32[]{:S(2)}) copy-start(f32[32,64,128]{2,1,0:T(8,128)} %copy-done.19) | copy-start | bytes 3145732
  726.5 8.2 copy-start.38
  739.6 5.3 copy-start.29
  739.6 5.3 copy-start.43
  739.6 5.3 copy-start.45
  739.6 5.3 copy-start.46
  739.6 5.3 copy-start.63
  739.6 5.3 copy-start.88
  739.6 5.3 copy-start.90
  739.6 5.3 copy-start.92
  742.9 4.5 copy-start.70
  742.9 4.5 copy-start.72
  747.4 6.4 copy-start.42
  747.7 11.0 %copy-start.4 = (f32[64,1024]{1,0:T(8,128)S(1)}, f32[64,1024]{1,0:T(8,128)}, u32[]{:S(2)}) copy-start(f32[64,1024]{1,0:T(8,128)} %copy-done.3) | copy-start | bytes 786436
  748.4 10.5 %copy-start.49 = (bf16[64,1024]{1,0:T(8,128)(2,1)S(1)}, bf16[64,1024]{1,0:T(8,128)(2,1)}, u32[]{:S(2)}) copy-start(bf16[64,1024]{1,0:T(8,128)(2,1)} %copy-done.48) | copy-start | bytes 393220
  748.4 19.2 %collective-permute-start.1 = (f32[3,2304]{1,0:T(4,128)}, f32[3,2304]{1,0:T(4,128)}, u32[]{:S(2)}, u32[]{:S(2)}) collective-permute-start(f32[3,2304]{1,0:T(4,128)} %pad_add_fusion.1), channel_id=1, source_target_pairs={{1,0},{2,1},{3,2},{4,3},{5,4},{6,5},{7,6},{8,7},{9,8},{10,9},{11,1... | collective-permute-start | bytes 82952 | tf_op jit(solution)/shard_map/ppermute | solution.py:1140
  753.8 6.9 copy-start.86
  753.8 8.5 copy-start.81
  754.8 5.8 copy-start.57
  754.8 5.9 copy-start.60
  754.8 5.9 copy-start.65
  754.8 5.9 copy-start.68
  758.8 5.4 copy-start.102
  763.2 6.4 copy-start.44
  763.2 6.4 copy-start.78
  769.6 7.6 copy-start.40
  (68 other events, 168.9 us)
Sparse Core Ops, SparseCore 0:
  11.5 251.0 all-gather.4
  266.0 174.8 all-gather.6
  517.8 283.5 reduce-scatter.1

commit v4 on v3

--- a/solution.py
+++ b/solution.py
@@ -119,16 +119,25 @@
     )(values, flat)
 
 
-def flat_dot_t_kernel(values_ref, flat_ref, out_ref):
-    found = dot_t(values_ref[...], whole_of(flat_ref))
-
-    @pl.when(pl.program_id(0) == 0)
+def flat_dot_t_kernel(values_ref, flat_ref, out_ref, total):
+    few = values_ref.shape[0] < 256
+    step = pl.program_id(0)
+    if few:
+        found = dot_t(whole_of(flat_ref), values_ref[...])
+    else:
+        found = dot_t(values_ref[...], whole_of(flat_ref))
+
+    @pl.when(step == 0)
     def _():
-        out_ref[...] = found
-
-    @pl.when(pl.program_id(0) > 0)
+        total[...] = found
+
+    @pl.when(step > 0)
     def _():
-        out_ref[...] += found
+        total[...] += found
+
+    @pl.when(step == pl.num_programs(0) - 1)
+    def _():
+        out_ref[...] = total[...].T if few else total[...]
 
 
 def flat_dot_t(values, flat, first, count):
@@ -142,6 +151,7 @@
             flat_block(n, D // n, lambda i: first + i),
         ],
         out_specs=pl.BlockSpec((rows, D), lambda i: (0, 0)),
+        scratch_shapes=[pltpu.VMEM((D, rows) if rows < 256 else (rows, D), F32)],
         compiler_params=pltpu.CompilerParams(vmem_limit_bytes=56 * 2**20),
         cost_estimate=pl.CostEstimate(
             flops=2 * rows * D * D * count, bytes_accessed=2 * D * D * count, transcendentals=0
@@ -150,7 +160,7 @@
 
 
 def input_grad_kernel(direct_ref, grad_ref, weight_ref, out_ref):
-    out_ref[...] = (direct_ref[...] + dot_t(grad_ref[...], weight_ref[...])).astype(BF)
+    out_ref[...] = (direct_ref[...] + dot_t(weight_ref[...], grad_ref[...]).T).astype(BF)
 
 
 def input_gradient(direct, grad, weight):
@@ -227,7 +237,7 @@
         out_specs=pl.BlockSpec(
             (devices, block, D), lambda i: (i % 4, jnp.minimum(i // 4, 1) + late(i) // 4, 0)
         ),
-        compiler_params=pltpu.CompilerParams(vmem_limit_bytes=32 * 2**20),
+        compiler_params=pltpu.CompilerParams(vmem_limit_bytes=56 * 2**20),
         cost_estimate=pl.CostEstimate(
             flops=6 * rows * FF * D, bytes_accessed=2**25, transcendentals=0
         ),
@@ -556,9 +566,13 @@
 SUM_TIMES = [0, 1, 3, 4, 6, 7]
 
 
+def columns_of(chunk):
+    return pl.ds(pl.multiple_of(chunk * SUM_COLUMNS, SUM_COLUMNS), SUM_COLUMNS)
+
+
 class Sums:
-    def __init__(self, here, find, left, right, out, kept, sent, got, send_sem, recv_sem):
-        self.here, self.find, self.left, self.right, self.out = here, find, left, right, out
+    def __init__(self, here, sources, out, kept, sent, got, send_sem, recv_sem):
+        self.here, self.sources, self.out = here, sources, out
         self.kept, self.sent, self.got = kept, sent, got
         self.send_sem, self.recv_sem = send_sem, recv_sem
         self.steps = here.halves()[::-1]
@@ -580,12 +594,6 @@
         for step in range(len(self.steps)):
             self.copy(chunk, step).wait_send()
 
-    def product(self, chunk, first, rows):
-        which, column = self.find(chunk)
-        left = self.left[which, pl.ds(first, rows)]
-        start = pl.multiple_of(column * SUM_COLUMNS, SUM_COLUMNS)
-        return dot(left, self.right[:, pl.ds(start, SUM_COLUMNS)])
-
     def begin(self, chunk):
         half = self.here.n // 2 * SUM_ROWS
         slot = chunk % SUM_SLOTS
@@ -594,9 +602,18 @@
         def _():
             self.sent_all(chunk - SUM_SLOTS)
 
-        self.sent[slot, pl.ds(half, half)] = self.product(chunk, half, half).astype(BF)
-        self.copy(chunk, 0).start()
-        self.kept[slot] = self.product(chunk, 0, half)
+        for first, stop, find, left, right in self.sources:
+
+            @pl.when((chunk >= first) & (chunk < stop))
+            def _():
+                which, column = find(chunk - first)
+
+                def product(row):
+                    return dot(left[which, pl.ds(row, half)], right[:, columns_of(column)])
+
+                self.sent[slot, pl.ds(half, half)] = product(half).astype(BF)
+                self.copy(chunk, 0).start()
+                self.kept[slot] = product(0)
 
     def go_on(self, chunk, step):
         slot, rows = chunk % SUM_SLOTS, self.steps[step - 1][0] * SUM_ROWS
@@ -610,18 +627,19 @@
         self.copy(chunk, step).start()
         self.kept[slot, pl.ds(0, half)] = total[:half]
 
+    def at(self, time):
+        for step in range(len(self.steps), -1, -1):
+            chunk = time - SUM_TIMES[step]
+
+            @pl.when((chunk >= 0) & (chunk < self.chunks))
+            def _():
+                if step == 0:
+                    self.begin(chunk)
+                else:
+                    self.go_on(chunk, step)
+
     def run(self, first, stop):
-        @pl.loop(first, stop)
-        def _(time):
-            for step in range(len(self.steps), -1, -1):
-                chunk = time - SUM_TIMES[step]
-
-                @pl.when((chunk >= 0) & (chunk < self.chunks))
-                def _():
-                    if step == 0:
-                        self.begin(chunk)
-                    else:
-                        self.go_on(chunk, step)
+        pl.loop(first, stop)(self.at)
 
     def end(self):
         @pl.loop(max(0, self.chunks - SUM_SLOTS), self.chunks)
@@ -649,22 +667,21 @@
     ]
 
 
-def columns_of(chunk):
-    return pl.ds(pl.multiple_of(chunk * SUM_COLUMNS, SUM_COLUMNS), SUM_COLUMNS)
-
-
 def local_find(chunk):
     return (chunk + 6) // 8, chunk
 
 
+def unpatch_find(chunk):
+    return 0, chunk
+
+
 def last_find(chunk):
-    late, rest = chunk // 16, chunk - 16
-    return late * (1 + (rest + 7) // 16 + (rest + 5) // 16), chunk
+    return (chunk + 7) // 16 + (chunk + 5) // 16, chunk
 
 
 def last_kernel(
     n, grad_ref, parted_ref, small_ref, order_ref, values_ref, right_ref,
-    d_weight_ref, d_small_ref, d_unpatch_ref, d_in_ref, d_out_ref,
+    d_weight_ref, d_small_ref, d_in_ref, d_out_ref,
     known, small_kept, small_got, g_send, g_recv, t_send, t_recv, left_ref, *scratch
 ):
     here = Place(n)
@@ -681,24 +698,20 @@
     spare = d_in_ref.shape[1] % SUM_COLUMNS
 
     def store(chunk, total):
-        @pl.when(chunk < 16)
+        @pl.when(chunk < 8)
         def _():
-            d_unpatch_ref[:, columns_of(chunk)] = total
-
-        @pl.when((chunk >= 16) & (chunk < 24))
-        def _():
-            d_in_ref[:, columns_of(chunk - 16)] = total
-
-        @pl.when(chunk == 24)
+            d_in_ref[:, columns_of(chunk)] = total
+
+        @pl.when(chunk == 8)
         def _():
             d_in_ref[:, pl.ds(8 * SUM_COLUMNS, spare)] = total[:, :spare]
 
-        @pl.when(chunk >= 25)
+        @pl.when(chunk >= 9)
         def _():
-            part = (chunk - 25) // 2
-            d_out_ref[rows_of(part, 1, SUM_ROWS), columns_of((chunk - 25) % 2)] = total
-
-    sums = Sums(here, last_find, left_ref, right_ref, store, *scratch)
+            part = (chunk - 9) // 2
+            d_out_ref[rows_of(part, 1, SUM_ROWS), columns_of((chunk - 9) % 2)] = total
+
+    sums = Sums(here, [(0, 13, last_find, left_ref, right_ref)], store, *scratch)
     steps = here.halves()
     copies = []
     for step in range(len(steps)):
@@ -711,11 +724,11 @@
         told = remote(small_kept.at[cut], small_got.at[cut], t_send.at[step], t_recv.at[step], partner)
         told.start()
         copies += [gather, told]
-        sums.run(3 * step, 3 * step + 3)
+        sums.run(2 * step, 2 * step + 2)
         gather.wait_recv()
         told.wait_recv()
         small_kept[mine] = small_kept[mine] + small_got[cut]
-    sums.run(3 * len(steps), sums.times)
+    sums.run(2 * len(steps), sums.times)
     d_small_ref[...] = small_kept[pl.ds(0, LOG_ROWS)]
     d_weight_ref[...] = lax.dot_general(
         parted_ref[...], known[...], (((0,), (0,)), ((), ())), preferred_element_type=F32
@@ -733,12 +746,11 @@
         out_shape=[
             jax.ShapeDtypeStruct((width, D), F32),
             jax.ShapeDtypeStruct((LOG_ROWS, 128), F32),
-            jax.ShapeDtypeStruct((SUM_ROWS, PATCH * D), F32),
             jax.ShapeDtypeStruct((SUM_ROWS, projections), F32),
             jax.ShapeDtypeStruct((2 * SUM_ROWS, D), F32),
         ],
         in_specs=[pl.BlockSpec(memory_space=pltpu.VMEM)] * 6,
-        out_specs=[pl.BlockSpec(memory_space=pltpu.VMEM)] * 5,
+        out_specs=[pl.BlockSpec(memory_space=pltpu.VMEM)] * 4,
         scratch_shapes=[
             pltpu.VMEM((n * rows, D), BF),
             pltpu.VMEM(small.shape, F32),
@@ -757,136 +769,341 @@
 LOG_ROWS = 8
 
 
-def states_kernel(
-    n, reverse, states_ref, logs_ref, order_ref, values_ref, right_ref, out_ref, sum_ref,
-    spread, logs, summed, s_send, s_recv, l_send, l_recv, b_send, b_recv, *scratch
+class Exchange:
+    def __init__(self, n, reverse, states, logs_in, out, spread, logs, summed, *sems):
+        self.n, self.reverse = n, reverse
+        self.me = lax.axis_index("seq")
+        self.states, self.logs_in, self.out = states, logs_in, out
+        self.spread, self.logs, self.summed = spread, logs, summed
+        self.sems = sems
+        self.rows = states.shape[0] // n
+
+    def spreading(self, other):
+        send, recv = self.sems[:2]
+        source = self.states.at[rows_of(other, 1, self.rows)]
+        target = self.spread.at[rows_of(self.me, 1, self.rows)]
+        return remote(source, target, send.at[other], recv.at[self.me], other)
+
+    def telling(self, other):
+        send, recv = self.sems[2:4]
+        target = self.logs.at[rows_of(self.me, 1, LOG_ROWS)]
+        return remote(self.logs_in, target, send.at[other], recv.at[self.me], other)
+
+    def returning(self, other):
+        send, recv = self.sems[4:6]
+        source = self.summed.at[rows_of(other, 1, self.rows)]
+        target = self.out.at[rows_of(self.me, 1, self.rows)]
+        return remote(source, target, send.at[other], recv.at[self.me], other)
+
+    def tell(self):
+        @pl.loop(1, self.n)
+        def _(hop):
+            self.telling(lax.rem(self.me + hop, self.n)).start()
+
+        target = self.logs.at[rows_of(self.me, 1, LOG_ROWS)]
+        pltpu.make_async_copy(self.logs_in, target, self.sems[3].at[self.me]).start()
+
+    def start(self):
+        @pl.loop(1, self.n)
+        def _(hop):
+            self.spreading(lax.rem(self.me + hop, self.n)).start()
+
+        mine = rows_of(self.me, 1, self.rows)
+        recv = self.sems[1].at[self.me]
+        pltpu.make_async_copy(self.states.at[mine], self.spread.at[mine], recv).start()
+
+    def join(self):
+        n, rows, summed, spread = self.n, self.rows, self.summed, self.spread
+
+        @pl.loop(0, n)
+        def _(other):
+            landed(spread.at[rows_of(other, 1, rows)], self.sems[1].at[other])
+            landed(self.logs.at[rows_of(other, 1, LOG_ROWS)], self.sems[3].at[other])
+
+        head = self.me * MHEADS // n
+        lane = lax.broadcasted_iota(jnp.int32, (LOG_ROWS, 128), 1)
+        row = lax.broadcasted_iota(jnp.int32, (LOG_ROWS, 128), 0)
+
+        def step(count, total):
+            place = n - 1 - count if self.reverse else count
+            cut = rows_of(place, 1, rows)
+            summed[cut] = total.astype(BF)
+            told = self.logs[rows_of(place, 1, LOG_ROWS)]
+            log = jnp.sum(jnp.where((lane == head) & (row == 0), told, 0.0), keepdims=True)
+            flag = jnp.sum(jnp.where((lane == MHEADS) & (row == 0), told, 0.0), keepdims=True)
+            decay = jnp.where(flag > 0.0, 0.0, jnp.exp(log))
+            return decay * total + spread[cut].astype(F32)
+
+        lax.fori_loop(0, n, step, jnp.zeros((rows, NSTATE), F32))
+
+        @pl.loop(1, n)
+        def _(hop):
+            self.returning(lax.rem(self.me + hop, n)).start()
+
+        mine = rows_of(self.me, 1, rows)
+        recv = self.sems[5].at[self.me]
+        pltpu.make_async_copy(summed.at[mine], self.out.at[mine], recv).start()
+
+    def arrive(self):
+        @pl.loop(0, self.n)
+        def _(other):
+            landed(self.out.at[rows_of(other, 1, self.rows)], self.sems[5].at[other])
+
+    def end(self):
+        @pl.loop(1, self.n)
+        def _(hop):
+            other = lax.rem(self.me + hop, self.n)
+            self.spreading(other).wait_send()
+            self.telling(other).wait_send()
+            self.returning(other).wait_send()
+
+
+def exchange_scratch(n):
+    total = MHEADS * MHEAD_DIM
+    return [
+        pltpu.VMEM((total, NSTATE), BF),
+        pltpu.VMEM((n * LOG_ROWS, 128), F32),
+        pltpu.VMEM((total, NSTATE), BF),
+    ] + [pltpu.SemaphoreType.DMA((n,))] * 6
+
+
+def states_kernel(n, reverse, states_ref, logs_ref, out_ref, *scratch):
+    greet(n)
+    exchange = Exchange(n, reverse, states_ref, logs_ref, out_ref, *scratch)
+    exchange.tell()
+    exchange.start()
+    exchange.join()
+    exchange.arrive()
+    exchange.end()
+
+
+def told_logs(logs):
+    return jnp.zeros((LOG_ROWS, 128), F32).at[0, : logs.shape[0]].set(logs)
+
+
+def pass_states(n, states, logs, reverse):
+    total = MHEADS * MHEAD_DIM
+    return pl.pallas_call(
+        functools.partial(states_kernel, n, reverse),
+        out_shape=jax.ShapeDtypeStruct((total, NSTATE), BF),
+        in_specs=[pl.BlockSpec(memory_space=pltpu.VMEM)] * 2,
+        out_specs=pl.BlockSpec(memory_space=pltpu.VMEM),
+        scratch_shapes=exchange_scratch(n),
+        compiler_params=pltpu.CompilerParams(
+            collective_id=3 if reverse else 2, has_side_effects=True, vmem_limit_bytes=16 * 2**20
+        ),
+        cost_estimate=pl.CostEstimate(flops=2**22, bytes_accessed=2**21, transcendentals=0),
+    )(states.reshape(total, NSTATE).astype(BF), told_logs(logs))
+
+
+NN, NT, TN = ((1,), (0,)), ((1,), (1,)), ((0,), (0,))
+
+
+def in_parts(value, count):
+    if value.dtype == BF:
+        return [value]
+    parts = []
+    for _ in range(count):
+        parts.append(value.astype(BF))
+        value = value - parts[-1].astype(F32)
+    return parts
+
+
+def dot_fine(left, right, dims, count=2):
+    total = None
+    for i, a in enumerate(in_parts(left, count)):
+        for j, b in enumerate(in_parts(right, count)):
+            if i + j < count:
+                found = lax.dot_general(a, b, (dims, ((), ())), preferred_element_type=F32)
+                total = found if total is None else total + found
+    return total
+
+
+def mixer_back_kernel(
+    n, logs_ref, order_ref, values_ref, right_ref, hidden_ref, slots_ref,
+    dy_ref, x_ref, keys_ref, queries_ref, state_ref, steps_ref, marks_ref, head_ref,
+    dx_ref, dkeys_ref, dqueries_ref, d_dt_ref, d_head_ref, sum_ref, unpatch_ref,
+    scores, d_scores, d_step, d_cum, d_turned, grads, back, left_ref, hidden_left, *scratch
 ):
-    me = lax.axis_index("seq")
-    rows = states_ref.shape[0] // n
+    rows, width = x_ref.shape[0], 2 * MHEAD_DIM
     greet(n)
-    sums = None
+    exchange = Exchange(n, True, grads, logs_ref, back, *scratch[:9])
 
     def store(chunk, total):
-        sum_ref[:, columns_of(chunk)] = total
-
-    if scratch:
-        left_ref = scratch[0]
-        sums = Sums(Place(n), local_find, left_ref, right_ref, store, *scratch[1:])
-
-    def spreading(other):
-        return remote(
-            states_ref.at[rows_of(other, 1, rows)],
-            spread.at[rows_of(me, 1, rows)],
-            s_send.at[other],
-            s_recv.at[me],
-            other,
-        )
-
-    def telling(other):
-        target = logs.at[rows_of(me, 1, LOG_ROWS)]
-        return remote(logs_ref, target, l_send.at[other], l_recv.at[me], other)
-
-    def returning(other):
-        return remote(
-            summed.at[rows_of(other, 1, rows)],
-            out_ref.at[rows_of(me, 1, rows)],
-            b_send.at[other],
-            b_recv.at[me],
-            other,
-        )
-
-    @pl.loop(1, n)
-    def _(hop):
-        other = lax.rem(me + hop, n)
-        spreading(other).start()
-        telling(other).start()
-
-    own = pltpu.make_async_copy(
-        states_ref.at[rows_of(me, 1, rows)], spread.at[rows_of(me, 1, rows)], s_recv.at[me]
-    )
-    own_logs = pltpu.make_async_copy(logs_ref, logs.at[rows_of(me, 1, LOG_ROWS)], l_recv.at[me])
-    own.start()
-    own_logs.start()
-    if sums:
-        turn(order_ref, left_ref, values_ref)
-        sums.run(0, 4)
-
-    @pl.loop(0, n)
-    def _(other):
-        landed(spread.at[rows_of(other, 1, rows)], s_recv.at[other])
-        landed(logs.at[rows_of(other, 1, LOG_ROWS)], l_recv.at[other])
-
-    head = me * MHEADS // n
-    lane = lax.broadcasted_iota(jnp.int32, (LOG_ROWS, 128), 1)
-    row = lax.broadcasted_iota(jnp.int32, (LOG_ROWS, 128), 0)
-
-    def join(step, total):
-        place = n - 1 - step if reverse else step
-        cut = rows_of(place, 1, rows)
-        summed[cut] = total.astype(BF)
-        told = logs[rows_of(place, 1, LOG_ROWS)]
-        log = jnp.sum(jnp.where((lane == head) & (row == 0), told, 0.0), keepdims=True)
-        flag = jnp.sum(jnp.where((lane == MHEADS) & (row == 0), told, 0.0), keepdims=True)
-        decay = jnp.where(flag > 0.0, 0.0, jnp.exp(log))
-        return decay * total + spread[cut].astype(F32)
-
-    lax.fori_loop(0, n, join, jnp.zeros((rows, NSTATE), F32))
-
-    @pl.loop(1, n)
-    def _(hop):
-        returning(lax.rem(me + hop, n)).start()
-
-    own_back = pltpu.make_async_copy(
-        summed.at[rows_of(me, 1, rows)], out_ref.at[rows_of(me, 1, rows)], b_recv.at[me]
-    )
-    own_back.start()
-    if sums:
-        sums.run(4, sums.times)
-        sums.end()
-
-    @pl.loop(0, n)
-    def _(other):
-        landed(out_ref.at[rows_of(other, 1, rows)], b_recv.at[other])
-
-    @pl.loop(1, n)
-    def _(hop):
-        other = lax.rem(me + hop, n)
-        spreading(other).wait_send()
-        telling(other).wait_send()
-        returning(other).wait_send()
-
-
-def pass_states(n, states, logs, reverse, order=None, lefts=None, right=None):
+        @pl.when(chunk < 16)
+        def _():
+            unpatch_ref[:, columns_of(chunk)] = total
+
+        @pl.when(chunk >= 16)
+        def _():
+            sum_ref[:, columns_of(chunk - 16)] = total
+
+    sources = [
+        (0, 16, unpatch_find, hidden_left, slots_ref),
+        (16, 24, local_find, left_ref, right_ref),
+    ]
+    sums = Sums(Place(n), sources, store, *scratch[9:])
+    exchange.tell()
+    turn(order_ref, hidden_left, hidden_ref)
+    turn(order_ref, left_ref, values_ref)
+
+    head_lane = lax.broadcasted_iota(jnp.int32, (1, MHEADS), 1)
+    lanes = lax.broadcasted_iota(jnp.int32, (1, width), 1)
+    halves = [lanes < MHEAD_DIM, lanes >= MHEAD_DIM]
+    step, cum = steps_ref[0, :rows, :MHEADS], steps_ref[1, :rows, :MHEADS]
+    turned_step, turned_cum = steps_ref.at[3], steps_ref.at[4]
+    reach = marks_ref[0][:, :rows]
+    from_before, to_after = marks_ref[1][:, 0:1], marks_ref[1][:, 1:2]
+    last_cum = cum[rows - 1 : rows]
+    to_end = jnp.exp(last_cum - cum) * to_after
+
+    def column(values, head):
+        return jnp.sum(jnp.where(head_lane == head, values, 0.0), axis=1, keepdims=True)
+
+    def at_head(head, values):
+        return jnp.where(head_lane == head, values, 0.0)
+
+    def of_pair(pair, values):
+        return jnp.where(halves[0], column(values, 2 * pair), column(values, 2 * pair + 1))
+
+    def columns(pair):
+        return pl.ds(pl.multiple_of(pair * width, width), width)
+
+    scores[...] = dot_fine(queries_ref[...], keys_ref[...], NT)
+    d_scores[...] = jnp.zeros_like(d_scores)
+    d_step[...] = jnp.zeros_like(d_step)
+    d_cum[...] = jnp.zeros_like(d_cum)
+    d_turned[...] = jnp.zeros_like(d_turned)
+    dqueries_ref[...] = jnp.zeros_like(dqueries_ref)
+    d_head_ref[...] = jnp.zeros_like(d_head_ref)
+
+    @pl.loop(0, MHEADS // 2)
+    def _(pair):
+        sums.at(pair)
+        x, dy, state = x_ref[:, columns(pair)], dy_ref[:, columns(pair)], state_ref[columns(pair)]
+        dx = of_pair(pair, head_ref[2:3]) * dy
+        inflow = jnp.exp(of_pair(pair, cum)) * from_before
+        dy_in = dy * inflow
+        carried = dy_in * dot_fine(queries_ref[...], state, NT)
+        dqueries_ref[...] += dot_fine(dy_in, state, NN)
+        grads[columns(pair)] = dot_fine(dy_in, queries_ref[...], TN).astype(BF)
+        for which, half in enumerate(halves):
+            head = 2 * pair + which
+            mine = pl.ds(head, 1)
+            gap = column(cum, head) - turned_cum[mine, :rows]
+            decay = jnp.exp(jnp.where(reach > 0.0, gap, 0.0)) * reach
+            weighted = scores[...] * decay
+            step_row = turned_step[mine, :rows]
+            mixing = weighted * step_row
+            d_mixing = dot_fine(dy, jnp.where(half, x, 0.0), NT)
+            dx += dot_fine(mixing, jnp.where(half, dy, 0.0), TN)
+            d_scores[...] += d_mixing * decay * step_row
+            d_gap = d_mixing * mixing
+            d_turned[0, mine, :rows] = jnp.sum(d_mixing * weighted, axis=0, keepdims=True)
+            d_turned[1, mine, :rows] = -jnp.sum(d_gap, axis=0, keepdims=True)
+            moved = jnp.sum(d_gap, axis=1, keepdims=True)
+            moved += jnp.sum(jnp.where(half, carried, 0.0), axis=1, keepdims=True)
+            d_cum[...] += at_head(head, moved)
+            skipped = jnp.sum(jnp.where(half, dy * x, 0.0), keepdims=True)
+            d_head_ref[2:3] += at_head(head, skipped)
+        dx_ref[:, columns(pair)] = dx
+
+    dkeys_ref[...] = dot_fine(d_scores[...], queries_ref[...], TN)
+    dqueries_ref[...] += dot_fine(d_scores[...], keys_ref[...], NN)
+    exchange.start()
+    sums.run(16, 20)
+    exchange.join()
+    sums.run(20, 24)
+    exchange.arrive()
+
+    @pl.loop(0, MHEADS // 2)
+    def _(pair):
+        @pl.when(pair < 7)
+        def _():
+            sums.at(24 + pair)
+
+        x, state, grad = x_ref[:, columns(pair)], state_ref[columns(pair)], back[columns(pair)]
+        weight = of_pair(pair, to_end * step)
+        d_weighted = dot_fine(keys_ref[...], grad, NT)
+        dkeys_ref[...] += dot_fine(x * weight, grad, NN)
+        dx_ref[:, columns(pair)] += weight * d_weighted
+        kept = grad.astype(F32) * state.astype(F32)
+        for which, half in enumerate(halves):
+            head = 2 * pair + which
+            d_weight = jnp.sum(jnp.where(half, x * d_weighted, 0.0), axis=1, keepdims=True)
+            d_step[...] += at_head(head, d_weight * column(to_end, head))
+            moved = d_weight * column(to_end * step, head)
+            d_cum[...] -= at_head(head, moved)
+            d_decay = jnp.sum(kept[which * MHEAD_DIM : (which + 1) * MHEAD_DIM], keepdims=True)
+            ended = jnp.sum(moved, keepdims=True)
+            ended += d_decay * jnp.exp(column(last_cum, head)) * from_before[rows - 1 : rows]
+            d_cum[rows - 1 : rows] += at_head(head, ended)
+
+    d_steps = d_step[...] + d_turned[0].T[:rows, :MHEADS]
+    d_cums = d_cum[...] + d_turned[1].T[:rows, :MHEADS]
+    later = lax.broadcasted_iota(jnp.int32, (rows, rows), 0) <= lax.broadcasted_iota(
+        jnp.int32, (rows, rows), 1
+    )
+    d_logs = dot_fine(later.astype(BF), d_cums, NN, 3)
+    rate = jnp.exp(head_ref[1:2])
+    d_raw = (d_steps - rate * d_logs) * steps_ref[2, :rows, :MHEADS]
+    d_dt_ref[...] = d_raw
+    d_head_ref[0:1] = jnp.sum(d_raw, axis=0, keepdims=True)
+    d_head_ref[1:2] = -rate * jnp.sum(step * d_logs, axis=0, keepdims=True)
+    sums.run(31, sums.times)
+    sums.end()
+    exchange.end()
+
+
+def mixer_back(n, logs, order, values, right, hidden, slots, dy, conv_out, state_in, dt_raw, head_params, starts):
+    rows = conv_out.shape[0]
+    x, keys, queries, step, cum, segment = block_parts(conv_out, dt_raw, head_params, starts)
+    slope = jax.nn.sigmoid(dt_raw + head_params[0])
+    square = [jnp.pad(v, ((0, 128 - v.shape[0]), (0, 128 - v.shape[1]))) for v in (step.T, cum.T)]
+    tall = [jnp.pad(v, ((0, 128 - rows), (0, 128 - MHEADS))) for v in (step, cum, slope)]
+    steps = jnp.stack(tall + square)
+    position = jnp.arange(rows)
+    reach = (position[:, None] >= position[None, :]) & (segment[:, None] == segment[None, :])
+    ends = jnp.stack([segment == 0, segment == segment[-1]], axis=1)
+    marks = jnp.stack(
+        [jnp.pad(v.astype(F32), ((0, 0), (0, 128 - v.shape[1]))) for v in (reach, ends)]
+    )
     total = MHEADS * MHEAD_DIM
-    told = jnp.zeros((LOG_ROWS, 128), F32).at[0, : logs.shape[0]].set(logs)
-    summing = lefts is not None
-    chunks = right.shape[1] // SUM_COLUMNS if summing else 0
-    small = jnp.zeros((LOG_ROWS, 128), F32)
-    operands = [states.reshape(total, NSTATE).astype(BF), told]
-    operands += [order, lefts, right] if summing else [small] * 3
-    out, found = pl.pallas_call(
-        functools.partial(states_kernel, n, reverse),
+    narrow = jax.ShapeDtypeStruct((rows, NSTATE), F32)
+    return pl.pallas_call(
+        functools.partial(mixer_back_kernel, n),
         out_shape=[
-            jax.ShapeDtypeStruct((total, NSTATE), BF),
-            jax.ShapeDtypeStruct((SUM_ROWS, chunks * SUM_COLUMNS) if summing else (LOG_ROWS, 128), F32),
+            jax.ShapeDtypeStruct((rows, DI), F32),
+            narrow,
+            narrow,
+            jax.ShapeDtypeStruct((rows, MHEADS), F32),
+            jax.ShapeDtypeStruct((8, MHEADS), F32),
+            jax.ShapeDtypeStruct((SUM_ROWS, right.shape[1]), F32),
+            jax.ShapeDtypeStruct((SUM_ROWS, slots.shape[1]), F32),
         ],
-        in_specs=[pl.BlockSpec(memory_space=pltpu.VMEM)] * 5,
-        out_specs=[pl.BlockSpec(memory_space=pltpu.VMEM)] * 2,
+        in_specs=[pl.BlockSpec(memory_space=pltpu.VMEM)] * 14,
+        out_specs=[pl.BlockSpec(memory_space=pltpu.VMEM)] * 7,
         scratch_shapes=[
+            pltpu.VMEM((rows, rows), F32),
+            pltpu.VMEM((rows, rows), F32),
+            pltpu.VMEM((rows, MHEADS), F32),
+            pltpu.VMEM((rows, MHEADS), F32),
+            pltpu.VMEM((2, 128, 128), F32),
             pltpu.VMEM((total, NSTATE), BF),
-            pltpu.VMEM((n * LOG_ROWS, 128), F32),
             pltpu.VMEM((total, NSTATE), BF),
         ]
-        + [pltpu.SemaphoreType.DMA((n,))] * 6
-        + (lefts_scratch(n, lefts) + sums_scratch(n, chunks) if summing else []),
+        + lefts_scratch(n, values)
+        + lefts_scratch(n, hidden)
+        + exchange_scratch(n)
+        + sums_scratch(n, 24),
         compiler_params=pltpu.CompilerParams(
-            collective_id=3 if reverse else 2,
-            has_side_effects=True,
-            vmem_limit_bytes=(48 if summing else 16) * 2**20,
+            collective_id=3, has_side_effects=True, vmem_limit_bytes=62 * 2**20
         ),
-        cost_estimate=pl.CostEstimate(flops=2**22, bytes_accessed=2**21, transcendentals=0),
-    )(*operands)
-    return out.astype(F32).reshape(MHEADS, MHEAD_DIM, NSTATE), found
+        cost_estimate=pl.CostEstimate(flops=2**32, bytes_accessed=2**24, transcendentals=2**20),
+    )(
+        told_logs(logs), order, values, right, hidden, slots, dy, conv_out[:, :DI], keys, queries,
+        state_in, steps, marks, head_params,
+    )
 
 
 FF_TILE = D
@@ -899,7 +1116,7 @@
     gate, up = dot(normed_ref[...], whole_of(gate_w_ref)), dot(normed_ref[...], whole_of(up_w_ref))
     hid = (silu(gate) * up).astype(BF)
     gate_ref[...], up_ref[...], hid_ref[...] = gate.astype(BF), up.astype(BF), hid
-    found = dot(hid, whole_of(down_ref))
+    found = dot(hid, down_ref[...])
 
     @pl.when(step == 0)
     def _():
@@ -914,16 +1131,16 @@
         out_ref[...] = total[...].astype(BF)
 
 
-def late_blocks(n):
-    tiles, block = FF // FF_TILE, FF // n
+def feed_forward_blocks(n):
+    tiles, first = FF // FF_TILE, PATCH + 4
     return [
-        flat_block(n, D // n, lambda i: i),
-        flat_block(n, D // n, lambda i: i + tiles),
-        pl.BlockSpec((n // tiles, block, D), lambda i: (i, 2 * FF // n // block, 0)),
+        flat_block(n, D // n, lambda i: first + i),
+        flat_block(n, D // n, lambda i: first + tiles + i),
+        pl.BlockSpec((FF_TILE, D), lambda i: (i, 0)),
     ]
 
 
-def feed_forward(stream, normed, flat):
+def feed_forward(stream, normed, flat, down):
     rows, tiles = stream.shape[0], FF // FF_TILE
     wide = pl.BlockSpec((rows, D), lambda i: (0, 0))
     tile = pl.BlockSpec((rows, FF_TILE), lambda i: (0, i))
@@ -935,7 +1152,7 @@
         in_specs=[
             wide,
             wide,
-            *late_blocks(flat.shape[0]),
+            *feed_forward_blocks(flat.shape[0]),
         ],
         out_specs=[wide, tile, tile, tile],
         scratch_shapes=[pltpu.VMEM((rows, D), F32)],
@@ -943,7 +1160,7 @@
         cost_estimate=pl.CostEstimate(
             flops=6 * rows * D * FF, bytes_accessed=2**25, transcendentals=rows * FF
         ),
-    )(stream, normed, flat, flat, flat)
+    )(stream, normed, flat, flat, down)
 
 
 def feed_forward_back_kernel(
@@ -951,7 +1168,7 @@
     both_ref, d_stream_ref, d_low_ref, d_gain_ref, total,
 ):
     step = pl.program_id(0)
-    d_hid = dot_t(grad_ref[...], whole_of(down_ref))
+    d_hid = dot_t(grad_ref[...], down_ref[...])
     gate, up = gate_ref[...].astype(F32), up_ref[...].astype(F32)
     s = jax.nn.sigmoid(gate)
     d_gate = (d_hid * up * (s * (1.0 + gate * (1.0 - s)))).astype(BF)
@@ -979,7 +1196,7 @@
         d_gain_ref[...] = jnp.sum(stream * r * d_normed, axis=0, keepdims=True)
 
 
-def feed_forward_back(grad, stream, gain, gate, up, flat):
+def feed_forward_back(grad, stream, gain, gate, up, flat, down):
     rows, tiles = stream.shape[0], FF // FF_TILE
     wide = pl.BlockSpec((rows, D), lambda i: (0, 0))
     tile = pl.BlockSpec((rows, FF_TILE), lambda i: (0, i))
@@ -999,7 +1216,7 @@
             narrow,
             tile,
             tile,
-            *late_blocks(flat.shape[0]),
+            *feed_forward_blocks(flat.shape[0]),
         ],
         out_specs=[pl.BlockSpec((2, rows, FF_TILE), lambda i: (0, 0, i)), wide, wide, narrow],
         scratch_shapes=[pltpu.VMEM((rows, D), F32)],
@@ -1007,7 +1224,7 @@
         cost_estimate=pl.CostEstimate(
             flops=6 * rows * D * FF, bytes_accessed=2**25, transcendentals=rows * FF
         ),
-    )(grad, stream, gain[None], gate, up, flat, flat, flat)
+    )(grad, stream, gain[None], gate, up, flat, flat, down)
     return both, d_stream, d_low, d_gain[0]
 
 
@@ -1015,25 +1232,33 @@
 
 
 def tile_mask():
-    row = lax.broadcasted_iota(jnp.int32, (ATTN_ROWS, ATTN_ROWS), 0)
-    column = lax.broadcasted_iota(jnp.int32, (ATTN_ROWS, ATTN_ROWS), 1)
+    row = lax.broadcasted_iota(jnp.int32, (ATTN_ROWS, 2 * ATTN_ROWS), 0)
+    column = lax.broadcasted_iota(jnp.int32, (ATTN_ROWS, 2 * ATTN_ROWS), 1) % ATTN_ROWS
     return (row // PATCH == column // PATCH) & (row >= column)
 
 
-def head_mask(which):
-    lane = lax.broadcasted_iota(jnp.int32, (1, 2 * AHEAD_DIM), 1)
-    return lane // AHEAD_DIM == which
-
-
-def only(values, mask):
-    return jnp.where(mask, values, jnp.zeros_like(values))
-
-
-def tile_probs(queries, key_rows, mask):
-    scores = dot_t(queries, key_rows) * AHEAD_DIM ** (-0.5)
-    scores = jnp.where(mask, scores, -1e30)
-    raised = jnp.exp(scores - jnp.max(scores, axis=-1, keepdims=True))
-    return raised / jnp.sum(raised, axis=-1, keepdims=True)
+def first_head():
+    return lax.broadcasted_iota(jnp.int32, (1, 2 * AHEAD_DIM), 1) < AHEAD_DIM
+
+
+def one_below_other(pair):
+    lanes, zeros = first_head(), jnp.zeros_like(pair)
+    return jnp.concatenate([jnp.where(lanes, pair, zeros), jnp.where(lanes, zeros, pair)], axis=0)
+
+
+def by_head(values, reduce):
+    first = reduce(values[:, :ATTN_ROWS], axis=-1, keepdims=True)
+    second = reduce(values[:, ATTN_ROWS:], axis=-1, keepdims=True)
+    shape = (values.shape[0], ATTN_ROWS)
+    return jnp.concatenate(
+        [jnp.broadcast_to(first, shape), jnp.broadcast_to(second, shape)], axis=1
+    )
+
+
+def pair_probs(queries, key_rows, mask):
+    scores = jnp.where(mask, dot_t(queries, key_rows) * AHEAD_DIM ** (-0.5), -1e30)
+    raised = jnp.exp(scores - by_head(scores, jnp.max))
+    return raised / by_head(raised, jnp.sum)
 
 
 def attention_kernel(triple_ref, out_ref):
@@ -1043,13 +1268,9 @@
         queries, key_rows, value_rows = [
             triple_ref[:, part * D + pair * width : part * D + (pair + 1) * width] for part in range(3)
         ]
-        total = None
-        for which in range(2):
-            lanes = head_mask(which)
-            probs = tile_probs(only(queries, lanes), key_rows, mask)
-            mixed = dot(probs.astype(BF), only(value_rows, lanes))
-            total = mixed if total is None else total + mixed
-        out_ref[:, pair * width : (pair + 1) * width] = total.astype(BF)
+        probs = pair_probs(queries, one_below_other(key_rows), mask)
+        mixed = dot(probs.astype(BF), one_below_other(value_rows))
+        out_ref[:, pair * width : (pair + 1) * width] = mixed.astype(BF)
 
 
 def attention(triple):
@@ -1067,34 +1288,24 @@
     mask = tile_mask()
     width = 2 * AHEAD_DIM
     scale = AHEAD_DIM ** (-0.5)
-    rows_first = (((0,), (0,)), ((), ()))
+
+    def of_keys(left, right):
+        found = lax.dot_general(left, right, (((0,), (0,)), ((), ())), preferred_element_type=F32)
+        return jnp.where(first_head(), found[:ATTN_ROWS], found[ATTN_ROWS:])
+
     for pair in range(AHEADS // 2):
         lo, hi = pair * width, (pair + 1) * width
         queries, key_rows, value_rows = [
             triple_ref[:, part * D + lo : part * D + hi] for part in range(3)
         ]
         grad = grad_ref[:, lo:hi]
-        totals = [None, None, None]
-        for which in range(2):
-            lanes = head_mask(which)
-            probs = tile_probs(only(queries, lanes), key_rows, mask)
-            grad_one = only(grad, lanes)
-            d_probs = dot_t(grad_one, value_rows)
-            d_scores = probs * (d_probs - jnp.sum(probs * d_probs, axis=-1, keepdims=True))
-            d_scores = d_scores.astype(BF)
-            found = [
-                scale * dot(d_scores, only(key_rows, lanes)),
-                scale
-                * lax.dot_general(
-                    d_scores, only(queries, lanes), rows_first, preferred_element_type=F32
-                ),
-                lax.dot_general(
-                    probs.astype(BF), grad_one, rows_first, preferred_element_type=F32
-                ),
-            ]
-            totals = found if which == 0 else [a + b for a, b in zip(totals, found)]
-        for part in range(3):
-            out_ref[:, part * D + lo : part * D + hi] = totals[part].astype(BF)
+        key_rows = one_below_other(key_rows)
+        probs = pair_probs(queries, key_rows, mask)
+        d_probs = dot_t(grad, one_below_other(value_rows))
+        d_scores = (probs * (d_probs - by_head(probs * d_probs, jnp.sum))).astype(BF)
+        out_ref[:, lo:hi] = (scale * dot(d_scores, key_rows)).astype(BF)
+        out_ref[:, D + lo : D + hi] = (scale * of_keys(d_scores, queries)).astype(BF)
+        out_ref[:, 2 * D + lo : 2 * D + hi] = of_keys(probs.astype(BF), grad).astype(BF)
 
 
 def attention_back(triple, grad):
@@ -1145,8 +1356,8 @@
     byte_wide = byte_acts.astype(F32)
     patches = byte_acts.reshape(-1, PATCH * D)
     patch_rows = patches.shape[0]
-    early = gather_flat(n, [unpatch_weight, qkv_weight, attn_out])
-    late = gather_flat(n, [gate_up, down_weight])
+    early = gather_flat(n, [unpatch_weight, qkv_weight, attn_out, gate_up])
+    late = lax.all_gather(down_weight, "seq", axis=0, tiled=True)
     small = [patch_gain, conv_weight.reshape(-1), conv_bias, mixer_gain, attn_gain, ffn_gain]
     cuts = list(np.cumsum([piece.shape[0] for piece in small]))
     small_shard = jnp.concatenate(small)
@@ -1197,7 +1408,7 @@
         functools.partial(block_state, starts=resets), conv_out, dt_raw, head_params
     )
     local_state, decay_total = state_parts
-    live.state_in, _ = pass_states(n, local_state, live.logs, False)
+    live.state_in = pass_states(n, local_state, live.logs, False)
     live.fence()
 
     mixer_y, output_back = jax.vjp(
@@ -1205,7 +1416,7 @@
         conv_out,
         dt_raw,
         head_params,
-        live.state_in,
+        live.state_in.astype(F32).reshape(MHEADS, MHEAD_DIM, NSTATE),
     )
     gate_act = silu(live.gate_z)
     gated = mixer_y * gate_act
@@ -1224,7 +1435,7 @@
     live.stream1 = live.stream0 + flat_dot(live.mixed, live.early, PATCH + 3, 1, F32)
     live.normed1 = rms_scale(live.stream1, live.ffn_gain).astype(BF)
     live.late = late
-    layer_out, gate, up, hid = feed_forward(live.stream1, live.normed1, live.late)
+    layer_out, gate, up, hid = feed_forward(live.stream1, live.normed1, live.early, live.late)
     live.gate, live.up, live.hid = gate, up, hid
     live.fence()
 
@@ -1243,7 +1454,7 @@
         live.order = (place[None, :] == source[:, None]).astype(BF)
 
     d_both, d_stream1, d_stream1_low, g_ffn_gain = feed_forward_back(
-        out_grad, live.stream1, live.ffn_gain, live.gate, live.up, live.late
+        out_grad, live.stream1, live.ffn_gain, live.gate, live.up, live.early, live.late
     )
     if small_slice:
         block = down_weight.shape[0]
@@ -1264,24 +1475,38 @@
     d_branch = d_hidden.astype(BF)
     d_gated, g_mixer_gain = rms_back(gated, live.mixer_gain, dot_t(d_branch, live.mixer_out))
     d_gate_z = d_gated * mixer_y * silu_slope(live.gate_z)
-    output_grads = output_back(d_gated * gate_act)
-    summed = []
     if small_slice:
-        summed = [
+        dx, dkeys, dqueries, d_dt, g_head, found, g_unpatch = mixer_back(
+            n,
+            live.logs,
             live.order,
             jnp.stack([live.mixed, live.normed0]),
             jnp.concatenate([d_stream1_low, d_triple], axis=1),
-        ]
-    state_grad, found = pass_states(n, output_grads[3], live.logs, True, *summed)
-    g_attn_out, g_qkv = found[:, :D], found[:, D:]
-    decay_grad = jnp.sum(state_grad * live.state_in, axis=(1, 2))
-    state_cot = state_back((state_grad, decay_grad))
-    conv_cot = conv_back(output_grads[0] + state_cot[0])
+            live.hidden[None],
+            d_slots,
+            d_gated * gate_act,
+            conv_out,
+            live.state_in,
+            dt_raw,
+            head_params,
+            resets,
+        )
+        g_attn_out, g_qkv = found[:, :D], found[:, D:]
+        conv_cot = conv_back(jnp.concatenate([dx, dkeys, dqueries], axis=1))
+        g_head = g_head[:3]
+    else:
+        output_grads = output_back(d_gated * gate_act)
+        state_grad = pass_states(n, output_grads[3], live.logs, True).astype(F32)
+        state_grad = state_grad.reshape(MHEADS, MHEAD_DIM, NSTATE)
+        state_in = live.state_in.astype(F32).reshape(MHEADS, MHEAD_DIM, NSTATE)
+        state_cot = state_back((state_grad, jnp.sum(state_grad * state_in, axis=(1, 2))))
+        conv_cot = conv_back(output_grads[0] + state_cot[0])
+        d_dt = output_grads[1] + state_cot[1]
+        g_head = output_grads[2] + state_cot[2]
     returned = passed_along(conv_cot[0][: CONV - 1], -1)
     d_conv_in = conv_cot[0][CONV - 1 :] + jnp.concatenate(
         [jnp.zeros((patch_rows - CONV + 1, CONV_CH), F32), returned * keep_tail[:, None]]
     )
-    d_dt = output_grads[1] + state_cot[1]
     d_projected = jnp.concatenate([d_gate_z, d_conv_in, d_dt], axis=1).astype(BF)
     d_projected = jnp.pad(d_projected, ((0, 0), (0, -d_projected.shape[1] % 128)))
     d_embedded, g_patch_gain = rms_back(
@@ -1291,7 +1516,7 @@
     input_grad = input_gradient(live.d_stream0, d_embedded, live.patch_w).reshape(-1, D)
 
     g_conv_weight = conv_cot[1].reshape(CONV, n, -1).transpose(1, 0, 2).reshape(n, -1)
-    g_head = jnp.broadcast_to((output_grads[2] + state_cot[2]).reshape(1, -1), (n, 3 * MHEADS))
+    g_head = jnp.broadcast_to(g_head.reshape(1, -1), (n, 3 * MHEADS))
     g_small = [g_patch_gain, g_conv_weight, conv_cot[2], g_mixer_gain, g_attn_gain, g_ffn_gain, g_head]
     g_small = jnp.concatenate([piece.reshape(n, -1) for piece in g_small], axis=1)
     small_width = g_small.shape[1]
@@ -1299,14 +1524,14 @@
     g_small = g_small.reshape(n * LOG_ROWS, 128)
     if small_slice:
         d_projected = jnp.pad(d_projected, ((0, 0), (0, -d_projected.shape[1] % SUM_COLUMNS)))
-        g_patch, g_small, g_unpatch, g_mixer_in, g_mixer_out = last_sums(
+        g_patch, g_small, g_mixer_in, g_mixer_out = last_sums(
             n,
             d_embedded,
             live.parted,
             g_small,
             live.order,
-            lefts_of(live.hidden, live.normed, live.gated_norm),
-            jnp.concatenate([d_slots, d_projected, d_branch, d_branch], axis=1),
+            lefts_of(live.normed, live.gated_norm),
+            jnp.concatenate([d_projected, d_branch, d_branch], axis=1),
             mixer_in.shape[1],
         )
     else:

time: 1010 us -> 971 us (0.961)
  local copies, waits for them, and re-layouts: 70 us -> 49.2 us
  matrix products: 41.7 us -> 24.1 us
  Pallas kernels: 781 us -> 798 us
  other arithmetic: 51.7 us -> 41 us
    pallas_call x2, Pallas kernels: 161 us -> 262 us  [the longest x1 203 us: mixer_back(): pl.pallas_call(functools.partial(mixer_back_kernel, n), out_shape=[jax.Sh...]
    pallas_call x1, Pallas kernels: 186 us -> 111 us  [last_sums(): pl.pallas_call(functools.partial(last_kernel, n), out_shape=[jax.ShapeDty...]
    all_gather x2 -> x1, waiting for transfers between devices: 34.5 us -> 0.01 us  [gather_flat(): return lax.all_gather(flat_rows(shards), 'seq', axis=0)]
    all_gather x0 -> x1, waiting for transfers between devices: none -> 28.1 us  [local(): late = lax.all_gather(down_weight, 'seq', axis=0, tiled=True)]
    pallas_call x1, Pallas kernels: 255 us -> 268 us  [gather_weights(): pl.pallas_call(functools.partial(gather_kernel, n, chunks, embed_time), o...]
    unnamed x226 -> x191, local copies, waits for them, and re-layouts: 21 us -> 17.8 us
  transfers between devices with their start and end apart: 5 -> 5, of which waited for: 1 -> 1; matrix products, arithmetic and copies ran while one was open for 14% -> 10% of each run, Pallas kernels for 71% -> 76%
where the time goes in v4:
time: 971 us; the launch traced here: 961 us
  Pallas kernels  798 us (82%)
  local copies, waits for them, and re-layouts  49.2 us (5%)
  other arithmetic  41 us (4%)
  waiting for transfers between devices  28.9 us (3%)
  matrix products  24.1 us (2%)
  between operations  16 us (2%)
    pallas_call x1, Pallas kernels, gather_weights(): pl.pallas_call(functools.partial(gather_kernel, n, chunks, embed_time), o...  268 us
    pallas_call x1, Pallas kernels, mixer_back(): pl.pallas_call(functools.partial(mixer_back_kernel, n), out_shape=[jax.Sh...  203 us
    pallas_call x1, Pallas kernels, last_sums(): pl.pallas_call(functools.partial(last_kernel, n), out_shape=[jax.ShapeDty...  111 us
    pallas_call x1, Pallas kernels, pass_states(): pl.pallas_call(functools.partial(states_kernel, n, reverse), out_shape=ja...  58.7 us
    all_gather x1, waiting for transfers between devices, local(): late = lax.all_gather(down_weight, 'seq', axis=0, tiled=True)  28.1 us
    pallas_call x3, Pallas kernels, flat_dot_t(): pl.pallas_call(flat_dot_t_kernel, grid=(count,), out_shape=jax.ShapeDtype...  26 us
    pallas_call x1, Pallas kernels, feed_forward_back(): pl.pallas_call(feed_forward_back_kernel, grid=(tiles,), out_shape=[jax.Sh...  24.6 us
    pallas_call x1, Pallas kernels, flat_grads(): pl.pallas_call(flat_grad_kernel, grid=(12,), out_shape=jax.ShapeDtypeStru...  23.6 us
  transfers between devices with their start and end apart: 5, of which 1 were waited for; matrix products, arithmetic and copies ran while one was open for 10% of the time, Pallas kernels for 76%

profile of v4, /device:TPU:0, one launch (start us, length us, event | category | flops | bytes accessed | tf_op | source)
XLA Modules:
  0.0 961.5 jit_solution(16169663200441155564)
XLA Ops:
  7.3 2.5 shard_map.316
  11.5 267.8 %shard_map.314 = (bf16[8192,1024]{1,0:T(8,128)(2,1)}, bf16[1024,4480]{1,0:T(8,128)(2,1)S(1)}, bf16[2048,1024]{1,0:T(8,128)(2,1)S(1)}, bf16[512,128]{1,0:T(8,128)...) custom-call(bf16[256,1024]{1,0:T(8,128)(2,1)S(1)} %copy-done.7, bf16[32,4480]{1,0:T(8,128)(2,1)S(1)} %pad.81.refs_1_, ...), custom_call_target="tpu_custom_call" | custom-call | bytes 33554432 | tf_op jit(solution)/shard_map/pallas_call | solution.py:538
  279.3 3.6 copy-done
  282.9 2.0 copy-done.1
  286.9 5.3 fusion.63
  292.4 3.1 collective-permute-start
  302.0 1.3 fusion.25
  304.5 1.7 convolution_convert_fusion
  306.3 58.7 %shard_map.315.state_ref = bf16[2048,128]{1,0:T(8,128)(2,1)S(1)} custom-call(bf16[2048,128]{1,0:T(8,128)(2,1)S(1)} %bitcast.82, f32[8,128]{1,0:T(8,128)S(1)} %scatter.6.logs_ref), custom_call_target="tpu_custom_call" | custom-call | flops 4194304 | bytes 2097152 | tf_op jit(solution)/shard_map/pallas_call | solution.py:886
  366.0 1.3 convolution_multiply_fusion
  367.4 2.1 fusion.3
  371.8 3.8 fusion.4.values_ref
  375.6 10.5 %shard_map.317 = f32[64,8192]{1,0:T(8,128)} custom-call(bf16[64,1024]{1,0:T(8,128)(2,1)} %fusion.4.values_ref, bf16[32,640,1024]{2,1,0:T(8,128)(2,1)} %bitcast.83), custom_call_target="tpu_custom_call" | custom-call | flops 1073741824 | bytes 16777216 | tf_op jit(solution)/shard_map/pallas_call | solution.py:106
  386.1 3.0 reshape.500
  389.1 1.9 multiply_reduce_fusion.4
  392.3 7.4 shard_map.318.triple_ref
  399.7 6.6 shard_map.319.values_ref
  406.2 4.5 shard_map.320
  410.7 1.9 multiply_reduce_fusion.3
  412.6 1.3 copy-done.10
  414.2 28.1 %all-gather.4.cloned.1.call-done.down_ref = bf16[4096,1024]{1,0:T(8,128)(2,1)} async-done(((bf16[128,1024]{1,0:T(8,128)(2,1)}), bf16[4096,1024]{1,0:T(8,128)(2,1)}) %all-gather.4.cloned.1.call-update) | async-done | bytes 8388624 | tf_op jit(solution)/shard_map/all_gather | solution.py:1360
  442.4 20.8 %shard_map.321 = (bf16[512,1024]{1,0:T(8,128)(2,1)}, bf16[512,4096]{1,0:T(8,128)(2,1)}, bf16[512,4096]{1,0:T(8,128)(2,1)}, bf16[512,4096]{1,0:T(8,128)(2,1)}) custom-call(f32[512,1024]{1,0:T(8,128)} %copy-done.10, bf16[512,1024]{1,0:T(8,128)(2,1)S(1)} %multiply_convert_fusion.normed_ref, bf16[32,640,1024]{2,1,0:T(8,128)(2,1)} %bitcast.86, ...), custom_call_target="tpu_custom_call" | custom-call | flops 12884901888 | bytes 33554432 | tf_op jit(solution)/shard_map/pallas_call | solution.py:1147
  463.2 24.6 %shard_map.322 = (bf16[2,512,4096]{2,1,0:T(8,128)(2,1)}, f32[512,1024]{1,0:T(8,128)}, bf16[512,1024]{1,0:T(8,128)(2,1)}, f32[1,1024]{1,0:T(1,128)}) custom-call(bf16[512,1024]{1,0:T(8,128)(2,1)} %grad_ref.3, f32[512,1024]{1,0:T(8,128)} %copy-done.10, f32[1,1024]{1,0:T(1,128)} %bitcast.108, bf16[512,4096]{1,0:T(8,128)(2,1)} %get-tuple-element.166.gate_ref, ...), custom_call_target="tpu_custom_call" | custom-call | flops 12884901888 | bytes 33554432 | tf_op jit(solution)/shard_map/pallas_call | solution.py:1204
  487.9 23.6 %shard_map.330 = bf16[32,384,1024]{2,1,0:T(8,128)(2,1)} custom-call(bf16[512,4096]{1,0:T(8,128)(2,1)} %get-tuple-element.202.hid_ref, bf16[512,1024]{1,0:T(8,128)(2,1)} %grad_ref.3, bf16[512,1024]{1,0:T(8,128)(2,1)} %copy-done.5, bf16[2,512,4096]{2,1,0:T(8,128)(2,1)} %get-tuple-element.204.both_ref), custom_call_target="tpu_custom_call" | custom-call | flops 12884901888 | bytes 33554432 | tf_op jit(solution)/shard_map/pallas_call | solution.py:227
  514.1 1.7 fusion.order_ref
  515.9 1.4 fusion.60
  517.3 4.9 shard_map.323
  522.2 2.9 convert_element_type.129.grad_ref
  525.2 18.2 %shard_map.324.values_ref = bf16[512,3072]{1,0:T(8,128)(2,1)} custom-call(bf16[512,3072]{1,0:T(8,128)(2,1)} %shard_map.318.triple_ref, bf16[512,1024]{1,0:T(8,128)(2,1)} %convert_element_type.129.grad_ref), custom_call_target="tpu_custom_call" | custom-call | tf_op jit(solution)/shard_map/pallas_call | solution.py:1313
  543.6 9.1 shard_map.325
  552.8 3.1 multiply_reduce_fusion
  556.4 2.0 subtract_add_fusion
  558.3 2.0 reshape.501.direct_ref
  562.2 11.9 %shard_map.326 = f32[64,1024]{1,0:T(8,128)} custom-call(bf16[64,8192]{1,0:T(8,128)(2,1)} %convert_element_type.130.values_ref.slots_ref, bf16[32,640,1024]{2,1,0:T(8,128)(2,1)} %bitcast.92), custom_call_target="tpu_custom_call" | custom-call | flops 1073741824 | bytes 16777216 | tf_op jit(solution)/shard_map/pallas_call | solution.py:145
  575.1 1.5 pad_maximum_fusion.1.values_ref
  576.6 1.5 copy-done.2
  578.1 1.5 multiply_reduce_fusion.9
  581.0 2.4 pad_maximum_fusion.right_ref
  583.4 203.4 %shard_map.327 = (f32[64,2048]{1,0:T(8,128)}, f32[64,128]{1,0:T(8,128)}, f32[64,128]{1,0:T(8,128)}, f32[64,32]{1,0:T(8,128)}, f32[8,32]{1,0:T(8,128)}, /*index=5*/f32[32,4096]{1,0:T(8,128)}, f32[32,8192]{1,0:T(8,128)}) custom-call(f32[8,128]{1,0:T(8,128)} %scatter.9.logs_ref, bf16[1024,1024]{1,0:T(8,128)(2,1)} %fusion.order_ref, ...), custom_call_target="tpu_custom_call" | custom-call | flops 4294967296 | bytes 16777216 | tf_op jit(solution)/shard_map/pallas_call | solution.py:1073
  789.5 2.3 fusion.56
  792.9 1.3 collective-permute-start.1
  798.8 1.7 pad_maximum_fusion.3.values_ref
  805.5 7.2 multiply_reduce_fusion.12
  815.4 111.3 %shard_map.329 = (f32[256,1024]{1,0:T(8,128)}, f32[8,128]{1,0:T(8,128)}, f32[32,4384]{1,0:T(8,128)}, f32[64,1024]{1,0:T(8,128)}) custom-call(bf16[64,1024]{1,0:T(8,128)(2,1)} %add_convert_fusion.grad_ref, bf16[2048,256]{1,0:T(8,128)(2,1)} %copy-done.9, f32[256,128]{1,0:T(8,128)} %reshape.515.small_ref, bf16[1024,1024]{1,0:T(8,128)(2,1)} %fusion.order_ref, ...), custom_call_target="tpu_custom_call" | custom-call | flops 4294967296 | bytes 16777216 | tf_op jit(solution)/shard_map/pallas_call | solution.py:744
  927.4 1.3 split.47
  930.7 11.8 %shard_map.328 = bf16[64,8192]{1,0:T(8,128)(2,1)} custom-call(f32[64,8192]{1,0:T(8,128)} %copy-done.12, bf16[64,1024]{1,0:T(8,128)(2,1)} %add_convert_fusion.grad_ref, bf16[8192,1024]{1,0:T(8,128)(2,1)} %get-tuple-element.190.weight_ref), custom_call_target="tpu_custom_call" | custom-call | flops 1073741824 | bytes 16777216 | tf_op jit(solution)/shard_map/pallas_call | solution.py:168
  942.5 2.3 reshape.504
  946.1 1.4 fusion.62
  (334 shorter events, 49.5 us)
Async XLA Ops:
  7.2 3.6 copy-start.26
  7.2 368.4 %all-gather.6.cloned.1.call-start = ((), (), s32[]{:S(2)}) async-start(), calls=%async_computation.3 | async-start | bytes 43253760 | tf_op jit(solution)/shard_map/all_gather | solution.py:89
  9.9 432.5 %all-gather.4.cloned.1.call-start = ((), (), s32[]{:S(2)}) async-start(), calls=%async_computation.1 | async-start | bytes 8650752 | tf_op jit(solution)/shard_map/all_gather | solution.py:1360
  10.6 936.9 %reduce-scatter.2.cloned.1.call-start = ((), (), s32[]{:S(2)}) async-start(), calls=%async_computation.2 | async-start | bytes 25952256 | tf_op jit(solution)/shard_map/reduce_scatter | solution.py:1462
  10.8 275.3 %copy-start.81 = (s32[64]{0:T(128)S(1)}, s32[64]{0:T(128)}, u32[]{:S(2)}) copy-start(s32[64]{0:T(128)} %param.24) | copy-start | bytes 772
  279.3 3.6 copy-start
  285.9 85.2 %copy-start.3 = (f32[64,1024]{1,0:T(8,128)}, f32[64,1024]{1,0:T(8,128)S(1)}, u32[]{:S(2)}) copy-start(f32[64,1024]{1,0:T(8,128)S(1)} %get-tuple-element.175) | copy-start | bytes 786436
  286.6 5.7 copy-start.75
  286.9 5.4 copy-start.36
  286.9 11.0 %copy-start.78 = (f32[3,32]{1,0:T(4,128)S(1)}, f32[3,32]{1,0:T(4,128)}, u32[]{:S(2)}) copy-start(f32[3,32]{1,0:T(4,128)} %head_ref.1) | copy-start | bytes 1156
  292.3 11.0 %copy-start.24 = (f32[64,4480]{1,0:T(8,128)}, f32[64,4480]{1,0:T(8,128)S(1)}, u32[]{:S(2)}) copy-start(f32[64,4480]{1,0:T(8,128)S(1)} %fusion.63) | copy-start | bytes 3440644
  292.3 10.9 %copy-start.18 = (f32[64,2304]{1,0:T(8,128)}, f32[64,2304]{1,0:T(8,128)S(1)}, u32[]{:S(2)}) copy-start(f32[64,2304]{1,0:T(8,128)S(1)} %fusion.36) | copy-start | bytes 1769476
  292.4 9.5 collective-permute-start
  301.1 68.8 %copy-start.22 = (f32[64,2048]{1,0:T(8,128)}, f32[64,2048]{1,0:T(8,128)S(1)}, u32[]{:S(2)}) copy-start(f32[64,2048]{1,0:T(8,128)S(1)} %slice.189) | copy-start | bytes 1572868
  301.4 111.3 %copy-start.62 = (f32[1024]{0:T(1024)}, f32[1024]{0:T(1024)S(1)}, u32[]{:S(2)}) copy-start(f32[1024]{0:T(1024)S(1)} %reshape.490) | copy-start | bytes 12292
  301.5 69.2 %copy-start.48 = (f32[2048]{0:T(1024)}, f32[2048]{0:T(1024)S(1)}, u32[]{:S(2)}) copy-start(f32[2048]{0:T(1024)S(1)} %reshape.491) | copy-start | bytes 24580
  304.1 60.8 %copy-start.34 = (f32[64,2048]{1,0:T(8,128)}, f32[64,2048]{1,0:T(8,128)S(1)}, u32[]{:S(2)}) copy-start(f32[64,2048]{1,0:T(8,128)S(1)} %slice.203.x_ref) | copy-start | bytes 1572868
  369.8 5.8 copy-start.20
  370.7 4.9 copy-start.72
  414.2 49.0 %copy-start.5 = (bf16[512,1024]{1,0:T(8,128)(2,1)}, bf16[512,1024]{1,0:T(8,128)(2,1)S(1)}, u32[]{:S(2)}) copy-start(bf16[512,1024]{1,0:T(8,128)(2,1)S(1)} %multiply_convert_fusion.normed_ref) | copy-start | bytes 3145732
  513.5 8.8 copy-start.65
  560.3 13.8 %copy-start.12 = (f32[64,8192]{1,0:T(8,128)}, f32[64,8192]{1,0:T(8,128)S(1)}, u32[]{:S(2)}) copy-start(f32[64,8192]{1,0:T(8,128)S(1)} %reshape.501.direct_ref) | copy-start | bytes 6291460
  562.2 12.9 %copy-start.14 = (bf16[512,1024]{1,0:T(8,128)(2,1)S(1)}, bf16[512,1024]{1,0:T(8,128)(2,1)}, u32[]{:S(2)}) copy-start(bf16[512,1024]{1,0:T(8,128)(2,1)} %multiply_convert_fusion.1.values_ref) | copy-start | bytes 3145732
  562.2 12.9 %copy-start.15 = (bf16[512,1024]{1,0:T(8,128)(2,1)S(1)}, bf16[512,1024]{1,0:T(8,128)(2,1)}, u32[]{:S(2)}) copy-start(bf16[512,1024]{1,0:T(8,128)(2,1)} %shard_map.319.values_ref) | copy-start | bytes 3145732
  562.2 14.4 %copy-start.17 = (f32[64,2048]{1,0:T(8,128)S(1)}, f32[64,2048]{1,0:T(8,128)}, u32[]{:S(2)}) copy-start(f32[64,2048]{1,0:T(8,128)} %copy-done.16) | copy-start | bytes 1572868
  562.2 14.4 %copy-start.49 = (f32[2048]{0:T(1024)S(1)}, f32[2048]{0:T(1024)}, u32[]{:S(2)}) copy-start(f32[2048]{0:T(1024)} %copy-done.48) | copy-start | bytes 24580
  562.2 14.4 %copy-start.73 = (f32[64]{0:T(128)S(1)}, f32[64]{0:T(128)}, u32[]{:S(2)}) copy-start(f32[64]{0:T(128)} %copy-done.72) | copy-start | bytes 772
  583.4 206.1 %copy-start.19 = (f32[64,2304]{1,0:T(8,128)S(1)}, f32[64,2304]{1,0:T(8,128)}, u32[]{:S(2)}) copy-start(f32[64,2304]{1,0:T(8,128)} %copy-done.18) | copy-start | bytes 1769476
  583.4 206.1 %copy-start.33 = (f32[64,2304]{1,0:T(8,128)S(1)}, f32[64,2304]{1,0:T(8,128)}, u32[]{:S(2)}) copy-start(f32[64,2304]{1,0:T(8,128)} %get-tuple-element.231) | copy-start | bytes 1769476
  583.4 206.1 %copy-start.45 = (f32[3,2304]{1,0:T(4,128)S(1)}, f32[3,2304]{1,0:T(4,128)}, u32[]{:S(2)}) copy-start(f32[3,2304]{1,0:T(4,128)} %copy-done.44) | copy-start | bytes 82948
  583.4 206.1 %copy-start.67 = (f32[64]{0:T(128)S(1)}, f32[64]{0:T(128)}, u32[]{:S(2)}) copy-start(f32[64]{0:T(128)} %copy-done.66) | copy-start | bytes 772
  583.4 206.2 %copy-start.69 = (f32[64]{0:T(128)S(1)}, f32[64]{0:T(128)}, u32[]{:S(2)}) copy-start(f32[64]{0:T(128)} %copy-done.68) | copy-start | bytes 772
  583.4 206.2 %copy-start.71 = (f32[64]{0:T(128)S(1)}, f32[64]{0:T(128)}, u32[]{:S(2)}) copy-start(f32[64]{0:T(128)} %copy-done.70) | copy-start | bytes 772
  786.8 5.0 copy-start.51
  786.8 5.0 copy-start.53
  786.9 5.0 copy-start.55
  786.9 5.0 copy-start.57
  792.2 5.0 copy-start.4
  792.9 11.7 %collective-permute-start.1 = (f32[3,2304]{1,0:T(4,128)}, f32[3,2304]{1,0:T(4,128)}, u32[]{:S(2)}, u32[]{:S(2)}) collective-permute-start(f32[3,2304]{1,0:T(4,128)} %pad_add_fusion.1), channel_id=1, source_target_pairs={{1,0},{2,1},{3,2},{4,3},{5,4},{6,5},{7,6},{8,7},{9,8},{10,9},{11,1... | collective-permute-start | bytes 82952 | tf_op jit(solution)/shard_map/ppermute | solution.py:1351
  798.7 4.2 copy-start.61
  798.7 4.4 copy-start.64
  798.7 5.0 copy-start.74
  798.8 5.7 copy-start.79
  798.8 5.8 copy-start.76
  798.8 6.7 copy-start.59
  798.8 6.7 copy-start.77
  805.5 8.1 copy-start.30
  805.5 8.1 copy-start.83
  (47 other events, 98.3 us)
Sparse Core Ops, SparseCore 0:
  10.9 353.8 all-gather.5
  367.7 74.6 all-gather.3
  511.7 316.7 reduce-scatter.1

commit v5 on v4

--- a/solution.py
+++ b/solution.py
@@ -159,29 +159,6 @@
     )(values, flat)
 
 
-def input_grad_kernel(direct_ref, grad_ref, weight_ref, out_ref):
-    out_ref[...] = (direct_ref[...] + dot_t(weight_ref[...], grad_ref[...]).T).astype(BF)
-
-
-def input_gradient(direct, grad, weight):
-    rows, columns = direct.shape
-    return pl.pallas_call(
-        input_grad_kernel,
-        grid=(columns // D,),
-        out_shape=jax.ShapeDtypeStruct((rows, columns), BF),
-        in_specs=[
-            pl.BlockSpec((rows, D), lambda i: (0, i)),
-            pl.BlockSpec((rows, D), lambda i: (0, 0)),
-            pl.BlockSpec((D, D), lambda i: (i, 0)),
-        ],
-        out_specs=pl.BlockSpec((rows, D), lambda i: (0, i)),
-        compiler_params=pltpu.CompilerParams(vmem_limit_bytes=56 * 2**20),
-        cost_estimate=pl.CostEstimate(
-            flops=2 * rows * columns * D, bytes_accessed=2 * columns * D, transcendentals=0
-        ),
-    )(direct, grad, weight)
-
-
 class Live:
     def fence(self):
         vars(self).update(lax.optimization_barrier(dict(vars(self))))
@@ -193,55 +170,63 @@
     return summed.astype(F32)
 
 
-def flat_grad_kernel(hid_ref, grad_ref, normed_ref, both_ref, out_ref):
+def turned_product(left, right):
+    found = lax.dot_general(left, right, (((0,), (0,)), ((), ())), preferred_element_type=F32)
+    return found.astype(BF)
+
+
+def down_grad_kernel(hid_ref, grad_ref, out_ref):
     devices, block = out_ref.shape[:2]
-    parts = block // SUM_ROWS
-
-    def product(left, right):
-        return lax.dot_general(
-            left, right, (((0,), (0,)), ((), ())), preferred_element_type=F32
-        ).astype(BF)
-
-    @pl.when(pl.program_id(0) < 4)
-    def _():
-        few = devices // parts
-        for part in range(parts):
-            cut = pl.ds(part * few * block, few * block)
-            found = product(hid_ref[:, cut], grad_ref[...])
-            out_ref[pl.ds(part * few, few)] = found.reshape(few, block, D)
-
-    @pl.when(pl.program_id(0) >= 4)
-    def _():
-        for part in range(parts):
-            found = product(normed_ref[...], both_ref[0, :, pl.ds(part * D, D)])
-            cut = pl.ds(part * SUM_ROWS, SUM_ROWS)
-            out_ref[:, cut] = found.reshape(devices, SUM_ROWS, D)
-
-
-def flat_grads(n, hid, out_grad, normed, both):
+    few = 256 // block
+    for first in range(0, devices, few):
+        found = turned_product(hid_ref[:, pl.ds(first * block, 256)], grad_ref[...])
+        out_ref[pl.ds(first, few)] = found.reshape(few, block, D)
+
+
+def down_grad(n, hid, out_grad):
     rows, block, devices = hid.shape[0], hid.shape[1] // n, n // 4
-
-    def late(step):
-        return jnp.maximum(step - 4, 0)
-
     return pl.pallas_call(
-        flat_grad_kernel,
-        grid=(12,),
+        down_grad_kernel,
+        grid=(4,),
         out_shape=jax.ShapeDtypeStruct((n, 3 * block, D), BF),
         in_specs=[
-            pl.BlockSpec((rows, devices * block), lambda i: (0, jnp.minimum(i, 3))),
+            pl.BlockSpec((rows, devices * block), lambda i: (0, i)),
             pl.BlockSpec((rows, D), lambda i: (0, 0)),
-            pl.BlockSpec((rows, devices * SUM_ROWS), lambda i: (0, late(i) % 4)),
-            pl.BlockSpec((1, rows, FF), lambda i: (late(i) // 4, 0, 0)),
         ],
-        out_specs=pl.BlockSpec(
-            (devices, block, D), lambda i: (i % 4, jnp.minimum(i // 4, 1) + late(i) // 4, 0)
-        ),
+        out_specs=pl.BlockSpec((devices, block, D), lambda i: (i, 0, 0)),
         compiler_params=pltpu.CompilerParams(vmem_limit_bytes=56 * 2**20),
         cost_estimate=pl.CostEstimate(
-            flops=6 * rows * FF * D, bytes_accessed=2**25, transcendentals=0
+            flops=2 * rows * FF * D, bytes_accessed=2**24, transcendentals=0
         ),
-    )(hid, out_grad, normed, both)
+    )(hid, out_grad)
+
+
+def gate_up_grad_kernel(normed_ref, both_ref, flat_ref, out_ref):
+    del flat_ref
+    devices, block = out_ref.shape[:2]
+    for part in range(block // SUM_ROWS):
+        found = turned_product(normed_ref[...], both_ref[0, :, pl.ds(part * D, D)])
+        out_ref[:, pl.ds(part * SUM_ROWS, SUM_ROWS)] = found.reshape(devices, SUM_ROWS, D)
+
+
+def gate_up_grad(normed, both, flat):
+    n, rows, devices = flat.shape[0], normed.shape[0], flat.shape[0] // 4
+    return pl.pallas_call(
+        gate_up_grad_kernel,
+        grid=(8,),
+        out_shape=jax.ShapeDtypeStruct(flat.shape, BF),
+        in_specs=[
+            pl.BlockSpec((rows, devices * SUM_ROWS), lambda i: (0, i % 4)),
+            pl.BlockSpec((1, rows, FF), lambda i: (i // 4, 0, 0)),
+            pl.BlockSpec(memory_space=pltpu.HBM),
+        ],
+        out_specs=pl.BlockSpec((devices, flat.shape[1] // 3, D), lambda i: (i % 4, 1 + i // 4, 0)),
+        input_output_aliases={2: 0},
+        compiler_params=pltpu.CompilerParams(vmem_limit_bytes=56 * 2**20),
+        cost_estimate=pl.CostEstimate(
+            flops=4 * rows * FF * D, bytes_accessed=2**25, transcendentals=0
+        ),
+    )(normed, both, flat)
 
 
 def dot(left, right):
@@ -406,16 +391,15 @@
 
 
 GATHER_TIMES = [0, 1, 2, 3, 5, 6]
-
-
-EMBED_ROWS = 1024
-
-
-def gather_kernel(n, chunks, embed_time, *refs):
-    count = (len(refs) - 11) // 2
-    shards, patches_ref, wholes = refs[:count], refs[count], refs[count + 1 : -10]
-    embedded_ref, parted_ref, total, held, held_sem, own_sem = refs[-10:-4]
-    send_sem, recv_sem, part_send, part_recv = refs[-4:]
+EMBED_TIMES = [2, 4, 6, 8, 10, 11]
+
+
+def gather_kernel(n, chunks, *refs):
+    count = (len(refs) - 13) // 2
+    shards, patches_ref, weight_ref = refs[:count], refs[count], refs[count + 1]
+    wholes = refs[count + 2 : -11]
+    embedded_ref, parted_ref, product, got, own_sem = refs[-11:-6]
+    send_sem, recv_sem, part_send, part_recv, sum_send, sum_recv = refs[-6:]
     here = Place(n)
     greet(n)
     owns = []
@@ -464,31 +448,47 @@
             part_of(place), target, part_send.at[place], part_recv.at[there], here.device(place)
         )
 
-    pieces = wholes[0].shape[0] // EMBED_ROWS
-
-    def fetch(piece):
-        source = wholes[0].at[pl.ds(piece * EMBED_ROWS, EMBED_ROWS)]
-        return pltpu.make_async_copy(source, held.at[piece % 2], held_sem.at[piece % 2])
-
-    def embed(piece):
-        if piece == 0:
-            fetch(0).start()
-        if piece + 1 < pieces:
-            fetch(piece + 1).start()
-        fetch(piece).wait()
-        found = dot(patches_ref[:, pl.ds(piece * EMBED_ROWS, EMBED_ROWS)], held[piece % 2])
-        total[...] = found if piece == 0 else total[...] + found
-
-    done = 0
+    half = n // 2
     own_part = pltpu.make_async_copy(part_of(0), parted_ref.at[rows_of(0, 1, rows)], part_recv.at[0])
-    for time in range(len(chunks) + GATHER_TIMES[-1]):
-        if time == embed_time:
-            own_part.start()
-
-            @pl.loop(1, n)
-            def _(place):
-                parting(place).start()
-
+    own_part.start()
+
+    @pl.loop(1, n)
+    def _(hop):
+        parting(n - hop).start()
+
+    def multiply(first):
+        @pl.loop(first, first + half)
+        def _(place):
+            landed(parted_ref.at[rows_of(place, 1, rows)], part_recv.at[place])
+
+        @pl.loop(0, half // 4)
+        def _(index):
+            cut = rows_of(first // 4 + index, 1, 4 * rows)
+            product[cut] = dot(parted_ref[cut], weight_ref[...])
+
+    def summing(step):
+        blocks, partner = steps[len(steps) - 1 - step]
+        cut = pl.ds(blocks * rows, blocks * rows)
+        return remote(product.at[cut], got.at[cut], sum_send.at[step], sum_recv.at[step], partner)
+
+    def add(step):
+        blocks = steps[len(steps) - 1 - step][0]
+        summing(step).wait_recv()
+        mine, cut = pl.ds(0, blocks * rows), pl.ds(blocks * rows, blocks * rows)
+        product[mine] += got[cut]
+
+    def embed(time):
+        if time == EMBED_TIMES[0]:
+            multiply(half)
+            summing(0).start()
+            multiply(0)
+        for step in range(len(steps)):
+            if time == EMBED_TIMES[step + 1]:
+                add(step)
+                if step + 1 < len(steps):
+                    summing(step + 1).start()
+
+    for time in range(max(len(chunks) + GATHER_TIMES[-1], EMBED_TIMES[-1] + 1)):
         for step in range(len(steps), -1, -1):
             chunk = time - GATHER_TIMES[step]
             if 0 <= chunk < len(chunks):
@@ -496,22 +496,15 @@
                     arrive(chunk, step - 1)
                 if step < len(steps):
                     send(chunk, step)
-        for _ in range(2):
-            if time >= embed_time and done < pieces:
-                embed(done)
-                done += 1
-    for piece in range(done, pieces):
-        embed(piece)
-    embedded_ref[...] = total[...]
-
-    @pl.loop(0, n)
-    def _(place):
-        landed(parted_ref.at[rows_of(place, 1, rows)], part_recv.at[place])
+        embed(time)
+    embedded_ref[...] = product[pl.ds(0, rows)]
 
     @pl.loop(1, n)
     def _(place):
         parting(place).wait_send()
 
+    for step in range(len(steps)):
+        summing(step).wait_send()
     for chunk in range(len(chunks)):
         for step in range(len(steps)):
 
@@ -520,14 +513,18 @@
                 sending(chunk, step, place).wait_send()
 
 
-def gather_weights(n, shards, cuts, patches):
+def gather_weights(n, shards, cuts, patches, patch_weight):
     if n != 32 or any(shard.shape[0] % 16 for shard in shards):
         wholes = [lax.all_gather(shard, "seq", axis=0, tiled=True) for shard in shards]
         parted = patches.reshape(patches.shape[0], n, -1).transpose(1, 0, 2)
         parted = lax.all_to_all(parted, "seq", 0, 0, tiled=True)
-        return wholes + [dot(patches, wholes[0]), parted.reshape(-1, parted.shape[-1])]
-    rows = patches.shape[0]
-    embed_time = shards[0].shape[0] // cuts[0][0] + GATHER_TIMES[-1]
+        parted = parted.reshape(-1, parted.shape[-1])
+        product = dot(parted, patch_weight)
+        return wholes + [
+            lax.psum_scatter(product, "seq", scatter_dimension=0, tiled=True),
+            parted,
+        ]
+    rows, phases = patches.shape[0], n.bit_length() - 1
     chunks = [
         (index, first, rows, column, min(columns, shard.shape[1] - column))
         for index, (shard, (rows, columns)) in enumerate(zip(shards, cuts))
@@ -536,7 +533,7 @@
     ]
     sems = [pltpu.SemaphoreType.DMA((len(chunks), n))] * 2
     return pl.pallas_call(
-        functools.partial(gather_kernel, n, chunks, embed_time),
+        functools.partial(gather_kernel, n, chunks),
         out_shape=[
             jax.ShapeDtypeStruct((n * shard.shape[0], shard.shape[1]), shard.dtype) for shard in shards
         ]
@@ -544,22 +541,22 @@
             jax.ShapeDtypeStruct((rows, D), F32),
             jax.ShapeDtypeStruct((n * rows, patches.shape[1] // n), BF),
         ],
-        in_specs=[pl.BlockSpec(memory_space=pltpu.VMEM)] * (len(shards) + 1),
+        in_specs=[pl.BlockSpec(memory_space=pltpu.VMEM)] * (len(shards) + 2),
         out_specs=[pl.BlockSpec(memory_space=pltpu.HBM)] * len(shards)
         + [pl.BlockSpec(memory_space=pltpu.VMEM)] * 2,
         scratch_shapes=[
-            pltpu.VMEM((rows, D), F32),
-            pltpu.VMEM((2, EMBED_ROWS, D), BF),
-            pltpu.SemaphoreType.DMA((2,)),
+            pltpu.VMEM((n * rows, D), F32),
+            pltpu.VMEM((n * rows, D), F32),
             pltpu.SemaphoreType.DMA((len(shards),)),
         ]
         + sems
-        + [pltpu.SemaphoreType.DMA((n,))] * 2,
+        + [pltpu.SemaphoreType.DMA((n,))] * 2
+        + [pltpu.SemaphoreType.DMA((phases,))] * 2,
         compiler_params=pltpu.CompilerParams(
-            collective_id=0, has_side_effects=True, vmem_limit_bytes=24 * 2**20
+            collective_id=0, has_side_effects=True, vmem_limit_bytes=32 * 2**20
         ),
         cost_estimate=pl.CostEstimate(flops=0, bytes_accessed=2**25, transcendentals=0),
-    )(*shards, patches)
+    )(*shards, patches, patch_weight)
 
 
 SUM_ROWS, SUM_COLUMNS, SUM_SLOTS = 32, 512, 8
@@ -667,22 +664,14 @@
     ]
 
 
-def local_find(chunk):
-    return (chunk + 6) // 8, chunk
-
-
-def unpatch_find(chunk):
-    return 0, chunk
-
-
 def last_find(chunk):
     return (chunk + 7) // 16 + (chunk + 5) // 16, chunk
 
 
 def last_kernel(
-    n, grad_ref, parted_ref, small_ref, order_ref, values_ref, right_ref,
-    d_weight_ref, d_small_ref, d_in_ref, d_out_ref,
-    known, small_kept, small_got, g_send, g_recv, t_send, t_recv, left_ref, *scratch
+    n, grad_ref, parted_ref, small_ref, order_ref, values_ref, right_ref, direct_ref, weight_ref,
+    d_weight_ref, d_small_ref, d_in_ref, d_out_ref, input_ref,
+    back, d_patches, b_send, b_recv, known, small_kept, small_got, g_send, g_recv, t_send, t_recv, left_ref, *scratch
 ):
     here = Place(n)
     rows = grad_ref.shape[0]
@@ -728,17 +717,44 @@
         gather.wait_recv()
         told.wait_recv()
         small_kept[mine] = small_kept[mine] + small_got[cut]
-    sums.run(2 * len(steps), sums.times)
-    d_small_ref[...] = small_kept[pl.ds(0, LOG_ROWS)]
+    width = weight_ref.shape[0]
+    back[...] = dot_t(known[...], weight_ref[...]).astype(BF)
+    mine = pl.ds(pl.multiple_of(here.me * width, 128), width)
+
+    def returning(place):
+        source, target = back.at[rows_of(place, 1, rows)], d_patches.at[:, mine]
+        there = here.place_there(place)
+        return remote(source, target, b_send.at[place], b_recv.at[there], here.device(place))
+
+    @pl.loop(1, n)
+    def _(place):
+        returning(place).start()
+
+    pltpu.make_async_copy(back.at[pl.ds(0, rows)], d_patches.at[:, mine], b_recv.at[0]).start()
+    sums.run(2 * len(steps), 2 * len(steps) + 1)
     d_weight_ref[...] = lax.dot_general(
         parted_ref[...], known[...], (((0,), (0,)), ((), ())), preferred_element_type=F32
     )
+    sums.run(2 * len(steps) + 1, sums.times)
+
+    @pl.loop(0, n)
+    def _(place):
+        cut = pl.ds(pl.multiple_of(here.device(place) * width, 128), width)
+        landed(d_patches.at[:, cut], b_recv.at[place])
+
+    input_ref[...] = (direct_ref[...] + d_patches[...].astype(F32)).astype(BF)
+
+    @pl.loop(1, n)
+    def _(place):
+        returning(place).wait_send()
+
+    d_small_ref[...] = small_kept[pl.ds(0, LOG_ROWS)]
     for copy in copies:
         copy.wait_send()
     sums.end()
 
 
-def last_sums(n, grad, parted, small, order, lefts, right, projections):
+def last_sums(n, grad, parted, small, order, lefts, right, direct, weight, projections):
     rows, width = grad.shape[0], parted.shape[1]
     phases, chunks = n.bit_length() - 1, right.shape[1] // SUM_COLUMNS
     return pl.pallas_call(
@@ -748,10 +764,15 @@
             jax.ShapeDtypeStruct((LOG_ROWS, 128), F32),
             jax.ShapeDtypeStruct((SUM_ROWS, projections), F32),
             jax.ShapeDtypeStruct((2 * SUM_ROWS, D), F32),
+            jax.ShapeDtypeStruct(direct.shape, BF),
         ],
-        in_specs=[pl.BlockSpec(memory_space=pltpu.VMEM)] * 6,
-        out_specs=[pl.BlockSpec(memory_space=pltpu.VMEM)] * 4,
+        in_specs=[pl.BlockSpec(memory_space=pltpu.VMEM)] * 8,
+        out_specs=[pl.BlockSpec(memory_space=pltpu.VMEM)] * 5,
         scratch_shapes=[
+            pltpu.VMEM((n * rows, width), BF),
+            pltpu.VMEM(direct.shape, BF),
+            pltpu.SemaphoreType.DMA((n,)),
+            pltpu.SemaphoreType.DMA((n,)),
             pltpu.VMEM((n * rows, D), BF),
             pltpu.VMEM(small.shape, F32),
             pltpu.VMEM(small.shape, F32),
@@ -763,7 +784,7 @@
             collective_id=1, has_side_effects=True, vmem_limit_bytes=62 * 2**20
         ),
         cost_estimate=pl.CostEstimate(flops=2**32, bytes_accessed=2**24, transcendentals=0),
-    )(grad, parted, small, order, lefts, right)
+    )(grad, parted, small, order, lefts, right, direct, weight)
 
 
 LOG_ROWS = 8
@@ -920,9 +941,9 @@
 
 
 def mixer_back_kernel(
-    n, logs_ref, order_ref, values_ref, right_ref, hidden_ref, slots_ref,
+    n, logs_ref, order_ref, mixed_ref, normed_ref, out_right_ref, qkv_right_ref, hidden_ref, slots_ref,
     dy_ref, x_ref, keys_ref, queries_ref, state_ref, steps_ref, marks_ref, head_ref,
-    dx_ref, dkeys_ref, dqueries_ref, d_dt_ref, d_head_ref, sum_ref, unpatch_ref,
+    dx_ref, d_dt_ref, d_head_ref, d_out_ref, d_qkv_ref, unpatch_ref, dkeys_ref, dqueries_ref,
     scores, d_scores, d_step, d_cum, d_turned, grads, back, left_ref, hidden_left, *scratch
 ):
     rows, width = x_ref.shape[0], 2 * MHEAD_DIM
@@ -930,22 +951,25 @@
     exchange = Exchange(n, True, grads, logs_ref, back, *scratch[:9])
 
     def store(chunk, total):
-        @pl.when(chunk < 16)
-        def _():
-            unpatch_ref[:, columns_of(chunk)] = total
-
-        @pl.when(chunk >= 16)
-        def _():
-            sum_ref[:, columns_of(chunk - 16)] = total
+        for (first, stop, *_), target in zip(sources, (unpatch_ref, d_out_ref, d_qkv_ref)):
+
+            @pl.when((chunk >= first) & (chunk < stop))
+            def _():
+                target[:, columns_of(chunk - first)] = total
+
+    def find(which):
+        return lambda chunk: (which, chunk)
 
     sources = [
-        (0, 16, unpatch_find, hidden_left, slots_ref),
-        (16, 24, local_find, left_ref, right_ref),
+        (0, 16, find(0), hidden_left, slots_ref),
+        (16, 18, find(0), left_ref, out_right_ref),
+        (18, 24, find(1), left_ref, qkv_right_ref),
     ]
     sums = Sums(Place(n), sources, store, *scratch[9:])
     exchange.tell()
     turn(order_ref, hidden_left, hidden_ref)
-    turn(order_ref, left_ref, values_ref)
+    left_ref[0] = dot_t(order_ref[...], mixed_ref[...]).astype(BF)
+    left_ref[1] = dot_t(order_ref[...], normed_ref[...]).astype(BF)
 
     head_lane = lax.broadcasted_iota(jnp.int32, (1, MHEADS), 1)
     lanes = lax.broadcasted_iota(jnp.int32, (1, width), 1)
@@ -1050,40 +1074,47 @@
     d_dt_ref[...] = d_raw
     d_head_ref[0:1] = jnp.sum(d_raw, axis=0, keepdims=True)
     d_head_ref[1:2] = -rate * jnp.sum(step * d_logs, axis=0, keepdims=True)
+    dx_ref[:, pl.ds(DI, NSTATE)] = dkeys_ref[...]
+    dx_ref[:, pl.ds(DI + NSTATE, NSTATE)] = dqueries_ref[...]
     sums.run(31, sums.times)
     sums.end()
     exchange.end()
 
 
-def mixer_back(n, logs, order, values, right, hidden, slots, dy, conv_out, state_in, dt_raw, head_params, starts):
-    rows = conv_out.shape[0]
-    x, keys, queries, step, cum, segment = block_parts(conv_out, dt_raw, head_params, starts)
+def mixer_tables(dt_raw, head_params, starts):
+    rows = dt_raw.shape[0]
+    step = jax.nn.softplus(dt_raw + head_params[0])
+    cum = jnp.cumsum(-step * jnp.exp(head_params[1]), axis=0)
+    segment = jnp.cumsum(starts, axis=0, dtype=jnp.int32)
     slope = jax.nn.sigmoid(dt_raw + head_params[0])
     square = [jnp.pad(v, ((0, 128 - v.shape[0]), (0, 128 - v.shape[1]))) for v in (step.T, cum.T)]
     tall = [jnp.pad(v, ((0, 128 - rows), (0, 128 - MHEADS))) for v in (step, cum, slope)]
-    steps = jnp.stack(tall + square)
     position = jnp.arange(rows)
     reach = (position[:, None] >= position[None, :]) & (segment[:, None] == segment[None, :])
     ends = jnp.stack([segment == 0, segment == segment[-1]], axis=1)
-    marks = jnp.stack(
-        [jnp.pad(v.astype(F32), ((0, 0), (0, 128 - v.shape[1]))) for v in (reach, ends)]
-    )
+    marks = [jnp.pad(v.astype(F32), ((0, 0), (0, 128 - v.shape[1]))) for v in (reach, ends)]
+    return jnp.stack(tall + square), jnp.stack(marks)
+
+
+def mixer_back(told, order, values, rights, hidden, slots, dy, conv_out, state_in, steps, marks, head_params):
+    n, rows = lax.axis_size("seq"), conv_out.shape[0]
+    x, keys, queries = jnp.split(conv_out, [DI, DI + NSTATE], axis=1)
     total = MHEADS * MHEAD_DIM
-    narrow = jax.ShapeDtypeStruct((rows, NSTATE), F32)
+    wide = sum(right.shape[1] for right in rights)
     return pl.pallas_call(
         functools.partial(mixer_back_kernel, n),
         out_shape=[
-            jax.ShapeDtypeStruct((rows, DI), F32),
-            narrow,
-            narrow,
+            jax.ShapeDtypeStruct((rows, CONV_CH), F32),
             jax.ShapeDtypeStruct((rows, MHEADS), F32),
             jax.ShapeDtypeStruct((8, MHEADS), F32),
-            jax.ShapeDtypeStruct((SUM_ROWS, right.shape[1]), F32),
-            jax.ShapeDtypeStruct((SUM_ROWS, slots.shape[1]), F32),
-        ],
-        in_specs=[pl.BlockSpec(memory_space=pltpu.VMEM)] * 14,
-        out_specs=[pl.BlockSpec(memory_space=pltpu.VMEM)] * 7,
+        ]
+        + [jax.ShapeDtypeStruct((SUM_ROWS, right.shape[1]), F32) for right in rights]
+        + [jax.ShapeDtypeStruct((SUM_ROWS, slots.shape[1]), F32)],
+        in_specs=[pl.BlockSpec(memory_space=pltpu.VMEM)] * 16,
+        out_specs=[pl.BlockSpec(memory_space=pltpu.VMEM)] * 6,
         scratch_shapes=[
+            pltpu.VMEM((rows, NSTATE), F32),
+            pltpu.VMEM((rows, NSTATE), F32),
             pltpu.VMEM((rows, rows), F32),
             pltpu.VMEM((rows, rows), F32),
             pltpu.VMEM((rows, MHEADS), F32),
@@ -1092,7 +1123,7 @@
             pltpu.VMEM((total, NSTATE), BF),
             pltpu.VMEM((total, NSTATE), BF),
         ]
-        + lefts_scratch(n, values)
+        + [pltpu.VMEM((2, n * SUM_ROWS, values[0].shape[0]), BF)]
         + lefts_scratch(n, hidden)
         + exchange_scratch(n)
         + sums_scratch(n, 24),
@@ -1101,7 +1132,7 @@
         ),
         cost_estimate=pl.CostEstimate(flops=2**32, bytes_accessed=2**24, transcendentals=2**20),
     )(
-        told_logs(logs), order, values, right, hidden, slots, dy, conv_out[:, :DI], keys, queries,
+        told, order, *values, *rights, hidden, slots, dy, x, keys, queries,
         state_in, steps, marks, head_params,
     )
 
@@ -1109,26 +1140,10 @@
 FF_TILE = D
 
 
-def feed_forward_kernel(
-    stream_ref, normed_ref, gate_w_ref, up_w_ref, down_ref, out_ref, gate_ref, up_ref, hid_ref, total
-):
-    step = pl.program_id(0)
+def feed_forward_kernel(normed_ref, gate_w_ref, up_w_ref, gate_ref, up_ref, hid_ref):
     gate, up = dot(normed_ref[...], whole_of(gate_w_ref)), dot(normed_ref[...], whole_of(up_w_ref))
-    hid = (silu(gate) * up).astype(BF)
-    gate_ref[...], up_ref[...], hid_ref[...] = gate.astype(BF), up.astype(BF), hid
-    found = dot(hid, down_ref[...])
-
-    @pl.when(step == 0)
-    def _():
-        total[...] = stream_ref[...] + found
-
-    @pl.when(step > 0)
-    def _():
-        total[...] += found
-
-    @pl.when(step == pl.num_programs(0) - 1)
-    def _():
-        out_ref[...] = total[...].astype(BF)
+    gate_ref[...], up_ref[...] = gate.astype(BF), up.astype(BF)
+    hid_ref[...] = (silu(gate) * up).astype(BF)
 
 
 def feed_forward_blocks(n):
@@ -1140,34 +1155,37 @@
     ]
 
 
-def feed_forward(stream, normed, flat, down):
-    rows, tiles = stream.shape[0], FF // FF_TILE
-    wide = pl.BlockSpec((rows, D), lambda i: (0, 0))
+def feed_forward(normed, flat):
+    rows = normed.shape[0]
     tile = pl.BlockSpec((rows, FF_TILE), lambda i: (0, i))
     return pl.pallas_call(
         feed_forward_kernel,
-        grid=(tiles,),
-        out_shape=[jax.ShapeDtypeStruct((rows, D), BF)]
-        + [jax.ShapeDtypeStruct((rows, FF), BF)] * 3,
-        in_specs=[
-            wide,
-            wide,
-            *feed_forward_blocks(flat.shape[0]),
-        ],
-        out_specs=[wide, tile, tile, tile],
-        scratch_shapes=[pltpu.VMEM((rows, D), F32)],
-        compiler_params=pltpu.CompilerParams(vmem_limit_bytes=52 * 2**20),
+        grid=(FF // FF_TILE,),
+        out_shape=[jax.ShapeDtypeStruct((rows, FF), BF)] * 3,
+        in_specs=[pl.BlockSpec((rows, D), lambda i: (0, 0)), *feed_forward_blocks(flat.shape[0])[:2]],
+        out_specs=[tile, tile, tile],
+        compiler_params=pltpu.CompilerParams(vmem_limit_bytes=56 * 2**20),
         cost_estimate=pl.CostEstimate(
-            flops=6 * rows * D * FF, bytes_accessed=2**25, transcendentals=rows * FF
+            flops=4 * rows * D * FF, bytes_accessed=2**25, transcendentals=rows * FF
         ),
-    )(stream, normed, flat, flat, down)
+    )(normed, flat, flat)
 
 
 def feed_forward_back_kernel(
-    grad_ref, stream_ref, gain_ref, gate_ref, up_ref, gate_w_ref, up_w_ref, down_ref,
-    both_ref, d_stream_ref, d_low_ref, d_gain_ref, total,
+    grad_ref, stream_ref, gain_ref, gate_ref, up_ref, hid_ref, gate_w_ref, up_w_ref, down_ref,
+    out_ref, both_ref, d_stream_ref, d_low_ref, d_gain_ref, layer, total,
 ):
     step = pl.program_id(0)
+    added = dot(hid_ref[...], down_ref[...])
+
+    @pl.when(step == 0)
+    def _():
+        layer[...] = stream_ref[...] + added
+
+    @pl.when(step > 0)
+    def _():
+        layer[...] += added
+
     d_hid = dot_t(grad_ref[...], down_ref[...])
     gate, up = gate_ref[...].astype(F32), up_ref[...].astype(F32)
     s = jax.nn.sigmoid(gate)
@@ -1186,6 +1204,7 @@
 
     @pl.when(step == pl.num_programs(0) - 1)
     def _():
+        out_ref[...] = layer[...].astype(BF)
         stream, d_normed = stream_ref[...], total[...]
         r = lax.rsqrt(jnp.mean(stream * stream, axis=-1, keepdims=True) + EPS)
         scaled = gain_ref[...] * d_normed
@@ -1196,15 +1215,16 @@
         d_gain_ref[...] = jnp.sum(stream * r * d_normed, axis=0, keepdims=True)
 
 
-def feed_forward_back(grad, stream, gain, gate, up, flat, down):
+def feed_forward_back(grad, stream, gain, gate, up, hid, flat, down):
     rows, tiles = stream.shape[0], FF // FF_TILE
     wide = pl.BlockSpec((rows, D), lambda i: (0, 0))
     tile = pl.BlockSpec((rows, FF_TILE), lambda i: (0, i))
     narrow = pl.BlockSpec((1, D), lambda i: (0, 0))
-    both, d_stream, d_low, d_gain = pl.pallas_call(
+    out, both, d_stream, d_low, d_gain = pl.pallas_call(
         feed_forward_back_kernel,
         grid=(tiles,),
         out_shape=[
+            jax.ShapeDtypeStruct((rows, D), BF),
             jax.ShapeDtypeStruct((2, rows, FF), BF),
             jax.ShapeDtypeStruct((rows, D), F32),
             jax.ShapeDtypeStruct((rows, D), BF),
@@ -1216,16 +1236,17 @@
             narrow,
             tile,
             tile,
+            tile,
             *feed_forward_blocks(flat.shape[0]),
         ],
-        out_specs=[pl.BlockSpec((2, rows, FF_TILE), lambda i: (0, 0, i)), wide, wide, narrow],
-        scratch_shapes=[pltpu.VMEM((rows, D), F32)],
-        compiler_params=pltpu.CompilerParams(vmem_limit_bytes=56 * 2**20),
+        out_specs=[wide, pl.BlockSpec((2, rows, FF_TILE), lambda i: (0, 0, i)), wide, wide, narrow],
+        scratch_shapes=[pltpu.VMEM((rows, D), F32)] * 2,
+        compiler_params=pltpu.CompilerParams(vmem_limit_bytes=60 * 2**20),
         cost_estimate=pl.CostEstimate(
-            flops=6 * rows * D * FF, bytes_accessed=2**25, transcendentals=rows * FF
+            flops=8 * rows * D * FF, bytes_accessed=2**25, transcendentals=rows * FF
         ),
-    )(grad, stream, gain[None], gate, up, flat, flat, down)
-    return both, d_stream, d_low, d_gain[0]
+    )(grad, stream, gain[None], gate, up, hid, flat, flat, down)
+    return out, both, d_stream, d_low, d_gain[0]
 
 
 ATTN_ROWS = 128
@@ -1284,7 +1305,10 @@
     )(triple)
 
 
-def attention_back_kernel(triple_ref, grad_ref, out_ref):
+def attention_back_kernel(
+    triple_ref, low_ref, d_stream_ref, stream_ref, gain_ref, out_w_ref, q_ref, k_ref, v_ref,
+    out_ref, d_out_ref, d_gain_ref,
+):
     mask = tile_mask()
     width = 2 * AHEAD_DIM
     scale = AHEAD_DIM ** (-0.5)
@@ -1293,12 +1317,13 @@
         found = lax.dot_general(left, right, (((0,), (0,)), ((), ())), preferred_element_type=F32)
         return jnp.where(first_head(), found[:ATTN_ROWS], found[ATTN_ROWS:])
 
+    grads = dot_t(low_ref[...], whole_of(out_w_ref)).astype(BF)
     for pair in range(AHEADS // 2):
         lo, hi = pair * width, (pair + 1) * width
         queries, key_rows, value_rows = [
             triple_ref[:, part * D + lo : part * D + hi] for part in range(3)
         ]
-        grad = grad_ref[:, lo:hi]
+        grad = grads[:, lo:hi]
         key_rows = one_below_other(key_rows)
         probs = pair_probs(queries, key_rows, mask)
         d_probs = dot_t(grad, one_below_other(value_rows))
@@ -1307,19 +1332,52 @@
         out_ref[:, D + lo : D + hi] = (scale * of_keys(d_scores, queries)).astype(BF)
         out_ref[:, 2 * D + lo : 2 * D + hi] = of_keys(probs.astype(BF), grad).astype(BF)
 
-
-def attention_back(triple, grad):
-    rows = triple.shape[0]
-    return pl.pallas_call(
+    d_normed = None
+    for part, ref in enumerate((q_ref, k_ref, v_ref)):
+        found = dot_t(out_ref[:, part * D : (part + 1) * D], whole_of(ref))
+        d_normed = found if part == 0 else d_normed + found
+    stream = stream_ref[...]
+    r = lax.rsqrt(jnp.mean(stream * stream, axis=-1, keepdims=True) + EPS)
+    scaled = gain_ref[...] * d_normed
+    inner = jnp.mean(stream * scaled, axis=-1, keepdims=True)
+    d_out_ref[...] = d_stream_ref[...] + r * scaled - stream * (r * r * r) * inner
+    gained = jnp.sum(stream * r * d_normed, axis=0, keepdims=True)
+
+    @pl.when(pl.program_id(0) == 0)
+    def _():
+        d_gain_ref[...] = gained
+
+    @pl.when(pl.program_id(0) > 0)
+    def _():
+        d_gain_ref[...] += gained
+
+
+def attention_back(triple, low, d_stream, stream, gain, flat):
+    rows, n = triple.shape[0], flat.shape[0]
+    wide = pl.BlockSpec((ATTN_ROWS, 3 * D), lambda i: (i, 0))
+    tile = pl.BlockSpec((ATTN_ROWS, D), lambda i: (i, 0))
+    narrow = pl.BlockSpec((1, D), lambda i: (0, 0))
+
+    def block(place):
+        return flat_block(n, D // n, lambda i: place)
+
+    d_triple, d_out, d_gain = pl.pallas_call(
         attention_back_kernel,
         grid=(rows // ATTN_ROWS,),
-        out_shape=jax.ShapeDtypeStruct((rows, 3 * D), BF),
-        in_specs=[
-            pl.BlockSpec((ATTN_ROWS, 3 * D), lambda i: (i, 0)),
-            pl.BlockSpec((ATTN_ROWS, D), lambda i: (i, 0)),
+        out_shape=[
+            jax.ShapeDtypeStruct((rows, 3 * D), BF),
+            jax.ShapeDtypeStruct((rows, D), F32),
+            jax.ShapeDtypeStruct((1, D), F32),
         ],
-        out_specs=pl.BlockSpec((ATTN_ROWS, 3 * D), lambda i: (i, 0)),
-    )(triple, grad)
+        in_specs=[wide, tile, tile, tile, narrow]
+        + [block(PATCH + 3), block(PATCH), block(PATCH + 1), block(PATCH + 2)],
+        out_specs=[wide, tile, narrow],
+        compiler_params=pltpu.CompilerParams(vmem_limit_bytes=56 * 2**20),
+        cost_estimate=pl.CostEstimate(
+            flops=8 * rows * D * D, bytes_accessed=2**24, transcendentals=0
+        ),
+    )(triple, low, d_stream, stream, gain[None], flat, flat, flat, flat)
+    return d_triple, d_out, d_gain[0]
 
 
 def local(
@@ -1362,16 +1420,16 @@
     cuts = list(np.cumsum([piece.shape[0] for piece in small]))
     small_shard = jnp.concatenate(small)
     small_shard = jnp.pad(small_shard, (0, -small_shard.shape[0] % 2048)).reshape(-1, 128)
-    live.patch_w, live.mixer_in, live.mixer_out, small_all, embedded, live.parted = gather_weights(
+    live.mixer_in, live.mixer_out, small_all, live.embedded, live.parted = gather_weights(
         n,
         [
-            patch_weight,
             jnp.pad(mixer_in, ((0, 0), (0, -mixer_in.shape[1] % 128))),
             mixer_out,
             small_shard,
         ],
-        [(32, D), (16, 2304), (32, D), (16, 128)],
+        [(16, 2304), (32, D), (16, 128)],
         patches,
+        patch_weight,
     )
     small_all = small_all.reshape(n, -1)[:, : cuts[-1]].astype(F32)
     parts = jnp.split(small_all, cuts[:-1], axis=1)
@@ -1380,7 +1438,6 @@
     live.conv_bias, live.mixer_gain, live.attn_gain, live.ffn_gain = [
         piece.reshape(-1) for piece in parts[2:]
     ]
-    live.embedded = embedded
     live.normed = rms_scale(live.embedded, live.patch_gain).astype(BF)
     projected = dot(live.normed, live.mixer_in)
     live.gate_z = projected[:, :DI]
@@ -1434,12 +1491,10 @@
     live.mixed = attention(live.triple)
     live.stream1 = live.stream0 + flat_dot(live.mixed, live.early, PATCH + 3, 1, F32)
     live.normed1 = rms_scale(live.stream1, live.ffn_gain).astype(BF)
-    live.late = late
-    layer_out, gate, up, hid = feed_forward(live.stream1, live.normed1, live.early, live.late)
-    live.gate, live.up, live.hid = gate, up, hid
-    live.fence()
-
+    live.gate, live.up, live.hid = feed_forward(live.normed1, live.early)
     small_slice = n == 32
+    if small_slice:
+        live.flat = down_grad(n, live.hid, out_grad)
 
     def lefts_of(*values):
         parts = []
@@ -1452,13 +1507,17 @@
         place = jnp.arange(n * SUM_ROWS)
         source = jnp.repeat(order * SUM_ROWS, SUM_ROWS) + place % SUM_ROWS
         live.order = (place[None, :] == source[:, None]).astype(BF)
-
-    d_both, d_stream1, d_stream1_low, g_ffn_gain = feed_forward_back(
-        out_grad, live.stream1, live.ffn_gain, live.gate, live.up, live.early, live.late
+        live.last_lefts = lefts_of(live.normed, live.gated_norm)
+        live.steps, live.marks = mixer_tables(dt_raw, head_params, resets)
+        live.told = told_logs(live.logs)
+    live.fence()
+
+    layer_out, d_both, d_stream1, d_stream1_low, g_ffn_gain = feed_forward_back(
+        out_grad, live.stream1, live.ffn_gain, live.gate, live.up, live.hid, live.early, late
     )
     if small_slice:
         block = down_weight.shape[0]
-        flat = flat_grads(n, live.hid, out_grad, live.normed1, d_both)
+        flat = gate_up_grad(live.normed1, d_both, live.flat)
         found = lax.psum_scatter(flat, "seq", scatter_dimension=0, tiled=True)[0].astype(F32)
         g_down = found[:block]
         g_gate_up = found[block:].reshape(-1, SUM_ROWS, D).transpose(1, 0, 2)
@@ -1466,33 +1525,32 @@
     else:
         g_down = summed_grad(live.hid, out_grad)
         g_gate_up = summed_grad(live.normed1, jnp.concatenate([d_both[0], d_both[1]], axis=1))
-    d_mixed = flat_dot_t(d_stream1_low, live.early, PATCH + 3, 1).astype(BF)
-    d_triple = attention_back(live.triple, d_mixed)
-    d_stream0, g_attn_gain = rms_back(live.stream0, live.attn_gain, flat_dot_t(d_triple, live.early, PATCH, 3))
-    live.d_stream0 = (d_stream1 + d_stream0).reshape(patch_rows, PATCH * D)
+    d_triple, d_stream0, g_attn_gain = attention_back(
+        live.triple, d_stream1_low, d_stream1, live.stream0, live.attn_gain, live.early
+    )
+    live.d_stream0 = d_stream0.reshape(patch_rows, PATCH * D)
+
     d_slots = live.d_stream0.astype(BF)
     d_hidden = flat_dot_t(d_slots, live.early, 0, PATCH)
     d_branch = d_hidden.astype(BF)
     d_gated, g_mixer_gain = rms_back(gated, live.mixer_gain, dot_t(d_branch, live.mixer_out))
     d_gate_z = d_gated * mixer_y * silu_slope(live.gate_z)
     if small_slice:
-        dx, dkeys, dqueries, d_dt, g_head, found, g_unpatch = mixer_back(
-            n,
-            live.logs,
+        d_conv_out, d_dt, g_head, g_attn_out, g_qkv, g_unpatch = mixer_back(
+            live.told,
             live.order,
-            jnp.stack([live.mixed, live.normed0]),
-            jnp.concatenate([d_stream1_low, d_triple], axis=1),
+            [live.mixed, live.normed0],
+            [d_stream1_low, d_triple],
             live.hidden[None],
             d_slots,
             d_gated * gate_act,
             conv_out,
             live.state_in,
-            dt_raw,
+            live.steps,
+            live.marks,
             head_params,
-            resets,
         )
-        g_attn_out, g_qkv = found[:, :D], found[:, D:]
-        conv_cot = conv_back(jnp.concatenate([dx, dkeys, dqueries], axis=1))
+        conv_cot = conv_back(d_conv_out)
         g_head = g_head[:3]
     else:
         output_grads = output_back(d_gated * gate_act)
@@ -1513,7 +1571,6 @@
         live.embedded, live.patch_gain, dot_t(d_projected, live.mixer_in)
     )
     d_embedded = (d_hidden + d_embedded).astype(BF)
-    input_grad = input_gradient(live.d_stream0, d_embedded, live.patch_w).reshape(-1, D)
 
     g_conv_weight = conv_cot[1].reshape(CONV, n, -1).transpose(1, 0, 2).reshape(n, -1)
     g_head = jnp.broadcast_to(g_head.reshape(1, -1), (n, 3 * MHEADS))
@@ -1524,14 +1581,16 @@
     g_small = g_small.reshape(n * LOG_ROWS, 128)
     if small_slice:
         d_projected = jnp.pad(d_projected, ((0, 0), (0, -d_projected.shape[1] % SUM_COLUMNS)))
-        g_patch, g_small, g_mixer_in, g_mixer_out = last_sums(
+        g_patch, g_small, g_mixer_in, g_mixer_out, input_grad = last_sums(
             n,
             d_embedded,
             live.parted,
             g_small,
             live.order,
-            lefts_of(live.normed, live.gated_norm),
+            live.last_lefts,
             jnp.concatenate([d_projected, d_branch, d_branch], axis=1),
+            live.d_stream0,
+            patch_weight,
             mixer_in.shape[1],
         )
     else:
@@ -1539,6 +1598,10 @@
         g_qkv = summed_grad(live.normed0, d_triple)
         known = lax.all_gather(d_embedded, "seq", axis=0, tiled=True)
         g_patch = dot(live.parted.T, known)
+        d_parted = dot_t(known, patch_weight).astype(BF).reshape(n, patch_rows, -1)
+        d_parted = lax.all_to_all(d_parted, "seq", 0, 0, tiled=True)
+        d_parted = d_parted.transpose(1, 0, 2).reshape(patch_rows, -1).astype(F32)
+        input_grad = (live.d_stream0 + d_parted).astype(BF)
         g_small = lax.psum_scatter(g_small, "seq", scatter_dimension=0, tiled=True)
         g_unpatch = summed_grad(live.hidden, d_slots)
         g_mixer_in = summed_grad(live.normed, d_projected)[:, : mixer_in.shape[1]]
@@ -1547,7 +1610,7 @@
     s = jnp.split(g_small, cuts)
     return (
         layer_out,
-        input_grad,
+        input_grad.reshape(-1, D),
         g_patch,
         s[0],
         g_mixer_in,

time: 971 us -> 936 us (0.964)
  waiting for transfers between devices: 28.9 us -> 6.98 us
  other arithmetic: 41 us -> 25.7 us
  Pallas kernels: 798 us -> 812 us
    pallas_call x4, Pallas kernels: 324 us -> 292 us  [the longest x1 251 us: gather_weights(): pl.pallas_call(functools.partial(gather_kernel, n, chunks), out_shape=[ja...]
    pallas_call x1, Pallas kernels: 111 us -> 140 us  [last_sums(): pl.pallas_call(functools.partial(last_kernel, n), out_shape=[jax.ShapeDty...]
    all_gather x1, waiting for transfers between devices: 28.1 us -> 6.24 us  [local(): late = lax.all_gather(down_weight, 'seq', axis=0, tiled=True)]
    pallas_call x1, Pallas kernels: 18.2 us -> 32.1 us  [attention_back(): pl.pallas_call(attention_back_kernel, grid=(rows // ATTN_ROWS,), out_shap...]
    pallas_call x1, Pallas kernels: 203 us -> 216 us  [mixer_back(): pl.pallas_call(functools.partial(mixer_back_kernel, n), out_shape=[jax.Sh...]
    pallas_call x3 -> x1, Pallas kernels: 26 us -> 14 us  [flat_dot_t(): pl.pallas_call(flat_dot_t_kernel, grid=(count,), out_shape=jax.ShapeDtype...]
  transfers between devices with their start and end apart: 5 -> 5, of which waited for: 1 -> 1; matrix products, arithmetic and copies ran while one was open for 10% -> 8% of each run, Pallas kernels for 76% -> 82%
where the time goes in v5:
time: 936 us; the launch traced here: 928 us
  Pallas kernels  812 us (87%)
  local copies, waits for them, and re-layouts  41.4 us (4%)
  other arithmetic  25.7 us (3%)
  matrix products  22.1 us (2%)
  between operations  16.1 us (2%)
    pallas_call x1, Pallas kernels, gather_weights(): pl.pallas_call(functools.partial(gather_kernel, n, chunks), out_shape=[ja...  251 us
    pallas_call x1, Pallas kernels, mixer_back(): pl.pallas_call(functools.partial(mixer_back_kernel, n), out_shape=[jax.Sh...  216 us
    pallas_call x1, Pallas kernels, last_sums(): pl.pallas_call(functools.partial(last_kernel, n), out_shape=[jax.ShapeDty...  140 us
    pallas_call x1, Pallas kernels, pass_states(): pl.pallas_call(functools.partial(states_kernel, n, reverse), out_shape=ja...  54.8 us
    pallas_call x1, Pallas kernels, attention_back(): pl.pallas_call(attention_back_kernel, grid=(rows // ATTN_ROWS,), out_shap...  32.1 us
    pallas_call x1, Pallas kernels, feed_forward_back(): pl.pallas_call(feed_forward_back_kernel, grid=(tiles,), out_shape=[jax.Sh...  31 us
    pallas_call x3, Pallas kernels, flat_dot(): pl.pallas_call(flat_dot_kernel, grid=(count,), out_shape=jax.ShapeDtypeSt...  22.8 us
  transfers between devices with their start and end apart: 5, of which 1 were waited for; matrix products, arithmetic and copies ran while one was open for 8% of the time, Pallas kernels for 82%

profile of v5, /device:TPU:0, one launch (start us, length us, event | category | flops | bytes accessed | tf_op | source)
XLA Modules:
  0.0 927.5 jit_solution(16124354696036889254)
XLA Ops:
  7.3 2.6 shard_map.316
  11.6 251.3 %shard_map.314 = (bf16[1024,4480]{1,0:T(8,128)(2,1)S(1)}, bf16[2048,1024]{1,0:T(8,128)(2,1)S(1)}, bf16[512,128]{1,0:T(8,128)(2,1)S(1)}, f32[64,1024]{1,0:T(8,128)S(1)}, bf16[2048,256]{1,0:T(8,128)(2,1)S(1)}) custom-call(bf16[32,4480]{1,0:T(8,128)(2,1)S(1)} %pad.81.refs_0_, bf16[64,1024]{1,0:T(8,128)(2,1)S(1)} %copy-done.7, ...), custom_call_target="tpu_custom_call" | custom-call | bytes 33554432 | tf_op jit(solution)/shard_map/pallas_call | solution.py:535
  262.9 3.6 copy-done
  266.5 2.1 copy-done.1
  270.6 5.3 fusion.63
  276.1 2.3 collective-permute-start
  285.1 1.8 fusion.order_ref
  288.0 1.3 fusion.25
  290.7 54.8 %shard_map.315.state_ref = bf16[2048,128]{1,0:T(8,128)(2,1)S(1)} custom-call(bf16[2048,128]{1,0:T(8,128)(2,1)S(1)} %bitcast.81, f32[8,128]{1,0:T(8,128)S(1)} %scatter.6.logs_ref), custom_call_target="tpu_custom_call" | custom-call | flops 4194304 | bytes 2097152 | tf_op jit(solution)/shard_map/pallas_call | solution.py:907
  346.9 3.1 fusion.3
  350.0 1.5 copy.137
  352.8 3.7 fusion.4.values_ref
  356.5 10.6 %shard_map.317 = f32[64,8192]{1,0:T(8,128)} custom-call(bf16[64,1024]{1,0:T(8,128)(2,1)} %fusion.4.values_ref, bf16[32,640,1024]{2,1,0:T(8,128)(2,1)} %bitcast.82), custom_call_target="tpu_custom_call" | custom-call | flops 1073741824 | bytes 16777216 | tf_op jit(solution)/shard_map/pallas_call | solution.py:106
  367.1 2.9 reshape.478
  370.0 1.9 multiply_reduce_fusion.1
  371.9 1.4 multiply_convert_fusion.1.values_ref.normed_ref
  373.4 7.6 shard_map.318.triple_ref
  380.9 6.6 shard_map.319.values_ref.mixed_ref
  388.6 4.5 shard_map.320
  394.0 1.9 multiply_reduce_fusion
  395.9 1.3 copy-done.10
  397.2 1.2 multiply_convert_fusion.normed_ref
  398.4 15.3 %shard_map.321 = (bf16[512,4096]{1,0:T(8,128)(2,1)}, bf16[512,4096]{1,0:T(8,128)(2,1)}, bf16[512,4096]{1,0:T(8,128)(2,1)}) custom-call(bf16[512,1024]{1,0:T(8,128)(2,1)} %multiply_convert_fusion.normed_ref, bf16[32,640,1024]{2,1,0:T(8,128)(2,1)} %bitcast.85, bf16[32,640,1024]{2,1,0:T(8,128)(2,1)} %bitcast.86), custom_call_target="tpu_custom_call" | custom-call | flops 8589934592 | bytes 33554432 | tf_op jit(solution)/shard_map/pallas_call | solution.py:1161
  413.7 8.8 shard_map.322.flat_ref
  422.5 6.2 all-gather.4.cloned.1.call-done.down_ref
  428.8 31.0 %shard_map.323 = (bf16[512,1024]{1,0:T(8,128)(2,1)}, bf16[2,512,4096]{2,1,0:T(8,128)(2,1)}, f32[512,1024]{1,0:T(8,128)}, bf16[512,1024]{1,0:T(8,128)(2,1)}, f32[1,1024]{1,0:T(1,128)}) custom-call(bf16[512,1024]{1,0:T(8,128)(2,1)} %grad_ref.3, f32[512,1024]{1,0:T(8,128)} %copy-done.10, f32[1,1024]{1,0:T(1,128)} %bitcast.108, ...), custom_call_target="tpu_custom_call" | custom-call | flops 17179869184 | bytes 33554432 | tf_op jit(solution)/shard_map/pallas_call | solution.py:1223
  459.8 16.5 %shard_map.328 = bf16[32,384,1024]{2,1,0:T(8,128)(2,1)} custom-call(bf16[512,1024]{1,0:T(8,128)(2,1)} %multiply_convert_fusion.normed_ref, bf16[2,512,4096]{2,1,0:T(8,128)(2,1)} %get-tuple-element.205.both_ref, bf16[32,384,1024]{2,1,0:T(8,128)(2,1)} %shard_map.322.flat_ref), custom_call_target="tpu_custom_call", output_to_operand_aliasing={{}: (2, {})} | custom-call | flops 8589934592 | bytes 33554432 | tf_op jit(solution)/shard_map/pallas_call | solution.py:214
  476.3 1.4 fusion.60
  477.7 32.1 %shard_map.324 = (bf16[512,3072]{1,0:T(8,128)(2,1)}, f32[512,1024]{1,0:T(8,128)}, f32[1,1024]{1,0:T(1,128)}) custom-call(bf16[512,3072]{1,0:T(8,128)(2,1)} %shard_map.318.triple_ref, bf16[512,1024]{1,0:T(8,128)(2,1)} %get-tuple-element.169.low_ref.out_right_ref, f32[512,1024]{1,0:T(8,128)} %get-tuple-element.170.d_stream_ref, f32[512,1024]{1,0:T(8,128)} %copy-done.9, ...), custom_call_target="tpu_custom_call" | custom-call | flops 4294967296 | bytes 16777216 | tf_op jit(solution)/shard_map/pallas_call | solution.py:1364
  509.8 2.0 reshape.483.direct_ref
  511.8 1.2 convert_element_type.127.values_ref.slots_ref
  513.0 14.0 %shard_map.325 = f32[64,1024]{1,0:T(8,128)} custom-call(bf16[64,8192]{1,0:T(8,128)(2,1)} %convert_element_type.127.values_ref.slots_ref, bf16[32,640,1024]{2,1,0:T(8,128)(2,1)} %bitcast.93), custom_call_target="tpu_custom_call" | custom-call | flops 1073741824 | bytes 16777216 | tf_op jit(solution)/shard_map/pallas_call | solution.py:145
  527.1 1.0 convert_element_type.128
  528.1 1.5 multiply_reduce_fusion.6
  529.7 1.2 multiply_convert_fusion.2
  530.9 215.9 %shard_map.326 = (f32[64,2304]{1,0:T(8,128)}, f32[64,32]{1,0:T(8,128)}, f32[8,32]{1,0:T(8,128)}, f32[32,1024]{1,0:T(8,128)}, f32[32,3072]{1,0:T(8,128)}, /*index=5*/f32[32,8192]{1,0:T(8,128)}) custom-call(f32[8,128]{1,0:T(8,128)} %scatter.9.logs_ref, bf16[1024,1024]{1,0:T(8,128)(2,1)} %fusion.order_ref, bf16[512,1024]{1,0:T(8,128)(2,1)} %shard_map.319.values_ref.mixed_ref, ...), custom_call_target="tpu_custom_call" | custom-call | flops 4294967296 | bytes 16777216 | tf_op jit(solution)/shard_map/pallas_call | solution.py:1104
  746.8 1.9 fusion.56
  749.2 1.3 collective-permute-start.1
  753.7 6.8 multiply_reduce_fusion.9
  763.1 139.9 %shard_map.327 = (f32[256,1024]{1,0:T(8,128)}, f32[8,128]{1,0:T(8,128)}, f32[32,4384]{1,0:T(8,128)}, f32[64,1024]{1,0:T(8,128)}, bf16[64,8192]{1,0:T(8,128)(2,1)}) custom-call(bf16[64,1024]{1,0:T(8,128)(2,1)} %add_convert_fusion.grad_ref, bf16[2048,256]{1,0:T(8,128)(2,1)} %copy-done.8, f32[256,128]{1,0:T(8,128)} %reshape.493.small_ref, ...), custom_call_target="tpu_custom_call" | custom-call | flops 4294967296 | bytes 16777216 | tf_op jit(solution)/shard_map/pallas_call | solution.py:760
  903.7 1.3 split.50
  905.7 1.3 split.52
  907.0 2.3 reshape.494
  910.7 1.4 fusion.62
  912.1 1.2 slice.196
  913.3 1.1 copy.140
  915.7 1.0 copy.152
  918.2 1.0 copy.155
  (292 shorter events, 29.6 us)
Async XLA Ops:
  7.2 3.5 copy-start.67
  7.2 3.6 copy-start.22
  7.2 349.3 %all-gather.6.cloned.1.call-start = ((), (), s32[]{:S(2)}) async-start(), calls=%async_computation.3 | async-start | bytes 43253760 | tf_op jit(solution)/shard_map/all_gather | solution.py:89
  9.9 418.8 %all-gather.4.cloned.1.call-start = ((), (), s32[]{:S(2)}) async-start(), calls=%async_computation.1 | async-start | bytes 8650752 | tf_op jit(solution)/shard_map/all_gather | solution.py:1418
  10.7 901.4 %reduce-scatter.2.cloned.1.call-start = ((), (), s32[]{:S(2)}) async-start(), calls=%async_computation.2 | async-start | bytes 25952256 | tf_op jit(solution)/shard_map/reduce_scatter | solution.py:1521
  10.8 259.0 %copy-start.68 = (s32[64]{0:T(128)S(1)}, s32[64]{0:T(128)}, u32[]{:S(2)}) copy-start(s32[64]{0:T(128)} %param.24) | copy-start | bytes 772
  262.9 3.6 copy-start
  269.6 83.2 %copy-start.3 = (f32[64,1024]{1,0:T(8,128)}, f32[64,1024]{1,0:T(8,128)S(1)}, u32[]{:S(2)}) copy-start(f32[64,1024]{1,0:T(8,128)S(1)} %get-tuple-element.174) | copy-start | bytes 786436
  269.8 6.1 copy-start.47
  270.4 5.6 copy-start.63
  270.6 10.1 %copy-start.65 = (f32[3,32]{1,0:T(4,128)S(1)}, f32[3,32]{1,0:T(4,128)}, u32[]{:S(2)}) copy-start(f32[3,32]{1,0:T(4,128)} %head_ref.1) | copy-start | bytes 1156
  275.9 11.1 %copy-start.20 = (f32[64,4480]{1,0:T(8,128)}, f32[64,4480]{1,0:T(8,128)S(1)}, u32[]{:S(2)}) copy-start(f32[64,4480]{1,0:T(8,128)S(1)} %fusion.63) | copy-start | bytes 3440644
  276.0 12.0 %copy-start.14 = (f32[64,2304]{1,0:T(8,128)}, f32[64,2304]{1,0:T(8,128)S(1)}, u32[]{:S(2)}) copy-start(f32[64,2304]{1,0:T(8,128)S(1)} %fusion.36) | copy-start | bytes 1769476
  276.1 11.9 %collective-permute-start = (bf16[3,2304]{1,0:T(4,128)(2,1)S(1)}, bf16[3,2304]{1,0:T(4,128)(2,1)S(1)}, u32[]{:S(2)}, u32[]{:S(2)}) collective-permute-start(bf16[3,2304]{1,0:T(4,128)(2,1)S(1)} %fusion.39), channel_id=1, source_target_pairs={{0,1},{1,2},{2,3},{3,4},{4,5},{5,6},{6,7},{7,8},{8,9},{9,10},{10,1... | collective-permute-start | bytes 41480 | tf_op jit(solution)/shard_map/ppermute | solution.py:1409
  284.0 3.0 copy-start.52
  284.9 4.4 copy-start.53
  284.9 4.4 copy-start.55
  284.9 4.4 copy-start.57
  287.1 64.5 %copy-start.18 = (f32[64,2048]{1,0:T(8,128)}, f32[64,2048]{1,0:T(8,128)S(1)}, u32[]{:S(2)}) copy-start(f32[64,2048]{1,0:T(8,128)S(1)} %slice.178) | copy-start | bytes 1572868
  287.2 84.7 %copy-start.49 = (f32[1024]{0:T(1024)}, f32[1024]{0:T(1024)S(1)}, u32[]{:S(2)}) copy-start(f32[1024]{0:T(1024)S(1)} %reshape.466) | copy-start | bytes 12292
  287.4 108.5 %copy-start.50 = (f32[1024]{0:T(1024)}, f32[1024]{0:T(1024)S(1)}, u32[]{:S(2)}) copy-start(f32[1024]{0:T(1024)S(1)} %reshape.468) | copy-start | bytes 12292
  287.5 64.9 %copy-start.36 = (f32[2048]{0:T(1024)}, f32[2048]{0:T(1024)S(1)}, u32[]{:S(2)}) copy-start(f32[2048]{0:T(1024)S(1)} %reshape.469) | copy-start | bytes 24580
  289.3 56.4 %copy-start.24 = (f32[64,2304]{1,0:T(8,128)}, f32[64,2304]{1,0:T(8,128)S(1)}, u32[]{:S(2)}) copy-start(f32[64,2304]{1,0:T(8,128)S(1)} %get-tuple-element.230) | copy-start | bytes 1769476
  351.6 4.9 copy-start.16
  352.4 4.1 copy-start.59
  367.1 2.9 copy-start.23
  371.9 22.1 %copy-start.9 = (f32[512,1024]{1,0:T(8,128)}, f32[512,1024]{1,0:T(8,128)S(1)}, u32[]{:S(2)}) copy-start(f32[512,1024]{1,0:T(8,128)S(1)} %get-tuple-element.171.stream_ref) | copy-start | bytes 6291460
  511.8 15.2 %copy-start.11 = (f32[64,8192]{1,0:T(8,128)}, f32[64,8192]{1,0:T(8,128)S(1)}, u32[]{:S(2)}) copy-start(f32[64,8192]{1,0:T(8,128)S(1)} %reshape.483.direct_ref) | copy-start | bytes 6291460
  513.0 15.0 %copy-start.2 = (bf16[2048,1024]{1,0:T(8,128)(2,1)S(1)}, bf16[2048,1024]{1,0:T(8,128)(2,1)}, u32[]{:S(2)}) copy-start(bf16[2048,1024]{1,0:T(8,128)(2,1)} %copy-done.1) | copy-start | bytes 12582916
  513.0 15.0 %copy-start.13 = (f32[64,2048]{1,0:T(8,128)S(1)}, f32[64,2048]{1,0:T(8,128)}, u32[]{:S(2)}) copy-start(f32[64,2048]{1,0:T(8,128)} %copy-done.12) | copy-start | bytes 1572868
  513.0 15.0 %copy-start.37 = (f32[2048]{0:T(1024)S(1)}, f32[2048]{0:T(1024)}, u32[]{:S(2)}) copy-start(f32[2048]{0:T(1024)} %copy-done.36) | copy-start | bytes 24580
  513.0 15.0 %copy-start.60 = (f32[64]{0:T(128)S(1)}, f32[64]{0:T(128)}, u32[]{:S(2)}) copy-start(f32[64]{0:T(128)} %copy-done.59) | copy-start | bytes 772
  530.8 215.9 %copy-start.15 = (f32[64,2304]{1,0:T(8,128)S(1)}, f32[64,2304]{1,0:T(8,128)}, u32[]{:S(2)}) copy-start(f32[64,2304]{1,0:T(8,128)} %copy-done.14) | copy-start | bytes 1769476
  530.8 215.9 %copy-start.26 = (f32[64,2304]{1,0:T(8,128)S(1)}, f32[64,2304]{1,0:T(8,128)}, u32[]{:S(2)}) copy-start(f32[64,2304]{1,0:T(8,128)} %get-tuple-element.231) | copy-start | bytes 1769476
  530.8 216.0 %copy-start.33 = (f32[3,2304]{1,0:T(4,128)S(1)}, f32[3,2304]{1,0:T(4,128)}, u32[]{:S(2)}) copy-start(f32[3,2304]{1,0:T(4,128)} %copy-done.32) | copy-start | bytes 82948
  530.9 216.0 %copy-start.54 = (f32[64]{0:T(128)S(1)}, f32[64]{0:T(128)}, u32[]{:S(2)}) copy-start(f32[64]{0:T(128)} %copy-done.53) | copy-start | bytes 772
  530.9 216.0 %copy-start.56 = (f32[64]{0:T(128)S(1)}, f32[64]{0:T(128)}, u32[]{:S(2)}) copy-start(f32[64]{0:T(128)} %copy-done.55) | copy-start | bytes 772
  530.9 216.0 %copy-start.58 = (f32[64]{0:T(128)S(1)}, f32[64]{0:T(128)}, u32[]{:S(2)}) copy-start(f32[64]{0:T(128)} %copy-done.57) | copy-start | bytes 772
  749.1 2.8 copy-start.62
  749.2 3.5 copy-start.61
  749.2 4.2 copy-start.66
  749.2 4.3 copy-start.64
  749.2 4.3 collective-permute-start.1
  750.7 2.9 copy-start.48
  753.6 7.7 copy-start.25
  914.6 3.0 copy-start.35
  915.4 2.8 copy-start.28
  916.7 3.2 copy-start.38
  (32 other events, 54.6 us)
Sparse Core Ops, SparseCore 0:
  10.9 339.2 all-gather.5
  353.1 75.6 all-gather.3
  476.4 329.4 reduce-scatter.1

commit v6 on v5

--- a/solution.py
+++ b/solution.py
@@ -54,7 +54,7 @@
                     for r1 in range(2):
                         rx, ry = (r1, r2) if owner == 0 else (r2, r1)
                         for rz in range(self.depth):
-                            table[me, place] = index(z ^ rz, y ^ ry, x ^ rx, owner)
+                            table[me, place] = index((z + rz) % self.depth, y ^ ry, x ^ rx, owner)
                             place += 1
         self.table = table
 
@@ -347,6 +347,11 @@
         rz, r1, r2, rc = self.split(place)
         s1, s2 = r1 + rc * (r2 - r1), r2 + rc * (r1 - r2)
         return ((rc * 2 + s2) * 2 + s1) * self.depth + rz
+
+    def sum_steps(self):
+        steps = [(blocks, blocks, partner) for blocks, partner in self.halves()[:-4:-1]]
+        above = self.me + ((self.z + 1) % self.depth - self.z) * 8
+        return steps + [(block, 1, above) for block in range(self.depth - 1, 0, -1)]
 
     def halves(self):
         steps, bit = [], 1
@@ -560,7 +565,7 @@
 
 
 SUM_ROWS, SUM_COLUMNS, SUM_SLOTS = 32, 512, 8
-SUM_TIMES = [0, 1, 3, 4, 6, 7]
+SUM_TIMES = [0, 1, 3, 4, 5, 6, 7]
 
 
 def columns_of(chunk):
@@ -572,13 +577,13 @@
         self.here, self.sources, self.out = here, sources, out
         self.kept, self.sent, self.got = kept, sent, got
         self.send_sem, self.recv_sem = send_sem, recv_sem
-        self.steps = here.halves()[::-1]
+        self.steps = here.sum_steps()
         self.chunks = got.shape[0]
         self.times = self.chunks + SUM_TIMES[-1]
 
     def copy(self, chunk, step):
-        blocks, partner = self.steps[step]
-        cut = pl.ds(blocks * SUM_ROWS, blocks * SUM_ROWS)
+        first, blocks, partner = self.steps[step]
+        cut = pl.ds(first * SUM_ROWS, blocks * SUM_ROWS)
         return remote(
             self.sent.at[chunk % SUM_SLOTS, cut],
             self.got.at[chunk, cut],
@@ -613,16 +618,20 @@
                 self.kept[slot] = product(0)
 
     def go_on(self, chunk, step):
-        slot, rows = chunk % SUM_SLOTS, self.steps[step - 1][0] * SUM_ROWS
+        slot, (first, blocks, _) = chunk % SUM_SLOTS, self.steps[step - 1]
         self.copy(chunk, step - 1).wait_recv()
-        total = self.kept[slot, pl.ds(0, rows)] + self.got[chunk, pl.ds(rows, rows)].astype(F32)
+        got = self.got[chunk, pl.ds(first * SUM_ROWS, blocks * SUM_ROWS)].astype(F32)
+        start = (first - blocks) * SUM_ROWS
+        total = self.kept[slot, pl.ds(start, blocks * SUM_ROWS)] + got
         if step == len(self.steps):
             self.out(chunk, total)
             return
-        half = rows // 2
-        self.sent[slot, pl.ds(half, half)] = total[half:].astype(BF)
+        next_first, next_blocks, _ = self.steps[step]
+        sent = total[next_first * SUM_ROWS - start :][: next_blocks * SUM_ROWS]
+        self.sent[slot, pl.ds(next_first * SUM_ROWS, next_blocks * SUM_ROWS)] = sent.astype(BF)
         self.copy(chunk, step).start()
-        self.kept[slot, pl.ds(0, half)] = total[:half]
+        if blocks > 1:
+            self.kept[slot, pl.ds(0, next_first * SUM_ROWS)] = total[: next_first * SUM_ROWS]
 
     def at(self, time):
         for step in range(len(self.steps), -1, -1):
@@ -654,7 +663,7 @@
 
 
 def sums_scratch(n, chunks):
-    rows, phases = n * SUM_ROWS, n.bit_length() - 1
+    rows, phases = n * SUM_ROWS, n // 8 + 2
     return [
         pltpu.VMEM((SUM_SLOTS, rows // 2, SUM_COLUMNS), F32),
         pltpu.VMEM((SUM_SLOTS, rows, SUM_COLUMNS), BF),
@@ -1249,7 +1258,7 @@
     return out, both, d_stream, d_low, d_gain[0]
 
 
-ATTN_ROWS = 128
+ATTN_ROWS, BACK_ROWS = 128, 256
 
 
 def tile_mask():
@@ -1318,19 +1327,22 @@
         return jnp.where(first_head(), found[:ATTN_ROWS], found[ATTN_ROWS:])
 
     grads = dot_t(low_ref[...], whole_of(out_w_ref)).astype(BF)
-    for pair in range(AHEADS // 2):
-        lo, hi = pair * width, (pair + 1) * width
-        queries, key_rows, value_rows = [
-            triple_ref[:, part * D + lo : part * D + hi] for part in range(3)
-        ]
-        grad = grads[:, lo:hi]
-        key_rows = one_below_other(key_rows)
-        probs = pair_probs(queries, key_rows, mask)
-        d_probs = dot_t(grad, one_below_other(value_rows))
-        d_scores = (probs * (d_probs - by_head(probs * d_probs, jnp.sum))).astype(BF)
-        out_ref[:, lo:hi] = (scale * dot(d_scores, key_rows)).astype(BF)
-        out_ref[:, D + lo : D + hi] = (scale * of_keys(d_scores, queries)).astype(BF)
-        out_ref[:, 2 * D + lo : 2 * D + hi] = of_keys(probs.astype(BF), grad).astype(BF)
+    for first in range(0, BACK_ROWS, ATTN_ROWS):
+        rows = slice(first, first + ATTN_ROWS)
+        for pair in range(AHEADS // 2):
+            lo, hi = pair * width, (pair + 1) * width
+            queries, key_rows, value_rows = [
+                triple_ref[rows, part * D + lo : part * D + hi] for part in range(3)
+            ]
+            grad = grads[rows, lo:hi]
+            key_rows = one_below_other(key_rows)
+            probs = pair_probs(queries, key_rows, mask)
+            d_probs = dot_t(grad, one_below_other(value_rows))
+            d_scores = (probs * (d_probs - by_head(probs * d_probs, jnp.sum))).astype(BF)
+            out_ref[rows, lo:hi] = (scale * dot(d_scores, key_rows)).astype(BF)
+            out_ref[rows, D + lo : D + hi] = (scale * of_keys(d_scores, queries)).astype(BF)
+            d_values = of_keys(probs.astype(BF), grad)
+            out_ref[rows, 2 * D + lo : 2 * D + hi] = d_values.astype(BF)
 
     d_normed = None
     for part, ref in enumerate((q_ref, k_ref, v_ref)):
@@ -1354,8 +1366,8 @@
 
 def attention_back(triple, low, d_stream, stream, gain, flat):
     rows, n = triple.shape[0], flat.shape[0]
-    wide = pl.BlockSpec((ATTN_ROWS, 3 * D), lambda i: (i, 0))
-    tile = pl.BlockSpec((ATTN_ROWS, D), lambda i: (i, 0))
+    wide = pl.BlockSpec((BACK_ROWS, 3 * D), lambda i: (i, 0))
+    tile = pl.BlockSpec((BACK_ROWS, D), lambda i: (i, 0))
     narrow = pl.BlockSpec((1, D), lambda i: (0, 0))
 
     def block(place):
@@ -1363,7 +1375,7 @@
 
     d_triple, d_out, d_gain = pl.pallas_call(
         attention_back_kernel,
-        grid=(rows // ATTN_ROWS,),
+        grid=(rows // BACK_ROWS,),
         out_shape=[
             jax.ShapeDtypeStruct((rows, 3 * D), BF),
             jax.ShapeDtypeStruct((rows, D), F32),

time: 936 us -> 932 us (level)
  no operation moved by 1% of the time
where the time goes in v6:
time: 932 us; the launch traced here: 924 us
  Pallas kernels  808 us (87%)
  local copies, waits for them, and re-layouts  41.4 us (4%)
  other arithmetic  25.7 us (3%)
  matrix products  22 us (2%)
  between operations  16.2 us (2%)
    pallas_call x1, Pallas kernels, gather_weights(): pl.pallas_call(functools.partial(gather_kernel, n, chunks), out_shape=[ja...  251 us
    pallas_call x1, Pallas kernels, mixer_back(): pl.pallas_call(functools.partial(mixer_back_kernel, n), out_shape=[jax.Sh...  225 us
    pallas_call x1, Pallas kernels, last_sums(): pl.pallas_call(functools.partial(last_kernel, n), out_shape=[jax.ShapeDty...  131 us
    pallas_call x1, Pallas kernels, pass_states(): pl.pallas_call(functools.partial(states_kernel, n, reverse), out_shape=ja...  54.8 us
    pallas_call x1, Pallas kernels, feed_forward_back(): pl.pallas_call(feed_forward_back_kernel, grid=(tiles,), out_shape=[jax.Sh...  31 us
    pallas_call x1, Pallas kernels, attention_back(): pl.pallas_call(attention_back_kernel, grid=(rows // BACK_ROWS,), out_shap...  28.3 us
    pallas_call x3, Pallas kernels, flat_dot(): pl.pallas_call(flat_dot_kernel, grid=(count,), out_shape=jax.ShapeDtypeSt...  22.8 us
  transfers between devices with their start and end apart: 5, of which 1 were waited for; matrix products, arithmetic and copies ran while one was open for 8% of the time, Pallas kernels for 82%

profile of v6, /device:TPU:0, one launch (start us, length us, event | category | flops | bytes accessed | tf_op | source)
XLA Modules:
  0.0 924.0 jit_solution(12382653819547960260)
XLA Ops:
  7.3 2.6 shard_map.316
  11.6 251.3 %shard_map.314 = (bf16[1024,4480]{1,0:T(8,128)(2,1)S(1)}, bf16[2048,1024]{1,0:T(8,128)(2,1)S(1)}, bf16[512,128]{1,0:T(8,128)(2,1)S(1)}, f32[64,1024]{1,0:T(8,128)S(1)}, bf16[2048,256]{1,0:T(8,128)(2,1)S(1)}) custom-call(bf16[32,4480]{1,0:T(8,128)(2,1)S(1)} %pad.81.refs_0_, bf16[64,1024]{1,0:T(8,128)(2,1)S(1)} %copy-done.7, ...), custom_call_target="tpu_custom_call" | custom-call | bytes 33554432 | tf_op jit(solution)/shard_map/pallas_call | solution.py:540
  262.9 3.6 copy-done
  266.5 2.1 copy-done.1
  270.6 5.3 fusion.63
  276.1 2.3 collective-permute-start
  285.1 1.8 fusion.order_ref
  288.0 1.3 fusion.25
  290.7 54.8 %shard_map.315.state_ref = bf16[2048,128]{1,0:T(8,128)(2,1)S(1)} custom-call(bf16[2048,128]{1,0:T(8,128)(2,1)S(1)} %bitcast.81, f32[8,128]{1,0:T(8,128)S(1)} %scatter.6.logs_ref), custom_call_target="tpu_custom_call" | custom-call | flops 4194304 | bytes 2097152 | tf_op jit(solution)/shard_map/pallas_call | solution.py:916
  346.9 3.1 fusion.3
  350.0 1.5 copy.137
  352.8 3.7 fusion.4.values_ref
  356.5 10.6 %shard_map.317 = f32[64,8192]{1,0:T(8,128)} custom-call(bf16[64,1024]{1,0:T(8,128)(2,1)} %fusion.4.values_ref, bf16[32,640,1024]{2,1,0:T(8,128)(2,1)} %bitcast.82), custom_call_target="tpu_custom_call" | custom-call | flops 1073741824 | bytes 16777216 | tf_op jit(solution)/shard_map/pallas_call | solution.py:106
  367.1 2.9 reshape.478
  370.0 1.9 multiply_reduce_fusion.1
  371.9 1.4 multiply_convert_fusion.1.values_ref.normed_ref
  373.3 7.6 shard_map.318.triple_ref
  380.9 6.6 shard_map.319.values_ref.mixed_ref
  388.6 4.5 shard_map.320
  394.0 1.9 multiply_reduce_fusion
  395.9 1.3 copy-done.10
  397.2 1.2 multiply_convert_fusion.normed_ref
  398.4 15.3 %shard_map.321 = (bf16[512,4096]{1,0:T(8,128)(2,1)}, bf16[512,4096]{1,0:T(8,128)(2,1)}, bf16[512,4096]{1,0:T(8,128)(2,1)}) custom-call(bf16[512,1024]{1,0:T(8,128)(2,1)} %multiply_convert_fusion.normed_ref, bf16[32,640,1024]{2,1,0:T(8,128)(2,1)} %bitcast.85, bf16[32,640,1024]{2,1,0:T(8,128)(2,1)} %bitcast.86), custom_call_target="tpu_custom_call" | custom-call | flops 8589934592 | bytes 33554432 | tf_op jit(solution)/shard_map/pallas_call | solution.py:1170
  413.7 8.8 shard_map.322.flat_ref
  422.5 6.2 all-gather.4.cloned.1.call-done.down_ref
  428.8 31.0 %shard_map.323 = (bf16[512,1024]{1,0:T(8,128)(2,1)}, bf16[2,512,4096]{2,1,0:T(8,128)(2,1)}, f32[512,1024]{1,0:T(8,128)}, bf16[512,1024]{1,0:T(8,128)(2,1)}, f32[1,1024]{1,0:T(1,128)}) custom-call(bf16[512,1024]{1,0:T(8,128)(2,1)} %grad_ref.3, f32[512,1024]{1,0:T(8,128)} %copy-done.10, f32[1,1024]{1,0:T(1,128)} %bitcast.108, ...), custom_call_target="tpu_custom_call" | custom-call | flops 17179869184 | bytes 33554432 | tf_op jit(solution)/shard_map/pallas_call | solution.py:1232
  459.8 16.5 %shard_map.328 = bf16[32,384,1024]{2,1,0:T(8,128)(2,1)} custom-call(bf16[512,1024]{1,0:T(8,128)(2,1)} %multiply_convert_fusion.normed_ref, bf16[2,512,4096]{2,1,0:T(8,128)(2,1)} %get-tuple-element.205.both_ref, bf16[32,384,1024]{2,1,0:T(8,128)(2,1)} %shard_map.322.flat_ref), custom_call_target="tpu_custom_call", output_to_operand_aliasing={{}: (2, {})} | custom-call | flops 8589934592 | bytes 33554432 | tf_op jit(solution)/shard_map/pallas_call | solution.py:214
  476.3 1.4 fusion.60
  477.7 28.3 %shard_map.324 = (bf16[512,3072]{1,0:T(8,128)(2,1)}, f32[512,1024]{1,0:T(8,128)}, f32[1,1024]{1,0:T(1,128)}) custom-call(bf16[512,3072]{1,0:T(8,128)(2,1)} %shard_map.318.triple_ref, bf16[512,1024]{1,0:T(8,128)(2,1)} %get-tuple-element.169.low_ref.out_right_ref, f32[512,1024]{1,0:T(8,128)} %get-tuple-element.170.d_stream_ref, f32[512,1024]{1,0:T(8,128)} %copy-done.9, ...), custom_call_target="tpu_custom_call" | custom-call | flops 4294967296 | bytes 16777216 | tf_op jit(solution)/shard_map/pallas_call | solution.py:1376
  506.0 2.0 reshape.483.direct_ref
  508.0 1.2 convert_element_type.127.values_ref.slots_ref
  509.2 14.0 %shard_map.325 = f32[64,1024]{1,0:T(8,128)} custom-call(bf16[64,8192]{1,0:T(8,128)(2,1)} %convert_element_type.127.values_ref.slots_ref, bf16[32,640,1024]{2,1,0:T(8,128)(2,1)} %bitcast.93), custom_call_target="tpu_custom_call" | custom-call | flops 1073741824 | bytes 16777216 | tf_op jit(solution)/shard_map/pallas_call | solution.py:145
  523.3 1.0 convert_element_type.128
  524.3 1.5 multiply_reduce_fusion.6
  525.9 1.2 multiply_convert_fusion.2
  527.1 224.7 %shard_map.326 = (f32[64,2304]{1,0:T(8,128)}, f32[64,32]{1,0:T(8,128)}, f32[8,32]{1,0:T(8,128)}, f32[32,1024]{1,0:T(8,128)}, f32[32,3072]{1,0:T(8,128)}, /*index=5*/f32[32,8192]{1,0:T(8,128)}) custom-call(f32[8,128]{1,0:T(8,128)} %scatter.9.logs_ref, bf16[1024,1024]{1,0:T(8,128)(2,1)} %fusion.order_ref, bf16[512,1024]{1,0:T(8,128)(2,1)} %shard_map.319.values_ref.mixed_ref, ...), custom_call_target="tpu_custom_call" | custom-call | flops 4294967296 | bytes 16777216 | tf_op jit(solution)/shard_map/pallas_call | solution.py:1113
  752.0 1.9 fusion.56
  754.3 1.5 collective-permute-start.1
  759.0 6.7 multiply_reduce_fusion.9
  768.4 131.0 %shard_map.327 = (f32[256,1024]{1,0:T(8,128)}, f32[8,128]{1,0:T(8,128)}, f32[32,4384]{1,0:T(8,128)}, f32[64,1024]{1,0:T(8,128)}, bf16[64,8192]{1,0:T(8,128)(2,1)}) custom-call(bf16[64,1024]{1,0:T(8,128)(2,1)} %add_convert_fusion.grad_ref, bf16[2048,256]{1,0:T(8,128)(2,1)} %copy-done.8, f32[256,128]{1,0:T(8,128)} %reshape.493.small_ref, ...), custom_call_target="tpu_custom_call" | custom-call | flops 4294967296 | bytes 16777216 | tf_op jit(solution)/shard_map/pallas_call | solution.py:769
  900.1 1.3 split.50
  902.2 1.3 split.52
  903.4 2.3 reshape.494
  907.1 1.4 fusion.62
  908.5 1.2 slice.196
  909.7 1.1 copy.140
  912.2 1.0 copy.152
  914.6 1.0 copy.155
  (292 shorter events, 29.6 us)
Async XLA Ops:
  7.2 3.5 copy-start.67
  7.2 3.6 copy-start.22
  7.2 349.3 %all-gather.6.cloned.1.call-start = ((), (), s32[]{:S(2)}) async-start(), calls=%async_computation.3 | async-start | bytes 43253760 | tf_op jit(solution)/shard_map/all_gather | solution.py:89
  9.9 418.8 %all-gather.4.cloned.1.call-start = ((), (), s32[]{:S(2)}) async-start(), calls=%async_computation.1 | async-start | bytes 8650752 | tf_op jit(solution)/shard_map/all_gather | solution.py:1430
  10.7 897.8 %reduce-scatter.2.cloned.1.call-start = ((), (), s32[]{:S(2)}) async-start(), calls=%async_computation.2 | async-start | bytes 25952256 | tf_op jit(solution)/shard_map/reduce_scatter | solution.py:1533
  10.8 259.0 %copy-start.68 = (s32[64]{0:T(128)S(1)}, s32[64]{0:T(128)}, u32[]{:S(2)}) copy-start(s32[64]{0:T(128)} %param.24) | copy-start | bytes 772
  262.9 3.6 copy-start
  269.6 83.2 %copy-start.3 = (f32[64,1024]{1,0:T(8,128)}, f32[64,1024]{1,0:T(8,128)S(1)}, u32[]{:S(2)}) copy-start(f32[64,1024]{1,0:T(8,128)S(1)} %get-tuple-element.174) | copy-start | bytes 786436
  269.8 6.1 copy-start.47
  270.4 5.6 copy-start.63
  270.6 10.1 %copy-start.65 = (f32[3,32]{1,0:T(4,128)S(1)}, f32[3,32]{1,0:T(4,128)}, u32[]{:S(2)}) copy-start(f32[3,32]{1,0:T(4,128)} %head_ref.1) | copy-start | bytes 1156
  275.9 11.1 %copy-start.20 = (f32[64,4480]{1,0:T(8,128)}, f32[64,4480]{1,0:T(8,128)S(1)}, u32[]{:S(2)}) copy-start(f32[64,4480]{1,0:T(8,128)S(1)} %fusion.63) | copy-start | bytes 3440644
  276.0 12.0 %copy-start.14 = (f32[64,2304]{1,0:T(8,128)}, f32[64,2304]{1,0:T(8,128)S(1)}, u32[]{:S(2)}) copy-start(f32[64,2304]{1,0:T(8,128)S(1)} %fusion.36) | copy-start | bytes 1769476
  276.1 11.9 %collective-permute-start = (bf16[3,2304]{1,0:T(4,128)(2,1)S(1)}, bf16[3,2304]{1,0:T(4,128)(2,1)S(1)}, u32[]{:S(2)}, u32[]{:S(2)}) collective-permute-start(bf16[3,2304]{1,0:T(4,128)(2,1)S(1)} %fusion.39), channel_id=1, source_target_pairs={{0,1},{1,2},{2,3},{3,4},{4,5},{5,6},{6,7},{7,8},{8,9},{9,10},{10,1... | collective-permute-start | bytes 41480 | tf_op jit(solution)/shard_map/ppermute | solution.py:1421
  284.0 3.0 copy-start.52
  284.9 4.4 copy-start.53
  284.9 4.4 copy-start.55
  284.9 4.4 copy-start.57
  287.1 64.5 %copy-start.18 = (f32[64,2048]{1,0:T(8,128)}, f32[64,2048]{1,0:T(8,128)S(1)}, u32[]{:S(2)}) copy-start(f32[64,2048]{1,0:T(8,128)S(1)} %slice.178) | copy-start | bytes 1572868
  287.2 84.7 %copy-start.49 = (f32[1024]{0:T(1024)}, f32[1024]{0:T(1024)S(1)}, u32[]{:S(2)}) copy-start(f32[1024]{0:T(1024)S(1)} %reshape.466) | copy-start | bytes 12292
  287.4 108.5 %copy-start.50 = (f32[1024]{0:T(1024)}, f32[1024]{0:T(1024)S(1)}, u32[]{:S(2)}) copy-start(f32[1024]{0:T(1024)S(1)} %reshape.468) | copy-start | bytes 12292
  287.5 64.9 %copy-start.36 = (f32[2048]{0:T(1024)}, f32[2048]{0:T(1024)S(1)}, u32[]{:S(2)}) copy-start(f32[2048]{0:T(1024)S(1)} %reshape.469) | copy-start | bytes 24580
  289.3 56.4 %copy-start.24 = (f32[64,2304]{1,0:T(8,128)}, f32[64,2304]{1,0:T(8,128)S(1)}, u32[]{:S(2)}) copy-start(f32[64,2304]{1,0:T(8,128)S(1)} %get-tuple-element.230) | copy-start | bytes 1769476
  351.6 4.9 copy-start.16
  352.4 4.1 copy-start.59
  367.1 2.9 copy-start.23
  371.9 22.1 %copy-start.9 = (f32[512,1024]{1,0:T(8,128)}, f32[512,1024]{1,0:T(8,128)S(1)}, u32[]{:S(2)}) copy-start(f32[512,1024]{1,0:T(8,128)S(1)} %get-tuple-element.171.stream_ref) | copy-start | bytes 6291460
  508.0 15.3 %copy-start.11 = (f32[64,8192]{1,0:T(8,128)}, f32[64,8192]{1,0:T(8,128)S(1)}, u32[]{:S(2)}) copy-start(f32[64,8192]{1,0:T(8,128)S(1)} %reshape.483.direct_ref) | copy-start | bytes 6291460
  509.2 15.0 %copy-start.2 = (bf16[2048,1024]{1,0:T(8,128)(2,1)S(1)}, bf16[2048,1024]{1,0:T(8,128)(2,1)}, u32[]{:S(2)}) copy-start(bf16[2048,1024]{1,0:T(8,128)(2,1)} %copy-done.1) | copy-start | bytes 12582916
  509.2 15.0 %copy-start.13 = (f32[64,2048]{1,0:T(8,128)S(1)}, f32[64,2048]{1,0:T(8,128)}, u32[]{:S(2)}) copy-start(f32[64,2048]{1,0:T(8,128)} %copy-done.12) | copy-start | bytes 1572868
  509.2 15.1 %copy-start.37 = (f32[2048]{0:T(1024)S(1)}, f32[2048]{0:T(1024)}, u32[]{:S(2)}) copy-start(f32[2048]{0:T(1024)} %copy-done.36) | copy-start | bytes 24580
  509.2 15.1 %copy-start.60 = (f32[64]{0:T(128)S(1)}, f32[64]{0:T(128)}, u32[]{:S(2)}) copy-start(f32[64]{0:T(128)} %copy-done.59) | copy-start | bytes 772
  527.1 224.8 %copy-start.15 = (f32[64,2304]{1,0:T(8,128)S(1)}, f32[64,2304]{1,0:T(8,128)}, u32[]{:S(2)}) copy-start(f32[64,2304]{1,0:T(8,128)} %copy-done.14) | copy-start | bytes 1769476
  527.1 224.8 %copy-start.26 = (f32[64,2304]{1,0:T(8,128)S(1)}, f32[64,2304]{1,0:T(8,128)}, u32[]{:S(2)}) copy-start(f32[64,2304]{1,0:T(8,128)} %get-tuple-element.231) | copy-start | bytes 1769476
  527.1 224.8 %copy-start.33 = (f32[3,2304]{1,0:T(4,128)S(1)}, f32[3,2304]{1,0:T(4,128)}, u32[]{:S(2)}) copy-start(f32[3,2304]{1,0:T(4,128)} %copy-done.32) | copy-start | bytes 82948
  527.1 224.9 %copy-start.54 = (f32[64]{0:T(128)S(1)}, f32[64]{0:T(128)}, u32[]{:S(2)}) copy-start(f32[64]{0:T(128)} %copy-done.53) | copy-start | bytes 772
  527.1 224.9 %copy-start.56 = (f32[64]{0:T(128)S(1)}, f32[64]{0:T(128)}, u32[]{:S(2)}) copy-start(f32[64]{0:T(128)} %copy-done.55) | copy-start | bytes 772
  527.1 224.9 %copy-start.58 = (f32[64]{0:T(128)S(1)}, f32[64]{0:T(128)}, u32[]{:S(2)}) copy-start(f32[64]{0:T(128)} %copy-done.57) | copy-start | bytes 772
  754.3 3.0 copy-start.62
  754.3 3.8 copy-start.61
  754.3 4.5 copy-start.66
  754.3 4.6 copy-start.64
  754.3 4.6 collective-permute-start.1
  756.1 2.9 copy-start.48
  759.0 7.6 copy-start.25
  911.0 3.0 copy-start.35
  911.8 2.8 copy-start.28
  913.1 3.2 copy-start.38
  (32 other events, 55.1 us)
Sparse Core Ops, SparseCore 0:
  10.9 339.2 all-gather.5
  353.1 75.6 all-gather.3
  476.4 299.5 reduce-scatter.1

commit v7 on v6

--- a/solution.py
+++ b/solution.py
@@ -692,7 +692,7 @@
         device = here.device(place)
         small_kept[rows_of(place, 1, LOG_ROWS)] = small_ref[rows_of(device, 1, LOG_ROWS)]
 
-    turn(order_ref, left_ref, values_ref)
+    left_ref[0] = dot_t(order_ref[...], values_ref[0]).astype(BF)
     spare = d_in_ref.shape[1] % SUM_COLUMNS
 
     def store(chunk, total):
@@ -723,6 +723,9 @@
         told.start()
         copies += [gather, told]
         sums.run(2 * step, 2 * step + 2)
+        if step == 0:
+            for index in range(1, values_ref.shape[0]):
+                left_ref[index] = dot_t(order_ref[...], values_ref[index]).astype(BF)
         gather.wait_recv()
         told.wait_recv()
         small_kept[mine] = small_kept[mine] + small_got[cut]
@@ -977,8 +980,6 @@
     sums = Sums(Place(n), sources, store, *scratch[9:])
     exchange.tell()
     turn(order_ref, hidden_left, hidden_ref)
-    left_ref[0] = dot_t(order_ref[...], mixed_ref[...]).astype(BF)
-    left_ref[1] = dot_t(order_ref[...], normed_ref[...]).astype(BF)
 
     head_lane = lax.broadcasted_iota(jnp.int32, (1, MHEADS), 1)
     lanes = lax.broadcasted_iota(jnp.int32, (1, width), 1)
@@ -1044,6 +1045,8 @@
     dkeys_ref[...] = dot_fine(d_scores[...], queries_ref[...], TN)
     dqueries_ref[...] += dot_fine(d_scores[...], keys_ref[...], NN)
     exchange.start()
+    left_ref[0] = dot_t(order_ref[...], mixed_ref[...]).astype(BF)
+    left_ref[1] = dot_t(order_ref[...], normed_ref[...]).astype(BF)
     sums.run(16, 20)
     exchange.join()
     sums.run(20, 24)

time: 932 us -> 928 us (level)
  no operation moved by 1% of the time
where the time goes in v7:
time: 928 us; the launch traced here: 919 us
  Pallas kernels  803 us (87%)
  local copies, waits for them, and re-layouts  41.4 us (4%)
  other arithmetic  25.7 us (3%)
  matrix products  22 us (2%)
  between operations  16.2 us (2%)
    pallas_call x1, Pallas kernels, gather_weights(): pl.pallas_call(functools.partial(gather_kernel, n, chunks), out_shape=[ja...  251 us
    pallas_call x1, Pallas kernels, mixer_back(): pl.pallas_call(functools.partial(mixer_back_kernel, n), out_shape=[jax.Sh...  218 us
    pallas_call x1, Pallas kernels, last_sums(): pl.pallas_call(functools.partial(last_kernel, n), out_shape=[jax.ShapeDty...  133 us
    pallas_call x1, Pallas kernels, pass_states(): pl.pallas_call(functools.partial(states_kernel, n, reverse), out_shape=ja...  54.8 us
    pallas_call x1, Pallas kernels, feed_forward_back(): pl.pallas_call(feed_forward_back_kernel, grid=(tiles,), out_shape=[jax.Sh...  31 us
    pallas_call x1, Pallas kernels, attention_back(): pl.pallas_call(attention_back_kernel, grid=(rows // BACK_ROWS,), out_shap...  28.3 us
    pallas_call x3, Pallas kernels, flat_dot(): pl.pallas_call(flat_dot_kernel, grid=(count,), out_shape=jax.ShapeDtypeSt...  22.8 us
  transfers between devices with their start and end apart: 5, of which 1 were waited for; matrix products, arithmetic and copies ran while one was open for 8% of the time, Pallas kernels for 82%

profile of v7, /device:TPU:0, one launch (start us, length us, event | category | flops | bytes accessed | tf_op | source)
XLA Modules:
  0.0 919.4 jit_solution(13389335958377993222)
XLA Ops:
  7.3 2.6 shard_map.316
  11.6 251.3 %shard_map.314 = (bf16[1024,4480]{1,0:T(8,128)(2,1)S(1)}, bf16[2048,1024]{1,0:T(8,128)(2,1)S(1)}, bf16[512,128]{1,0:T(8,128)(2,1)S(1)}, f32[64,1024]{1,0:T(8,128)S(1)}, bf16[2048,256]{1,0:T(8,128)(2,1)S(1)}) custom-call(bf16[32,4480]{1,0:T(8,128)(2,1)S(1)} %pad.81.refs_0_, bf16[64,1024]{1,0:T(8,128)(2,1)S(1)} %copy-done.7, ...), custom_call_target="tpu_custom_call" | custom-call | bytes 33554432 | tf_op jit(solution)/shard_map/pallas_call | solution.py:540
  262.9 3.6 copy-done
  266.5 2.1 copy-done.1
  270.6 5.3 fusion.63
  276.1 2.3 collective-permute-start
  285.1 1.8 fusion.order_ref
  288.0 1.3 fusion.25
  290.7 54.8 %shard_map.315.state_ref = bf16[2048,128]{1,0:T(8,128)(2,1)S(1)} custom-call(bf16[2048,128]{1,0:T(8,128)(2,1)S(1)} %bitcast.81, f32[8,128]{1,0:T(8,128)S(1)} %scatter.6.logs_ref), custom_call_target="tpu_custom_call" | custom-call | flops 4194304 | bytes 2097152 | tf_op jit(solution)/shard_map/pallas_call | solution.py:919
  346.9 3.1 fusion.3
  350.0 1.5 copy.137
  352.8 3.7 fusion.4.values_ref
  356.5 10.6 %shard_map.317 = f32[64,8192]{1,0:T(8,128)} custom-call(bf16[64,1024]{1,0:T(8,128)(2,1)} %fusion.4.values_ref, bf16[32,640,1024]{2,1,0:T(8,128)(2,1)} %bitcast.82), custom_call_target="tpu_custom_call" | custom-call | flops 1073741824 | bytes 16777216 | tf_op jit(solution)/shard_map/pallas_call | solution.py:106
  367.1 2.9 reshape.478
  370.0 1.9 multiply_reduce_fusion.1
  371.9 1.4 multiply_convert_fusion.1.values_ref.normed_ref
  373.3 7.6 shard_map.318.triple_ref
  380.9 6.6 shard_map.319.values_ref.mixed_ref
  388.6 4.5 shard_map.320
  394.0 1.9 multiply_reduce_fusion
  395.9 1.3 copy-done.10
  397.2 1.2 multiply_convert_fusion.normed_ref
  398.4 15.3 %shard_map.321 = (bf16[512,4096]{1,0:T(8,128)(2,1)}, bf16[512,4096]{1,0:T(8,128)(2,1)}, bf16[512,4096]{1,0:T(8,128)(2,1)}) custom-call(bf16[512,1024]{1,0:T(8,128)(2,1)} %multiply_convert_fusion.normed_ref, bf16[32,640,1024]{2,1,0:T(8,128)(2,1)} %bitcast.85, bf16[32,640,1024]{2,1,0:T(8,128)(2,1)} %bitcast.86), custom_call_target="tpu_custom_call" | custom-call | flops 8589934592 | bytes 33554432 | tf_op jit(solution)/shard_map/pallas_call | solution.py:1173
  413.7 8.8 shard_map.322.flat_ref
  422.5 6.2 all-gather.4.cloned.1.call-done.down_ref
  428.8 31.0 %shard_map.323 = (bf16[512,1024]{1,0:T(8,128)(2,1)}, bf16[2,512,4096]{2,1,0:T(8,128)(2,1)}, f32[512,1024]{1,0:T(8,128)}, bf16[512,1024]{1,0:T(8,128)(2,1)}, f32[1,1024]{1,0:T(1,128)}) custom-call(bf16[512,1024]{1,0:T(8,128)(2,1)} %grad_ref.3, f32[512,1024]{1,0:T(8,128)} %copy-done.10, f32[1,1024]{1,0:T(1,128)} %bitcast.108, ...), custom_call_target="tpu_custom_call" | custom-call | flops 17179869184 | bytes 33554432 | tf_op jit(solution)/shard_map/pallas_call | solution.py:1235
  459.8 16.5 %shard_map.328 = bf16[32,384,1024]{2,1,0:T(8,128)(2,1)} custom-call(bf16[512,1024]{1,0:T(8,128)(2,1)} %multiply_convert_fusion.normed_ref, bf16[2,512,4096]{2,1,0:T(8,128)(2,1)} %get-tuple-element.205.both_ref, bf16[32,384,1024]{2,1,0:T(8,128)(2,1)} %shard_map.322.flat_ref), custom_call_target="tpu_custom_call", output_to_operand_aliasing={{}: (2, {})} | custom-call | flops 8589934592 | bytes 33554432 | tf_op jit(solution)/shard_map/pallas_call | solution.py:214
  476.3 1.4 fusion.60
  477.7 28.3 %shard_map.324 = (bf16[512,3072]{1,0:T(8,128)(2,1)}, f32[512,1024]{1,0:T(8,128)}, f32[1,1024]{1,0:T(1,128)}) custom-call(bf16[512,3072]{1,0:T(8,128)(2,1)} %shard_map.318.triple_ref, bf16[512,1024]{1,0:T(8,128)(2,1)} %get-tuple-element.169.low_ref.out_right_ref, f32[512,1024]{1,0:T(8,128)} %get-tuple-element.170.d_stream_ref, f32[512,1024]{1,0:T(8,128)} %copy-done.9, ...), custom_call_target="tpu_custom_call" | custom-call | flops 4294967296 | bytes 16777216 | tf_op jit(solution)/shard_map/pallas_call | solution.py:1379
  506.0 2.0 reshape.483.direct_ref
  508.0 1.2 convert_element_type.127.values_ref.slots_ref
  509.2 14.0 %shard_map.325 = f32[64,1024]{1,0:T(8,128)} custom-call(bf16[64,8192]{1,0:T(8,128)(2,1)} %convert_element_type.127.values_ref.slots_ref, bf16[32,640,1024]{2,1,0:T(8,128)(2,1)} %bitcast.93), custom_call_target="tpu_custom_call" | custom-call | flops 1073741824 | bytes 16777216 | tf_op jit(solution)/shard_map/pallas_call | solution.py:145
  523.3 1.0 convert_element_type.128
  524.3 1.5 multiply_reduce_fusion.6
  525.9 1.2 multiply_convert_fusion.2
  527.1 218.0 %shard_map.326 = (f32[64,2304]{1,0:T(8,128)}, f32[64,32]{1,0:T(8,128)}, f32[8,32]{1,0:T(8,128)}, f32[32,1024]{1,0:T(8,128)}, f32[32,3072]{1,0:T(8,128)}, /*index=5*/f32[32,8192]{1,0:T(8,128)}) custom-call(f32[8,128]{1,0:T(8,128)} %scatter.9.logs_ref, bf16[1024,1024]{1,0:T(8,128)(2,1)} %fusion.order_ref, bf16[512,1024]{1,0:T(8,128)(2,1)} %shard_map.319.values_ref.mixed_ref, ...), custom_call_target="tpu_custom_call" | custom-call | flops 4294967296 | bytes 16777216 | tf_op jit(solution)/shard_map/pallas_call | solution.py:1116
  745.2 1.9 fusion.56
  747.6 1.5 collective-permute-start.1
  752.3 6.6 multiply_reduce_fusion.9
  761.6 133.2 %shard_map.327 = (f32[256,1024]{1,0:T(8,128)}, f32[8,128]{1,0:T(8,128)}, f32[32,4384]{1,0:T(8,128)}, f32[64,1024]{1,0:T(8,128)}, bf16[64,8192]{1,0:T(8,128)(2,1)}) custom-call(bf16[64,1024]{1,0:T(8,128)(2,1)} %add_convert_fusion.grad_ref, bf16[2048,256]{1,0:T(8,128)(2,1)} %copy-done.8, f32[256,128]{1,0:T(8,128)} %reshape.493.small_ref, ...), custom_call_target="tpu_custom_call" | custom-call | flops 4294967296 | bytes 16777216 | tf_op jit(solution)/shard_map/pallas_call | solution.py:772
  895.5 1.3 split.50
  897.6 1.3 split.52
  898.8 2.3 reshape.494
  902.5 1.4 fusion.62
  903.9 1.2 slice.196
  905.1 1.1 copy.140
  907.5 1.0 copy.152
  910.0 1.0 copy.155
  (292 shorter events, 29.6 us)
Async XLA Ops:
  7.2 3.5 copy-start.67
  7.2 3.6 copy-start.22
  7.2 349.3 %all-gather.6.cloned.1.call-start = ((), (), s32[]{:S(2)}) async-start(), calls=%async_computation.3 | async-start | bytes 43253760 | tf_op jit(solution)/shard_map/all_gather | solution.py:89
  9.9 418.8 %all-gather.4.cloned.1.call-start = ((), (), s32[]{:S(2)}) async-start(), calls=%async_computation.1 | async-start | bytes 8650752 | tf_op jit(solution)/shard_map/all_gather | solution.py:1433
  10.7 893.2 %reduce-scatter.2.cloned.1.call-start = ((), (), s32[]{:S(2)}) async-start(), calls=%async_computation.2 | async-start | bytes 25952256 | tf_op jit(solution)/shard_map/reduce_scatter | solution.py:1536
  10.8 259.0 %copy-start.68 = (s32[64]{0:T(128)S(1)}, s32[64]{0:T(128)}, u32[]{:S(2)}) copy-start(s32[64]{0:T(128)} %param.24) | copy-start | bytes 772
  262.9 3.6 copy-start
  269.6 83.2 %copy-start.3 = (f32[64,1024]{1,0:T(8,128)}, f32[64,1024]{1,0:T(8,128)S(1)}, u32[]{:S(2)}) copy-start(f32[64,1024]{1,0:T(8,128)S(1)} %get-tuple-element.174) | copy-start | bytes 786436
  269.8 6.1 copy-start.47
  270.4 5.6 copy-start.63
  270.6 10.1 %copy-start.65 = (f32[3,32]{1,0:T(4,128)S(1)}, f32[3,32]{1,0:T(4,128)}, u32[]{:S(2)}) copy-start(f32[3,32]{1,0:T(4,128)} %head_ref.1) | copy-start | bytes 1156
  275.9 11.1 %copy-start.20 = (f32[64,4480]{1,0:T(8,128)}, f32[64,4480]{1,0:T(8,128)S(1)}, u32[]{:S(2)}) copy-start(f32[64,4480]{1,0:T(8,128)S(1)} %fusion.63) | copy-start | bytes 3440644
  276.0 12.0 %copy-start.14 = (f32[64,2304]{1,0:T(8,128)}, f32[64,2304]{1,0:T(8,128)S(1)}, u32[]{:S(2)}) copy-start(f32[64,2304]{1,0:T(8,128)S(1)} %fusion.36) | copy-start | bytes 1769476
  276.1 11.9 %collective-permute-start = (bf16[3,2304]{1,0:T(4,128)(2,1)S(1)}, bf16[3,2304]{1,0:T(4,128)(2,1)S(1)}, u32[]{:S(2)}, u32[]{:S(2)}) collective-permute-start(bf16[3,2304]{1,0:T(4,128)(2,1)S(1)} %fusion.39), channel_id=1, source_target_pairs={{0,1},{1,2},{2,3},{3,4},{4,5},{5,6},{6,7},{7,8},{8,9},{9,10},{10,1... | collective-permute-start | bytes 41480 | tf_op jit(solution)/shard_map/ppermute | solution.py:1424
  284.0 3.0 copy-start.52
  284.9 4.4 copy-start.53
  284.9 4.4 copy-start.55
  284.9 4.4 copy-start.57
  287.1 64.5 %copy-start.18 = (f32[64,2048]{1,0:T(8,128)}, f32[64,2048]{1,0:T(8,128)S(1)}, u32[]{:S(2)}) copy-start(f32[64,2048]{1,0:T(8,128)S(1)} %slice.178) | copy-start | bytes 1572868
  287.2 84.7 %copy-start.49 = (f32[1024]{0:T(1024)}, f32[1024]{0:T(1024)S(1)}, u32[]{:S(2)}) copy-start(f32[1024]{0:T(1024)S(1)} %reshape.466) | copy-start | bytes 12292
  287.4 108.5 %copy-start.50 = (f32[1024]{0:T(1024)}, f32[1024]{0:T(1024)S(1)}, u32[]{:S(2)}) copy-start(f32[1024]{0:T(1024)S(1)} %reshape.468) | copy-start | bytes 12292
  287.5 64.9 %copy-start.36 = (f32[2048]{0:T(1024)}, f32[2048]{0:T(1024)S(1)}, u32[]{:S(2)}) copy-start(f32[2048]{0:T(1024)S(1)} %reshape.469) | copy-start | bytes 24580
  289.3 56.4 %copy-start.24 = (f32[64,2304]{1,0:T(8,128)}, f32[64,2304]{1,0:T(8,128)S(1)}, u32[]{:S(2)}) copy-start(f32[64,2304]{1,0:T(8,128)S(1)} %get-tuple-element.230) | copy-start | bytes 1769476
  351.6 4.9 copy-start.16
  352.4 4.1 copy-start.59
  367.1 2.9 copy-start.23
  371.9 22.1 %copy-start.9 = (f32[512,1024]{1,0:T(8,128)}, f32[512,1024]{1,0:T(8,128)S(1)}, u32[]{:S(2)}) copy-start(f32[512,1024]{1,0:T(8,128)S(1)} %get-tuple-element.171.stream_ref) | copy-start | bytes 6291460
  508.0 15.3 %copy-start.11 = (f32[64,8192]{1,0:T(8,128)}, f32[64,8192]{1,0:T(8,128)S(1)}, u32[]{:S(2)}) copy-start(f32[64,8192]{1,0:T(8,128)S(1)} %reshape.483.direct_ref) | copy-start | bytes 6291460
  509.2 15.0 %copy-start.2 = (bf16[2048,1024]{1,0:T(8,128)(2,1)S(1)}, bf16[2048,1024]{1,0:T(8,128)(2,1)}, u32[]{:S(2)}) copy-start(bf16[2048,1024]{1,0:T(8,128)(2,1)} %copy-done.1) | copy-start | bytes 12582916
  509.2 15.0 %copy-start.13 = (f32[64,2048]{1,0:T(8,128)S(1)}, f32[64,2048]{1,0:T(8,128)}, u32[]{:S(2)}) copy-start(f32[64,2048]{1,0:T(8,128)} %copy-done.12) | copy-start | bytes 1572868
  509.2 15.1 %copy-start.37 = (f32[2048]{0:T(1024)S(1)}, f32[2048]{0:T(1024)}, u32[]{:S(2)}) copy-start(f32[2048]{0:T(1024)} %copy-done.36) | copy-start | bytes 24580
  509.2 15.1 %copy-start.60 = (f32[64]{0:T(128)S(1)}, f32[64]{0:T(128)}, u32[]{:S(2)}) copy-start(f32[64]{0:T(128)} %copy-done.59) | copy-start | bytes 772
  527.1 218.1 %copy-start.15 = (f32[64,2304]{1,0:T(8,128)S(1)}, f32[64,2304]{1,0:T(8,128)}, u32[]{:S(2)}) copy-start(f32[64,2304]{1,0:T(8,128)} %copy-done.14) | copy-start | bytes 1769476
  527.1 218.1 %copy-start.26 = (f32[64,2304]{1,0:T(8,128)S(1)}, f32[64,2304]{1,0:T(8,128)}, u32[]{:S(2)}) copy-start(f32[64,2304]{1,0:T(8,128)} %get-tuple-element.231) | copy-start | bytes 1769476
  527.1 218.1 %copy-start.33 = (f32[3,2304]{1,0:T(4,128)S(1)}, f32[3,2304]{1,0:T(4,128)}, u32[]{:S(2)}) copy-start(f32[3,2304]{1,0:T(4,128)} %copy-done.32) | copy-start | bytes 82948
  527.1 218.1 %copy-start.54 = (f32[64]{0:T(128)S(1)}, f32[64]{0:T(128)}, u32[]{:S(2)}) copy-start(f32[64]{0:T(128)} %copy-done.53) | copy-start | bytes 772
  527.1 218.1 %copy-start.56 = (f32[64]{0:T(128)S(1)}, f32[64]{0:T(128)}, u32[]{:S(2)}) copy-start(f32[64]{0:T(128)} %copy-done.55) | copy-start | bytes 772
  527.1 218.1 %copy-start.58 = (f32[64]{0:T(128)S(1)}, f32[64]{0:T(128)}, u32[]{:S(2)}) copy-start(f32[64]{0:T(128)} %copy-done.57) | copy-start | bytes 772
  747.5 3.0 copy-start.62
  747.5 3.8 copy-start.61
  747.5 4.5 copy-start.66
  747.6 4.6 copy-start.64
  747.6 4.6 collective-permute-start.1
  749.4 2.9 copy-start.48
  752.3 7.6 copy-start.25
  906.4 3.0 copy-start.35
  907.2 2.8 copy-start.28
  908.5 3.2 copy-start.38
  (32 other events, 55.1 us)
Sparse Core Ops, SparseCore 0:
  10.9 339.2 all-gather.5
  353.1 75.6 all-gather.3
  476.4 300.2 reduce-scatter.1
